TPU v7x, 32 devices: a whole 2x2x4 slice. The times are simulated.
32 devices in a mesh: dp: 8 (over z, x), row: 2 (over y), col: 2 (over core).
Axes of the slice: x: 2, y: 2, z: 4, core: 2. Of those that a mesh axis runs over, the one named last changes fastest.
Arguments:
- hidden_in: bfloat16 [16384, 960], P(('dp', 'row'), 'col'), may hold values from -6 to 6
- query_weight: bfloat16 [960, 2, 576], P('col', 'row'), may hold values from -0.1875 to 0.1875
- key_weight: bfloat16 [960, 2, 192], P('col', 'row'), may hold values from -0.1875 to 0.1875
- value_weight: bfloat16 [960, 2, 192], P('col', 'row'), may hold values from -0.1875 to 0.1875
- output_weight: bfloat16 [2, 576, 960], P('row', None, 'col'), may hold values from -1.5 to 1.5
- gate_weight: bfloat16 [960, 2560], P('col', 'row'), may hold values from -0.1875 to 0.1875
- up_weight: bfloat16 [960, 2560], P('col', 'row'), may hold values from -0.1875 to 0.1875
- down_weight: bfloat16 [2560, 960], P('row', 'col'), may hold values from -0.125 to 0.125
- attn_gain: bfloat16 [960], P('col'), may hold values from 0.5 to 1.5
- ffn_gain: bfloat16 [960], P('col'), may hold values from 0.5 to 1.5
- out_grad: bfloat16 [16384, 960], P(('dp', 'row'), 'col'), may hold values from -6 to 6
- segment_ids: int32 [16384], P(('dp', 'col')), may hold values from 0 to 15, as said below
Outputs:
- block_out: bfloat16 [16384, 960], P(('dp', 'row'), 'col')
- input_grad: bfloat16 [16384, 960], P(('dp', 'row'), 'col')
- query_weight_grad: float32 [960, 2, 576], P('col', 'row')
- key_weight_grad: float32 [960, 2, 192], P('col', 'row')
- value_weight_grad: float32 [960, 2, 192], P('col', 'row')
- output_weight_grad: float32 [2, 576, 960], P('row', None, 'col')
- gate_weight_grad: float32 [960, 2560], P('col', 'row')
- up_weight_grad: float32 [960, 2560], P('col', 'row')
- down_weight_grad: float32 [2560, 960], P('row', 'col')
- attn_gain_grad: float32 [960], P('col')
- ffn_gain_grad: float32 [960], P('col')
Inputs may be any that keep to these rules, and one draw needn't show every extreme that they name: `segment_ids`: inside each aligned window of 1024 tokens the ids start at 0 and rise by one where a new sequence begins, so no sequence crosses a window's edge; some window holds a single sequence of 1024 tokens.
All inputs are finite; a program needn't handle non-finite values.
Results may differ from a plain program's by a relative error of at most 0.013.
Values may be sent and summed in bfloat16 or wider, within the bound.
No kernel may reach another device: no remote copies, remote signals or barrier semaphores. Data moves between devices by JAX's collectives and lax.ppermute only.
A program may use at most 256 MiB of HBM per device.

v0:
```python
import math

import jax
import jax.numpy as jnp
from jax import lax
from jax.sharding import PartitionSpec as P

D = 960
HEADS = 15
HDIM = 64
MAXLEN = 1024


NORM_EPS = 1e-05
ROPE_BASE = 100000.0
MASKED_SCORE = -1e30


def matmul(left, right, left_dim, right_dim):
    return lax.dot_general(
        left, right, (((left_dim,), (right_dim,)), ((), ())), preferred_element_type=jnp.float32
    )


def row_tokens(piece_rows):
    return lax.all_gather(piece_rows, "row", axis=0, tiled=True)


def col_tokens(piece_rows):
    return lax.all_gather(piece_rows, "col", axis=0, tiled=True)


def col_partial(gathered, weight, weight_dim):
    return lax.psum_scatter(
        matmul(gathered, weight, 1, weight_dim), "col", scatter_dimension=0, tiled=True
    )


def row_partial(gathered, weight, weight_dim):
    return lax.psum_scatter(
        matmul(gathered, weight, 1, weight_dim), "row", scatter_dimension=0, tiled=True
    )


def feature_total(values):
    return lax.psum(values, "col")


def positions_of(segment):
    position_index = jnp.arange(segment.shape[0], dtype=jnp.int32)
    is_start = jnp.concatenate([jnp.ones((1,), dtype=bool), segment[1:] != segment[:-1]])
    seg_begin = lax.cummax(
        jnp.where(is_start, position_index, jnp.zeros_like(position_index)), axis=0
    )
    return position_index - seg_begin


def rope_tables(position):
    half_dim = HDIM // 2
    frequency = ROPE_BASE ** (-(jnp.arange(half_dim, dtype=jnp.float32) * 2.0 / HDIM))
    angles = position.astype(jnp.float32)[:, None] * frequency[None, :]
    cosine_table = jnp.concatenate([jnp.cos(angles), jnp.cos(angles)], axis=1)
    sine_table = jnp.concatenate([jnp.sin(angles), jnp.sin(angles)], axis=1)
    return (cosine_table, sine_table)


def rotate(heads_in, cosine_table, sine_table):
    half_dim = heads_in.shape[-1] // 2
    turned = jnp.concatenate([-heads_in[..., half_dim:], heads_in[..., :half_dim]], axis=-1)
    return heads_in * cosine_table[:, None, :] + turned * sine_table[:, None, :]


def rotate_back(heads_in, cosine_table, sine_table):
    half_dim = heads_in.shape[-1] // 2
    sined = heads_in * sine_table[:, None, :]
    turned = jnp.concatenate([sined[..., half_dim:], -sined[..., :half_dim]], axis=-1)
    return heads_in * cosine_table[:, None, :] + turned


def allowed_pairs(segment):
    position_index = jnp.arange(segment.shape[0], dtype=jnp.int32)
    return (segment[:, None] == segment[None, :]) & (
        position_index[None, :] <= position_index[:, None]
    )


def window_scores(grouped, key_heads, segment):
    score_scale = 1.0 / math.sqrt(grouped.shape[-1])
    scores = (
        jnp.einsum("qgjd,kgd->gjqk", grouped, key_heads, preferred_element_type=jnp.float32)
        * score_scale
    )
    return jnp.where(allowed_pairs(segment)[None, None], scores, MASKED_SCORE)


def attend(packed):
    queries, key_heads, values, segment = packed
    span_rows = queries.shape[0]
    grouped = queries.reshape(span_rows, key_heads.shape[1], -1, queries.shape[2])
    scores = window_scores(grouped, key_heads, segment)
    highest = jnp.max(scores, axis=-1, keepdims=True)
    weights_exp = jnp.exp(scores - highest)
    row_total = jnp.sum(weights_exp, axis=-1, keepdims=True)
    probs_low = (weights_exp / row_total).astype(jnp.bfloat16)
    mixture = jnp.einsum("gjqk,kgd->qgjd", probs_low, values, preferred_element_type=jnp.float32)
    return (
        mixture.reshape(span_rows, -1, queries.shape[2]),
        (highest + jnp.log(row_total))[..., 0],
    )


def attend_back(packed):
    queries, key_heads, values, segment, log_total, grad_mixture = packed
    span_rows = queries.shape[0]
    score_scale = 1.0 / math.sqrt(queries.shape[2])
    grouped = queries.reshape(span_rows, key_heads.shape[1], -1, queries.shape[2])
    grad_grouped = grad_mixture.reshape(grouped.shape)
    scores = window_scores(grouped, key_heads, segment)
    probability = jnp.exp(scores - log_total[..., None])
    probs_low = probability.astype(jnp.bfloat16)
    grad_values = jnp.einsum(
        "gjqk,qgjd->kgd", probs_low, grad_grouped, preferred_element_type=jnp.float32
    )
    grad_probs = jnp.einsum(
        "qgjd,kgd->gjqk", grad_grouped, values, preferred_element_type=jnp.float32
    )
    inner_sum = jnp.sum(grad_probs * probability, axis=-1, keepdims=True)
    grad_scores = (probability * (grad_probs - inner_sum)).astype(jnp.bfloat16)
    grad_queries = (
        jnp.einsum("gjqk,kgd->qgjd", grad_scores, key_heads, preferred_element_type=jnp.float32)
        * score_scale
    )
    grad_keys = (
        jnp.einsum("gjqk,qgjd->kgd", grad_scores, grouped, preferred_element_type=jnp.float32)
        * score_scale
    )
    return (grad_queries.reshape(span_rows, -1, queries.shape[2]), grad_keys, grad_values)


def per_device(
    hidden_in,
    query_weight,
    key_weight,
    value_weight,
    output_weight,
    gate_weight,
    up_weight,
    down_weight,
    attn_gain,
    ffn_gain,
    out_grad,
    segment_ids,
):
    slot_heads = query_weight.shape[2] // HDIM
    slot_kv = key_weight.shape[2] // HDIM
    slot_index = lax.axis_index("row")
    live_heads = (
        jnp.arange(slot_heads) < slot_heads - slot_index * (2 * slot_heads - HEADS)
    ).astype(jnp.float32)
    joined_weight = jnp.concatenate(
        [query_weight[:, 0], key_weight[:, 0], value_weight[:, 0]], axis=1
    )
    out_weight = output_weight[0]
    mlp_weight = jnp.concatenate([gate_weight, up_weight], axis=1)
    ff_half = gate_weight.shape[1]
    query_cols = slot_heads * HDIM
    key_cols = slot_kv * HDIM
    gain_in = attn_gain.astype(jnp.float32)
    gain_mid = ffn_gain.astype(jnp.float32)
    residual = hidden_in.astype(jnp.float32)
    level_in = lax.rsqrt(feature_total(jnp.sum(residual * residual, axis=1)) / D + NORM_EPS)[
        :, None
    ]
    normed_in = (residual * level_in * gain_in).astype(jnp.bfloat16)
    rows_in = row_tokens(normed_in)
    joined = col_partial(rows_in, joined_weight, 0)
    tokens = joined.shape[0]
    windows = tokens // MAXLEN
    segment_win = segment_ids.reshape(windows, MAXLEN)
    position = jax.vmap(positions_of)(segment_win).reshape(tokens)
    cosine_table, sine_table = rope_tables(position)
    queries = rotate(
        joined[:, :query_cols].reshape(tokens, slot_heads, HDIM), cosine_table, sine_table
    ).astype(jnp.bfloat16)
    key_heads = rotate(
        joined[:, query_cols : query_cols + key_cols].reshape(tokens, slot_kv, HDIM),
        cosine_table,
        sine_table,
    ).astype(jnp.bfloat16)
    values = joined[:, query_cols + key_cols :].reshape(tokens, slot_kv, HDIM).astype(jnp.bfloat16)

    def windowed(array_in):
        return array_in.reshape((windows, MAXLEN) + array_in.shape[1:])

    mixture, log_total = lax.map(
        attend, (windowed(queries), windowed(key_heads), windowed(values), segment_win)
    )
    attended = (
        (mixture.reshape(tokens, slot_heads, HDIM) * live_heads[None, :, None])
        .reshape(tokens, query_cols)
        .astype(jnp.bfloat16)
    )
    rows_att = col_tokens(attended)
    residual_mid = residual + row_partial(rows_att, out_weight, 0)
    level_mid = lax.rsqrt(
        feature_total(jnp.sum(residual_mid * residual_mid, axis=1)) / D + NORM_EPS
    )[:, None]
    normed_mid = (residual_mid * level_mid * gain_mid).astype(jnp.bfloat16)
    rows_mid = row_tokens(normed_mid)
    gate_up = col_partial(rows_mid, mlp_weight, 0)
    gate_part = gate_up[:, :ff_half]
    up_part = gate_up[:, ff_half:]
    sigmoid_gate = jax.nn.sigmoid(gate_part)
    active = (gate_part * sigmoid_gate * up_part).astype(jnp.bfloat16)
    rows_act = col_tokens(active)
    block_out = (residual_mid + row_partial(rows_act, down_weight, 0)).astype(jnp.bfloat16)
    grad_top = out_grad.astype(jnp.float32)
    rows_grad = row_tokens(out_grad)
    grad_active = col_partial(rows_grad, down_weight, 1)
    grad_down = matmul(rows_act, rows_grad, 0, 0)
    grad_gate = grad_active * up_part * sigmoid_gate * (1.0 + gate_part * (1.0 - sigmoid_gate))
    grad_up = grad_active * gate_part * sigmoid_gate
    grad_gate_up = jnp.concatenate([grad_gate, grad_up], axis=1).astype(jnp.bfloat16)
    rows_gate_up = col_tokens(grad_gate_up)
    grad_normed_mid = row_partial(rows_gate_up, mlp_weight, 1)
    grad_mlp = matmul(rows_mid, rows_gate_up, 0, 0)
    scaled_mid = grad_normed_mid * gain_mid
    grad_gain_mid = jnp.sum(grad_normed_mid * residual_mid * level_mid, axis=0)
    inner_mid = feature_total(jnp.sum(scaled_mid * residual_mid, axis=1))[:, None]
    grad_mid = grad_top + scaled_mid * level_mid - residual_mid * level_mid**3 * inner_mid / D
    grad_branch = grad_mid.astype(jnp.bfloat16)
    rows_branch = row_tokens(grad_branch)
    grad_attended = col_partial(rows_branch, out_weight, 1)
    grad_out_weight = matmul(rows_att, rows_branch, 0, 0)
    grad_mixture = (
        grad_attended.reshape(tokens, slot_heads, HDIM) * live_heads[None, :, None]
    ).astype(jnp.bfloat16)
    grad_queries, grad_keys, grad_values = lax.map(
        attend_back,
        (
            windowed(queries),
            windowed(key_heads),
            windowed(values),
            segment_win,
            log_total,
            windowed(grad_mixture),
        ),
    )
    grad_joined = jnp.concatenate(
        [
            rotate_back(
                grad_queries.reshape(tokens, slot_heads, HDIM), cosine_table, sine_table
            ).reshape(tokens, query_cols),
            rotate_back(grad_keys.reshape(tokens, slot_kv, HDIM), cosine_table, sine_table).reshape(
                tokens, key_cols
            ),
            grad_values.reshape(tokens, key_cols),
        ],
        axis=1,
    ).astype(jnp.bfloat16)
    rows_joined = col_tokens(grad_joined)
    grad_normed_in = row_partial(rows_joined, joined_weight, 1)
    grad_joined_weight = matmul(rows_in, rows_joined, 0, 0)
    scaled_in = grad_normed_in * gain_in
    grad_gain_in = jnp.sum(grad_normed_in * residual * level_in, axis=0)
    inner_in = feature_total(jnp.sum(scaled_in * residual, axis=1))[:, None]
    input_grad = (grad_mid + scaled_in * level_in - residual * level_in**3 * inner_in / D).astype(
        jnp.bfloat16
    )
    gain_in_total, gain_mid_total = lax.psum((grad_gain_in, grad_gain_mid), ("dp", "row"))
    summed_joined, summed_out, summed_mlp, summed_down = lax.psum(
        (grad_joined_weight, grad_out_weight, grad_mlp, grad_down), "dp"
    )
    query_grad = summed_joined[:, :query_cols][:, None, :]
    key_grad = summed_joined[:, query_cols : query_cols + key_cols][:, None, :]
    value_grad = summed_joined[:, query_cols + key_cols :][:, None, :]
    return (
        block_out,
        input_grad,
        query_grad,
        key_grad,
        value_grad,
        summed_out[None],
        summed_mlp[:, :ff_half],
        summed_mlp[:, ff_half:],
        summed_down,
        gain_in_total,
        gain_mid_total,
    )


def solution(mesh):
    return jax.shard_map(
        per_device,
        mesh=mesh,
        in_specs=(
            P(("dp", "row"), "col"),
            P("col", "row", None),
            P("col", "row", None),
            P("col", "row", None),
            P("row", None, "col"),
            P("col", "row"),
            P("col", "row"),
            P("row", "col"),
            P("col"),
            P("col"),
            P(("dp", "row"), "col"),
            P(("dp", "col")),
        ),
        out_specs=(
            P(("dp", "row"), "col"),
            P(("dp", "row"), "col"),
            P("col", "row", None),
            P("col", "row", None),
            P("col", "row", None),
            P("row", None, "col"),
            P("col", "row"),
            P("col", "row"),
            P("row", "col"),
            P("col"),
            P("col"),
        ),
        check_vma=False,
    )
```

profile of v0, /device:TPU:0, one launch (start us, length us, event | category | flops | bytes accessed | tf_op | source)
XLA Modules:
  0.0 1088.8 jit_solution(5258306081464424872)
XLA Ops:
  15.2 34.3 %all-gather.9.cloned.1.call-done = bf16[2048,480]{0,1:T(8,128)(2,1)} async-done(((bf16[1024,480]{0,1:T(8,128)(2,1)}), bf16[2048,480]{0,1:T(8,128)(2,1)}) %all-gather.9.cloned.1.call-update) | async-done | bytes 1966096 | tf_op jit(solution)/shard_map/all_gather | solution.py:26
  60.2 12.8 %reduce-scatter.9.cloned.1.call-done = f32[1024,960]{0,1:T(8,128)} async-done(((f32[2048,960]{0,1:T(8,128)}), f32[1024,960]{0,1:T(8,128)}) %reduce-scatter.9.cloned.1.call-update) | async-done | bytes 3932176 | tf_op jit(solution)/shard_map/reduce_scatter | solution.py:34
  77.6 15.1 %fusion.9 = (f32[3,3,1024]{2,1,0:T(4,128)S(1)}, f32[3,1024,1024,3]{2,1,3,0:T(8,128)}) fusion(pred[1024,1024]{0,1:T(8,128)(4,1)S(1)} %fusion.10, bf16[1024,3,64,1]{0,2,3,1:T(8,128)(2,1)S(1)} %fusion.42, bf16[1024,3,3,64]{0,3,2,1:T(8,128)(2,1)S(1)} %fusion.12), kind=kOutput, calls=%fused_computation.14 | convolution fusion | flops 1236261888 | bytes 40407040 | tf_op jit(solution)/shard_map/while/body/eval_jaxpr/qgjd,kgd->gjqk/dot_general | solution.py:90
  92.7 16.3 %fusion.3 = f32[3,3,1024]{2,1,0:T(4,128)S(1)} fusion(f32[3,3,1024]{2,1,0:T(4,128)S(1)} %get-tuple-element.123, f32[3,1024,1024,3]{2,1,3,0:T(8,128)} %get-tuple-element.124, pred[1024,1024]{0,1:T(8,128)(4,1)S(1)} %fusion.10), kind=kLoop, calls=%fused_computation.9 | loop fusion | flops 37739520 | bytes 38871040 | tf_op jit(solution)/shard_map/while/body/eval_jaxpr/reduce_sum | solution.py:103
  110.2 17.4 %fusion.8 = f32[3,64,3,1024]{3,1,2,0:T(8,128)} fusion(bf16[1024,3,64,1]{0,2,3,1:T(8,128)(2,1)S(1)} %bitcast.144, f32[3,3,1024]{2,1,0:T(4,128)S(1)} %fusion.3, f32[3,3,1024]{2,1,0:T(4,128)S(1)} %get-tuple-element.123, f32[3,1024,1024,3]{2,1,3,0:T(8,128)} %get-tuple-element.124, pred[1024,1024]{0,1:T(8,128)(4,1)S(1)} %fusion.10), kind=kOutput, calls=%fused_computation.13 | convolution fusion | flops 1255145472 | bytes 41623552 | tf_op jit(solution)/shard_map/while/body/eval_jaxpr/gjqk,kgd->qgjd/dot_general | solution.py:105
  130.7 12.2 %all-gather.11.cloned.1.call-done = bf16[2048,576]{0,1:T(8,128)(2,1)} async-done(((bf16[1024,576]{0,1:T(8,128)(2,1)}), bf16[2048,576]{0,1:T(8,128)(2,1)}) %all-gather.11.cloned.1.call-update) | async-done | bytes 2359312 | tf_op jit(solution)/shard_map/all_gather | solution.py:30
  149.1 52.4 %reduce-scatter.11.cloned.1.call-done = f32[1024,480]{0,1:T(8,128)} async-done(((f32[2048,480]{0,1:T(8,128)}), f32[1024,480]{0,1:T(8,128)}) %reduce-scatter.11.cloned.1.call-update) | async-done | bytes 1966096 | tf_op jit(solution)/shard_map/reduce_scatter | solution.py:40
  211.4 23.2 %all-gather.17.cloned.1.call-done = bf16[2048,480]{0,1:T(8,128)(2,1)} async-done(((bf16[1024,480]{0,1:T(8,128)(2,1)}), bf16[2048,480]{0,1:T(8,128)(2,1)}) %all-gather.17.cloned.1.call-update) | async-done | bytes 1966096 | tf_op jit(solution)/shard_map/all_gather | solution.py:26
  234.6 8.4 fusion.58
  247.3 20.9 %all-gather.13.cloned.1.call-done = bf16[2048,480]{0,1:T(8,128)(2,1)} async-done(((bf16[1024,480]{0,1:T(8,128)(2,1)}), bf16[2048,480]{0,1:T(8,128)(2,1)}) %all-gather.13.cloned.1.call-update) | async-done | bytes 1966096 | tf_op jit(solution)/shard_map/all_gather | solution.py:26
  268.3 14.7 %fusion.56 = f32[2048,2560]{1,0:T(8,128)} fusion(bf16[2048,480]{0,1:T(8,128)(2,1)} %all-gather.13.cloned.1.call-done, bf16[480,2560]{1,0:T(8,128)(2,1)} %constant_dynamic-update-slice_fusion), kind=kOutput, calls=%fused_computation.119 | convolution fusion | flops 5033164800 | bytes 25395200 | tf_op jit(solution)/shard_map/dot_general | solution.py:20
  289.6 34.2 %reduce-scatter.13.cloned.1.call-done = f32[1024,2560]{1,0:T(8,128)} async-done(((f32[2048,2560]{1,0:T(8,128)}), f32[1024,2560]{1,0:T(8,128)}) %reduce-scatter.13.cloned.1.call-update) | async-done | bytes 10485776 | tf_op jit(solution)/shard_map/reduce_scatter | solution.py:34
  323.9 8.0 multiply_convert_fusion.1
  334.7 24.2 %all-gather.19.cloned.1.call-done = bf16[2048,2560]{1,0:T(8,128)(2,1)} async-done(((bf16[1024,2560]{1,0:T(8,128)(2,1)}), bf16[2048,2560]{1,0:T(8,128)(2,1)}) %all-gather.19.cloned.1.call-update) | async-done | bytes 10485776 | tf_op jit(solution)/shard_map/all_gather | solution.py:30
  358.9 10.0 fusion.59
  369.0 53.2 %reduce-scatter.19.cloned.1.call-done = f32[1024,480]{0,1:T(8,128)} async-done(((f32[2048,480]{0,1:T(8,128)}), f32[1024,480]{0,1:T(8,128)}) %reduce-scatter.19.cloned.1.call-update) | async-done | bytes 1966096 | tf_op jit(solution)/shard_map/reduce_scatter | solution.py:40
  431.6 31.3 %all-gather.21.cloned.1.call-done = bf16[2048,480]{0,1:T(8,128)(2,1)} async-done(((bf16[1024,480]{0,1:T(8,128)(2,1)}), bf16[2048,480]{0,1:T(8,128)(2,1)}) %all-gather.21.cloned.1.call-update) | async-done | bytes 1966096 | tf_op jit(solution)/shard_map/all_gather | solution.py:26
  469.0 12.0 %reduce-scatter.21.cloned.1.call-done = f32[1024,576]{0,1:T(8,128)} async-done(((f32[2048,576]{0,1:T(8,128)}), f32[1024,576]{0,1:T(8,128)}) %reduce-scatter.21.cloned.1.call-update) | async-done | bytes 2359312 | tf_op jit(solution)/shard_map/reduce_scatter | solution.py:34
  481.0 17.5 %fusion.29 = bf16[3,64,1024]{2,1,0:T(8,128)(2,1)} fusion(f32[3,3,1024]{2,1,0:T(4,128)S(1)} %log_add_fusion, f32[3,1024,1024,3]{2,1,3,0:T(8,128)} %get-tuple-element.124, pred[1024,1024]{0,1:T(8,128)(4,1)S(1)} %fusion.10, f32[1024,3,3,64]{0,3,2,1:T(8,128)} %bitcast.142, f32[3,3]{1,0:T(4,128)S(1)} %fusion.45), kind=kOutput, calls=%fused_computation.60 | convolution fusion | flops 1247084544 | bytes 41586724 | tf_op jit(solution)/shard_map/while/body/eval_jaxpr/gjqk,qgjd->kgd/dot_general | solution.py:121
  498.5 27.5 %fusion = (f32[3,3,1024]{2,1,0:T(4,128)S(1)}, f32[3,1024,1024,3]{2,1,3,0:T(8,128)}) fusion(f32[3,3,1024]{2,1,0:T(4,128)S(1)} %log_add_fusion, f32[3,1024,1024,3]{2,1,3,0:T(8,128)} %get-tuple-element.124, pred[1024,1024]{0,1:T(8,128)(4,1)S(1)} %fusion.10, bf16[1024,3,64,1]{0,2,3,1:T(8,128)(2,1)S(1)} %bitcast.145, f32[1024,3,3,64]{0,3,2,1:T(8,128)} %bitcast.143, ...), kind=kOutput, calls=%fused_computation.2 | convolution fusion | flops 1256315904 | bytes 79372320 | tf_op jit(solution)/shard_map/while/body/eval_jaxpr/qgjd,kgd->gjqk/dot_general | solution.py:124
  526.0 31.5 %fusion.2 = bf16[3,3,1024,1024]{2,3,1,0:T(8,128)(2,1)} fusion(f32[3,1024,1024,3]{2,1,3,0:T(8,128)} %get-tuple-element.126, f32[3,3,1024]{2,1,0:T(4,128)S(1)} %get-tuple-element.125, f32[3,3,1024]{2,1,0:T(4,128)S(1)} %log_add_fusion, f32[3,1024,1024,3]{2,1,3,0:T(8,128)} %get-tuple-element.124, pred[1024,1024]{0,1:T(8,128)(4,1)S(1)} %fusion.10), kind=kLoop, calls=%fused_computation.4 | loop fusion | flops 56623104 | bytes 95494144 | tf_op jit(solution)/shard_map/while/body/eval_jaxpr/convert_element_type | solution.py:128
  557.6 11.4 %convolution_multiply_fusion = f32[3,64,3,1024]{3,1,2,0:T(8,128)} fusion(bf16[1024,3,64,1]{0,2,3,1:T(8,128)(2,1)} %copy-done.13, bf16[3,3,1024,1024]{2,3,1,0:T(8,128)(2,1)} %fusion.2), kind=kOutput, calls=%fused_computation.56 | convolution fusion | flops 1208549376 | bytes 21626880 | tf_op jit(solution)/shard_map/while/body/eval_jaxpr/gjqk,kgd->qgjd/dot_general | solution.py:130
  569.0 13.4 %broadcast_multiply_fusion = (f32[1024,3,64]{0,2,1:T(8,128)}, f32[1024,3,64]{0,2,1:T(8,128)}) fusion(f32[1024,64]{0,1:T(8,128)S(1)} %copy-done.8, bf16[1024,3,3,64]{0,3,2,1:T(8,128)(2,1)S(1)} %copy-done.5, bf16[3,3,1024,1024]{2,3,1,0:T(8,128)(2,1)} %fusion.2), kind=kOutput, calls=%fused_computation.83 | convolution fusion | flops 1208156160 | bytes 21889024 | tf_op jit(solution)/shard_map/while/body/eval_jaxpr/gjqk,qgjd->kgd/dot_general | solution.py:134
  591.3 14.0 %all-gather.23.cloned.1.call-done = bf16[2048,960]{0,1:T(8,128)(2,1)} async-done(((bf16[1024,960]{0,1:T(8,128)(2,1)}), bf16[2048,960]{0,1:T(8,128)(2,1)}) %all-gather.23.cloned.1.call-update) | async-done | bytes 3932176 | tf_op jit(solution)/shard_map/all_gather | solution.py:30
  611.9 11.1 %all-gather.15.cloned.1.call-done = bf16[2048,1280]{1,0:T(8,128)(2,1)} async-done(((bf16[1024,1280]{1,0:T(8,128)(2,1)}), bf16[2048,1280]{1,0:T(8,128)(2,1)}) %all-gather.15.cloned.1.call-update) | async-done | bytes 5242896 | tf_op jit(solution)/shard_map/all_gather | solution.py:30
  623.0 7.1 fusion.57
  630.2 8.5 fusion.62
  638.7 11.1 %fusion.61 = f32[480,2560]{1,0:T(8,128)} fusion(bf16[2048,480]{0,1:T(8,128)(2,1)S(1)} %copy-done.43, bf16[2048,2560]{1,0:T(8,128)(2,1)} %all-gather.19.cloned.1.call-done), kind=kOutput, calls=%fused_computation.124 | convolution fusion | flops 5033164800 | bytes 17367040 | tf_op jit(solution)/shard_map/dot_general | solution.py:20
  656.6 21.7 %reduce-scatter.23.cloned.1.call-done = f32[1024,480]{0,1:T(8,128)} async-done(((f32[2048,480]{0,1:T(8,128)}), f32[1024,480]{0,1:T(8,128)}) %reduce-scatter.23.cloned.1.call-update) | async-done | bytes 1966096 | tf_op jit(solution)/shard_map/reduce_scatter | solution.py:40
  680.5 42.2 %all-reduce = (f32[480]{0:T(512)}, f32[480]{0:T(512)}) all-reduce(f32[480]{0:T(512)S(1)} %get-tuple-element.86, f32[480]{0:T(512)S(1)} %get-tuple-element.84), channel_id=1, replica_groups=mesh['dp'=8,'row'=2,'col'=2] {'dp','row'}, use_global_device_ids=true, to_apply=%region_26.27 | all-reduce | flops 960 | bytes 7680 | tf_op jit(solution)/shard_map/psum | solution.py:270
  725.4 8.3 reduce-scatter.15.cloned.1.call-done
  739.6 329.5 %all-reduce.4.cloned.1.call-done = (f32[480,960]{1,0:T(8,128)}, f32[1,576,480]{2,1,0:T(8,128)}, f32[480,2560]{1,0:T(8,128)}, f32[1280,480]{0,1:T(8,128)}) async-done(((f32[480,960]{1,0:T(8,128)}, f32[1,576,480]{2,1,0:T(8,128)}, f32[480,2560]{1,0:T(8,128)}, f32[1280,480]{0,1:T(8,128)}), (f32[480,960]{1,0:T(8,128)}, f32[1,576,480]{2,1,0:T(8,128)}, f32[480,2560]{1,0:T(8,128)}, ...) | async-done | bytes 10321936 | tf_op jit(solution)/shard_map/psum | solution.py:271
  (201 shorter events, 118.3 us)
Async XLA Ops:
  7.2 227.5 %copy-start = (bf16[1280,480]{0,1:T(8,128)(2,1)S(1)}, bf16[1280,480]{0,1:T(8,128)(2,1)}, u32[]{:S(2)}) copy-start(bf16[1280,480]{0,1:T(8,128)(2,1)} %param.19) | copy-start | bytes 3686404
  7.2 42.3 %copy-start.46 = (bf16[480,1,192]{0,2,1:T(8,128)(2,1)S(1)}, bf16[480,1,192]{0,2,1:T(8,128)(2,1)}, u32[]{:S(2)}) copy-start(bf16[480,1,192]{0,2,1:T(8,128)(2,1)} %param.15) | copy-start | bytes 552964
  7.2 42.3 %copy-start.48 = (bf16[480,1,192]{0,2,1:T(8,128)(2,1)S(1)}, bf16[480,1,192]{0,2,1:T(8,128)(2,1)}, u32[]{:S(2)}) copy-start(bf16[480,1,192]{0,2,1:T(8,128)(2,1)} %param.14) | copy-start | bytes 552964
  7.2 42.3 %copy-start.44 = (bf16[480,1,576]{0,2,1:T(8,128)(2,1)S(1)}, bf16[480,1,576]{0,2,1:T(8,128)(2,1)}, u32[]{:S(2)}) copy-start(bf16[480,1,576]{0,2,1:T(8,128)(2,1)} %param.13) | copy-start | bytes 1658884
  7.2 42.3 %all-gather.9.cloned.1.call-start = ((), (), s32[]{:S(2)}) async-start(), calls=%async_computation.8 | async-start | bytes 2949120 | tf_op jit(solution)/shard_map/all_gather | solution.py:26
  8.1 48.3 %copy-start.36 = (f32[480]{0:T(512)}, f32[480]{0:T(512)S(1)}, u32[]{:S(2)}) copy-start(f32[480]{0:T(512)S(1)} %convert_element_type.80) | copy-start | bytes 5764
  12.7 43.7 %copy-start.30 = (f32[1024]{0:T(1024)}, f32[1024]{0:T(1024)S(1)}, u32[]{:S(2)}) copy-start(f32[1024]{0:T(1024)S(1)} %get-tuple-element.120) | copy-start | bytes 12292
  15.2 57.9 %reduce-scatter.9.cloned.1.call-start = ((), (), s32[]{:S(2)}) async-start(), calls=%async_computation.9 | async-start | bytes 11796480 | tf_op jit(solution)/shard_map/reduce_scatter | solution.py:34
  56.4 86.5 %all-gather.11.cloned.1.call-start = ((), (), s32[]{:S(2)}) async-start(), calls=%async_computation.10 | async-start | bytes 3538944 | tf_op jit(solution)/shard_map/all_gather | solution.py:30
  130.6 70.9 %reduce-scatter.11.cloned.1.call-start = ((), (), s32[]{:S(2)}) async-start(), calls=%async_computation.11 | async-start | bytes 5898240 | tf_op jit(solution)/shard_map/reduce_scatter | solution.py:40
  148.2 53.3 %copy-start.1 = (bf16[1024,480]{0,1:T(8,128)(2,1)S(1)}, bf16[1024,480]{0,1:T(8,128)(2,1)}, u32[]{:S(2)}) copy-start(bf16[1024,480]{0,1:T(8,128)(2,1)} %param.12) | copy-start | bytes 2949124
  148.2 86.4 %all-gather.17.cloned.1.call-start = ((), (), s32[]{:S(2)}) async-start(), calls=%async_computation.16 | async-start | bytes 2949120 | tf_op jit(solution)/shard_map/all_gather | solution.py:26
  148.8 119.4 %all-gather.13.cloned.1.call-start = ((), (), s32[]{:S(2)}) async-start(), calls=%async_computation.12 | async-start | bytes 2949120 | tf_op jit(solution)/shard_map/all_gather | solution.py:26
  149.1 58.8 %copy-start.33 = (f32[480]{0:T(512)}, f32[480]{0:T(512)S(1)}, u32[]{:S(2)}) copy-start(f32[480]{0:T(512)S(1)} %convert_element_type.89) | copy-start | bytes 5764
  211.4 78.2 %reduce-scatter.17.cloned.1.call-start = ((), (), s32[]{:S(2)}) async-start(), calls=%async_computation.17 | async-start | bytes 15728640 | tf_op jit(solution)/shard_map/reduce_scatter | solution.py:34
  243.1 80.8 %reduce-scatter.13.cloned.1.call-start = ((), (), s32[]{:S(2)}) async-start(), calls=%async_computation.13 | async-start | bytes 31457280 | tf_op jit(solution)/shard_map/reduce_scatter | solution.py:34
  283.0 75.9 %all-gather.19.cloned.1.call-start = ((), (), s32[]{:S(2)}) async-start(), calls=%async_computation.18 | async-start | bytes 15728640 | tf_op jit(solution)/shard_map/all_gather | solution.py:30
  334.6 87.6 %reduce-scatter.19.cloned.1.call-start = ((), (), s32[]{:S(2)}) async-start(), calls=%async_computation.19 | async-start | bytes 5898240 | tf_op jit(solution)/shard_map/reduce_scatter | solution.py:40
  368.9 53.3 %copy-start.29 = (f32[1024]{0:T(1024)S(1)}, f32[1024]{0:T(1024)}, u32[]{:S(2)}) copy-start(f32[1024]{0:T(1024)} %copy-done.28) | copy-start | bytes 12292
  368.9 53.3 %copy-start.34 = (f32[480]{0:T(512)S(1)}, f32[480]{0:T(512)}, u32[]{:S(2)}) copy-start(f32[480]{0:T(512)} %copy-done.33) | copy-start | bytes 5764
  368.9 58.5 %copy-start.6 = (bf16[1024,480]{0,1:T(8,128)(2,1)S(1)}, bf16[1024,480]{0,1:T(8,128)(2,1)}, u32[]{:S(2)}) copy-start(bf16[1024,480]{0,1:T(8,128)(2,1)} %param.22) | copy-start | bytes 2949124
  368.9 58.5 %copy-start.35 = (f32[1024]{0:T(1024)S(1)}, f32[1024]{0:T(1024)}, u32[]{:S(2)}) copy-start(f32[1024]{0:T(1024)} %get-tuple-element.121) | copy-start | bytes 12292
  369.0 93.9 %all-gather.21.cloned.1.call-start = ((), (), s32[]{:S(2)}) async-start(), calls=%async_computation.20 | async-start | bytes 2949120 | tf_op jit(solution)/shard_map/all_gather | solution.py:26
  431.1 49.9 %reduce-scatter.21.cloned.1.call-start = ((), (), s32[]{:S(2)}) async-start(), calls=%async_computation.21 | async-start | bytes 7077888 | tf_op jit(solution)/shard_map/reduce_scatter | solution.py:34
  468.2 137.0 %all-gather.23.cloned.1.call-start = ((), (), s32[]{:S(2)}) async-start(), calls=%async_computation.22 | async-start | bytes 5898240 | tf_op jit(solution)/shard_map/all_gather | solution.py:30
  590.6 32.4 %all-gather.15.cloned.1.call-start = ((), (), s32[]{:S(2)}) async-start(), calls=%async_computation.14 | async-start | bytes 7864320 | tf_op jit(solution)/shard_map/all_gather | solution.py:30
  591.2 87.1 %reduce-scatter.23.cloned.1.call-start = ((), (), s32[]{:S(2)}) async-start(), calls=%async_computation.23 | async-start | bytes 5898240 | tf_op jit(solution)/shard_map/reduce_scatter | solution.py:40
  611.6 122.1 %reduce-scatter.15.cloned.1.call-start = ((), (), s32[]{:S(2)}) async-start(), calls=%async_computation.15 | async-start | bytes 5898240 | tf_op jit(solution)/shard_map/reduce_scatter | solution.py:40
  630.1 438.9 %all-reduce.4.cloned.1.call-start = ((), (), s32[]{:S(2)}) async-start(), calls=%async_computation.24 | async-start | bytes 21037056 | tf_op jit(solution)/shard_map/psum | solution.py:271
  656.5 21.8 %copy-start.37 = (f32[480]{0:T(512)S(1)}, f32[480]{0:T(512)}, u32[]{:S(2)}) copy-start(f32[480]{0:T(512)} %copy-done.36) | copy-start | bytes 5764
  656.6 77.1 %copy-start.7 = (bf16[1024,480]{0,1:T(8,128)(2,1)S(1)}, bf16[1024,480]{0,1:T(8,128)(2,1)}, u32[]{:S(2)}) copy-start(bf16[1024,480]{0,1:T(8,128)(2,1)} %param.22) | copy-start | bytes 2949124
  656.6 77.1 %copy-start.38 = (f32[1024]{0:T(1024)S(1)}, f32[1024]{0:T(1024)}, u32[]{:S(2)}) copy-start(f32[1024]{0:T(1024)} %get-tuple-element.119) | copy-start | bytes 12292
  (35 other events, 288.9 us)
Sparse Core Ops, SparseCore 0:
  15.3 34.2 all-gather.8
  56.5 16.4 reduce-scatter.8
  130.7 12.1 all-gather.10
  148.4 53.1 reduce-scatter.10
  202.9 31.6 all-gather.16
  236.6 31.6 all-gather.12
  270.6 19.0 reduce-scatter.16
  291.9 31.9 reduce-scatter.12
  334.7 24.1 all-gather.18
  369.1 53.1 reduce-scatter.18
  431.2 31.6 all-gather.20
  468.3 12.6 reduce-scatter.20
  590.7 14.4 all-gather.22
  606.6 16.3 all-gather.14
  625.1 53.1 reduce-scatter.22
  680.5 53.1 reduce-scatter.14
  739.2 329.7 all-reduce.3
where the time goes:
time: 1090 us
  waiting for transfers between devices  704 us (65%)
  matrix products  192 us (18%)
  other arithmetic  97.6 us (9%)
  blocking collectives  52.3 us (5%)
  local copies, waits for them, and re-layouts  27 us (2%)
  between operations  14.7 us (1%)
    psum x1, waiting for transfers between devices, per_device(): lax.psum((grad_joined_weight, grad_out_weight, grad_mlp, grad_down), 'dp')  329 us
    reduce_scatter x4, waiting for transfers between devices, row_partial(): lax.psum_scatter(matmul(gathered, weight, 1, weight_dim), 'row', scatter_...  136 us
    all_gather x4, waiting for transfers between devices, row_tokens(): return lax.all_gather(piece_rows, 'row', axis=0, tiled=True)  110 us
    dot_general x12, matrix products, matmul(): lax.dot_general(left, right, (((left_dim,), (right_dim,)), ((), ())), pre...  89.6 us
    reduce_scatter x4, waiting for transfers between devices, col_partial(): lax.psum_scatter(matmul(gathered, weight, 1, weight_dim), 'col', scatter_...  65.7 us
    all_gather x4, waiting for transfers between devices, col_tokens(): return lax.all_gather(piece_rows, 'col', axis=0, tiled=True)  61.6 us
    psum x1, blocking collectives, per_device(): lax.psum((grad_gain_in, grad_gain_mid), ('dp', 'row'))  42.2 us
    convert_element_type x1, other arithmetic, attend_back(): grad_scores = (probability * (grad_probs - inner_sum)).astype(jnp.bfloat16)  31.5 us
  transfers between devices with their start and end apart: 17, of which 17 were waited for; matrix products, arithmetic and copies ran while one was open for 8% of the time, Pallas kernels for 0%

commit v1 on v0

v1 whole, which is shorter than its diff:
```python
import functools
import math

import jax
import jax.numpy as jnp
from jax import lax
from jax.experimental import pallas as pl
from jax.experimental.pallas import tpu as pltpu
from jax.sharding import PartitionSpec as P

D = 960
HEADS = 15
KV_HEADS = 5
GROUP = 3
HDIM = 64
MAXLEN = 1024
SLOTS = 9
BLOCK = MAXLEN // 4
LOCAL = 2 * BLOCK
HALF = D // 2

NORM_EPS = 1e-05
ROPE_BASE = 100000.0
MASKED_SCORE = -1e30
SCALE = 1.0 / math.sqrt(HDIM)
BF16 = jnp.bfloat16
F32 = jnp.float32
VMEM_BYTES = 56 * 1024 * 1024

QUERY_AT = [(0, h * HDIM) for h in range(9)] + [(1, h * HDIM) for h in range(6)]
KEY_AT = [(0, 576 + h * HDIM) for h in range(3)] + [(1, 576 + h * HDIM) for h in range(2)]
VALUE_AT = [(0, 768 + h * HDIM) for h in range(3)] + [(1, 768 + h * HDIM) for h in range(2)]
KEY_BLOCKS = ((1, 4), (2, 3))
HELD = ((0, 3), (1, 2))


def dot(left, right, left_dim=1, right_dim=0):
    return lax.dot_general(
        left, right, (((left_dim,), (right_dim,)), ((), ())), preferred_element_type=F32
    )


def params():
    return pltpu.CompilerParams(vmem_limit_bytes=VMEM_BYTES)


def level_of(rows):
    return lax.rsqrt(jnp.sum(rows * rows, axis=1, keepdims=True) / D + NORM_EPS)


def turn(chunk):
    lane = lax.broadcasted_iota(jnp.int32, chunk.shape, 1)
    return jnp.where(lane % HDIM < HDIM // 2, pltpu.roll(chunk, 96, 1), pltpu.roll(chunk, 32, 1))


def qkv_kernel(x_ref, gain_ref, cos_ref, sin_ref, w0_ref, w1_ref, nm_ref, q_ref, kv_ref):
    rows = x_ref[...].astype(F32)
    nm = (rows * level_of(rows) * gain_ref[...]).astype(BF16)
    nm_ref[...] = nm
    cosine, sine = cos_ref[...], sin_ref[...]
    joined = [dot(nm, w0_ref[...]), dot(nm, w1_ref[...])]
    turned = {}

    def piece(block, lane, rotate):
        start = lane // 128 * 128
        stop = min(start + 128, D)
        chunk = joined[block][:, start:stop]
        if rotate:
            if (block, start) not in turned:
                turned[block, start] = chunk * cosine + turn(chunk) * sine
            chunk = turned[block, start]
        return chunk[:, lane - start : lane - start + HDIM]

    for h, (block, lane) in enumerate(QUERY_AT):
        q_ref[h] = (piece(block, lane, True).astype(BF16).astype(F32) * SCALE).astype(BF16)
    for g, (block, lane) in enumerate(KEY_AT):
        kv_ref[g] = piece(block, lane, True).astype(BF16)
    for g, (block, lane) in enumerate(VALUE_AT):
        kv_ref[KV_HEADS + g] = piece(block, lane, False).astype(BF16)


def fill_bias(bias_ref, index_ref, begin_ref):
    key_index = lax.broadcasted_iota(jnp.int32, (MAXLEN, LOCAL), 0)
    allowed = (key_index >= begin_ref[...]) & (key_index <= index_ref[...])
    bias_ref[...] = jnp.where(allowed, 0.0, MASKED_SCORE)


def attend_kernel(
    core_ref, index_ref, begin_ref, q_ref, k_ref, v_ref, x_ref, gain_ref, wo_ref,
    att_ref, mid_ref, nm_ref, lse_ref, bias_ref, heads_ref,
):
    group = pl.program_id(0)

    @pl.when(group == 0)
    def _():
        fill_bias(bias_ref, index_ref, begin_ref)

    for core in range(2):

        @pl.when(core_ref[0] == core)
        def _():
            for slot in range(2):
                rows = pl.ds(slot * BLOCK, BLOCK)
                span = KEY_BLOCKS[core][slot] * BLOCK
                keys = k_ref[0, :span, :]
                values = v_ref[0, :span, :]
                bias = bias_ref[:span, slot * BLOCK : (slot + 1) * BLOCK]
                for j in range(GROUP):
                    scores = dot(keys, q_ref[j, rows, :], 1, 1) + bias
                    highest = jnp.max(scores, axis=0, keepdims=True)
                    weights = jnp.exp(scores - highest)
                    total = jnp.sum(weights, axis=0, keepdims=True)
                    mixed = dot(values, weights.astype(BF16), 0, 0) / total
                    heads_ref[group * GROUP + j, rows, :] = mixed.T.astype(BF16)
                    lse_ref[0, j : j + 1, rows] = highest + jnp.log(total)

    @pl.when(group == KV_HEADS - 1)
    def _():
        att = jnp.concatenate([heads_ref[h] for h in range(HEADS)], axis=1)
        att_ref[...] = att
        mid = x_ref[...].astype(F32) + dot(att, wo_ref[...])
        mid_ref[...] = mid
        nm_ref[...] = (mid * level_of(mid) * gain_ref[...]).astype(BF16)


def mlp_kernel(nm_ref, og_ref, wg_ref, wu_ref, wd_ref, out_ref, gnm_ref, act_ref, ggu_ref):
    nm, og = nm_ref[...], og_ref[...]
    hidden = wg_ref.shape[1]
    gate = dot(nm, wg_ref[...])
    up = dot(nm, wu_ref[...])
    sig = jax.nn.sigmoid(gate)
    silu = gate * sig
    act = (silu * up).astype(BF16)
    act_ref[...] = act
    grad_act = dot(og, wd_ref[...], 1, 1)
    grad_gate = (grad_act * up * sig * (1.0 + gate * (1.0 - sig))).astype(BF16)
    grad_up = (grad_act * silu).astype(BF16)
    ggu_ref[:, :hidden] = grad_gate
    ggu_ref[:, hidden:] = grad_up
    gnm = dot(grad_gate, wg_ref[...], 1, 1) + dot(grad_up, wu_ref[...], 1, 1)
    gnm_ref[...] = gnm.astype(gnm_ref.dtype)
    out_ref[...] = dot(act, wd_ref[...]).astype(out_ref.dtype)


def mid_back_kernel(
    og_ref, mid_ref, own_ref, got_ref, gain_ref, wo_ref, gmid_ref, gb_ref, gatt_ref, ggain_ref
):
    mid = mid_ref[...]
    level = level_of(mid)
    gnm = own_ref[...] + got_ref[...].astype(F32)
    scaled = gnm * gain_ref[...]
    ggain_ref[...] = jnp.sum(gnm * mid * level, axis=0, keepdims=True)
    inner = jnp.sum(scaled * mid, axis=1, keepdims=True)
    gmid = og_ref[...].astype(F32) + scaled * level - mid * (level**3 * inner / D)
    gmid_ref[...] = gmid
    gb = gmid.astype(BF16)
    gb_ref[...] = gb
    gatt = dot(gb, wo_ref[...], 1, 1).astype(BF16)
    for h in range(HEADS):
        gatt_ref[h] = gatt[:, h * HDIM : (h + 1) * HDIM]


def attend_back_kernel(
    core_ref, index_ref, begin_ref, q_ref, k_ref, v_ref, gatt_ref, lse_ref,
    dq_ref, mine_ref, other_ref, bias_ref, dkv_ref,
):
    @pl.when(pl.program_id(0) == 0)
    def _():
        fill_bias(bias_ref, index_ref, begin_ref)

    for core in range(2):

        @pl.when(core_ref[0] == core)
        def _():
            dkv_ref[...] = jnp.zeros_like(dkv_ref)
            for slot in range(2):
                rows = pl.ds(slot * BLOCK, BLOCK)
                span = KEY_BLOCKS[core][slot] * BLOCK
                keys = k_ref[0, :span, :]
                values = v_ref[0, :span, :]
                bias = bias_ref[:span, slot * BLOCK : (slot + 1) * BLOCK]
                for j in range(GROUP):
                    queries = q_ref[j, rows, :]
                    grads = gatt_ref[j, rows, :]
                    scores = dot(keys, queries, 1, 1) + bias
                    probs = jnp.exp(scores - lse_ref[0, j : j + 1, rows])
                    dprobs = dot(values, grads, 1, 1)
                    inner = jnp.sum(probs * dprobs, axis=0, keepdims=True)
                    dscores = (probs * (dprobs - inner)).astype(BF16)
                    dkv_ref[1, :span, :] += dot(probs.astype(BF16), grads)
                    dkv_ref[0, :span, :] += dot(dscores, queries)
                    dq_ref[j, rows, :] = dot(dscores, keys, 0, 0) * SCALE
            for kind in range(2):
                for slot in range(2):
                    rows = pl.ds(slot * BLOCK, BLOCK)
                    here, there = HELD[core][slot], HELD[1 - core][slot]
                    mine_ref[kind, 0, rows, :] = dkv_ref[kind, here * BLOCK : (here + 1) * BLOCK, :]
                    other_ref[kind, 0, rows, :] = dkv_ref[
                        kind, there * BLOCK : (there + 1) * BLOCK, :
                    ].astype(BF16)


def joined_back_kernel(
    dq_ref, mine_ref, got_ref, cos_ref, sin_ref, w0_ref, w1_ref, x_ref, gain_ref, gmid_ref,
    gj0_ref, gj1_ref, grad_ref, ggain_ref,
):
    cosine, sine = cos_ref[...], sin_ref[...]
    zero = jnp.zeros((LOCAL, HDIM), F32)

    def head(kind, h):
        if h is None:
            return zero
        if kind == "q":
            return dq_ref[h]
        which = 0 if kind == "k" else 1
        return mine_ref[which, h] + got_ref[which, h].astype(F32)

    layout = (
        [("q", h) for h in range(9)] + [("k", h) for h in range(3)] + [("v", h) for h in range(3)],
        [("q", h) for h in range(9, 15)] + [("q", None)] * 3 + [("k", 3), ("k", 4), ("k", None)]
        + [("v", 3), ("v", 4), ("v", None)],
    )
    gnm = None
    for heads, gj_ref, w_ref in zip(layout, (gj0_ref, gj1_ref), (w0_ref, w1_ref)):
        parts = []
        for at in range(0, 12, 2):
            chunk = jnp.concatenate([head(*heads[at]), head(*heads[at + 1])], axis=1)
            parts.append((chunk * cosine - turn(chunk) * sine).astype(BF16))
        parts += [head(*heads[at]).astype(BF16) for at in range(12, 15)]
        gj = jnp.concatenate(parts, axis=1)
        gj_ref[...] = gj
        product = dot(gj, w_ref[...], 1, 1)
        gnm = product if gnm is None else gnm + product
    rows = x_ref[...].astype(F32)
    level = level_of(rows)
    scaled = gnm * gain_ref[...]
    ggain_ref[...] = jnp.sum(gnm * rows * level, axis=0, keepdims=True)
    inner = jnp.sum(scaled * rows, axis=1, keepdims=True)
    grad = gmid_ref[...] + scaled * level - rows * (level**3 * inner / D)
    grad_ref[...] = grad.astype(BF16)


def shape(dims, dtype=BF16):
    return jax.ShapeDtypeStruct(dims, dtype)


def whole(dims):
    return pl.BlockSpec(dims, lambda *_: (0,) * len(dims))


def cost(flops, moved):
    return pl.CostEstimate(flops=int(flops), bytes_accessed=int(moved), transcendentals=0)


SMEM_SPEC = pl.BlockSpec(memory_space=pltpu.SMEM)


def project(x, gain, cosine, sine, w0, w1):
    return pl.pallas_call(
        qkv_kernel,
        out_shape=(
            shape((LOCAL, D)), shape((HEADS, LOCAL, HDIM)), shape((2 * KV_HEADS, LOCAL, HDIM))
        ),
        compiler_params=params(),
        cost_estimate=cost(4 * LOCAL * D * D, 10e6),
    )(x, gain, cosine, sine, w0, w1)


def attend(core, index, begin, q, kv, x, gain, wo):
    per_group = lambda *dims: pl.BlockSpec(dims, lambda g: (g, 0, 0))
    return pl.pallas_call(
        attend_kernel,
        grid=(KV_HEADS,),
        in_specs=[
            SMEM_SPEC, whole((1, LOCAL)), whole((1, LOCAL)), per_group(GROUP, LOCAL, HDIM),
            per_group(1, MAXLEN, HDIM),
            pl.BlockSpec((1, MAXLEN, HDIM), lambda g: (g + KV_HEADS, 0, 0)),
            whole((LOCAL, D)), whole((1, D)), whole((D, D)),
        ],
        out_specs=(
            whole((LOCAL, D)), whole((LOCAL, D)), whole((LOCAL, D)), per_group(1, 8, LOCAL)
        ),
        out_shape=(
            shape((LOCAL, D)), shape((LOCAL, D), F32), shape((LOCAL, D)),
            shape((KV_HEADS, 8, LOCAL), F32),
        ),
        scratch_shapes=[
            pltpu.VMEM((MAXLEN, LOCAL), F32), pltpu.VMEM((HEADS, LOCAL, HDIM), BF16)
        ],
        compiler_params=params(),
        cost_estimate=cost(12e9, 12e6),
    )(core, index, begin, q, kv, kv, x, gain, wo)


def feed_forward(nm, og, wg, wu, wd, dtype):
    hidden = wg.shape[1]
    rows = lambda width: pl.BlockSpec((BLOCK, width), lambda i: (i, 0))
    return pl.pallas_call(
        mlp_kernel,
        grid=(LOCAL // BLOCK,),
        in_specs=[
            rows(D), rows(D), whole((D, hidden)), whole((D, hidden)), whole((hidden, D))
        ],
        out_specs=(rows(D), rows(D), rows(hidden), rows(2 * hidden)),
        out_shape=(
            shape((LOCAL, D), dtype), shape((LOCAL, D), dtype), shape((LOCAL, hidden)),
            shape((LOCAL, 2 * hidden)),
        ),
        compiler_params=params(),
        cost_estimate=cost(12 * LOCAL * D * hidden, 16e6),
    )(nm, og, wg, wu, wd)


def mid_back(og, mid, own, got, gain, wo):
    return pl.pallas_call(
        mid_back_kernel,
        out_shape=(
            shape((LOCAL, D), F32), shape((LOCAL, D)), shape((HEADS, LOCAL, HDIM)),
            shape((1, D), F32),
        ),
        compiler_params=params(),
        cost_estimate=cost(2 * LOCAL * D * D, 14e6),
    )(og, mid, own, got, gain, wo)


def attend_back(core, index, begin, q, kv, gatt, lse):
    per_group = lambda *dims: pl.BlockSpec(dims, lambda g: (g, 0, 0))
    pair = pl.BlockSpec((2, 1, LOCAL, HDIM), lambda g: (0, g, 0, 0))
    return pl.pallas_call(
        attend_back_kernel,
        grid=(KV_HEADS,),
        in_specs=[
            SMEM_SPEC, whole((1, LOCAL)), whole((1, LOCAL)), per_group(GROUP, LOCAL, HDIM),
            per_group(1, MAXLEN, HDIM),
            pl.BlockSpec((1, MAXLEN, HDIM), lambda g: (g + KV_HEADS, 0, 0)),
            per_group(GROUP, LOCAL, HDIM), per_group(1, 8, LOCAL),
        ],
        out_specs=(per_group(GROUP, LOCAL, HDIM), pair, pair),
        out_shape=(
            shape((HEADS, LOCAL, HDIM), F32), shape((2, KV_HEADS, LOCAL, HDIM), F32),
            shape((2, KV_HEADS, LOCAL, HDIM)),
        ),
        scratch_shapes=[
            pltpu.VMEM((MAXLEN, LOCAL), F32), pltpu.VMEM((2, MAXLEN, HDIM), F32)
        ],
        compiler_params=params(),
        cost_estimate=cost(30e9, 20e6),
    )(core, index, begin, q, kv, kv, gatt, lse)


def joined_back(dq, mine, got, cosine, sine, w0, w1, x, gain, gmid):
    return pl.pallas_call(
        joined_back_kernel,
        out_shape=(
            shape((LOCAL, D)), shape((LOCAL, D)), shape((LOCAL, D)), shape((1, D), F32)
        ),
        compiler_params=params(),
        cost_estimate=cost(4 * LOCAL * D * D, 20e6),
    )(dq, mine, got, cosine, sine, w0, w1, x, gain, gmid)


def swap(array, axis):
    return lax.ppermute(array, axis, [(0, 1), (1, 0)])


def stages(count):
    found, stride = [], 1
    for size in (2,) + (4,) * 16:
        size = min(size, count // stride)
        if size < 2:
            break
        found.append((stride, size))
        stride *= size
    return found


def shift_pairs(count, stride, size, step):
    pairs = []
    for i in range(count):
        digit = i // stride % size
        pairs.append((i, i + ((digit + step) % size - digit) * stride))
    return pairs


def sum_over_dp(array, count):
    steps = stages(count)
    sizes = [size for _, size in steps]
    rows, cols = array.shape
    place = lax.axis_index("dp")
    total = array.reshape(*sizes, rows // count, cols)
    for stride, size in steps:
        digit = place // stride % size
        kept = lax.dynamic_index_in_dim(total, digit, 0, keepdims=False).astype(F32)
        for step in range(1, size):
            sent = lax.dynamic_index_in_dim(total, (digit + step) % size, 0, keepdims=False)
            kept = kept + lax.ppermute(
                sent.astype(BF16), "dp", shift_pairs(count, stride, size, step)
            ).astype(F32)
        total = kept
    total = total.astype(BF16)
    for stride, size in reversed(steps):
        digit = place // stride % size
        spread = jnp.zeros((size,) + total.shape, BF16)
        spread = lax.dynamic_update_index_in_dim(spread, total, digit, 0)
        for step in range(1, size):
            got = lax.ppermute(total, "dp", shift_pairs(count, stride, size, step))
            spread = lax.dynamic_update_index_in_dim(spread, got, (digit - step) % size, 0)
        total = spread
    return total.reshape(rows, cols).astype(F32)


def segment_begin(segment):
    index = jnp.arange(segment.shape[0], dtype=jnp.int32)
    is_start = jnp.concatenate([jnp.ones((1,), dtype=bool), segment[1:] != segment[:-1]])
    return lax.cummax(jnp.where(is_start, index, jnp.zeros_like(index)), axis=0)


def rope_tables(position):
    half_dim = HDIM // 2
    frequency = ROPE_BASE ** (-(jnp.arange(half_dim, dtype=F32) * 2.0 / HDIM))
    angles = position.astype(F32)[:, None] * frequency[None, :]
    cosine, sine = jnp.cos(angles), jnp.sin(angles)
    return (
        jnp.concatenate([cosine] * 4, axis=1),
        jnp.concatenate([-sine, sine, -sine, sine], axis=1),
    )


def per_device(
    count,
    hidden_in,
    query_weight,
    key_weight,
    value_weight,
    output_weight,
    gate_weight,
    up_weight,
    down_weight,
    attn_gain,
    ffn_gain,
    out_grad,
    segment_ids,
):
    col, row = lax.axis_index("col"), lax.axis_index("row")
    first, top = col == 0, row == 0
    hidden = gate_weight.shape[1]

    def ordered(own, got):
        return jnp.where(first, own, got), jnp.where(first, got, own)

    def own_tokens(array):
        outer = jnp.concatenate([array[:BLOCK], array[3 * BLOCK :]], axis=0)
        return ordered(outer, array[BLOCK : 3 * BLOCK])

    def in_window(own, got, axis=0):
        outer, inner = ordered(own, got)
        return jnp.concatenate(
            [
                lax.slice_in_dim(outer, 0, BLOCK, axis=axis),
                inner,
                lax.slice_in_dim(outer, BLOCK, LOCAL, axis=axis),
            ],
            axis=axis,
        )

    def token_rows(array):
        own, other = own_tokens(array)
        return jnp.concatenate(ordered(own, swap(other, "col")), axis=1)

    def feature_cols(array):
        keep, send = ordered(array[:, :HALF], array[:, HALF:])
        return in_window(keep, swap(send, "col"))

    def joined_by_col(own, axis):
        return jnp.concatenate(ordered(own, swap(own, "col")), axis=axis)

    joined_weight = jnp.concatenate(
        [query_weight[:, 0], key_weight[:, 0], value_weight[:, 0]], axis=1
    )
    joined_far = swap(joined_weight, "row")
    x = token_rows(hidden_in)
    gains = joined_by_col(jnp.stack([attn_gain, ffn_gain]), 1).astype(F32)
    gain_in, gain_mid = gains[:1], gains[1:]
    near_weight = joined_by_col(joined_weight, 0)
    far_weight = joined_by_col(joined_far, 0)
    w0 = jnp.where(top, near_weight, far_weight)
    w1 = jnp.where(top, far_weight, near_weight)
    out_weight = output_weight[0]
    out_far = swap(out_weight, "row")
    near_out = joined_by_col(out_weight, 1)
    far_out = joined_by_col(out_far, 1)
    wo = jnp.concatenate(
        [
            jnp.where(top, near_out, far_out),
            jnp.where(top, far_out, near_out)[: (HEADS - SLOTS) * HDIM],
        ],
        axis=0,
    )

    segment = jnp.where(col == row, segment_ids, swap(segment_ids, "col"))
    begin, _ = own_tokens(segment_begin(segment))
    index, _ = own_tokens(jnp.arange(MAXLEN, dtype=jnp.int32))
    cosine, sine = rope_tables(index - begin)
    index, begin = index[None], begin[None]
    core = col.astype(jnp.int32)[None]

    nm_in, q, kv_own = project(x, gain_in, cosine, sine, w0, w1)
    kv = in_window(kv_own, swap(kv_own, "col"), 1)
    att, mid, nm, lse = attend(core, index, begin, q, kv, x, gain_mid, wo)

    og = token_rows(out_grad)
    og_far = swap(og, "row")
    wg = joined_by_col(gate_weight, 0)
    wu = joined_by_col(up_weight, 0)
    wd = joined_by_col(down_weight, 1)
    nm_far = swap(nm, "row")
    out_own, gnm_own, act, ggu = feed_forward(nm, og, wg, wu, wd, F32)
    out_far, gnm_far, act_far, ggu_far = feed_forward(nm_far, og_far, wg, wu, wd, BF16)
    gnm_got = swap(gnm_far, "row")
    out_got = swap(out_far, "row")

    def halves(array):
        return ordered(array[:, :HALF], array[:, HALF:])

    def weight_grads(rows, grads):
        keep, send = rows
        return dot(keep, grads, 0, 0), dot(send, grads, 0, 0).astype(BF16)

    nm_all = jnp.concatenate([nm, nm_far], axis=0)
    og_all = jnp.concatenate([og, og_far], axis=0)
    act_all = jnp.concatenate([act, act_far], axis=0)
    ggu_all = jnp.concatenate([ggu, ggu_far], axis=0)
    og_keep, og_send = halves(og_all)
    down_keep, down_send = dot(act_all, og_keep, 0, 0), dot(act_all, og_send, 0, 0).astype(BF16)
    down_sum = down_keep + swap(down_send, "col").astype(F32)
    mlp_keep, mlp_send = weight_grads(halves(nm_all), ggu_all)
    mlp_sum = mlp_keep + swap(mlp_send, "col").astype(F32)
    down_grad = sum_over_dp(down_sum, count)
    mlp_grad = sum_over_dp(
        jnp.concatenate([mlp_sum[:, :hidden], mlp_sum[:, hidden:]], axis=0), count
    )

    block_out = feature_cols((mid + out_own + out_got.astype(F32)).astype(BF16))

    gmid, gb, gatt, ggain_mid = mid_back(og, mid, gnm_own, gnm_got, gain_mid, wo)

    gb_keep, gb_send = halves(gb)
    wo_keep = dot(att, gb_keep, 0, 0)
    wo_send = dot(att, gb_send, 0, 0).astype(BF16)
    wo_sum = wo_keep + swap(wo_send, "col").astype(F32)

    def row_blocks(low, high):
        return jnp.where(top, low, high), jnp.where(top, high, low)

    wo_low = wo_sum[: SLOTS * HDIM]
    wo_high = jnp.pad(wo_sum[SLOTS * HDIM :], ((0, (2 * SLOTS - HEADS) * HDIM), (0, 0)))
    wo_near, wo_far = row_blocks(wo_low, wo_high)
    wo_near = wo_near + swap(wo_far.astype(BF16), "row").astype(F32)
    wo_grad = sum_over_dp(wo_near, count)

    dq, dkv_own, dkv_other = attend_back(core, index, begin, q, kv, gatt, lse)
    dkv_got = swap(dkv_other, "col")
    gj0, gj1, grad, ggain_in = joined_back(
        dq, dkv_own, dkv_got, cosine, sine, w0, w1, x, gain_in, gmid
    )
    nm_keep, nm_send = halves(nm_in)
    gj_near, gj_far = row_blocks(gj0, gj1)
    far_keep, far_send = weight_grads((nm_keep, nm_send), gj_far)
    near_keep, near_send = weight_grads((nm_keep, nm_send), gj_near)
    far_sum = far_keep + swap(far_send, "col").astype(F32)
    near_sum = near_keep + swap(near_send, "col").astype(F32)
    near_sum = near_sum + swap(far_sum.astype(BF16), "row").astype(F32)
    padded = jnp.pad(near_sum, ((0, 512 - HALF), (0, 0)))
    joined_grad = sum_over_dp(padded, count)[:HALF]

    input_grad = feature_cols(grad)
    gain_grads = lax.psum(jnp.concatenate([ggain_in, ggain_mid], axis=0), ("dp", "row", "col"))
    gain_grads = jnp.where(first, gain_grads[:, :HALF], gain_grads[:, HALF:])

    query_cols = SLOTS * HDIM
    key_cols = SLOTS // GROUP * HDIM
    return (
        block_out,
        input_grad,
        joined_grad[:, :query_cols][:, None, :],
        joined_grad[:, query_cols : query_cols + key_cols][:, None, :],
        joined_grad[:, query_cols + key_cols :][:, None, :],
        wo_grad[None],
        mlp_grad[:HALF],
        mlp_grad[HALF:],
        down_grad,
        gain_grads[0],
        gain_grads[1],
    )


def solution(mesh):
    return jax.shard_map(
        functools.partial(per_device, mesh.shape["dp"]),
        mesh=mesh,
        in_specs=(
            P(("dp", "row"), "col"),
            P("col", "row", None),
            P("col", "row", None),
            P("col", "row", None),
            P("row", None, "col"),
            P("col", "row"),
            P("col", "row"),
            P("row", "col"),
            P("col"),
            P("col"),
            P(("dp", "row"), "col"),
            P(("dp", "col")),
        ),
        out_specs=(
            P(("dp", "row"), "col"),
            P(("dp", "row"), "col"),
            P("col", "row", None),
            P("col", "row", None),
            P("col", "row", None),
            P("row", None, "col"),
            P("col", "row"),
            P("col", "row"),
            P("row", "col"),
            P("col"),
            P("col"),
        ),
        check_vma=False,
    )
```

time: 1090 us -> 567 us (0.52)
  waiting for transfers between devices: 704 us -> 195 us
  matrix products: 192 us -> 35.7 us
  Pallas kernels: 0 us -> 98.6 us
  local copies, waits for them, and re-layouts: 27 us -> 81.1 us
  starting transfers between devices: 1.7 us -> 51 us
  other arithmetic: 97.6 us -> 59 us
  between operations: 14.7 us -> 1.94 us
  blocking collectives: 52.3 us -> 39.6 us
    psum x1 -> x0, waiting for transfers between devices: 329 us -> none  [per_device(): lax.psum((grad_joined_weight, grad_out_weight, grad_mlp, grad_down), 'dp')]
    reduce_scatter x8 -> x0, waiting for transfers between devices: 201 us -> none  [the longest x4 136 us: row_partial(): lax.psum_scatter(matmul(gathered, weight, 1, weight_dim), 'row', scatter_...]
    ppermute x0 -> x60, waiting for transfers between devices: none -> 195 us  [the longest x16 77.9 us: sum_over_dp(): got = lax.ppermute(total, 'dp', shift_pairs(count, stride, size, step))]
    all_gather x8 -> x0, waiting for transfers between devices: 171 us -> none  [the longest x4 110 us: row_tokens(): return lax.all_gather(piece_rows, 'row', axis=0, tiled=True)]
    dot_general x18 -> x10, matrix products: 192 us -> 35.7 us  [dot(): lax.dot_general(left, right, (((left_dim,), (right_dim,)), ((), ())), pre...]
    pallas_call x0 -> x7, Pallas kernels: none -> 98.6 us  [the longest x2 28.2 us: feed_forward(): pl.pallas_call(mlp_kernel, grid=(LOCAL // BLOCK,), in_specs=[rows(D), row...]
    ppermute x0 -> x60, starting transfers between devices: none -> 51 us  [the longest x16 20.9 us: sum_over_dp(): lax.ppermute(sent.astype(BF16), 'dp', shift_pairs(count, stride, size, st...]
    convert_element_type x13 -> x7, other arithmetic: 51 us -> 5.32 us  [the longest x1 2.52 us: per_device(): block_out = feature_cols((mid + out_own + out_got.astype(F32)).astype(BF16))]
  transfers between devices with their start and end apart: 17 -> 60, of which waited for: 17 -> 22; matrix products, arithmetic and copies ran while one was open for 8% -> 27% of each run, Pallas kernels for 0% -> 11%
where the time goes in v1:
time: 567 us; the launch traced here: 562 us
  waiting for transfers between devices  195 us (34%)
  Pallas kernels  98.6 us (17%)
  local copies, waits for them, and re-layouts  81.1 us (14%)
  other arithmetic  59 us (10%)
  starting transfers between devices  51 us (9%)
  blocking collectives  39.6 us (7%)
  matrix products  35.7 us (6%)
    ppermute x16, waiting for transfers between devices, sum_over_dp(): got = lax.ppermute(total, 'dp', shift_pairs(count, stride, size, step))  77.9 us
    ppermute x16, waiting for transfers between devices, sum_over_dp(): lax.ppermute(sent.astype(BF16), 'dp', shift_pairs(count, stride, size, st...  77.3 us
    ppermute x28, waiting for transfers between devices, swap(): return lax.ppermute(array, axis, [(0, 1), (1, 0)])  40 us
    psum x1, blocking collectives, per_device(): lax.psum(jnp.concatenate([ggain_in, ggain_mid], axis=0), ('dp', 'row', 'c...  39.6 us
    dot_general x10, matrix products, dot(): lax.dot_general(left, right, (((left_dim,), (right_dim,)), ((), ())), pre...  35.7 us
    unnamed x116, local copies, waits for them, and re-layouts  30.9 us
    pallas_call x2, Pallas kernels, feed_forward(): pl.pallas_call(mlp_kernel, grid=(LOCAL // BLOCK,), in_specs=[rows(D), row...  28.2 us
    pallas_call x1, Pallas kernels, attend_back(): pl.pallas_call(attend_back_kernel, grid=(KV_HEADS,), in_specs=[SMEM_SPEC,...  23.8 us
  transfers between devices with their start and end apart: 60, of which 22 were waited for; matrix products, arithmetic and copies ran while one was open for 27% of the time, Pallas kernels for 11%

profile of v1, /device:TPU:0, one launch (start us, length us, event | category | flops | bytes accessed | tf_op | source)
XLA Modules:
  0.0 562.2 jit_solution(16793394619864265643)
XLA Ops:
  31.8 11.5 %collective-permute-done.8 = bf16[576,480]{1,0:T(8,128)(2,1)} collective-permute-done((bf16[576,480]{1,0:T(8,128)(2,1)}, bf16[576,480]{1,0:T(8,128)(2,1)}, u32[]{:S(2)}, u32[]{:S(2)}) %collective-permute-start.8) | collective-permute-done | bytes 552992 | tf_op jit(solution)/shard_map/ppermute | solution.py:363
  56.7 3.8 broadcast_select_fusion.7
  65.3 3.1 broadcast_select_fusion
  68.4 7.0 %shard_map.203 = (bf16[512,960]{1,0:T(8,128)(2,1)}, bf16[15,512,64]{2,1,0:T(8,128)(2,1)}, bf16[10,512,64]{2,1,0:T(8,128)(2,1)}) custom-call(bf16[512,960]{1,0:T(8,128)(2,1)} %pad_maximum_fusion.12.x_ref, f32[1,960]{1,0:T(1,128)} %get-tuple-element.172.gain_ref, f32[512,128]{1,0:T(8,128)} %get-tuple-element.186.cos_ref, ...), custom_call_target="tpu_custom_call" | custom-call | flops 1887436800 | bytes 10000000 | tf_op jit(solution)/shard_map/pallas_call | solution.py:259
  78.3 3.3 pad_maximum_fusion.4.wu_ref
  86.3 3.1 pad_maximum_fusion.5
  93.5 22.2 %shard_map.204 = (bf16[512,960]{1,0:T(8,128)(2,1)}, f32[512,960]{1,0:T(8,128)}, bf16[512,960]{1,0:T(8,128)(2,1)}, f32[5,8,512]{2,1,0:T(8,128)}) custom-call(s32[1]{0:T(128)} %bitcast.core_ref, s32[1,512]{1,0:T(1,128)} %bitcast.195, s32[1,512]{1,0:T(1,128)} %broadcast_select_fusion.48.begin_ref, bf16[15,512,64]{2,1,0:T(8,128)(2,1)} %get-tuple-element.37.q_ref, ...), custom_call_target="tpu_custom_call" | custom-call | flops 12000000000 | bytes 12000000 | tf_op jit(solution)/shard_map/pallas_call | solution.py:271
  118.0 14.5 %shard_map.205 = (f32[512,960]{1,0:T(8,128)}, f32[512,960]{1,0:T(8,128)}, bf16[512,1280]{1,0:T(8,128)(2,1)}, bf16[512,2560]{1,0:T(8,128)(2,1)}) custom-call(bf16[512,960]{1,0:T(8,128)(2,1)} %get-tuple-element.40.nm_ref, bf16[512,960]{1,0:T(8,128)(2,1)} %copy-done.1, bf16[960,1280]{1,0:T(8,128)(2,1)} %pad_maximum_fusion.3.wg_ref, ...), custom_call_target="tpu_custom_call" | custom-call | flops 7549747200 | bytes 16000000 | tf_op jit(solution)/shard_map/pallas_call | solution.py:298
  136.9 3.8 collective-permute-done.14
  141.9 13.7 %shard_map.206 = (bf16[512,960]{1,0:T(8,128)(2,1)}, bf16[512,960]{1,0:T(8,128)(2,1)}, bf16[512,1280]{1,0:T(8,128)(2,1)}, bf16[512,2560]{1,0:T(8,128)(2,1)}) custom-call(bf16[512,960]{1,0:T(8,128)(2,1)} %copy.122.nm_ref, bf16[512,960]{1,0:T(8,128)(2,1)} %copy.123.og_ref, bf16[960,1280]{1,0:T(8,128)(2,1)} %pad_maximum_fusion.3.wg_ref, ...), custom_call_target="tpu_custom_call" | custom-call | flops 7549747200 | bytes 16000000 | tf_op jit(solution)/shard_map/pallas_call | solution.py:298
  165.0 7.0 %convolution_convert_fusion = bf16[480,2560]{1,0:T(8,128)(2,1)} fusion(bf16[1024,2560]{1,0:T(8,128)(2,1)} %constant_dynamic-update-slice_fusion, pred[]{:T(512)S(6)} %eq.58, bf16[512,960]{1,0:T(8,128)(2,1)S(1)} %copy-done.12, bf16[512,960]{1,0:T(8,128)(2,1)S(1)} %copy-done.10), kind=kOutput, calls=%fused_computation.2 | convolution fusion | flops 2522234880 | bytes 9666561 | tf_op jit(solution)/shard_map/dot_general | solution.py:38
  176.6 6.5 %collective-permute-done.16 = bf16[512,960]{0,1:T(8,128)(2,1)} collective-permute-done((bf16[512,960]{0,1:T(8,128)(2,1)}, bf16[512,960]{0,1:T(8,128)(2,1)}, u32[]{:S(2)}, u32[]{:S(2)}) %collective-permute-start.16) | collective-permute-done | bytes 983072 | tf_op jit(solution)/shard_map/ppermute | solution.py:363
  188.8 13.1 %collective-permute-done.18 = bf16[512,960]{0,1:T(8,128)(2,1)} collective-permute-done((bf16[512,960]{0,1:T(8,128)(2,1)}, bf16[512,960]{0,1:T(8,128)(2,1)}, u32[]{:S(2)}, u32[]{:S(2)}) %collective-permute-start.18) | collective-permute-done | bytes 983072 | tf_op jit(solution)/shard_map/ppermute | solution.py:363
  204.1 7.0 %shard_map.207 = (f32[512,960]{1,0:T(8,128)}, bf16[512,960]{1,0:T(8,128)(2,1)}, bf16[15,512,64]{2,1,0:T(8,128)(2,1)}, f32[1,960]{1,0:T(1,128)}) custom-call(bf16[512,960]{1,0:T(8,128)(2,1)} %copy-done.1, f32[512,960]{1,0:T(8,128)} %get-tuple-element.39.mid_ref, f32[512,960]{1,0:T(8,128)} %get-tuple-element.43.own_ref, bf16[512,960]{1,0:T(8,128)(2,1)} %copy.127.got_ref, ...), custom_call_target="tpu_custom_call" | custom-call | flops 943718400 | bytes 14000000 | tf_op jit(solution)/shard_map/pallas_call | solution.py:315
  211.1 23.8 %shard_map.208 = (f32[15,512,64]{2,1,0:T(8,128)}, f32[2,5,512,64]{3,2,1,0:T(8,128)}, bf16[2,5,512,64]{3,2,1,0:T(8,128)(2,1)}) custom-call(s32[1]{0:T(128)} %bitcast.core_ref, s32[1,512]{1,0:T(1,128)} %bitcast.196, s32[1,512]{1,0:T(1,128)} %broadcast_select_fusion.48.begin_ref, bf16[15,512,64]{2,1,0:T(8,128)(2,1)} %get-tuple-element.37.q_ref, ...), custom_call_target="tpu_custom_call" | custom-call | flops 30000001024 | bytes 20000000 | tf_op jit(solution)/shard_map/pallas_call | solution.py:329
  239.4 3.9 convolution_add_fusion
  253.9 10.4 %shard_map.209 = (bf16[512,960]{1,0:T(8,128)(2,1)}, bf16[512,960]{1,0:T(8,128)(2,1)}, bf16[512,960]{1,0:T(8,128)(2,1)}, f32[1,960]{1,0:T(1,128)}) custom-call(f32[15,512,64]{2,1,0:T(8,128)} %get-tuple-element.47.dq_ref, f32[2,5,512,64]{3,2,1,0:T(8,128)} %get-tuple-element.48.mine_ref, bf16[2,5,512,64]{3,2,1,0:T(8,128)(2,1)} %copy.129.got_ref, ...), custom_call_target="tpu_custom_call" | custom-call | flops 1887436800 | bytes 20000000 | tf_op jit(solution)/shard_map/pallas_call | solution.py:352
  264.4 3.2 convolution_convert_fusion.3
  270.5 39.6 %psum.7 = f32[2,960]{1,0:T(2,128)S(1)} all-reduce(f32[2,960]{1,0:T(2,128)S(1)} %pad_maximum_fusion.23), channel_id=1, replica_groups=mesh['dp'=8,'row'=2,'col'=2] {'dp','row','col'}, use_global_device_ids=true, to_apply=%region_2.3 | all-reduce | flops 1920 | bytes 15360 | tf_op jit(solution)/shard_map/psum | solution.py:577
  310.7 3.8 fusion.36
  322.0 9.8 %collective-permute-done.54 = bf16[160,480]{1,0:T(8,128)(2,1)S(1)} collective-permute-done((bf16[160,480]{1,0:T(8,128)(2,1)S(1)}, bf16[160,480]{1,0:T(8,128)(2,1)S(1)}, u32[]{:S(2)}, u32[]{:S(2)}) %collective-permute-start.54) | collective-permute-done | bytes 153632 | tf_op jit(solution)/shard_map/ppermute | solution.py:396
  336.4 5.2 collective-permute-done.56
  341.6 8.1 %collective-permute-done.57 = bf16[160,480]{1,0:T(8,128)(2,1)S(1)} collective-permute-done((bf16[160,480]{1,0:T(8,128)(2,1)S(1)}, bf16[160,480]{1,0:T(8,128)(2,1)S(1)}, u32[]{:S(2)}, u32[]{:S(2)}) %collective-permute-start.57) | collective-permute-done | bytes 153632 | tf_op jit(solution)/shard_map/ppermute | solution.py:406
  351.3 4.7 collective-permute-done.58
  357.7 6.2 %convert_add_fusion = f32[480,2560]{1,0:T(8,128)S(1)} fusion(bf16[480,2560]{1,0:T(8,128)(2,1)} %collective-permute-done.42, bf16[1024,2560]{1,0:T(8,128)(2,1)} %constant_dynamic-update-slice_fusion, pred[]{:T(512)S(6)} %eq.58, bf16[512,960]{1,0:T(8,128)(2,1)S(1)} %copy-done.13, bf16[512,960]{1,0:T(8,128)(2,1)S(1)} %copy-done.11), kind=kOutput, calls=%fused_computation.1 | convolution fusion | flops 2523463680 | bytes 14581761 | tf_op jit(solution)/shard_map/dot_general | solution.py:38
  373.5 31.1 %collective-permute-done.34 = bf16[4,72,480]{2,1,0:T(8,128)(2,1)S(1)} collective-permute-done((bf16[4,72,480]{2,1,0:T(8,128)(2,1)S(1)}, bf16[4,72,480]{2,1,0:T(8,128)(2,1)S(1)}, u32[]{:S(2)}, u32[]{:S(2)}) %collective-permute-start.34) | collective-permute-done | bytes 276512 | tf_op jit(solution)/shard_map/ppermute | solution.py:396
  425.0 5.2 collective-permute-done.23
  436.2 6.2 %collective-permute-done.24 = bf16[4,64,960]{2,1,0:T(8,128)(2,1)S(1)} collective-permute-done((bf16[4,64,960]{2,1,0:T(8,128)(2,1)S(1)}, bf16[4,64,960]{2,1,0:T(8,128)(2,1)S(1)}, u32[]{:S(2)}, u32[]{:S(2)}) %collective-permute-start.24) | collective-permute-done | bytes 491552 | tf_op jit(solution)/shard_map/ppermute | solution.py:396
  453.9 24.9 %collective-permute-done.26 = bf16[64,960]{1,0:T(8,128)(2,1)S(1)} collective-permute-done((bf16[64,960]{1,0:T(8,128)(2,1)S(1)}, bf16[64,960]{1,0:T(8,128)(2,1)S(1)}, u32[]{:S(2)}, u32[]{:S(2)}) %collective-permute-start.26) | collective-permute-done | bytes 122912 | tf_op jit(solution)/shard_map/ppermute | solution.py:396
  489.8 27.9 %collective-permute-done.29 = bf16[64,960]{1,0:T(8,128)(2,1)S(1)} collective-permute-done((bf16[64,960]{1,0:T(8,128)(2,1)S(1)}, bf16[64,960]{1,0:T(8,128)(2,1)S(1)}, u32[]{:S(2)}, u32[]{:S(2)}) %collective-permute-start.29) | collective-permute-done | bytes 122912 | tf_op jit(solution)/shard_map/ppermute | solution.py:406
  523.8 8.8 %collective-permute-done.31 = bf16[4,64,960]{2,1,0:T(8,128)(2,1)S(1)} collective-permute-done((bf16[4,64,960]{2,1,0:T(8,128)(2,1)S(1)}, bf16[4,64,960]{2,1,0:T(8,128)(2,1)S(1)}, u32[]{:S(2)}, u32[]{:S(2)}) %collective-permute-start.31) | collective-permute-done | bytes 491552 | tf_op jit(solution)/shard_map/ppermute | solution.py:406
  541.5 16.6 %collective-permute-done.50 = bf16[4,120,1280]{2,1,0:T(8,128)(2,1)} collective-permute-done((bf16[4,120,1280]{2,1,0:T(8,128)(2,1)}, bf16[4,120,1280]{2,1,0:T(8,128)(2,1)}, u32[]{:S(2)}, u32[]{:S(2)}) %collective-permute-start.50) | collective-permute-done | bytes 1228832 | tf_op jit(solution)/shard_map/ppermute | solution.py:406
  (363 shorter events, 201.4 us)
Async XLA Ops:
  5.6 42.7 %collective-permute-start.4 = (bf16[480,960]{1,0:T(8,128)(2,1)}, bf16[480,960]{1,0:T(8,128)(2,1)}, u32[]{:S(2)}, u32[]{:S(2)}) collective-permute-start(bf16[480,960]{1,0:T(8,128)(2,1)} %pad_maximum_fusion.16), channel_id=1, source_target_pairs={{0,2},{2,0},{1,3},{3,1},{4,6},{6,4},{5,7},{7,5},{8,10},{10,8},{9,1... | collective-permute-start | bytes 2764808 | tf_op jit(solution)/shard_map/ppermute | solution.py:363
  8.6 35.2 %collective-permute-start.3 = (bf16[480,960]{1,0:T(8,128)(2,1)}, bf16[480,960]{1,0:T(8,128)(2,1)}, u32[]{:S(2)}, u32[]{:S(2)}) collective-permute-start(bf16[480,960]{1,0:T(8,128)(2,1)} %pad_maximum_fusion.16), channel_id=1, source_target_pairs={{0,1},{1,0},{2,3},{3,2},{4,5},{5,4},{6,7},{7,6},{8,9},{9,8},{10,11... | collective-permute-start | bytes 2764808 | tf_op jit(solution)/shard_map/ppermute | solution.py:363
  19.8 23.5 %collective-permute-start.8 = (bf16[576,480]{1,0:T(8,128)(2,1)}, bf16[576,480]{1,0:T(8,128)(2,1)}, u32[]{:S(2)}, u32[]{:S(2)}) collective-permute-start(bf16[576,480]{1,0:T(8,128)(2,1)} %bitcast.12), channel_id=1, source_target_pairs={{0,2},{2,0},{1,3},{3,1},{4,6},{6,4},{5,7},{7,5},{8,10},{10,8},{9,1... | collective-permute-start | bytes 1658888 | tf_op jit(solution)/shard_map/ppermute | solution.py:363
  29.1 25.2 %collective-permute-start.13 = (bf16[1280,480]{0,1:T(8,128)(2,1)}, bf16[1280,480]{0,1:T(8,128)(2,1)}, u32[]{:S(2)}, u32[]{:S(2)}) collective-permute-start(bf16[1280,480]{0,1:T(8,128)(2,1)} %param.19), channel_id=1, source_target_pairs={{0,1},{1,0},{2,3},{3,2},{4,5},{5,4},{6,7},{7,6},{8,9},{9,8},{10,11... | collective-permute-start | bytes 3686408 | tf_op jit(solution)/shard_map/ppermute | solution.py:363
  48.3 35.7 %collective-permute-start.15 = (bf16[512,960]{0,1:T(8,128)(2,1)}, bf16[512,960]{0,1:T(8,128)(2,1)}, u32[]{:S(2)}, u32[]{:S(2)}) collective-permute-start(bf16[512,960]{0,1:T(8,128)(2,1)} %copy.121), channel_id=1, source_target_pairs={{0,2},{2,0},{1,3},{3,1},{4,6},{6,4},{5,7},{7,5},{8,10},{10,8},{9,1... | collective-permute-start | bytes 2949128 | tf_op jit(solution)/shard_map/ppermute | solution.py:363
  117.2 23.4 %collective-permute-start.14 = (bf16[512,960]{0,1:T(8,128)(2,1)S(1)}, bf16[512,960]{0,1:T(8,128)(2,1)S(1)}, u32[]{:S(2)}, u32[]{:S(2)}) collective-permute-start(bf16[512,960]{0,1:T(8,128)(2,1)S(1)} %copy.120), channel_id=1, source_target_pairs={{0,2},{2,0},{1,3},{3,1},{4,6},{6,4},{5,7},{7,5},{8,10},{10,8},{9,1... | collective-permute-start | bytes 2949128 | tf_op jit(solution)/shard_map/ppermute | solution.py:363
  158.0 25.0 %collective-permute-start.16 = (bf16[512,960]{0,1:T(8,128)(2,1)}, bf16[512,960]{0,1:T(8,128)(2,1)}, u32[]{:S(2)}, u32[]{:S(2)}) collective-permute-start(bf16[512,960]{0,1:T(8,128)(2,1)} %copy.124), channel_id=1, source_target_pairs={{0,2},{2,0},{1,3},{3,1},{4,6},{6,4},{5,7},{7,5},{8,10},{10,8},{9,1... | collective-permute-start | bytes 2949128 | tf_op jit(solution)/shard_map/ppermute | solution.py:363
  161.1 40.7 %collective-permute-start.18 = (bf16[512,960]{0,1:T(8,128)(2,1)}, bf16[512,960]{0,1:T(8,128)(2,1)}, u32[]{:S(2)}, u32[]{:S(2)}) collective-permute-start(bf16[512,960]{0,1:T(8,128)(2,1)} %copy.126), channel_id=1, source_target_pairs={{0,2},{2,0},{1,3},{3,1},{4,6},{6,4},{5,7},{7,5},{8,10},{10,8},{9,1... | collective-permute-start | bytes 2949128 | tf_op jit(solution)/shard_map/ppermute | solution.py:363
  172.0 185.7 %collective-permute-start.42 = (bf16[480,2560]{1,0:T(8,128)(2,1)}, bf16[480,2560]{1,0:T(8,128)(2,1)}, u32[]{:S(2)}, u32[]{:S(2)}) collective-permute-start(bf16[480,2560]{1,0:T(8,128)(2,1)} %convolution_convert_fusion), channel_id=1, source_target_pairs={{0,1},{1,0},{2,3},{3,2},{4,5},{5,4},{6,7},{7,6},{8,9},{9,8},{10,11... | collective-permute-start | bytes 7372808 | tf_op jit(solution)/shard_map/ppermute | solution.py:363
  176.6 62.9 %collective-permute-start.51 = (bf16[1280,480]{0,1:T(8,128)(2,1)}, bf16[1280,480]{0,1:T(8,128)(2,1)}, u32[]{:S(2)}, u32[]{:S(2)}) collective-permute-start(bf16[1280,480]{0,1:T(8,128)(2,1)} %convolution_convert_fusion.1), channel_id=1, source_target_pairs={{0,1},{1,0},{2,3},{3,2},{4,5},{5,4},{6,7},{7,6},{8,9},{9,8},{10,11... | collective-permute-start | bytes 3686408 | tf_op jit(solution)/shard_map/ppermute | solution.py:363
  188.8 59.7 %collective-permute-start.17 = (bf16[512,480]{1,0:T(8,128)(2,1)}, bf16[512,480]{1,0:T(8,128)(2,1)}, u32[]{:S(2)}, u32[]{:S(2)}) collective-permute-start(bf16[512,480]{1,0:T(8,128)(2,1)} %broadcast_select_fusion.28), channel_id=1, source_target_pairs={{0,1},{1,0},{2,3},{3,2},{4,5},{5,4},{6,7},{7,6},{8,9},{9,8},{10,11... | collective-permute-start | bytes 1474568 | tf_op jit(solution)/shard_map/ppermute | solution.py:363
  238.9 79.2 %collective-permute-start.32 = (bf16[960,480]{1,0:T(8,128)(2,1)}, bf16[960,480]{1,0:T(8,128)(2,1)}, u32[]{:S(2)}, u32[]{:S(2)}) collective-permute-start(bf16[960,480]{1,0:T(8,128)(2,1)} %convolution_convert_fusion.2), channel_id=1, source_target_pairs={{0,1},{1,0},{2,3},{3,2},{4,5},{5,4},{6,7},{7,6},{8,9},{9,8},{10,11... | collective-permute-start | bytes 2764808 | tf_op jit(solution)/shard_map/ppermute | solution.py:363
  246.9 67.7 %collective-permute-start.52 = (bf16[4,160,480]{2,1,0:T(8,128)(2,1)S(1)}, bf16[4,160,480]{2,1,0:T(8,128)(2,1)S(1)}, u32[]{:S(2)}, u32[]{:S(2)}) collective-permute-start(bf16[4,160,480]{2,1,0:T(8,128)(2,1)S(1)} %fusion.20), channel_id=1, source_target_pairs={{0,4},{4,0},{8,12},{12,8},{16,20},{20,16},{24,28},{28,24},{1,5},{5... | collective-permute-start | bytes 1843208 | tf_op jit(solution)/shard_map/ppermute | solution.py:396
  270.5 63.0 %collective-permute-start.20 = (bf16[512,480]{1,0:T(8,128)(2,1)}, bf16[512,480]{1,0:T(8,128)(2,1)}, u32[]{:S(2)}, u32[]{:S(2)}) collective-permute-start(bf16[512,480]{1,0:T(8,128)(2,1)} %broadcast_select_fusion.24), channel_id=1, source_target_pairs={{0,1},{1,0},{2,3},{3,2},{4,5},{5,4},{6,7},{7,6},{8,9},{9,8},{10,11... | collective-permute-start | bytes 1474568 | tf_op jit(solution)/shard_map/ppermute | solution.py:363
  322.0 48.5 %collective-permute-start.22 = (bf16[480,960]{1,0:T(8,128)(2,1)}, bf16[480,960]{1,0:T(8,128)(2,1)}, u32[]{:S(2)}, u32[]{:S(2)}) collective-permute-start(bf16[480,960]{1,0:T(8,128)(2,1)} %convolution_convert_fusion.3), channel_id=1, source_target_pairs={{0,1},{1,0},{2,3},{3,2},{4,5},{5,4},{6,7},{7,6},{8,9},{9,8},{10,11... | collective-permute-start | bytes 2764808 | tf_op jit(solution)/shard_map/ppermute | solution.py:363
  331.8 93.2 %collective-permute-start.21 = (bf16[480,960]{1,0:T(8,128)(2,1)}, bf16[480,960]{1,0:T(8,128)(2,1)}, u32[]{:S(2)}, u32[]{:S(2)}) collective-permute-start(bf16[480,960]{1,0:T(8,128)(2,1)} %convolution_convert_fusion.4), channel_id=1, source_target_pairs={{0,1},{1,0},{2,3},{3,2},{4,5},{5,4},{6,7},{7,6},{8,9},{9,8},{10,11... | collective-permute-start | bytes 2764808 | tf_op jit(solution)/shard_map/ppermute | solution.py:363
  331.8 34.7 %collective-permute-start.33 = (bf16[576,480]{1,0:T(8,128)(2,1)S(1)}, bf16[576,480]{1,0:T(8,128)(2,1)}, u32[]{:S(2)}, u32[]{:S(2)}) collective-permute-start(bf16[576,480]{1,0:T(8,128)(2,1)S(1)} %fusion.2), channel_id=1, source_target_pairs={{0,2},{2,0},{1,3},{3,1},{4,6},{6,4},{5,7},{7,5},{8,10},{10,8},{9,1... | collective-permute-start | bytes 1658888 | tf_op jit(solution)/shard_map/ppermute | solution.py:363
  356.0 49.7 %collective-permute-start.59 = (bf16[4,160,480]{2,1,0:T(8,128)(2,1)S(1)}, bf16[4,160,480]{2,1,0:T(8,128)(2,1)S(1)}, u32[]{:S(2)}, u32[]{:S(2)}) collective-permute-start(bf16[4,160,480]{2,1,0:T(8,128)(2,1)S(1)} %bitcast_dynamic-update-slice_fusion.12), channel_id=1, source_target_pairs={{0,4},{4,0},{8,12},{12,8},{16,20},{20,16},{24,28},{28,24},{1,5},{5... | collective-permute-start | bytes 1843208 | tf_op jit(solution)/shard_map/ppermute | solution.py:406
  365.8 68.7 %collective-permute-start.43 = (bf16[4,120,1280]{2,1,0:T(8,128)(2,1)}, bf16[4,120,1280]{2,1,0:T(8,128)(2,1)}, u32[]{:S(2)}, u32[]{:S(2)}) collective-permute-start(bf16[4,120,1280]{2,1,0:T(8,128)(2,1)} %fusion), channel_id=1, source_target_pairs={{0,4},{4,0},{8,12},{12,8},{16,20},{20,16},{24,28},{28,24},{1,5},{5... | collective-permute-start | bytes 3686408 | tf_op jit(solution)/shard_map/ppermute | solution.py:396
  369.8 34.8 %collective-permute-start.34 = (bf16[4,72,480]{2,1,0:T(8,128)(2,1)S(1)}, bf16[4,72,480]{2,1,0:T(8,128)(2,1)S(1)}, u32[]{:S(2)}, u32[]{:S(2)}) collective-permute-start(bf16[4,72,480]{2,1,0:T(8,128)(2,1)S(1)} %fusion.43), channel_id=1, source_target_pairs={{0,4},{4,0},{8,12},{12,8},{16,20},{20,16},{24,28},{28,24},{1,5},{5... | collective-permute-start | bytes 829448 | tf_op jit(solution)/shard_map/ppermute | solution.py:396
  423.4 23.7 %collective-permute-start.41 = (bf16[4,72,480]{2,1,0:T(8,128)(2,1)S(1)}, bf16[4,72,480]{2,1,0:T(8,128)(2,1)S(1)}, u32[]{:S(2)}, u32[]{:S(2)}) collective-permute-start(bf16[4,72,480]{2,1,0:T(8,128)(2,1)S(1)} %bitcast_dynamic-update-slice_fusion.20), channel_id=1, source_target_pairs={{0,4},{4,0},{8,12},{12,8},{16,20},{20,16},{24,28},{28,24},{1,5},{5... | collective-permute-start | bytes 829448 | tf_op jit(solution)/shard_map/ppermute | solution.py:406
  445.0 34.0 %collective-permute-start.46 = (bf16[120,1280]{1,0:T(8,128)(2,1)S(1)}, bf16[120,1280]{1,0:T(8,128)(2,1)S(1)}, u32[]{:S(2)}, u32[]{:S(2)}) collective-permute-start(bf16[120,1280]{1,0:T(8,128)(2,1)S(1)} %get-tuple-element.128), channel_id=1, source_target_pairs={{0,24},{4,28},{8,0},{12,4},{16,8},{20,12},{24,16},{28,20},{1,25},{... | collective-permute-start | bytes 921608 | tf_op jit(solution)/shard_map/ppermute | solution.py:396
  446.5 32.6 %collective-permute-start.45 = (bf16[120,1280]{1,0:T(8,128)(2,1)S(1)}, bf16[120,1280]{1,0:T(8,128)(2,1)S(1)}, u32[]{:S(2)}, u32[]{:S(2)}) collective-permute-start(bf16[120,1280]{1,0:T(8,128)(2,1)S(1)} %get-tuple-element.129), channel_id=1, source_target_pairs={{0,16},{4,20},{8,24},{12,28},{16,0},{20,4},{24,8},{28,12},{1,17},{... | collective-permute-start | bytes 921608 | tf_op jit(solution)/shard_map/ppermute | solution.py:396
  446.5 32.6 %collective-permute-start.44 = (bf16[120,1280]{1,0:T(8,128)(2,1)S(1)}, bf16[120,1280]{1,0:T(8,128)(2,1)S(1)}, u32[]{:S(2)}, u32[]{:S(2)}) collective-permute-start(bf16[120,1280]{1,0:T(8,128)(2,1)S(1)} %get-tuple-element.127), channel_id=1, source_target_pairs={{0,8},{4,12},{8,16},{12,20},{16,24},{20,28},{24,0},{28,4},{1,9},{5... | collective-permute-start | bytes 921608 | tf_op jit(solution)/shard_map/ppermute | solution.py:396
  447.1 31.7 %collective-permute-start.26 = (bf16[64,960]{1,0:T(8,128)(2,1)S(1)}, bf16[64,960]{1,0:T(8,128)(2,1)S(1)}, u32[]{:S(2)}, u32[]{:S(2)}) collective-permute-start(bf16[64,960]{1,0:T(8,128)(2,1)S(1)} %get-tuple-element.159), channel_id=1, source_target_pairs={{0,16},{4,20},{8,24},{12,28},{16,0},{20,4},{24,8},{28,12},{1,17},{... | collective-permute-start | bytes 368648 | tf_op jit(solution)/shard_map/ppermute | solution.py:396
  450.0 28.8 %collective-permute-start.25 = (bf16[64,960]{1,0:T(8,128)(2,1)S(1)}, bf16[64,960]{1,0:T(8,128)(2,1)S(1)}, u32[]{:S(2)}, u32[]{:S(2)}) collective-permute-start(bf16[64,960]{1,0:T(8,128)(2,1)S(1)} %get-tuple-element.157), channel_id=1, source_target_pairs={{0,8},{4,12},{8,16},{12,20},{16,24},{20,28},{24,0},{28,4},{1,9},{5... | collective-permute-start | bytes 368648 | tf_op jit(solution)/shard_map/ppermute | solution.py:396
  481.0 38.4 %collective-permute-start.47 = (bf16[120,1280]{1,0:T(8,128)(2,1)S(1)}, bf16[120,1280]{1,0:T(8,128)(2,1)S(1)}, u32[]{:S(2)}, u32[]{:S(2)}) collective-permute-start(bf16[120,1280]{1,0:T(8,128)(2,1)S(1)} %get-tuple-element.110), channel_id=1, source_target_pairs={{0,8},{4,12},{8,16},{12,20},{16,24},{20,28},{24,0},{28,4},{1,9},{5... | collective-permute-start | bytes 921608 | tf_op jit(solution)/shard_map/ppermute | solution.py:406
  483.4 36.8 %collective-permute-start.48 = (bf16[120,1280]{1,0:T(8,128)(2,1)S(1)}, bf16[120,1280]{1,0:T(8,128)(2,1)S(1)}, u32[]{:S(2)}, u32[]{:S(2)}) collective-permute-start(bf16[120,1280]{1,0:T(8,128)(2,1)S(1)} %get-tuple-element.110), channel_id=1, source_target_pairs={{0,16},{4,20},{8,24},{12,28},{16,0},{20,4},{24,8},{28,12},{1,17},{... | collective-permute-start | bytes 921608 | tf_op jit(solution)/shard_map/ppermute | solution.py:406
  485.4 35.5 %collective-permute-start.49 = (bf16[120,1280]{1,0:T(8,128)(2,1)S(1)}, bf16[120,1280]{1,0:T(8,128)(2,1)S(1)}, u32[]{:S(2)}, u32[]{:S(2)}) collective-permute-start(bf16[120,1280]{1,0:T(8,128)(2,1)S(1)} %get-tuple-element.110), channel_id=1, source_target_pairs={{0,24},{4,28},{8,0},{12,4},{16,8},{20,12},{24,16},{28,20},{1,25},{... | collective-permute-start | bytes 921608 | tf_op jit(solution)/shard_map/ppermute | solution.py:406
  485.8 31.9 %collective-permute-start.29 = (bf16[64,960]{1,0:T(8,128)(2,1)S(1)}, bf16[64,960]{1,0:T(8,128)(2,1)S(1)}, u32[]{:S(2)}, u32[]{:S(2)}) collective-permute-start(bf16[64,960]{1,0:T(8,128)(2,1)S(1)} %get-tuple-element.114), channel_id=1, source_target_pairs={{0,16},{4,20},{8,24},{12,28},{16,0},{20,4},{24,8},{28,12},{1,17},{... | collective-permute-start | bytes 368648 | tf_op jit(solution)/shard_map/ppermute | solution.py:406
  487.3 30.4 %collective-permute-start.30 = (bf16[64,960]{1,0:T(8,128)(2,1)S(1)}, bf16[64,960]{1,0:T(8,128)(2,1)S(1)}, u32[]{:S(2)}, u32[]{:S(2)}) collective-permute-start(bf16[64,960]{1,0:T(8,128)(2,1)S(1)} %get-tuple-element.114), channel_id=1, source_target_pairs={{0,24},{4,28},{8,0},{12,4},{16,8},{20,12},{24,16},{28,20},{1,25},{... | collective-permute-start | bytes 368648 | tf_op jit(solution)/shard_map/ppermute | solution.py:406
  521.6 36.4 %collective-permute-start.50 = (bf16[4,120,1280]{2,1,0:T(8,128)(2,1)}, bf16[4,120,1280]{2,1,0:T(8,128)(2,1)}, u32[]{:S(2)}, u32[]{:S(2)}) collective-permute-start(bf16[4,120,1280]{2,1,0:T(8,128)(2,1)} %bitcast_dynamic-update-slice_fusion.6), channel_id=1, source_target_pairs={{0,4},{4,0},{8,12},{12,8},{16,20},{20,16},{24,28},{28,24},{1,5},{5... | collective-permute-start | bytes 3686408 | tf_op jit(solution)/shard_map/ppermute | solution.py:406
  (78 other events, 608.2 us)

commit v2 on v0

v2 whole, which is shorter than its diff:
```python
import functools
import math

import jax
import jax.numpy as jnp
from jax import lax
from jax.experimental import pallas as pl
from jax.experimental.pallas import tpu as pltpu
from jax.sharding import PartitionSpec as P

D = 960
HALF = D // 2
HDIM = 64
ROT = HDIM // 2
GROUP = 3
GROUPS = 3
QUERY = GROUPS * GROUP * HDIM
KEY = GROUPS * HDIM
MAXLEN = 1024
BLOCK = MAXLEN // 4
LOCAL = 2 * BLOCK
LIVE = (3, 2)

NORM_EPS = 1e-05
ROPE_BASE = 100000.0
MASKED_SCORE = -1e30
SCALE = 1.0 / math.sqrt(HDIM)
BF16 = jnp.bfloat16
F32 = jnp.float32
VMEM_BYTES = 56 * 1024 * 1024

HELD = ((0, 3), (1, 2))
LAID = ((0, 3, 1, 2), (0, 1, 2))
SPANS = ((1, 4), (2, 3))


def dot(left, right, left_dim=1, right_dim=0):
    return lax.dot_general(
        left, right, (((left_dim,), (right_dim,)), ((), ())), preferred_element_type=F32
    )


def shape(dims, dtype=BF16):
    return jax.ShapeDtypeStruct(dims, dtype)


def whole(dims):
    return pl.BlockSpec(dims, lambda *_: (0,) * len(dims))


SMEM_SPEC = pl.BlockSpec(memory_space=pltpu.SMEM)


def run(kernel, ins, outs, flops, grid=None, in_specs=None, out_specs=None, scratch=(), after=()):
    moved = sum(a.size * a.dtype.itemsize for a in ins)
    moved += sum(math.prod(o.shape) * jnp.dtype(o.dtype).itemsize for o in outs)
    if in_specs is None:
        in_specs = [whole(a.shape) for a in ins]
    if out_specs is None:
        out_specs = [whole(o.shape) for o in outs]
    count = len(ins)

    def body(*refs):
        kernel(*refs[:count], *refs[count + len(after) :])

    return pl.pallas_call(
        body,
        grid=grid if grid is not None else (1,),
        in_specs=list(in_specs) + [pl.BlockSpec(memory_space=pl.ANY)] * len(after),
        out_specs=tuple(out_specs),
        out_shape=tuple(outs),
        scratch_shapes=list(scratch),
        compiler_params=pltpu.CompilerParams(vmem_limit_bytes=VMEM_BYTES),
        cost_estimate=pl.CostEstimate(
            flops=int(flops), bytes_accessed=int(moved), transcendentals=0
        ),
    )(*ins, *after)


def level_of(own, got):
    total = jnp.sum(own * own, axis=0, keepdims=True) + jnp.sum(got * got, axis=0, keepdims=True)
    return lax.rsqrt(total / D + NORM_EPS)


def project_heads(nm, cos_ref, sin_ref, own_ref, got_ref, q_ref, kv_ref):
    cosine, sine = cos_ref[...], sin_ref[...]
    joined = dot(own_ref[...], nm[:HALF]) + dot(got_ref[...], nm[HALF:])
    for at in range(0, QUERY + KEY, HDIM):
        low, high = joined[at : at + ROT], joined[at + ROT : at + HDIM]
        parts = (low * cosine - high * sine, high * cosine + low * sine)
        for part, turned in enumerate(parts):
            turned = turned.astype(BF16)
            if at < QUERY:
                turned = (turned.astype(F32) * SCALE).astype(BF16)
                q_ref[at + part * ROT : at + (part + 1) * ROT, :] = turned
            else:
                row = at - QUERY + part * ROT
                kv_ref[row : row + ROT, :] = turned
    kv_ref[KEY:, :] = joined[QUERY + KEY :].astype(BF16)


def project_near_kernel(
    xo_ref, xg_ref, go_ref, gg_ref, cos_ref, sin_ref, own_ref, got_ref, nm_ref, q_ref, kv_ref
):
    own, got = xo_ref[...].astype(F32), xg_ref[...].astype(F32)
    level = level_of(own, got)
    nm_ref[:HALF, :] = (own * level * go_ref[...]).astype(BF16)
    nm_ref[HALF:, :] = (got * level * gg_ref[...]).astype(BF16)
    project_heads(nm_ref[...], cos_ref, sin_ref, own_ref, got_ref, q_ref, kv_ref)


def project_far_kernel(nm_ref, cos_ref, sin_ref, own_ref, got_ref, q_ref, kv_ref):
    project_heads(nm_ref[...], cos_ref, sin_ref, own_ref, got_ref, q_ref, kv_ref)


def laid(core, own, got, axis):
    if core == 0:
        return jnp.concatenate([own, got], axis=axis)
    return jnp.concatenate([lax.slice_in_dim(got, 0, BLOCK, axis=axis), own], axis=axis)


def fill_bias(core, bias_ref, begin_ref):
    for at, block in enumerate(LAID[core]):
        for slot in range(2):
            cols = slice(slot * BLOCK, (slot + 1) * BLOCK)
            key = block * BLOCK + lax.broadcasted_iota(jnp.int32, (BLOCK, BLOCK), 0)
            query = HELD[core][slot] * BLOCK + lax.broadcasted_iota(jnp.int32, (BLOCK, BLOCK), 1)
            allowed = (key >= begin_ref[:, cols]) & (key <= query)
            bias_ref[at * BLOCK : (at + 1) * BLOCK, cols] = jnp.where(allowed, 0.0, MASKED_SCORE)


def attend_kernel(
    where_ref, begin_ref, q_ref, ko_ref, vo_ref, kg_ref, vg_ref, att_ref, lse_ref, bias_ref
):
    group = pl.program_id(0)
    live = group < where_ref[1]

    @pl.when(jnp.logical_not(live))
    def _():
        att_ref[...] = jnp.zeros_like(att_ref)
        lse_ref[...] = jnp.zeros_like(lse_ref)

    for core in range(2):

        @pl.when(live & (where_ref[0] == core))
        def _():
            @pl.when(group == 0)
            def _():
                fill_bias(core, bias_ref, begin_ref)

            keys = laid(core, ko_ref[...], kg_ref[...], 1).T
            values = laid(core, vo_ref[...], vg_ref[...], 1)
            for slot in range(2):
                cols = slice(slot * BLOCK, (slot + 1) * BLOCK)
                span = SPANS[core][slot] * BLOCK
                for j in range(GROUP):
                    heads = slice(j * HDIM, (j + 1) * HDIM)
                    scores = dot(keys[:span], q_ref[heads, cols]) + bias_ref[:span, cols]
                    highest = jnp.max(scores, axis=0, keepdims=True)
                    weights = jnp.exp(scores - highest)
                    total = jnp.sum(weights, axis=0, keepdims=True)
                    mixed = dot(values[:, :span], weights.astype(BF16)) / total
                    att_ref[heads, cols] = mixed.astype(BF16)
                    lse_ref[0, j : j + 1, cols] = highest + jnp.log(total)


def mid_kernel(
    near_ref, far_ref, no_ref, ng_ref, fo_ref, fg_ref, xo_ref, xg_ref, go_ref, gg_ref,
    mid_ref, nm_ref,
):
    near, far = near_ref[...], far_ref[...]
    own = xo_ref[...].astype(F32) + dot(no_ref[...], near, 0, 0) + dot(fo_ref[...], far, 0, 0)
    got = xg_ref[...].astype(F32) + dot(ng_ref[...], near, 0, 0) + dot(fg_ref[...], far, 0, 0)
    mid_ref[:HALF, :] = own
    mid_ref[HALF:, :] = got
    level = level_of(own, got)
    nm_ref[:HALF, :] = (own * level * go_ref[...]).astype(BF16)
    nm_ref[HALF:, :] = (got * level * gg_ref[...]).astype(BF16)


def mlp_kernel(
    nm_ref, og_ref, wgo_ref, wgg_ref, wuo_ref, wug_ref, wdo_ref, wdg_ref,
    out_ref, gnm_ref, act_ref, gg_ref, gu_ref, out_sum, gnm_sum,
):
    step = pl.program_id(0)

    def inward(own_ref, got_ref, rows_ref):
        return dot(own_ref[...], rows_ref[:HALF, :], 0, 0) + dot(
            got_ref[...], rows_ref[HALF:, :], 0, 0
        )

    @pl.when(step == 0)
    def _():
        out_sum[...] = jnp.zeros_like(out_sum)
        gnm_sum[...] = jnp.zeros_like(gnm_sum)

    gate = inward(wgo_ref, wgg_ref, nm_ref)
    up = inward(wuo_ref, wug_ref, nm_ref)
    grad_act = inward(wdo_ref, wdg_ref, og_ref)
    sig = jax.nn.sigmoid(gate)
    silu = gate * sig
    act = (silu * up).astype(BF16)
    grad_gate = (grad_act * up * sig * (1.0 + gate * (1.0 - sig))).astype(BF16)
    grad_up = (grad_act * silu).astype(BF16)
    act_ref[...] = act
    gg_ref[...] = grad_gate
    gu_ref[...] = grad_up
    gnm_sum[:HALF, :] += dot(wgo_ref[...], grad_gate) + dot(wuo_ref[...], grad_up)
    gnm_sum[HALF:, :] += dot(wgg_ref[...], grad_gate) + dot(wug_ref[...], grad_up)
    out_sum[:HALF, :] += dot(wdo_ref[...], act)
    out_sum[HALF:, :] += dot(wdg_ref[...], act)

    @pl.when(step == pl.num_programs(0) - 1)
    def _():
        out_ref[...] = out_sum[...].astype(out_ref.dtype)
        gnm_ref[...] = gnm_sum[...].astype(gnm_ref.dtype)


def grads_kernel(rows_ref, rows_far_ref, cols_ref, cols_far_ref, keep_ref, send_ref):
    for half, out_ref in enumerate((keep_ref, send_ref)):
        rows = slice(half * HALF, (half + 1) * HALF)
        product = dot(rows_ref[rows, :], cols_ref[...], 1, 1)
        product += dot(rows_far_ref[rows, :], cols_far_ref[...], 1, 1)
        out_ref[...] = product.astype(BF16)


def mid_back_kernel(
    og_ref, mid_ref, part_ref, back_ref, go_ref, gg_ref, no_ref, ng_ref, fo_ref, fg_ref,
    gmid_ref, gb_ref, near_ref, far_ref, ggain_ref,
):
    own, got = mid_ref[:HALF, :], mid_ref[HALF:, :]
    level = level_of(own, got)
    gnm = part_ref[...] + back_ref[...].astype(F32)
    scaled_own, scaled_got = gnm[:HALF] * go_ref[...], gnm[HALF:] * gg_ref[...]
    inner = jnp.sum(scaled_own * own, axis=0, keepdims=True)
    inner += jnp.sum(scaled_got * got, axis=0, keepdims=True)
    pull = level**3 * inner / D
    for rows, mid, scaled in (
        (slice(0, HALF), own, scaled_own), (slice(HALF, D), got, scaled_got)
    ):
        ggain_ref[rows, :] = jnp.sum(gnm[rows] * mid * level, axis=1, keepdims=True)
        gmid = og_ref[rows, :].astype(F32) + scaled * level - mid * pull
        gmid_ref[rows, :] = gmid
        gb_ref[rows, :] = gmid.astype(BF16)
    gb_own, gb_got = gb_ref[:HALF, :], gb_ref[HALF:, :]
    near_ref[...] = (dot(no_ref[...], gb_own) + dot(ng_ref[...], gb_got)).astype(BF16)
    far_ref[...] = (dot(fo_ref[...], gb_own) + dot(fg_ref[...], gb_got)).astype(BF16)


def attend_back_kernel(
    where_ref, begin_ref, q_ref, ko_ref, vo_ref, kg_ref, vg_ref, gatt_ref, lse_ref,
    dq_ref, own_ref, got_ref, bias_ref, dk_ref, dv_ref,
):
    group = pl.program_id(0)
    live = group < where_ref[1]

    @pl.when(jnp.logical_not(live))
    def _():
        dq_ref[...] = jnp.zeros_like(dq_ref)
        own_ref[...] = jnp.zeros_like(own_ref)
        got_ref[...] = jnp.zeros_like(got_ref)

    for core in range(2):

        @pl.when(live & (where_ref[0] == core))
        def _():
            @pl.when(group == 0)
            def _():
                fill_bias(core, bias_ref, begin_ref)

            keys_t = laid(core, ko_ref[...], kg_ref[...], 1)
            keys = keys_t.T
            values = laid(core, vo_ref[...], vg_ref[...], 1).T
            dk_ref[...] = jnp.zeros_like(dk_ref)
            dv_ref[...] = jnp.zeros_like(dv_ref)
            for slot in range(2):
                cols = slice(slot * BLOCK, (slot + 1) * BLOCK)
                span = SPANS[core][slot] * BLOCK
                for j in range(GROUP):
                    heads = slice(j * HDIM, (j + 1) * HDIM)
                    queries, grads = q_ref[heads, cols], gatt_ref[heads, cols]
                    scores = dot(keys[:span], queries) + bias_ref[:span, cols]
                    probs = jnp.exp(scores - lse_ref[0, j : j + 1, cols])
                    dprobs = dot(values[:span], grads)
                    inner = jnp.sum(probs * dprobs, axis=0, keepdims=True)
                    dscores = (probs * (dprobs - inner)).astype(BF16)
                    dv_ref[:span, :] += dot(probs.astype(BF16), grads.T)
                    dk_ref[:span, :] += dot(dscores, queries.T)
                    dq_ref[heads, cols] = dot(keys_t[:, :span], dscores) * SCALE
            for kind, grad_ref in enumerate((dk_ref, dv_ref)):
                if core == 0:
                    own_ref[kind, 0] = grad_ref[:LOCAL, :].T
                    got_ref[kind, 0] = grad_ref[LOCAL:, :].T.astype(BF16)
                else:
                    own_ref[kind, 0] = grad_ref[BLOCK : BLOCK + LOCAL, :].T
                    got_ref[kind, 0, :, :BLOCK] = grad_ref[:BLOCK, :].T.astype(BF16)
                    got_ref[kind, 0, :, BLOCK:] = jnp.zeros((HDIM, BLOCK), BF16)


def turn_back(cos_ref, sin_ref, dq_ref, own_ref, got_ref, gj_ref):
    cosine, sine = cos_ref[...], sin_ref[...]

    def back(at, grad):
        low, high = grad[:ROT], grad[ROT:]
        gj_ref[at : at + ROT, :] = (low * cosine + high * sine).astype(BF16)
        gj_ref[at + ROT : at + HDIM, :] = (high * cosine - low * sine).astype(BF16)

    for at in range(0, QUERY, HDIM):
        back(at, dq_ref[at : at + HDIM, :])
    for g in range(GROUPS):
        back(QUERY + g * HDIM, own_ref[0, g] + got_ref[0, g].astype(F32))
        at = QUERY + KEY + g * HDIM
        gj_ref[at : at + HDIM, :] = (own_ref[1, g] + got_ref[1, g].astype(F32)).astype(BF16)


def joined_far_kernel(
    dq_ref, own_ref, got_ref, cos_ref, sin_ref, wo_ref, wg_ref, nm_ref,
    gnm_ref, keep_ref, send_ref, gj_ref,
):
    turn_back(cos_ref, sin_ref, dq_ref, own_ref, got_ref, gj_ref)
    gj = gj_ref[...]
    send_ref[...] = dot(gj, nm_ref[HALF:, :], 1, 1).astype(BF16)
    keep_ref[...] = dot(gj, nm_ref[:HALF, :], 1, 1).astype(BF16)
    gnm_ref[:HALF, :] = dot(wo_ref[...], gj, 0, 0)
    gnm_ref[HALF:, :] = dot(wg_ref[...], gj, 0, 0)


def joined_near_kernel(
    dq_ref, own_ref, got_ref, cos_ref, sin_ref, wo_ref, wg_ref, nm_ref, part_ref, xo_ref, xg_ref,
    go_ref, gg_ref, gmid_ref, keep_ref, send_ref, grad_ref, ggain_ref, gj_ref,
):
    turn_back(cos_ref, sin_ref, dq_ref, own_ref, got_ref, gj_ref)
    gj = gj_ref[...]
    send_ref[...] = dot(gj, nm_ref[HALF:, :], 1, 1).astype(BF16)
    keep_ref[...] = dot(gj, nm_ref[:HALF, :], 1, 1).astype(BF16)
    gnm_own = part_ref[:HALF, :] + dot(wo_ref[...], gj, 0, 0)
    gnm_got = part_ref[HALF:, :] + dot(wg_ref[...], gj, 0, 0)
    own, got = xo_ref[...].astype(F32), xg_ref[...].astype(F32)
    level = level_of(own, got)
    scaled_own, scaled_got = gnm_own * go_ref[...], gnm_got * gg_ref[...]
    inner = jnp.sum(scaled_own * own, axis=0, keepdims=True)
    inner += jnp.sum(scaled_got * got, axis=0, keepdims=True)
    pull = level**3 * inner / D
    for rows, x, gnm, scaled in (
        (slice(0, HALF), own, gnm_own, scaled_own), (slice(HALF, D), got, gnm_got, scaled_got)
    ):
        ggain_ref[rows, :] = jnp.sum(gnm * x * level, axis=1, keepdims=True)
        grad_ref[rows, :] = (gmid_ref[rows, :] + scaled * level - x * pull).astype(BF16)


def per_group(rows, at=0):
    return pl.BlockSpec((rows, LOCAL), lambda g: (g + at, 0))


LSE_SPEC = pl.BlockSpec((1, 8, LOCAL), lambda g: (g, 0, 0))
KV_SPECS = [per_group(HDIM), per_group(HDIM, GROUPS)] * 2
PAIR_SPEC = pl.BlockSpec((2, 1, HDIM, LOCAL), lambda g: (0, g, 0, 0))


def attend(where, begin, q, kv, kv_got, after=()):
    return run(
        attend_kernel,
        (where, begin, q, kv, kv, kv_got, kv_got),
        (shape((QUERY, LOCAL)), shape((GROUPS, 8, LOCAL), F32)),
        6e9,
        grid=(GROUPS,),
        in_specs=[SMEM_SPEC, whole((1, LOCAL)), per_group(GROUP * HDIM)] + KV_SPECS,
        out_specs=(per_group(GROUP * HDIM), LSE_SPEC),
        scratch=[pltpu.VMEM((MAXLEN, LOCAL), F32)],
        after=after,
    )


def attend_back(where, begin, q, kv, kv_got, gatt, lse, after=()):
    return run(
        attend_back_kernel,
        (where, begin, q, kv, kv, kv_got, kv_got, gatt, lse),
        (
            shape((QUERY, LOCAL), F32), shape((2, GROUPS, HDIM, LOCAL), F32),
            shape((2, GROUPS, HDIM, LOCAL)),
        ),
        14e9,
        grid=(GROUPS,),
        in_specs=[SMEM_SPEC, whole((1, LOCAL)), per_group(GROUP * HDIM)]
        + KV_SPECS
        + [per_group(GROUP * HDIM), LSE_SPEC],
        out_specs=(per_group(GROUP * HDIM), PAIR_SPEC, PAIR_SPEC),
        scratch=[
            pltpu.VMEM((MAXLEN, LOCAL), F32), pltpu.VMEM((MAXLEN, HDIM), F32),
            pltpu.VMEM((MAXLEN, HDIM), F32),
        ],
        after=after,
    )


def feed_forward(nm, og, weights, dtype, after=()):
    hidden = weights[0].shape[1]
    chunk = 256
    cols = pl.BlockSpec((HALF, chunk), lambda i: (0, i))
    rows = pl.BlockSpec((chunk, LOCAL), lambda i: (i, 0))
    act = shape((hidden, LOCAL))
    return run(
        mlp_kernel,
        (nm, og) + weights,
        (shape((D, LOCAL), dtype), shape((D, LOCAL), dtype), act, act, act),
        12 * LOCAL * D * hidden,
        grid=(hidden // chunk,),
        in_specs=[whole((D, LOCAL))] * 2 + [cols] * 6,
        out_specs=(whole((D, LOCAL)), whole((D, LOCAL)), rows, rows, rows),
        scratch=[pltpu.VMEM((D, LOCAL), F32)] * 2,
        after=after,
    )


def weight_grads(rows, rows_far, cols, cols_far, after=()):
    hidden = cols.shape[0]
    part = hidden // 2
    taken = pl.BlockSpec((part, LOCAL), lambda i: (i, 0))
    given = pl.BlockSpec((HALF, part), lambda i: (i, 0))
    return run(
        grads_kernel,
        (rows, rows_far, cols, cols_far),
        (shape((2 * HALF, part)),) * 2,
        4 * LOCAL * D * hidden,
        grid=(2,),
        in_specs=[whole((D, LOCAL))] * 2 + [taken] * 2,
        out_specs=(given, given),
        after=after,
    )


def swap(array, axis):
    return lax.ppermute(array, axis, [(0, 1), (1, 0)])


def stages(count):
    found, stride = [], 1
    for size in (2,) + (4,) * 16:
        size = min(size, count // stride)
        if size < 2:
            break
        found.append((stride, size))
        stride *= size
    return found


def shift_pairs(count, stride, size, step):
    pairs = []
    for i in range(count):
        digit = i // stride % size
        pairs.append((i, i + ((digit + step) % size - digit) * stride))
    return pairs


def split_rows(array, count):
    rows, cols = array.shape
    return array.reshape(*[size for _, size in stages(count)], rows // count, cols)


def reduce_stage(total, count, stage):
    stride, size = stages(count)[stage]
    digit = lax.axis_index("dp") // stride % size
    kept = lax.dynamic_index_in_dim(total, digit, 0, keepdims=False).astype(F32)
    for step in range(1, size):
        sent = lax.dynamic_index_in_dim(total, (digit + step) % size, 0, keepdims=False)
        got = lax.ppermute(sent, "dp", shift_pairs(count, stride, size, step))
        kept = kept + got.astype(F32)
    return kept.astype(BF16)


def gather_stage(part, count, stage):
    stride, size = stages(count)[stage]
    digit = lax.axis_index("dp") // stride % size
    spread = jnp.zeros((size,) + part.shape, BF16)
    spread = lax.dynamic_update_index_in_dim(spread, part, digit, 0)
    for step in range(1, size):
        got = lax.ppermute(part, "dp", shift_pairs(count, stride, size, step))
        spread = lax.dynamic_update_index_in_dim(spread, got, (digit - step) % size, 0)
    return spread


def sum_over_dp(array, count):
    total = split_rows(array, count)
    for stage in range(len(stages(count))):
        total = reduce_stage(total, count, stage)
    for stage in reversed(range(len(stages(count)))):
        total = gather_stage(total, count, stage)
    return total.reshape(array.shape).astype(F32)


def add(keep, got):
    return (keep.astype(F32) + got.astype(F32)).astype(BF16)


def segment_begin(segment):
    index = jnp.arange(segment.shape[0], dtype=jnp.int32)
    is_start = jnp.concatenate([jnp.ones((1,), dtype=bool), segment[1:] != segment[:-1]])
    return lax.cummax(jnp.where(is_start, index, jnp.zeros_like(index)), axis=0)


def rope_tables(position):
    frequency = ROPE_BASE ** (-(jnp.arange(ROT, dtype=F32) * 2.0 / HDIM))
    angles = frequency[:, None] * position.astype(F32)[None, :]
    return jnp.cos(angles), jnp.sin(angles)


def per_device(
    count,
    hidden_in,
    query_weight,
    key_weight,
    value_weight,
    output_weight,
    gate_weight,
    up_weight,
    down_weight,
    attn_gain,
    ffn_gain,
    out_grad,
    segment_ids,
):
    col, row = lax.axis_index("col"), lax.axis_index("row")
    first = col == 0

    def own_tokens(array):
        outer = jnp.concatenate([array[..., :BLOCK], array[..., 3 * BLOCK :]], axis=-1)
        inner = array[..., BLOCK : 3 * BLOCK]
        return jnp.where(first, outer, inner), jnp.where(first, inner, outer)

    def in_window(own, got):
        outer, inner = jnp.where(first, own, got), jnp.where(first, got, own)
        return jnp.concatenate([outer[:, :BLOCK], inner, outer[:, BLOCK:]], axis=1)

    w_near = jnp.concatenate(
        [query_weight[:, 0].T, key_weight[:, 0].T, value_weight[:, 0].T], axis=0
    )
    w_far = swap(w_near, "row")
    x_own, x_other = own_tokens(hidden_in.T)
    x_got = swap(x_other, "col")
    gains = jnp.stack([attn_gain, ffn_gain])
    gains_got = swap(gains, "col").astype(F32)
    gains = gains.astype(F32)
    gin_own, gmid_own = gains[0][:, None], gains[1][:, None]
    gin_got, gmid_got = gains_got[0][:, None], gains_got[1][:, None]
    segment = jnp.where(col == row, segment_ids, swap(segment_ids, "col"))
    begin, _ = own_tokens(segment_begin(segment))
    index, _ = own_tokens(jnp.arange(MAXLEN, dtype=jnp.int32))
    cosine, sine = rope_tables(index - begin)
    begin = begin[None]
    live_near = jnp.where(row == 0, LIVE[0], LIVE[1])
    where_near = jnp.stack([col, live_near]).astype(jnp.int32)
    where_far = jnp.stack([col, LIVE[0] + LIVE[1] - live_near]).astype(jnp.int32)

    w_near_got = swap(w_near, "col")
    heads = (shape((QUERY, LOCAL)), shape((2 * KEY, LOCAL)))
    nm_in, q_near, kv_near = run(
        project_near_kernel,
        (x_own, x_got, gin_own, gin_got, cosine, sine, w_near, w_near_got),
        (shape((D, LOCAL)),) + heads,
        2 * LOCAL * D * D,
    )
    kv_near_got = swap(kv_near, "col")
    wo_near = output_weight[0]
    wo_far = swap(wo_near, "row")
    wo_near_got = swap(wo_near, "col")
    att_near, lse_near = attend(where_near, begin, q_near, kv_near, kv_near_got)
    w_far_got = swap(w_far, "col")
    q_far, kv_far = run(
        project_far_kernel,
        (nm_in, cosine, sine, w_far, w_far_got),
        heads,
        2 * LOCAL * D * D,
    )
    kv_far_got = swap(kv_far, "col")
    att_far, lse_far = attend(where_far, begin, q_far, kv_far, kv_far_got)
    wo_far_got = swap(wo_far, "col")
    mid, nm = run(
        mid_kernel,
        (
            att_near, att_far, wo_near, wo_near_got, wo_far, wo_far_got, x_own, x_got,
            gmid_own, gmid_got,
        ),
        (shape((D, LOCAL), F32), shape((D, LOCAL))),
        2 * LOCAL * D * D,
    )

    og_own, og_other = own_tokens(out_grad.T)
    og = jnp.concatenate([og_own, swap(og_other, "col")], axis=0)
    og_far = swap(og, "row")
    mlp_weights = ()
    for weight in (gate_weight, up_weight, down_weight.T):
        mlp_weights += (weight, swap(weight, "col"))
    nm_far = swap(nm, "row")
    out_part, gnm_part, act, gg, gu = feed_forward(nm, og, mlp_weights, F32)
    out_send, gnm_send, act_far, gg_far, gu_far = feed_forward(nm_far, og_far, mlp_weights, BF16)
    gnm_back = swap(gnm_send, "row")
    down_keep, down_send = weight_grads(og, og_far, act, act_far)
    down_sum = add(down_keep, swap(down_send, "col"))
    gate_keep, gate_send = weight_grads(nm, nm_far, gg, gg_far)
    gate_sum = add(gate_keep, swap(gate_send, "col"))
    up_keep, up_send = weight_grads(nm, nm_far, gu, gu_far)
    up_sum = add(up_keep, swap(up_send, "col"))

    gmid, gb, gatt_near, gatt_far, ggain_mid = run(
        mid_back_kernel,
        (
            og, mid, gnm_part, gnm_back, gmid_own, gmid_got, wo_near, wo_near_got, wo_far,
            wo_far_got,
        ),
        (
            shape((D, LOCAL), F32), shape((D, LOCAL)), shape((QUERY, LOCAL)),
            shape((QUERY, LOCAL)), shape((D, 1), F32),
        ),
        2 * LOCAL * D * D,
    )

    wo_far_sum = add(
        dot(att_far, gb[:HALF], 1, 1), swap(dot(att_far, gb[HALF:], 1, 1).astype(BF16), "col")
    )
    wo_near_sum = add(
        dot(att_near, gb[:HALF], 1, 1), swap(dot(att_near, gb[HALF:], 1, 1).astype(BF16), "col")
    )
    wo_sum = add(wo_near_sum, swap(wo_far_sum, "row"))

    dq_far, own_far, other_far = attend_back(
        where_far, begin, q_far, kv_far, kv_far_got, gatt_far, lse_far
    )
    got_far = swap(other_far, "col")
    joined = shape((D, HALF))
    gnm_in_part, far_keep, far_send = run(
        joined_far_kernel,
        (dq_far, own_far, got_far, cosine, sine, w_far, w_far_got, nm_in),
        (shape((D, LOCAL), F32), joined, joined),
        4 * LOCAL * D * D,
        scratch=[pltpu.VMEM((D, LOCAL), BF16)],
    )
    dq_near, own_near, other_near = attend_back(
        where_near, begin, q_near, kv_near, kv_near_got, gatt_near, lse_near
    )
    got_near = swap(other_near, "col")
    near_keep, near_send, grad, ggain_in = run(
        joined_near_kernel,
        (
            dq_near, own_near, got_near, cosine, sine, w_near, w_near_got, nm_in, gnm_in_part,
            x_own, x_got, gin_own, gin_got, gmid,
        ),
        (joined, joined, shape((D, LOCAL)), shape((D, 1), F32)),
        4 * LOCAL * D * D,
        scratch=[pltpu.VMEM((D, LOCAL), BF16)],
    )
    ggain = jnp.concatenate([ggain_in, ggain_mid], axis=1).T.astype(BF16)
    ggain_sum = add(ggain[:, :HALF], swap(ggain[:, HALF:], "col"))
    far_sum = add(far_keep, swap(far_send, "col"))
    near_sum = add(near_keep, swap(near_send, "col"))
    near_sum = add(near_sum, swap(far_sum, "row"))
    ggain_sum = add(ggain_sum, swap(ggain_sum, "row"))
    last_sum = jnp.concatenate([near_sum, jnp.pad(ggain_sum, ((0, 62), (0, 0)))], axis=0)

    def feature_cols(array):
        return in_window(array[:HALF], swap(array[HALF:], "col")).T

    out_back = swap(out_send, "row")
    block_out = feature_cols((mid + out_part + out_back.astype(F32)).astype(BF16))
    input_grad = feature_cols(grad)

    def widened(array):
        total = sum_over_dp(array, count)
        return jnp.concatenate([total[:HALF], total[HALF:]], axis=1)

    down_grad = widened(down_sum).T
    gate_grad = widened(gate_sum)
    up_grad = widened(up_sum)
    out_weight_grad = sum_over_dp(wo_sum, count)
    last = sum_over_dp(last_sum, count)
    return (
        block_out,
        input_grad,
        last[:QUERY].T[:, None, :],
        last[QUERY : QUERY + KEY].T[:, None, :],
        last[QUERY + KEY : D].T[:, None, :],
        out_weight_grad[None],
        gate_grad,
        up_grad,
        down_grad,
        last[D],
        last[D + 1],
    )


def solution(mesh):
    return jax.shard_map(
        functools.partial(per_device, mesh.shape["dp"]),
        mesh=mesh,
        in_specs=(
            P(("dp", "row"), "col"),
            P("col", "row", None),
            P("col", "row", None),
            P("col", "row", None),
            P("row", None, "col"),
            P("col", "row"),
            P("col", "row"),
            P("row", "col"),
            P("col"),
            P("col"),
            P(("dp", "row"), "col"),
            P(("dp", "col")),
        ),
        out_specs=(
            P(("dp", "row"), "col"),
            P(("dp", "row"), "col"),
            P("col", "row", None),
            P("col", "row", None),
            P("col", "row", None),
            P("row", None, "col"),
            P("col", "row"),
            P("col", "row"),
            P("row", "col"),
            P("col"),
            P("col"),
        ),
        check_vma=False,
    )
```

time: 1090 us -> 453 us (0.42)
  waiting for transfers between devices: 704 us -> 161 us
  matrix products: 192 us -> 7.1 us
  Pallas kernels: 0 us -> 128 us
  starting transfers between devices: 1.7 us -> 93.8 us
  other arithmetic: 97.6 us -> 34.8 us
  blocking collectives: 52.3 us -> 0 us
  between operations: 14.7 us -> 1.95 us
    psum x1 -> x0, waiting for transfers between devices: 329 us -> none  [per_device(): lax.psum((grad_joined_weight, grad_out_weight, grad_mlp, grad_down), 'dp')]
    reduce_scatter x8 -> x0, waiting for transfers between devices: 201 us -> none  [the longest x4 136 us: row_partial(): lax.psum_scatter(matmul(gathered, weight, 1, weight_dim), 'row', scatter_...]
    dot_general x18 -> x4, matrix products: 192 us -> 7.1 us  [dot(): lax.dot_general(left, right, (((left_dim,), (right_dim,)), ((), ())), pre...]
    all_gather x8 -> x0, waiting for transfers between devices: 171 us -> none  [the longest x4 110 us: row_tokens(): return lax.all_gather(piece_rows, 'row', axis=0, tiled=True)]
    ppermute x0 -> x74, waiting for transfers between devices: none -> 161 us  [the longest x34 57.4 us: swap(): return lax.ppermute(array, axis, [(0, 1), (1, 0)])]
    pallas_call x0 -> x15, Pallas kernels: none -> 128 us  [run(): pl.pallas_call(body, grid=grid if grid is not None else (1,), in_specs=li...]
    ppermute x0 -> x74, starting transfers between devices: none -> 93.8 us  [the longest x20 42 us: reduce_stage(): got = lax.ppermute(sent, 'dp', shift_pairs(count, stride, size, step))]
    psum x5 -> x0, blocking collectives: 52.3 us -> none  [the longest x1 42.2 us: per_device(): lax.psum((grad_gain_in, grad_gain_mid), ('dp', 'row'))]
  transfers between devices with their start and end apart: 17 -> 74, of which waited for: 17 -> 30; matrix products, arithmetic and copies ran while one was open for 8% -> 12% of each run, Pallas kernels for 0% -> 25%
where the time goes in v2:
time: 453 us; the launch traced here: 448 us
  waiting for transfers between devices  161 us (36%)
  Pallas kernels  128 us (28%)
  starting transfers between devices  93.8 us (21%)
  other arithmetic  34.8 us (8%)
  local copies, waits for them, and re-layouts  21.4 us (5%)
  matrix products  7.1 us (2%)
    pallas_call x15, Pallas kernels, run(): pl.pallas_call(body, grid=grid if grid is not None else (1,), in_specs=li...  128 us
    ppermute x34, waiting for transfers between devices, swap(): return lax.ppermute(array, axis, [(0, 1), (1, 0)])  57.4 us
    ppermute x20, waiting for transfers between devices, reduce_stage(): got = lax.ppermute(sent, 'dp', shift_pairs(count, stride, size, step))  57.1 us
    ppermute x20, waiting for transfers between devices, gather_stage(): got = lax.ppermute(part, 'dp', shift_pairs(count, stride, size, step))  46.5 us
    ppermute x20, starting transfers between devices, reduce_stage(): got = lax.ppermute(sent, 'dp', shift_pairs(count, stride, size, step))  42 us
    ppermute x20, starting transfers between devices, gather_stage(): got = lax.ppermute(part, 'dp', shift_pairs(count, stride, size, step))  36.4 us
    ppermute x34, starting transfers between devices, swap(): return lax.ppermute(array, axis, [(0, 1), (1, 0)])  15.4 us
  transfers between devices with their start and end apart: 74, of which 30 were waited for; matrix products, arithmetic and copies ran while one was open for 12% of the time, Pallas kernels for 25%

profile of v2, /device:TPU:0, one launch (start us, length us, event | category | flops | bytes accessed | tf_op | source)
XLA Modules:
  0.0 448.0 jit_solution(17821215022910314743)
XLA Ops:
  20.1 7.6 %collective-permute-done.5.refs_3_.refs_5_ = bf16[960,480]{1,0:T(8,128)(2,1)} collective-permute-done((bf16[960,480]{1,0:T(8,128)(2,1)S(1)}, bf16[960,480]{1,0:T(8,128)(2,1)}, u32[]{:S(2)}, u32[]{:S(2)}) %collective-permute-start.5) | collective-permute-done | bytes 921632 | tf_op jit(solution)/shard_map/ppermute | solution.py:433
  45.2 11.3 %shard_map.204 = (bf16[576,512]{1,0:T(8,128)(2,1)}, f32[3,8,512]{2,1,0:T(8,128)}) custom-call(s32[2]{0:T(128)} %pad_add_fusion.refs_0_, s32[1,512]{1,0:T(1,128)} %broadcast_select_fusion.8.refs_1_, bf16[576,512]{1,0:T(8,128)(2,1)} %get-tuple-element.56.refs_2_, bf16[384,512]{1,0:T(8,128)(2,1)} %get-tuple-element.57.refs_3_.refs_4_, ...), custom_call_target="tpu_custom_call" | custom-call | flops 6000000000 | bytes 2803720 | tf_op jit(solution)/shard_map/pallas_call | solution.py:66
  57.6 8.1 %shard_map.206 = (bf16[576,512]{1,0:T(8,128)(2,1)}, f32[3,8,512]{2,1,0:T(8,128)}) custom-call(s32[2]{0:T(128)} %pad_add_fusion.1.refs_0_, s32[1,512]{1,0:T(1,128)} %broadcast_select_fusion.8.refs_1_, bf16[576,512]{1,0:T(8,128)(2,1)} %get-tuple-element.60.refs_2_, bf16[384,512]{1,0:T(8,128)(2,1)} %get-tuple-element.61.refs_3_.refs_4_, ...), custom_call_target="tpu_custom_call" | custom-call | flops 6000000000 | bytes 2803720 | tf_op jit(solution)/shard_map/pallas_call | solution.py:66
  66.9 5.7 %shard_map.207 = (f32[960,512]{1,0:T(8,128)}, bf16[960,512]{1,0:T(8,128)(2,1)}) custom-call(bf16[576,512]{1,0:T(8,128)(2,1)} %get-tuple-element.58.refs_0_, bf16[576,512]{1,0:T(8,128)(2,1)} %get-tuple-element.62.refs_1_, bf16[576,480]{1,0:T(8,128)(2,1)} %bitcast.228, bf16[576,480]{1,0:T(8,128)(2,1)} %collective-permute-done.8.refs_3_.refs_7_, ...), custom_call_target="tpu_custom_call" | custom-call | flops 943718400 | bytes 7327488 | tf_op jit(solution)/shard_map/pallas_call | solution.py:66
  74.4 16.0 %collective-permute-done.16.refs_1_ = bf16[960,512]{1,0:T(8,128)(2,1)S(1)} collective-permute-done((bf16[960,512]{1,0:T(8,128)(2,1)S(1)}, bf16[960,512]{1,0:T(8,128)(2,1)S(1)}, u32[]{:S(2)}, u32[]{:S(2)}) %collective-permute-start.16) | collective-permute-done | bytes 983072 | tf_op jit(solution)/shard_map/ppermute | solution.py:433
  90.4 20.2 %collective-permute-done.15.refs_0_.refs_1_ = bf16[960,512]{1,0:T(8,128)(2,1)S(1)} collective-permute-done((bf16[960,512]{1,0:T(8,128)(2,1)}, bf16[960,512]{1,0:T(8,128)(2,1)S(1)}, u32[]{:S(2)}, u32[]{:S(2)}) %collective-permute-start.15) | collective-permute-done | bytes 983072 | tf_op jit(solution)/shard_map/ppermute | solution.py:433
  111.5 15.1 %shard_map.209 = (bf16[960,512]{1,0:T(8,128)(2,1)}, bf16[960,512]{1,0:T(8,128)(2,1)}, bf16[1280,512]{1,0:T(8,128)(2,1)}, bf16[1280,512]{1,0:T(8,128)(2,1)}, bf16[1280,512]{1,0:T(8,128)(2,1)}) custom-call(bf16[960,512]{1,0:T(8,128)(2,1)} %copy-done.31, bf16[960,512]{1,0:T(8,128)(2,1)} %copy-done.32, bf16[480,1280]{1,0:T(8,128)(2,1)} %refs_2_.3, ...), custom_call_target="tpu_custom_call" | custom-call | flops 7549747200 | bytes 15237120 | tf_op jit(solution)/shard_map/pallas_call | solution.py:66
  126.9 15.3 %shard_map.208 = (f32[960,512]{1,0:T(8,128)}, f32[960,512]{1,0:T(8,128)}, bf16[1280,512]{1,0:T(8,128)(2,1)}, bf16[1280,512]{1,0:T(8,128)(2,1)}, bf16[1280,512]{1,0:T(8,128)(2,1)}) custom-call(bf16[960,512]{1,0:T(8,128)(2,1)} %get-tuple-element.64.refs_0_, bf16[960,512]{1,0:T(8,128)(2,1)} %copy-done.4, bf16[480,1280]{1,0:T(8,128)(2,1)} %refs_2_.3, ...), custom_call_target="tpu_custom_call" | custom-call | flops 7549747200 | bytes 17203200 | tf_op jit(solution)/shard_map/pallas_call | solution.py:66
  144.1 6.2 %shard_map.215 = (bf16[960,640]{1,0:T(8,128)(2,1)}, bf16[960,640]{1,0:T(8,128)(2,1)}) custom-call(bf16[960,512]{1,0:T(8,128)(2,1)} %get-tuple-element.64.refs_0_, bf16[960,512]{1,0:T(8,128)(2,1)} %copy-done.31, bf16[1280,512]{1,0:T(8,128)(2,1)} %get-tuple-element.89.refs_2_, bf16[1280,512]{1,0:T(8,128)(2,1)} %get-tuple-element.90.refs_3_), custom_call_target="tpu_custom_call" | custom-call | flops 2516582400 | bytes 7045120 | tf_op jit(solution)/shard_map/pallas_call | solution.py:66
  150.3 6.2 %shard_map.217 = (bf16[960,640]{1,0:T(8,128)(2,1)}, bf16[960,640]{1,0:T(8,128)(2,1)}) custom-call(bf16[960,512]{1,0:T(8,128)(2,1)} %copy-done.4, bf16[960,512]{1,0:T(8,128)(2,1)} %copy-done.32, bf16[1280,512]{1,0:T(8,128)(2,1)} %get-tuple-element.97.refs_2_, bf16[1280,512]{1,0:T(8,128)(2,1)} %get-tuple-element.98.refs_3_), custom_call_target="tpu_custom_call" | custom-call | flops 2516582400 | bytes 7045120 | tf_op jit(solution)/shard_map/pallas_call | solution.py:66
  157.1 6.4 %shard_map.216 = (bf16[960,640]{1,0:T(8,128)(2,1)}, bf16[960,640]{1,0:T(8,128)(2,1)}) custom-call(bf16[960,512]{1,0:T(8,128)(2,1)} %get-tuple-element.64.refs_0_, bf16[960,512]{1,0:T(8,128)(2,1)} %copy-done.31, bf16[1280,512]{1,0:T(8,128)(2,1)} %get-tuple-element.93.refs_2_, bf16[1280,512]{1,0:T(8,128)(2,1)} %get-tuple-element.94.refs_3_), custom_call_target="tpu_custom_call" | custom-call | flops 2516582400 | bytes 7045120 | tf_op jit(solution)/shard_map/pallas_call | solution.py:66
  171.8 7.0 %shard_map.210 = (f32[960,512]{1,0:T(8,128)}, bf16[960,512]{1,0:T(8,128)(2,1)}, bf16[576,512]{1,0:T(8,128)(2,1)}, bf16[576,512]{1,0:T(8,128)(2,1)}, f32[960,1]{1,0:T(8,128)}) custom-call(bf16[960,512]{1,0:T(8,128)(2,1)} %copy-done.4, f32[960,512]{1,0:T(8,128)} %get-tuple-element.63.refs_1_, f32[960,512]{1,0:T(8,128)} %get-tuple-element.67.refs_2_, ...), custom_call_target="tpu_custom_call" | custom-call | flops 943718400 | bytes 12246528 | tf_op jit(solution)/shard_map/pallas_call | solution.py:66
  178.8 13.6 %shard_map.211 = (f32[576,512]{1,0:T(8,128)}, f32[2,3,64,512]{3,2,1,0:T(8,128)}, bf16[2,3,64,512]{3,2,1,0:T(8,128)(2,1)}) custom-call(s32[2]{0:T(128)} %pad_add_fusion.refs_0_, s32[1,512]{1,0:T(1,128)} %broadcast_select_fusion.8.refs_1_, bf16[576,512]{1,0:T(8,128)(2,1)} %get-tuple-element.56.refs_2_, bf16[384,512]{1,0:T(8,128)(2,1)} %get-tuple-element.57.refs_3_.refs_4_, ...), custom_call_target="tpu_custom_call" | custom-call | flops 14000000000 | bytes 5163016 | tf_op jit(solution)/shard_map/pallas_call | solution.py:66
  192.4 10.1 %shard_map.212 = (f32[576,512]{1,0:T(8,128)}, f32[2,3,64,512]{3,2,1,0:T(8,128)}, bf16[2,3,64,512]{3,2,1,0:T(8,128)(2,1)}) custom-call(s32[2]{0:T(128)} %pad_add_fusion.1.refs_0_, s32[1,512]{1,0:T(1,128)} %broadcast_select_fusion.8.refs_1_, bf16[576,512]{1,0:T(8,128)(2,1)} %get-tuple-element.60.refs_2_, bf16[384,512]{1,0:T(8,128)(2,1)} %get-tuple-element.61.refs_3_.refs_4_, ...), custom_call_target="tpu_custom_call" | custom-call | flops 14000000000 | bytes 5163016 | tf_op jit(solution)/shard_map/pallas_call | solution.py:66
  216.9 6.1 %shard_map.213 = (f32[960,512]{1,0:T(8,128)}, bf16[960,480]{1,0:T(8,128)(2,1)}, bf16[960,480]{1,0:T(8,128)(2,1)}) custom-call(f32[576,512]{1,0:T(8,128)} %get-tuple-element.76.refs_0_, f32[2,3,64,512]{3,2,1,0:T(8,128)} %get-tuple-element.77.refs_1_, bf16[2,3,64,512]{3,2,1,0:T(8,128)(2,1)} %copy-done.36, ...), custom_call_target="tpu_custom_call" | custom-call | flops 1887436800 | bytes 9125888 | tf_op jit(solution)/shard_map/pallas_call | solution.py:66
  223.0 8.2 %shard_map.214 = (bf16[960,480]{1,0:T(8,128)(2,1)}, bf16[960,480]{1,0:T(8,128)(2,1)}, bf16[960,512]{1,0:T(8,128)(2,1)}, f32[960,1]{1,0:T(8,128)}) custom-call(f32[576,512]{1,0:T(8,128)} %get-tuple-element.71.refs_0_, f32[2,3,64,512]{3,2,1,0:T(8,128)} %get-tuple-element.72.refs_1_, bf16[2,3,64,512]{3,2,1,0:T(8,128)(2,1)} %collective-permute-done.20.refs_2_, ...), custom_call_target="tpu_custom_call" | custom-call | flops 1887436800 | bytes 13065728 | tf_op jit(solution)/shard_map/pallas_call | solution.py:66
  247.1 8.6 %collective-permute-done.66 = bf16[4,120,640]{2,1,0:T(8,128)(2,1)S(1)} collective-permute-done((bf16[4,120,640]{2,1,0:T(8,128)(2,1)S(1)}, bf16[4,120,640]{2,1,0:T(8,128)(2,1)S(1)}, u32[]{:S(2)}, u32[]{:S(2)}) %collective-permute-start.66) | collective-permute-done | bytes 614432 | tf_op jit(solution)/shard_map/ppermute | solution.py:466
  259.2 7.6 %collective-permute-done.57 = bf16[4,120,640]{2,1,0:T(8,128)(2,1)S(1)} collective-permute-done((bf16[4,120,640]{2,1,0:T(8,128)(2,1)S(1)}, bf16[4,120,640]{2,1,0:T(8,128)(2,1)S(1)}, u32[]{:S(2)}, u32[]{:S(2)}) %collective-permute-start.57) | collective-permute-done | bytes 614432 | tf_op jit(solution)/shard_map/ppermute | solution.py:466
  275.0 5.0 %collective-permute-done.50 = bf16[120,640]{1,0:T(8,128)(2,1)S(1)} collective-permute-done((bf16[120,640]{1,0:T(8,128)(2,1)S(1)}, bf16[120,640]{1,0:T(8,128)(2,1)S(1)}, u32[]{:S(2)}, u32[]{:S(2)}) %collective-permute-start.50) | collective-permute-done | bytes 153632 | tf_op jit(solution)/shard_map/ppermute | solution.py:466
  280.0 8.6 %collective-permute-start.58 = (bf16[120,640]{1,0:T(8,128)(2,1)S(1)}, bf16[120,640]{1,0:T(8,128)(2,1)S(1)}, u32[]{:S(2)}, u32[]{:S(2)}) collective-permute-start(bf16[120,640]{1,0:T(8,128)(2,1)S(1)} %get-tuple-element.138), channel_id=1, source_target_pairs={{0,8},{4,12},{8,16},{12,20},{16,24},{20,28},{24,0},{28,4},{1,9},{5... | collective-permute-start | bytes 460808 | tf_op jit(solution)/shard_map/ppermute | solution.py:466
  292.7 7.3 %collective-permute-start.67 = (bf16[120,640]{1,0:T(8,128)(2,1)S(1)}, bf16[120,640]{1,0:T(8,128)(2,1)S(1)}, u32[]{:S(2)}, u32[]{:S(2)}) collective-permute-start(bf16[120,640]{1,0:T(8,128)(2,1)S(1)} %get-tuple-element.135), channel_id=1, source_target_pairs={{0,8},{4,12},{8,16},{12,20},{16,24},{20,28},{24,0},{28,4},{1,9},{5... | collective-permute-start | bytes 460808 | tf_op jit(solution)/shard_map/ppermute | solution.py:466
  320.2 5.8 %collective-permute-start.63 = (bf16[120,640]{1,0:T(8,128)(2,1)S(1)}, bf16[120,640]{1,0:T(8,128)(2,1)S(1)}, u32[]{:S(2)}, u32[]{:S(2)}) collective-permute-start(bf16[120,640]{1,0:T(8,128)(2,1)S(1)} %get-tuple-element.104), channel_id=1, source_target_pairs={{0,24},{4,28},{8,0},{12,4},{16,8},{20,12},{24,16},{28,20},{1,25},{... | collective-permute-start | bytes 460808 | tf_op jit(solution)/shard_map/ppermute | solution.py:477
  326.2 4.9 %collective-permute-start.70 = (bf16[120,640]{1,0:T(8,128)(2,1)S(1)}, bf16[120,640]{1,0:T(8,128)(2,1)S(1)}, u32[]{:S(2)}, u32[]{:S(2)}) collective-permute-start(bf16[120,640]{1,0:T(8,128)(2,1)S(1)} %get-tuple-element.102), channel_id=1, source_target_pairs={{0,8},{4,12},{8,16},{12,20},{16,24},{20,28},{24,0},{28,4},{1,9},{5... | collective-permute-start | bytes 460808 | tf_op jit(solution)/shard_map/ppermute | solution.py:477
  331.1 5.0 %collective-permute-done.62 = bf16[120,640]{1,0:T(8,128)(2,1)S(1)} collective-permute-done((bf16[120,640]{1,0:T(8,128)(2,1)S(1)}, bf16[120,640]{1,0:T(8,128)(2,1)S(1)}, u32[]{:S(2)}, u32[]{:S(2)}) %collective-permute-start.62) | collective-permute-done | bytes 153632 | tf_op jit(solution)/shard_map/ppermute | solution.py:477
  340.5 5.5 %collective-permute-done.71 = bf16[120,640]{1,0:T(8,128)(2,1)S(1)} collective-permute-done((bf16[120,640]{1,0:T(8,128)(2,1)S(1)}, bf16[120,640]{1,0:T(8,128)(2,1)S(1)}, u32[]{:S(2)}, u32[]{:S(2)}) %collective-permute-start.71) | collective-permute-done | bytes 153632 | tf_op jit(solution)/shard_map/ppermute | solution.py:477
  362.0 5.1 %collective-permute-done.43 = bf16[72,480]{1,0:T(8,128)(2,1)S(1)} collective-permute-done((bf16[72,480]{1,0:T(8,128)(2,1)S(1)}, bf16[72,480]{1,0:T(8,128)(2,1)S(1)}, u32[]{:S(2)}, u32[]{:S(2)}) %collective-permute-start.43) | collective-permute-done | bytes 69152 | tf_op jit(solution)/shard_map/ppermute | solution.py:477
  367.0 5.2 %collective-permute-done.44 = bf16[72,480]{1,0:T(8,128)(2,1)S(1)} collective-permute-done((bf16[72,480]{1,0:T(8,128)(2,1)S(1)}, bf16[72,480]{1,0:T(8,128)(2,1)S(1)}, u32[]{:S(2)}, u32[]{:S(2)}) %collective-permute-start.44) | collective-permute-done | bytes 69152 | tf_op jit(solution)/shard_map/ppermute | solution.py:477
  378.0 7.5 %collective-permute-done.64 = bf16[4,120,640]{2,1,0:T(8,128)(2,1)S(1)} collective-permute-done((bf16[4,120,640]{2,1,0:T(8,128)(2,1)S(1)}, bf16[4,120,640]{2,1,0:T(8,128)(2,1)S(1)}, u32[]{:S(2)}, u32[]{:S(2)}) %collective-permute-start.64) | collective-permute-done | bytes 614432 | tf_op jit(solution)/shard_map/ppermute | solution.py:477
  387.5 5.3 %collective-permute-done.25 = bf16[960,480]{1,0:T(8,128)(2,1)S(1)} collective-permute-done((bf16[960,480]{1,0:T(8,128)(2,1)S(1)}, bf16[960,480]{1,0:T(8,128)(2,1)S(1)}, u32[]{:S(2)}, u32[]{:S(2)}) %collective-permute-start.25) | collective-permute-done | bytes 921632 | tf_op jit(solution)/shard_map/ppermute | solution.py:433
  395.4 15.6 %collective-permute-done.28 = bf16[4,128,480]{2,1,0:T(8,128)(2,1)S(1)} collective-permute-done((bf16[4,128,480]{2,1,0:T(8,128)(2,1)S(1)}, bf16[4,128,480]{2,1,0:T(8,128)(2,1)S(1)}, u32[]{:S(2)}, u32[]{:S(2)}) %collective-permute-start.28) | collective-permute-done | bytes 491552 | tf_op jit(solution)/shard_map/ppermute | solution.py:466
  417.6 7.9 %collective-permute-done.30 = bf16[128,480]{1,0:T(8,128)(2,1)S(1)} collective-permute-done((bf16[128,480]{1,0:T(8,128)(2,1)S(1)}, bf16[128,480]{1,0:T(8,128)(2,1)S(1)}, u32[]{:S(2)}, u32[]{:S(2)}) %collective-permute-start.30) | collective-permute-done | bytes 122912 | tf_op jit(solution)/shard_map/ppermute | solution.py:466
  439.7 4.9 %collective-permute-done.35 = bf16[4,128,480]{2,1,0:T(8,128)(2,1)S(1)} collective-permute-done((bf16[4,128,480]{2,1,0:T(8,128)(2,1)S(1)}, bf16[4,128,480]{2,1,0:T(8,128)(2,1)S(1)}, u32[]{:S(2)}, u32[]{:S(2)}) %collective-permute-start.35) | collective-permute-done | bytes 491552 | tf_op jit(solution)/shard_map/ppermute | solution.py:477
  (334 shorter events, 173.3 us)
Async XLA Ops:
  2.1 29.7 %collective-permute-start.3 = (bf16[960,480]{1,0:T(8,128)(2,1)S(1)}, bf16[960,480]{1,0:T(8,128)(2,1)S(1)}, u32[]{:S(2)}, u32[]{:S(2)}) collective-permute-start(bf16[960,480]{1,0:T(8,128)(2,1)S(1)} %pad_maximum_fusion.2.refs_6_.refs_5_), channel_id=1, source_target_pairs={{0,1},{1,0},{2,3},{3,2},{4,5},{5,4},{6,7},{7,6},{8,9},{9,8},{10,11... | collective-permute-start | bytes 2764808 | tf_op jit(solution)/shard_map/ppermute | solution.py:433
  2.7 25.0 %collective-permute-start.5 = (bf16[960,480]{1,0:T(8,128)(2,1)S(1)}, bf16[960,480]{1,0:T(8,128)(2,1)}, u32[]{:S(2)}, u32[]{:S(2)}) collective-permute-start(bf16[960,480]{1,0:T(8,128)(2,1)S(1)} %pad_maximum_fusion.2.refs_6_.refs_5_), channel_id=1, source_target_pairs={{0,2},{2,0},{1,3},{3,1},{4,6},{6,4},{5,7},{7,5},{8,10},{10,8},{9,1... | collective-permute-start | bytes 2764808 | tf_op jit(solution)/shard_map/ppermute | solution.py:433
  6.6 23.4 %collective-permute-start.1 = (bf16[480,512]{1,0:T(8,128)(2,1)}, bf16[480,512]{1,0:T(8,128)(2,1)S(1)}, u32[]{:S(2)}, u32[]{:S(2)}) collective-permute-start(bf16[480,512]{1,0:T(8,128)(2,1)} %get-tuple-element.123), channel_id=1, source_target_pairs={{0,1},{1,0},{2,3},{3,2},{4,5},{5,4},{6,7},{7,6},{8,9},{9,8},{10,11... | collective-permute-start | bytes 1474568 | tf_op jit(solution)/shard_map/ppermute | solution.py:433
  16.5 49.2 %collective-permute-start.8 = (bf16[576,480]{1,0:T(8,128)(2,1)S(1)}, bf16[576,480]{1,0:T(8,128)(2,1)}, u32[]{:S(2)}, u32[]{:S(2)}) collective-permute-start(bf16[576,480]{1,0:T(8,128)(2,1)S(1)} %bitcast.230), channel_id=1, source_target_pairs={{0,1},{1,0},{2,3},{3,2},{4,5},{5,4},{6,7},{7,6},{8,9},{9,8},{10,11... | collective-permute-start | bytes 1658888 | tf_op jit(solution)/shard_map/ppermute | solution.py:433
  19.2 18.9 %collective-permute-start.11 = (bf16[480,512]{1,0:T(8,128)(2,1)}, bf16[480,512]{1,0:T(8,128)(2,1)}, u32[]{:S(2)}, u32[]{:S(2)}) collective-permute-start(bf16[480,512]{1,0:T(8,128)(2,1)} %get-tuple-element.122), channel_id=1, source_target_pairs={{0,1},{1,0},{2,3},{3,2},{4,5},{5,4},{6,7},{7,6},{8,9},{9,8},{10,11... | collective-permute-start | bytes 1474568 | tf_op jit(solution)/shard_map/ppermute | solution.py:433
  30.1 26.5 %collective-permute-start.9 = (bf16[576,480]{1,0:T(8,128)(2,1)S(1)}, bf16[576,480]{1,0:T(8,128)(2,1)S(1)}, u32[]{:S(2)}, u32[]{:S(2)}) collective-permute-start(bf16[576,480]{1,0:T(8,128)(2,1)S(1)} %bitcast.231), channel_id=1, source_target_pairs={{0,2},{2,0},{1,3},{3,1},{4,6},{6,4},{5,7},{7,5},{8,10},{10,8},{9,1... | collective-permute-start | bytes 1658888 | tf_op jit(solution)/shard_map/ppermute | solution.py:433
  38.1 36.3 %collective-permute-start.12 = (bf16[480,1280]{1,0:T(8,128)(2,1)}, bf16[480,1280]{1,0:T(8,128)(2,1)}, u32[]{:S(2)}, u32[]{:S(2)}) collective-permute-start(bf16[480,1280]{1,0:T(8,128)(2,1)} %refs_2_.3), channel_id=1, source_target_pairs={{0,1},{1,0},{2,3},{3,2},{4,5},{5,4},{6,7},{7,6},{8,9},{9,8},{10,11... | collective-permute-start | bytes 3686408 | tf_op jit(solution)/shard_map/ppermute | solution.py:433
  39.5 34.9 %collective-permute-start.13 = (bf16[480,1280]{1,0:T(8,128)(2,1)}, bf16[480,1280]{1,0:T(8,128)(2,1)}, u32[]{:S(2)}, u32[]{:S(2)}) collective-permute-start(bf16[480,1280]{1,0:T(8,128)(2,1)} %refs_4_.3), channel_id=1, source_target_pairs={{0,1},{1,0},{2,3},{3,2},{4,5},{5,4},{6,7},{7,6},{8,9},{9,8},{10,11... | collective-permute-start | bytes 3686408 | tf_op jit(solution)/shard_map/ppermute | solution.py:433
  56.5 17.9 %collective-permute-start.14 = (bf16[480,1280]{1,0:T(8,128)(2,1)}, bf16[480,1280]{1,0:T(8,128)(2,1)}, u32[]{:S(2)}, u32[]{:S(2)}) collective-permute-start(bf16[480,1280]{1,0:T(8,128)(2,1)} %bitcast.23.refs_6_), channel_id=1, source_target_pairs={{0,1},{1,0},{2,3},{3,2},{4,5},{5,4},{6,7},{7,6},{8,9},{9,8},{10,11... | collective-permute-start | bytes 3686408 | tf_op jit(solution)/shard_map/ppermute | solution.py:433
  65.7 24.7 %collective-permute-start.16 = (bf16[960,512]{1,0:T(8,128)(2,1)S(1)}, bf16[960,512]{1,0:T(8,128)(2,1)S(1)}, u32[]{:S(2)}, u32[]{:S(2)}) collective-permute-start(bf16[960,512]{1,0:T(8,128)(2,1)S(1)} %pad_maximum_fusion.3.refs_1_.refs_0_), channel_id=1, source_target_pairs={{0,2},{2,0},{1,3},{3,1},{4,6},{6,4},{5,7},{7,5},{8,10},{10,8},{9,1... | collective-permute-start | bytes 2949128 | tf_op jit(solution)/shard_map/ppermute | solution.py:433
  72.6 37.9 %collective-permute-start.15 = (bf16[960,512]{1,0:T(8,128)(2,1)}, bf16[960,512]{1,0:T(8,128)(2,1)S(1)}, u32[]{:S(2)}, u32[]{:S(2)}) collective-permute-start(bf16[960,512]{1,0:T(8,128)(2,1)} %get-tuple-element.64.refs_0_), channel_id=1, source_target_pairs={{0,2},{2,0},{1,3},{3,1},{4,6},{6,4},{5,7},{7,5},{8,10},{10,8},{9,1... | collective-permute-start | bytes 2949128 | tf_op jit(solution)/shard_map/ppermute | solution.py:433
  126.6 36.8 %collective-permute-start.17 = (bf16[960,512]{1,0:T(8,128)(2,1)}, bf16[960,512]{1,0:T(8,128)(2,1)}, u32[]{:S(2)}, u32[]{:S(2)}) collective-permute-start(bf16[960,512]{1,0:T(8,128)(2,1)} %get-tuple-element.66), channel_id=1, source_target_pairs={{0,2},{2,0},{1,3},{3,1},{4,6},{6,4},{5,7},{7,5},{8,10},{10,8},{9,1... | collective-permute-start | bytes 2949128 | tf_op jit(solution)/shard_map/ppermute | solution.py:433
  142.3 28.6 %collective-permute-start.19 = (bf16[960,512]{1,0:T(8,128)(2,1)}, bf16[960,512]{1,0:T(8,128)(2,1)S(1)}, u32[]{:S(2)}, u32[]{:S(2)}) collective-permute-start(bf16[960,512]{1,0:T(8,128)(2,1)} %get-tuple-element.68), channel_id=1, source_target_pairs={{0,2},{2,0},{1,3},{3,1},{4,6},{6,4},{5,7},{7,5},{8,10},{10,8},{9,1... | collective-permute-start | bytes 2949128 | tf_op jit(solution)/shard_map/ppermute | solution.py:433
  150.3 56.4 %collective-permute-start.47 = (bf16[960,640]{1,0:T(8,128)(2,1)}, bf16[960,640]{1,0:T(8,128)(2,1)S(1)}, u32[]{:S(2)}, u32[]{:S(2)}) collective-permute-start(bf16[960,640]{1,0:T(8,128)(2,1)} %get-tuple-element.92), channel_id=1, source_target_pairs={{0,1},{1,0},{2,3},{3,2},{4,5},{5,4},{6,7},{7,6},{8,9},{9,8},{10,11... | collective-permute-start | bytes 3686408 | tf_op jit(solution)/shard_map/ppermute | solution.py:433
  156.6 52.9 %collective-permute-start.65 = (bf16[960,640]{1,0:T(8,128)(2,1)}, bf16[960,640]{1,0:T(8,128)(2,1)}, u32[]{:S(2)}, u32[]{:S(2)}) collective-permute-start(bf16[960,640]{1,0:T(8,128)(2,1)} %get-tuple-element.100), channel_id=1, source_target_pairs={{0,1},{1,0},{2,3},{3,2},{4,5},{5,4},{6,7},{7,6},{8,9},{9,8},{10,11... | collective-permute-start | bytes 3686408 | tf_op jit(solution)/shard_map/ppermute | solution.py:433
  163.4 48.3 %collective-permute-start.56 = (bf16[960,640]{1,0:T(8,128)(2,1)}, bf16[960,640]{1,0:T(8,128)(2,1)}, u32[]{:S(2)}, u32[]{:S(2)}) collective-permute-start(bf16[960,640]{1,0:T(8,128)(2,1)} %get-tuple-element.96), channel_id=1, source_target_pairs={{0,1},{1,0},{2,3},{3,2},{4,5},{5,4},{6,7},{7,6},{8,9},{9,8},{10,11... | collective-permute-start | bytes 3686408 | tf_op jit(solution)/shard_map/ppermute | solution.py:433
  166.1 73.7 %collective-permute-start.18 = (bf16[480,512]{1,0:T(8,128)(2,1)}, bf16[480,512]{1,0:T(8,128)(2,1)}, u32[]{:S(2)}, u32[]{:S(2)}) collective-permute-start(bf16[480,512]{1,0:T(8,128)(2,1)} %slice.226), channel_id=1, source_target_pairs={{0,1},{1,0},{2,3},{3,2},{4,5},{5,4},{6,7},{7,6},{8,9},{9,8},{10,11... | collective-permute-start | bytes 1474568 | tf_op jit(solution)/shard_map/ppermute | solution.py:433
  192.4 30.6 %collective-permute-start.20 = (bf16[2,3,64,512]{3,2,1,0:T(8,128)(2,1)}, bf16[2,3,64,512]{3,2,1,0:T(8,128)(2,1)}, u32[]{:S(2)}, u32[]{:S(2)}) collective-permute-start(bf16[2,3,64,512]{3,2,1,0:T(8,128)(2,1)} %get-tuple-element.73), channel_id=1, source_target_pairs={{0,1},{1,0},{2,3},{3,2},{4,5},{5,4},{6,7},{7,6},{8,9},{9,8},{10,11... | collective-permute-start | bytes 1179656 | tf_op jit(solution)/shard_map/ppermute | solution.py:433
  209.5 33.7 %collective-permute-start.37 = (bf16[576,480]{1,0:T(8,128)(2,1)}, bf16[576,480]{1,0:T(8,128)(2,1)}, u32[]{:S(2)}, u32[]{:S(2)}) collective-permute-start(bf16[576,480]{1,0:T(8,128)(2,1)} %convolution_convert_fusion), channel_id=1, source_target_pairs={{0,1},{1,0},{2,3},{3,2},{4,5},{5,4},{6,7},{7,6},{8,9},{9,8},{10,11... | collective-permute-start | bytes 1658888 | tf_op jit(solution)/shard_map/ppermute | solution.py:433
  211.8 93.7 %collective-permute-start.36 = (bf16[576,480]{1,0:T(8,128)(2,1)}, bf16[576,480]{1,0:T(8,128)(2,1)}, u32[]{:S(2)}, u32[]{:S(2)}) collective-permute-start(bf16[576,480]{1,0:T(8,128)(2,1)} %convolution_convert_fusion.1), channel_id=1, source_target_pairs={{0,1},{1,0},{2,3},{3,2},{4,5},{5,4},{6,7},{7,6},{8,9},{9,8},{10,11... | collective-permute-start | bytes 1658888 | tf_op jit(solution)/shard_map/ppermute | solution.py:433
  215.4 30.0 %collective-permute-start.48 = (bf16[4,120,640]{2,1,0:T(8,128)(2,1)}, bf16[4,120,640]{2,1,0:T(8,128)(2,1)}, u32[]{:S(2)}, u32[]{:S(2)}) collective-permute-start(bf16[4,120,640]{2,1,0:T(8,128)(2,1)} %dynamic-slice_bitcast_fusion.2), channel_id=1, source_target_pairs={{0,4},{4,0},{8,12},{12,8},{16,20},{20,16},{24,28},{28,24},{1,5},{5... | collective-permute-start | bytes 1843208 | tf_op jit(solution)/shard_map/ppermute | solution.py:466
  239.7 27.1 %collective-permute-start.57 = (bf16[4,120,640]{2,1,0:T(8,128)(2,1)S(1)}, bf16[4,120,640]{2,1,0:T(8,128)(2,1)S(1)}, u32[]{:S(2)}, u32[]{:S(2)}) collective-permute-start(bf16[4,120,640]{2,1,0:T(8,128)(2,1)S(1)} %dynamic-slice_bitcast_fusion.1), channel_id=1, source_target_pairs={{0,4},{4,0},{8,12},{12,8},{16,20},{20,16},{24,28},{28,24},{1,5},{5... | collective-permute-start | bytes 1843208 | tf_op jit(solution)/shard_map/ppermute | solution.py:466
  243.2 26.7 %collective-permute-start.22 = (bf16[480,512]{1,0:T(8,128)(2,1)S(1)}, bf16[480,512]{1,0:T(8,128)(2,1)S(1)}, u32[]{:S(2)}, u32[]{:S(2)}) collective-permute-start(bf16[480,512]{1,0:T(8,128)(2,1)S(1)} %slice.190), channel_id=1, source_target_pairs={{0,1},{1,0},{2,3},{3,2},{4,5},{5,4},{6,7},{7,6},{8,9},{9,8},{10,11... | collective-permute-start | bytes 1474568 | tf_op jit(solution)/shard_map/ppermute | solution.py:433
  245.4 62.6 %collective-permute-start.38 = (bf16[576,480]{1,0:T(8,128)(2,1)S(1)}, bf16[576,480]{1,0:T(8,128)(2,1)S(1)}, u32[]{:S(2)}, u32[]{:S(2)}) collective-permute-start(bf16[576,480]{1,0:T(8,128)(2,1)S(1)} %fusion.2), channel_id=1, source_target_pairs={{0,2},{2,0},{1,3},{3,1},{4,6},{6,4},{5,7},{7,5},{8,10},{10,8},{9,1... | collective-permute-start | bytes 1658888 | tf_op jit(solution)/shard_map/ppermute | solution.py:433
  255.6 17.1 %collective-permute-start.51 = (bf16[120,640]{1,0:T(8,128)(2,1)S(1)}, bf16[120,640]{1,0:T(8,128)(2,1)S(1)}, u32[]{:S(2)}, u32[]{:S(2)}) collective-permute-start(bf16[120,640]{1,0:T(8,128)(2,1)S(1)} %get-tuple-element.142), channel_id=1, source_target_pairs={{0,24},{4,28},{8,0},{12,4},{16,8},{20,12},{24,16},{28,20},{1,25},{... | collective-permute-start | bytes 460808 | tf_op jit(solution)/shard_map/ppermute | solution.py:466
  300.3 60.5 %collective-permute-start.24 = (bf16[960,480]{1,0:T(8,128)(2,1)S(1)}, bf16[960,480]{1,0:T(8,128)(2,1)S(1)}, u32[]{:S(2)}, u32[]{:S(2)}) collective-permute-start(bf16[960,480]{1,0:T(8,128)(2,1)S(1)} %copy-done.28), channel_id=1, source_target_pairs={{0,1},{1,0},{2,3},{3,2},{4,5},{5,4},{6,7},{7,6},{8,9},{9,8},{10,11... | collective-permute-start | bytes 2764808 | tf_op jit(solution)/shard_map/ppermute | solution.py:433
  304.7 82.8 %collective-permute-start.23 = (bf16[960,480]{1,0:T(8,128)(2,1)S(1)}, bf16[960,480]{1,0:T(8,128)(2,1)S(1)}, u32[]{:S(2)}, u32[]{:S(2)}) collective-permute-start(bf16[960,480]{1,0:T(8,128)(2,1)S(1)} %copy-done.27), channel_id=1, source_target_pairs={{0,1},{1,0},{2,3},{3,2},{4,5},{5,4},{6,7},{7,6},{8,9},{9,8},{10,11... | collective-permute-start | bytes 2764808 | tf_op jit(solution)/shard_map/ppermute | solution.py:433
  355.5 21.5 %collective-permute-start.55 = (bf16[4,120,640]{2,1,0:T(8,128)(2,1)S(1)}, bf16[4,120,640]{2,1,0:T(8,128)(2,1)S(1)}, u32[]{:S(2)}, u32[]{:S(2)}) collective-permute-start(bf16[4,120,640]{2,1,0:T(8,128)(2,1)S(1)} %bitcast_dynamic-update-slice_fusion.18), channel_id=1, source_target_pairs={{0,4},{4,0},{8,12},{12,8},{16,20},{20,16},{24,28},{28,24},{1,5},{5... | collective-permute-start | bytes 1843208 | tf_op jit(solution)/shard_map/ppermute | solution.py:477
  356.8 28.8 %collective-permute-start.64 = (bf16[4,120,640]{2,1,0:T(8,128)(2,1)S(1)}, bf16[4,120,640]{2,1,0:T(8,128)(2,1)S(1)}, u32[]{:S(2)}, u32[]{:S(2)}) collective-permute-start(bf16[4,120,640]{2,1,0:T(8,128)(2,1)S(1)} %bitcast_dynamic-update-slice_fusion.14), channel_id=1, source_target_pairs={{0,4},{4,0},{8,12},{12,8},{16,20},{20,16},{24,28},{28,24},{1,5},{5... | collective-permute-start | bytes 1843208 | tf_op jit(solution)/shard_map/ppermute | solution.py:477
  359.5 55.1 %collective-permute-start.73 = (bf16[4,120,640]{2,1,0:T(8,128)(2,1)S(1)}, bf16[4,120,640]{2,1,0:T(8,128)(2,1)S(1)}, u32[]{:S(2)}, u32[]{:S(2)}) collective-permute-start(bf16[4,120,640]{2,1,0:T(8,128)(2,1)S(1)} %bitcast_dynamic-update-slice_fusion.10), channel_id=1, source_target_pairs={{0,4},{4,0},{8,12},{12,8},{16,20},{20,16},{24,28},{28,24},{1,5},{5... | collective-permute-start | bytes 1843208 | tf_op jit(solution)/shard_map/ppermute | solution.py:477
  377.0 61.3 %collective-permute-start.46 = (bf16[4,72,480]{2,1,0:T(8,128)(2,1)S(1)}, bf16[4,72,480]{2,1,0:T(8,128)(2,1)S(1)}, u32[]{:S(2)}, u32[]{:S(2)}) collective-permute-start(bf16[4,72,480]{2,1,0:T(8,128)(2,1)S(1)} %bitcast_dynamic-update-slice_fusion.26), channel_id=1, source_target_pairs={{0,4},{4,0},{8,12},{12,8},{16,20},{20,16},{24,28},{28,24},{1,5},{5... | collective-permute-start | bytes 829448 | tf_op jit(solution)/shard_map/ppermute | solution.py:477
  393.3 17.7 %collective-permute-start.28 = (bf16[4,128,480]{2,1,0:T(8,128)(2,1)S(1)}, bf16[4,128,480]{2,1,0:T(8,128)(2,1)S(1)}, u32[]{:S(2)}, u32[]{:S(2)}) collective-permute-start(bf16[4,128,480]{2,1,0:T(8,128)(2,1)S(1)} %dynamic-slice_bitcast_fusion.3), channel_id=1, source_target_pairs={{0,4},{4,0},{8,12},{12,8},{16,20},{20,16},{24,28},{28,24},{1,5},{5... | collective-permute-start | bytes 1474568 | tf_op jit(solution)/shard_map/ppermute | solution.py:466
  (79 other events, 609.8 us)

commit v3 on v2

--- a/solution.py
+++ b/solution.py
@@ -28,6 +28,7 @@
 BF16 = jnp.bfloat16
 F32 = jnp.float32
 VMEM_BYTES = 56 * 1024 * 1024
+COST = 0.03
 
 HELD = ((0, 3), (1, 2))
 LAID = ((0, 3, 1, 2), (0, 1, 2))
@@ -72,7 +73,7 @@
         scratch_shapes=list(scratch),
         compiler_params=pltpu.CompilerParams(vmem_limit_bytes=VMEM_BYTES),
         cost_estimate=pl.CostEstimate(
-            flops=int(flops), bytes_accessed=int(moved), transcendentals=0
+            flops=int(flops * COST), bytes_accessed=int(moved * COST), transcendentals=0
         ),
     )(*ins, *after)
 
@@ -457,35 +458,60 @@
     return array.reshape(*[size for _, size in stages(count)], rows // count, cols)
 
 
-def reduce_stage(total, count, stage):
+def reduce_stage(total, count, stage, held=()):
     stride, size = stages(count)[stage]
     digit = lax.axis_index("dp") // stride % size
     kept = lax.dynamic_index_in_dim(total, digit, 0, keepdims=False).astype(F32)
+    found = []
     for step in range(1, size):
         sent = lax.dynamic_index_in_dim(total, (digit + step) % size, 0, keepdims=False)
-        got = lax.ppermute(sent, "dp", shift_pairs(count, stride, size, step))
+        found.append(lax.ppermute(sent, "dp", shift_pairs(count, stride, size, step)))
+    for got in hold_all(found, held):
         kept = kept + got.astype(F32)
     return kept.astype(BF16)
 
 
-def gather_stage(part, count, stage):
+def gather_stage(part, count, stage, held=()):
     stride, size = stages(count)[stage]
     digit = lax.axis_index("dp") // stride % size
+    found = [
+        lax.ppermute(part, "dp", shift_pairs(count, stride, size, step)) for step in range(1, size)
+    ]
     spread = jnp.zeros((size,) + part.shape, BF16)
     spread = lax.dynamic_update_index_in_dim(spread, part, digit, 0)
-    for step in range(1, size):
-        got = lax.ppermute(part, "dp", shift_pairs(count, stride, size, step))
+    for step, got in enumerate(hold_all(found, held), 1):
         spread = lax.dynamic_update_index_in_dim(spread, got, (digit - step) % size, 0)
     return spread
 
 
-def sum_over_dp(array, count):
-    total = split_rows(array, count)
-    for stage in range(len(stages(count))):
-        total = reduce_stage(total, count, stage)
-    for stage in reversed(range(len(stages(count)))):
-        total = gather_stage(total, count, stage)
-    return total.reshape(array.shape).astype(F32)
+def reduce_first(array, count, held=()):
+    return reduce_stage(split_rows(array, count), count, 0, held)
+
+
+def reduce_rest(total, count, held=()):
+    for stage in range(1, len(stages(count))):
+        total = reduce_stage(total, count, stage, held)
+    return total
+
+
+def gather_rest(total, count, held=()):
+    for stage in reversed(range(1, len(stages(count)))):
+        total = gather_stage(total, count, stage, held)
+    return total
+
+
+def gather_first(total, count, dims, held=()):
+    return gather_stage(total, count, 0, held).reshape(dims).astype(F32)
+
+
+def hold_all(arrays, others):
+    if not others:
+        return arrays
+    return lax.optimization_barrier(tuple(arrays) + tuple(others))[: len(arrays)]
+
+
+def hold(array, *others):
+    return lax.optimization_barrier((array,) + others)[0]
 
 
 def add(keep, got):
@@ -572,8 +598,11 @@
         2 * LOCAL * D * D,
     )
     kv_far_got = swap(kv_far, "col")
-    att_far, lse_far = attend(where_far, begin, q_far, kv_far, kv_far_got)
+    att_far, lse_far = attend(where_far, begin, q_far, kv_far, kv_far_got, after=(wo_far,))
     wo_far_got = swap(wo_far, "col")
+    og_own, og_other = own_tokens(out_grad.T)
+    og = jnp.concatenate([og_own, swap(og_other, "col")], axis=0)
+    og_far = swap(og, "row")
     mid, nm = run(
         mid_kernel,
         (
@@ -582,24 +611,23 @@
         ),
         (shape((D, LOCAL), F32), shape((D, LOCAL))),
         2 * LOCAL * D * D,
-    )
-
-    og_own, og_other = own_tokens(out_grad.T)
-    og = jnp.concatenate([og_own, swap(og_other, "col")], axis=0)
-    og_far = swap(og, "row")
+        after=(og_far,),
+    )
+
     mlp_weights = ()
     for weight in (gate_weight, up_weight, down_weight.T):
         mlp_weights += (weight, swap(weight, "col"))
     nm_far = swap(nm, "row")
     out_part, gnm_part, act, gg, gu = feed_forward(nm, og, mlp_weights, F32)
-    out_send, gnm_send, act_far, gg_far, gu_far = feed_forward(nm_far, og_far, mlp_weights, BF16)
+    out_send, gnm_send, act_far, gg_far, gu_far = feed_forward(
+        nm_far, og_far, mlp_weights, BF16, after=(act,)
+    )
     gnm_back = swap(gnm_send, "row")
     down_keep, down_send = weight_grads(og, og_far, act, act_far)
-    down_sum = add(down_keep, swap(down_send, "col"))
-    gate_keep, gate_send = weight_grads(nm, nm_far, gg, gg_far)
-    gate_sum = add(gate_keep, swap(gate_send, "col"))
-    up_keep, up_send = weight_grads(nm, nm_far, gu, gu_far)
-    up_sum = add(up_keep, swap(up_send, "col"))
+    gate_keep, gate_send = weight_grads(nm, nm_far, gg, gg_far, after=(down_keep,))
+    down_sum = add(down_keep, hold(swap(down_send, "col"), gate_keep))
+    up_keep, up_send = weight_grads(nm, nm_far, gu, gu_far, after=(down_sum,))
+    gate_sum = add(gate_keep, hold(swap(gate_send, "col"), up_keep))
 
     gmid, gb, gatt_near, gatt_far, ggain_mid = run(
         mid_back_kernel,
@@ -612,19 +640,23 @@
             shape((QUERY, LOCAL)), shape((D, 1), F32),
         ),
         2 * LOCAL * D * D,
-    )
-
-    wo_far_sum = add(
-        dot(att_far, gb[:HALF], 1, 1), swap(dot(att_far, gb[HALF:], 1, 1).astype(BF16), "col")
-    )
-    wo_near_sum = add(
-        dot(att_near, gb[:HALF], 1, 1), swap(dot(att_near, gb[HALF:], 1, 1).astype(BF16), "col")
-    )
-    wo_sum = add(wo_near_sum, swap(wo_far_sum, "row"))
+        after=(gate_sum,),
+    )
+    up_sum = add(up_keep, hold(swap(up_send, "col"), ggain_mid))
+    down_x = reduce_first(down_sum, count, (ggain_mid,))
 
     dq_far, own_far, other_far = attend_back(
-        where_far, begin, q_far, kv_far, kv_far_got, gatt_far, lse_far
-    )
+        where_far, begin, q_far, kv_far, kv_far_got, gatt_far, lse_far, after=(down_x, up_sum)
+    )
+    gate_x = reduce_first(gate_sum, count, (dq_far,))
+    down_z = reduce_rest(down_x, count, (dq_far,))
+
+    def out_grads(att):
+        send = dot(att, gb[HALF:], 1, 1).astype(BF16)
+        return add(dot(att, gb[:HALF], 1, 1), hold(swap(send, "col"), dq_far))
+
+    wo_far_sum = out_grads(att_far)
+    wo_near_sum = out_grads(att_near)
     got_far = swap(other_far, "col")
     joined = shape((D, HALF))
     gnm_in_part, far_keep, far_send = run(
@@ -632,11 +664,17 @@
         (dq_far, own_far, got_far, cosine, sine, w_far, w_far_got, nm_in),
         (shape((D, LOCAL), F32), joined, joined),
         4 * LOCAL * D * D,
+        after=(gate_x, down_z, wo_far_sum, wo_near_sum),
         scratch=[pltpu.VMEM((D, LOCAL), BF16)],
     )
     dq_near, own_near, other_near = attend_back(
-        where_near, begin, q_near, kv_near, kv_near_got, gatt_near, lse_near
-    )
+        where_near, begin, q_near, kv_near, kv_near_got, gatt_near, lse_near, after=(far_keep,)
+    )
+    far_sum = add(far_keep, hold(swap(far_send, "col"), dq_near))
+    wo_sum = add(wo_near_sum, hold(swap(wo_far_sum, "row"), dq_near))
+    up_x = reduce_first(up_sum, count, (dq_near,))
+    gate_z = reduce_rest(gate_x, count, (dq_near,))
+    down_y = gather_rest(down_z, count, (dq_near,))
     got_near = swap(other_near, "col")
     near_keep, near_send, grad, ggain_in = run(
         joined_near_kernel,
@@ -646,11 +684,11 @@
         ),
         (joined, joined, shape((D, LOCAL)), shape((D, 1), F32)),
         4 * LOCAL * D * D,
+        after=(up_x, gate_z, down_y, wo_sum, far_sum),
         scratch=[pltpu.VMEM((D, LOCAL), BF16)],
     )
     ggain = jnp.concatenate([ggain_in, ggain_mid], axis=1).T.astype(BF16)
     ggain_sum = add(ggain[:, :HALF], swap(ggain[:, HALF:], "col"))
-    far_sum = add(far_keep, swap(far_send, "col"))
     near_sum = add(near_keep, swap(near_send, "col"))
     near_sum = add(near_sum, swap(far_sum, "row"))
     ggain_sum = add(ggain_sum, swap(ggain_sum, "row"))
@@ -659,19 +697,24 @@
     def feature_cols(array):
         return in_window(array[:HALF], swap(array[HALF:], "col")).T
 
-    out_back = swap(out_send, "row")
+    out_back = swap(hold(out_send, gnm_back), "row")
     block_out = feature_cols((mid + out_part + out_back.astype(F32)).astype(BF16))
     input_grad = feature_cols(grad)
 
-    def widened(array):
-        total = sum_over_dp(array, count)
+    def widened(part):
+        total = gather_first(part, count, (D, down_sum.shape[1]), (ggain_in,))
         return jnp.concatenate([total[:HALF], total[HALF:]], axis=1)
 
-    down_grad = widened(down_sum).T
-    gate_grad = widened(gate_sum)
-    up_grad = widened(up_sum)
-    out_weight_grad = sum_over_dp(wo_sum, count)
-    last = sum_over_dp(last_sum, count)
+    down_grad = widened(down_y).T
+    up_z = reduce_rest(up_x, count, (ggain_in,))
+    gate_grad = widened(gather_rest(gate_z, count, (ggain_in,)))
+    up_grad = widened(gather_rest(up_z, count, (last_sum,)))
+    out_z = reduce_rest(
+        reduce_first(wo_sum, count, (ggain_in,)), count, (last_sum,)
+    )
+    out_weight_grad = gather_first(gather_rest(out_z, count), count, wo_sum.shape)
+    last_z = reduce_rest(reduce_first(last_sum, count), count)
+    last = gather_first(gather_rest(last_z, count), count, last_sum.shape)
     return (
         block_out,
         input_grad,

time: 453 us -> 399 us (0.88)
  waiting for transfers between devices: 161 us -> 115 us
  starting transfers between devices: 93.8 us -> 76.7 us
  local copies, waits for them, and re-layouts: 21.4 us -> 28.9 us
    ppermute x40, waiting for transfers between devices: 104 us -> 55.5 us  [the longest x20 34.7 us: reduce_stage(): lax.ppermute(sent, 'dp', shift_pairs(count, stride, size, step))]
    ppermute x40, starting transfers between devices: 78.4 us -> 61 us  [the longest x20 31.3 us: reduce_stage(): lax.ppermute(sent, 'dp', shift_pairs(count, stride, size, step))]
    dynamic_update_slice x20, local copies, waits for them, and re-layouts: 0.58 us -> 6.39 us  [gather_stage(): lax.dynamic_update_index_in_dim(spread, got, (digit - step) % size, 0)]
    convert_element_type x7 -> x8, other arithmetic: 6.76 us -> 9.79 us  [add(): return (keep.astype(F32) + got.astype(F32)).astype(BF16)]
  transfers between devices with their start and end apart: 74 -> 74, of which waited for: 30 -> 20; matrix products, arithmetic and copies ran while one was open for 12% -> 15% of each run, Pallas kernels for 25% -> 27%
where the time goes in v3:
time: 399 us; the launch traced here: 394 us
  Pallas kernels  128 us (32%)
  waiting for transfers between devices  115 us (29%)
  starting transfers between devices  76.7 us (19%)
  other arithmetic  34.5 us (9%)
  local copies, waits for them, and re-layouts  28.9 us (7%)
  matrix products  8.67 us (2%)
    pallas_call x15, Pallas kernels, run(): pl.pallas_call(body, grid=grid if grid is not None else (1,), in_specs=li...  128 us
    ppermute x34, waiting for transfers between devices, swap(): return lax.ppermute(array, axis, [(0, 1), (1, 0)])  59.8 us
    ppermute x20, waiting for transfers between devices, reduce_stage(): lax.ppermute(sent, 'dp', shift_pairs(count, stride, size, step))  34.7 us
    ppermute x20, starting transfers between devices, reduce_stage(): lax.ppermute(sent, 'dp', shift_pairs(count, stride, size, step))  31.3 us
    ppermute x20, starting transfers between devices, gather_stage(): lax.ppermute(part, 'dp', shift_pairs(count, stride, size, step))  29.7 us
    ppermute x20, waiting for transfers between devices, gather_stage(): lax.ppermute(part, 'dp', shift_pairs(count, stride, size, step))  20.8 us
    ppermute x34, starting transfers between devices, swap(): return lax.ppermute(array, axis, [(0, 1), (1, 0)])  15.7 us
    convert_element_type x8, other arithmetic, add(): return (keep.astype(F32) + got.astype(F32)).astype(BF16)  9.79 us
  transfers between devices with their start and end apart: 74, of which 20 were waited for; matrix products, arithmetic and copies ran while one was open for 15% of the time, Pallas kernels for 27%

profile of v3, /device:TPU:0, one launch (start us, length us, event | category | flops | bytes accessed | tf_op | source)
XLA Modules:
  0.0 394.1 jit_solution(15808930977542380543)
XLA Ops:
  10.4 17.5 %collective-permute-done.5.refs_3_.refs_5_ = bf16[960,480]{1,0:T(8,128)(2,1)} collective-permute-done((bf16[960,480]{1,0:T(8,128)(2,1)S(1)}, bf16[960,480]{1,0:T(8,128)(2,1)}, u32[]{:S(2)}, u32[]{:S(2)}) %collective-permute-start.5) | collective-permute-done | bytes 921632 | tf_op jit(solution)/shard_map/ppermute | solution.py:434
  31.7 4.5 %shard_map.203 = (bf16[960,512]{1,0:T(8,128)(2,1)}, bf16[576,512]{1,0:T(8,128)(2,1)}, bf16[384,512]{1,0:T(8,128)(2,1)}) custom-call(bf16[480,512]{1,0:T(8,128)(2,1)} %get-tuple-element.196.refs_0_.refs_6_.refs_9_, bf16[480,512]{1,0:T(8,128)(2,1)} %copy-done.17, f32[480,1]{1,0:T(8,128)} %copy.25.refs_2_.refs_11_, f32[480,1]{1,0:T(8,128)} %copy.26.refs_3_.refs_12_, ...), custom_call_target="tpu_custom_call" | custom-call | flops 28311552 | bytes 147816 | tf_op jit(solution)/shard_map/pallas_call | solution.py:67
  37.2 4.0 %shard_map.205 = (bf16[576,512]{1,0:T(8,128)(2,1)}, bf16[384,512]{1,0:T(8,128)(2,1)}) custom-call(bf16[960,512]{1,0:T(8,128)(2,1)} %get-tuple-element.95.refs_0_.refs_7_, f32[32,512]{1,0:T(8,128)} %get-tuple-element.235.refs_4_.refs_1_.refs_3_, f32[32,512]{1,0:T(8,128)} %get-tuple-element.234.refs_5_.refs_2_.refs_4_, ...), custom_call_target="tpu_custom_call" | custom-call | flops 28311552 | bytes 118210 | tf_op jit(solution)/shard_map/pallas_call | solution.py:67
  46.6 11.3 %shard_map.204 = (bf16[576,512]{1,0:T(8,128)(2,1)}, f32[3,8,512]{2,1,0:T(8,128)}) custom-call(s32[2]{0:T(128)} %pad_add_fusion.refs_0_, s32[1,512]{1,0:T(1,128)} %broadcast_select_fusion.8.refs_1_, bf16[576,512]{1,0:T(8,128)(2,1)} %get-tuple-element.92.refs_2_, bf16[384,512]{1,0:T(8,128)(2,1)} %get-tuple-element.93.refs_3_.refs_4_, ...), custom_call_target="tpu_custom_call" | custom-call | flops 180000000 | bytes 84111 | tf_op jit(solution)/shard_map/pallas_call | solution.py:67
  57.9 8.1 %shard_map.206 = (bf16[576,512]{1,0:T(8,128)(2,1)}, f32[3,8,512]{2,1,0:T(8,128)}) custom-call(s32[2]{0:T(128)} %pad_add_fusion.1.refs_0_, s32[1,512]{1,0:T(1,128)} %broadcast_select_fusion.8.refs_1_, bf16[576,512]{1,0:T(8,128)(2,1)} %get-tuple-element.96.refs_2_, bf16[384,512]{1,0:T(8,128)(2,1)} %get-tuple-element.97.refs_3_.refs_4_, ...), custom_call_target="tpu_custom_call" | custom-call | flops 180000000 | bytes 84111 | tf_op jit(solution)/shard_map/pallas_call | solution.py:67
  67.2 5.8 %shard_map.207 = (f32[960,512]{1,0:T(8,128)}, bf16[960,512]{1,0:T(8,128)(2,1)}) custom-call(bf16[576,512]{1,0:T(8,128)(2,1)} %get-tuple-element.94.refs_0_, bf16[576,512]{1,0:T(8,128)(2,1)} %get-tuple-element.98.refs_1_, bf16[576,480]{1,0:T(8,128)(2,1)} %bitcast.19.refs_2_.refs_6_, bf16[576,480]{1,0:T(8,128)(2,1)} %collective-permute-done.9.refs_3_.refs_7_, ...), custom_call_target="tpu_custom_call" | custom-call | flops 28311552 | bytes 219824 | tf_op jit(solution)/shard_map/pallas_call | solution.py:67
  73.6 15.7 %shard_map.208 = (f32[960,512]{1,0:T(8,128)}, f32[960,512]{1,0:T(8,128)}, bf16[1280,512]{1,0:T(8,128)(2,1)}, bf16[1280,512]{1,0:T(8,128)(2,1)}, bf16[1280,512]{1,0:T(8,128)(2,1)}) custom-call(bf16[960,512]{1,0:T(8,128)(2,1)} %get-tuple-element.100.refs_0_, bf16[960,512]{1,0:T(8,128)(2,1)} %copy-done, bf16[480,1280]{1,0:T(8,128)(2,1)} %refs_2_.3, ...), custom_call_target="tpu_custom_call" | custom-call | flops 226492416 | bytes 516096 | tf_op jit(solution)/shard_map/pallas_call | solution.py:67
  89.3 7.0 %collective-permute-done.16.refs_0_.refs_1_ = bf16[960,512]{1,0:T(8,128)(2,1)S(1)} collective-permute-done((bf16[960,512]{1,0:T(8,128)(2,1)}, bf16[960,512]{1,0:T(8,128)(2,1)S(1)}, u32[]{:S(2)}, u32[]{:S(2)}) %collective-permute-start.16) | collective-permute-done | bytes 983072 | tf_op jit(solution)/shard_map/ppermute | solution.py:434
  97.3 14.6 %shard_map.209 = (bf16[960,512]{1,0:T(8,128)(2,1)}, bf16[960,512]{1,0:T(8,128)(2,1)}, bf16[1280,512]{1,0:T(8,128)(2,1)}, bf16[1280,512]{1,0:T(8,128)(2,1)}, bf16[1280,512]{1,0:T(8,128)(2,1)}) custom-call(bf16[960,512]{1,0:T(8,128)(2,1)} %copy-done.5, bf16[960,512]{1,0:T(8,128)(2,1)} %copy-done.6, bf16[480,1280]{1,0:T(8,128)(2,1)} %refs_2_.3, ...), custom_call_target="tpu_custom_call" | custom-call | flops 226492416 | bytes 457113 | tf_op jit(solution)/shard_map/pallas_call | solution.py:67
  111.9 6.3 %shard_map.210 = (bf16[960,640]{1,0:T(8,128)(2,1)}, bf16[960,640]{1,0:T(8,128)(2,1)}) custom-call(bf16[960,512]{1,0:T(8,128)(2,1)} %copy-done, bf16[960,512]{1,0:T(8,128)(2,1)} %copy-done.6, bf16[1280,512]{1,0:T(8,128)(2,1)} %get-tuple-element.102.refs_8_.refs_2_, bf16[1280,512]{1,0:T(8,128)(2,1)} %get-tuple-element.109.refs_3_), custom_call_target="tpu_custom_call" | custom-call | flops 75497472 | bytes 211353 | tf_op jit(solution)/shard_map/pallas_call | solution.py:67
  118.8 6.3 %shard_map.211 = (bf16[960,640]{1,0:T(8,128)(2,1)}, bf16[960,640]{1,0:T(8,128)(2,1)}) custom-call(bf16[960,512]{1,0:T(8,128)(2,1)} %get-tuple-element.100.refs_0_, bf16[960,512]{1,0:T(8,128)(2,1)} %copy-done.5, bf16[1280,512]{1,0:T(8,128)(2,1)} %get-tuple-element.107.refs_2_, bf16[1280,512]{1,0:T(8,128)(2,1)} %get-tuple-element.108.refs_3_, ...), custom_call_target="tpu_custom_call" | custom-call | flops 75497472 | bytes 211353 | tf_op jit(solution)/shard_map/pallas_call | solution.py:67
  125.3 17.3 %collective-permute-done.17.refs_3_ = bf16[960,512]{1,0:T(8,128)(2,1)S(1)} collective-permute-done((bf16[960,512]{1,0:T(8,128)(2,1)}, bf16[960,512]{1,0:T(8,128)(2,1)S(1)}, u32[]{:S(2)}, u32[]{:S(2)}) %collective-permute-start.17) | collective-permute-done | bytes 983072 | tf_op jit(solution)/shard_map/ppermute | solution.py:434
  145.8 6.3 %shard_map.212 = (bf16[960,640]{1,0:T(8,128)(2,1)}, bf16[960,640]{1,0:T(8,128)(2,1)}) custom-call(bf16[960,512]{1,0:T(8,128)(2,1)} %get-tuple-element.100.refs_0_, bf16[960,512]{1,0:T(8,128)(2,1)} %copy-done.5, bf16[1280,512]{1,0:T(8,128)(2,1)} %get-tuple-element.113.refs_2_, bf16[1280,512]{1,0:T(8,128)(2,1)} %get-tuple-element.114.refs_3_, ...), custom_call_target="tpu_custom_call" | custom-call | flops 75497472 | bytes 211353 | tf_op jit(solution)/shard_map/pallas_call | solution.py:67
  153.2 2.7 add_convert_fusion.1.refs_10_
  158.3 7.1 %shard_map.213 = (f32[960,512]{1,0:T(8,128)}, bf16[960,512]{1,0:T(8,128)(2,1)}, bf16[576,512]{1,0:T(8,128)(2,1)}, bf16[576,512]{1,0:T(8,128)(2,1)}, f32[960,1]{1,0:T(8,128)}) custom-call(bf16[960,512]{1,0:T(8,128)(2,1)} %copy-done, f32[960,512]{1,0:T(8,128)} %get-tuple-element.99.refs_1_, f32[960,512]{1,0:T(8,128)} %get-tuple-element.106.refs_2_, ...), custom_call_target="tpu_custom_call" | custom-call | flops 28311552 | bytes 367395 | tf_op jit(solution)/shard_map/pallas_call | solution.py:67
  188.9 10.1 %shard_map.214 = (f32[576,512]{1,0:T(8,128)}, f32[2,3,64,512]{3,2,1,0:T(8,128)}, bf16[2,3,64,512]{3,2,1,0:T(8,128)(2,1)}) custom-call(s32[2]{0:T(128)} %pad_add_fusion.1.refs_0_, s32[1,512]{1,0:T(1,128)} %broadcast_select_fusion.8.refs_1_, bf16[576,512]{1,0:T(8,128)(2,1)} %get-tuple-element.96.refs_2_, bf16[384,512]{1,0:T(8,128)(2,1)} %get-tuple-element.97.refs_3_.refs_4_, ...), custom_call_target="tpu_custom_call" | custom-call | flops 420000000 | bytes 154890 | tf_op jit(solution)/shard_map/pallas_call | solution.py:67
  200.8 3.3 collective-permute-start.38
  213.6 2.9 collective-permute-start.35
  216.6 6.1 %shard_map.215 = (f32[960,512]{1,0:T(8,128)}, bf16[960,480]{1,0:T(8,128)(2,1)}, bf16[960,480]{1,0:T(8,128)(2,1)}) custom-call(f32[576,512]{1,0:T(8,128)} %get-tuple-element.127.refs_0_, f32[2,3,64,512]{3,2,1,0:T(8,128)} %get-tuple-element.128.refs_1_, bf16[2,3,64,512]{3,2,1,0:T(8,128)(2,1)} %copy-done.40, ...), custom_call_target="tpu_custom_call" | custom-call | flops 56623104 | bytes 273776 | tf_op jit(solution)/shard_map/pallas_call | solution.py:67
  222.7 13.6 %shard_map.216 = (f32[576,512]{1,0:T(8,128)}, f32[2,3,64,512]{3,2,1,0:T(8,128)}, bf16[2,3,64,512]{3,2,1,0:T(8,128)(2,1)}) custom-call(s32[2]{0:T(128)} %pad_add_fusion.refs_0_, s32[1,512]{1,0:T(1,128)} %broadcast_select_fusion.8.refs_1_, bf16[576,512]{1,0:T(8,128)(2,1)} %get-tuple-element.92.refs_2_, bf16[384,512]{1,0:T(8,128)(2,1)} %get-tuple-element.93.refs_3_.refs_4_, ...), custom_call_target="tpu_custom_call" | custom-call | flops 420000000 | bytes 154890 | tf_op jit(solution)/shard_map/pallas_call | solution.py:67
  243.3 8.0 %collective-permute-done.39 = bf16[576,480]{1,0:T(8,128)(2,1)S(1)} collective-permute-done((bf16[576,480]{1,0:T(8,128)(2,1)S(1)}, bf16[576,480]{1,0:T(8,128)(2,1)S(1)}, u32[]{:S(2)}, u32[]{:S(2)}) %collective-permute-start.39) | collective-permute-done | bytes 552992 | tf_op jit(solution)/shard_map/ppermute | solution.py:434
  261.3 8.2 %shard_map.217 = (bf16[960,480]{1,0:T(8,128)(2,1)}, bf16[960,480]{1,0:T(8,128)(2,1)}, bf16[960,512]{1,0:T(8,128)(2,1)}, f32[960,1]{1,0:T(8,128)}) custom-call(f32[576,512]{1,0:T(8,128)} %get-tuple-element.138.refs_0_, f32[2,3,64,512]{3,2,1,0:T(8,128)} %get-tuple-element.139.refs_1_, bf16[2,3,64,512]{3,2,1,0:T(8,128)(2,1)} %copy-done.39, ...), custom_call_target="tpu_custom_call" | custom-call | flops 56623104 | bytes 391971 | tf_op jit(solution)/shard_map/pallas_call | solution.py:67
  271.0 3.1 collective-permute-start.64
  292.8 9.5 %collective-permute-done.45 = bf16[2,480]{1,0:T(2,128)(2,1)S(1)} collective-permute-done((bf16[2,480]{1,0:T(2,128)(2,1)S(1)}, bf16[2,480]{1,0:T(2,128)(2,1)S(1)}, u32[]{:S(2)}, u32[]{:S(2)}) %collective-permute-start.45) | collective-permute-done | bytes 1952 | tf_op jit(solution)/shard_map/ppermute | solution.py:434
  304.5 10.1 %collective-permute-done.65 = bf16[4,120,640]{2,1,0:T(8,128)(2,1)S(1)} collective-permute-done((bf16[4,120,640]{2,1,0:T(8,128)(2,1)S(1)}, bf16[4,120,640]{2,1,0:T(8,128)(2,1)S(1)}, u32[]{:S(2)}, u32[]{:S(2)}) %collective-permute-start.65) | collective-permute-done | bytes 614432 | tf_op jit(solution)/shard_map/ppermute | solution.py:478
  314.6 3.3 collective-permute-start.55
  324.9 2.7 collective-permute-start.58
  336.8 20.9 %collective-permute-done.46 = bf16[4,128,480]{2,1,0:T(8,128)(2,1)S(1)} collective-permute-done((bf16[4,128,480]{2,1,0:T(8,128)(2,1)S(1)}, bf16[4,128,480]{2,1,0:T(8,128)(2,1)S(1)}, u32[]{:S(2)}, u32[]{:S(2)}) %collective-permute-start.46) | collective-permute-done | bytes 491552 | tf_op jit(solution)/shard_map/ppermute | solution.py:468
  366.3 4.4 %collective-permute-done.48 = bf16[128,480]{1,0:T(8,128)(2,1)S(1)} collective-permute-done((bf16[128,480]{1,0:T(8,128)(2,1)S(1)}, bf16[128,480]{1,0:T(8,128)(2,1)S(1)}, u32[]{:S(2)}, u32[]{:S(2)}) %collective-permute-start.48) | collective-permute-done | bytes 122912 | tf_op jit(solution)/shard_map/ppermute | solution.py:468
  370.8 3.3 collective-permute-start.50
  377.6 3.4 collective-permute-done.51
  385.2 5.6 %collective-permute-done.53 = bf16[4,128,480]{2,1,0:T(8,128)(2,1)S(1)} collective-permute-done((bf16[4,128,480]{2,1,0:T(8,128)(2,1)S(1)}, bf16[4,128,480]{2,1,0:T(8,128)(2,1)S(1)}, u32[]{:S(2)}, u32[]{:S(2)}) %collective-permute-start.53) | collective-permute-done | bytes 491552 | tf_op jit(solution)/shard_map/ppermute | solution.py:478
  (361 shorter events, 139.0 us)
Async XLA Ops:
  2.1 29.6 %collective-permute-start.3 = (bf16[960,480]{1,0:T(8,128)(2,1)S(1)}, bf16[960,480]{1,0:T(8,128)(2,1)}, u32[]{:S(2)}, u32[]{:S(2)}) collective-permute-start(bf16[960,480]{1,0:T(8,128)(2,1)S(1)} %pad_maximum_fusion.2.refs_6_.refs_5_), channel_id=1, source_target_pairs={{0,1},{1,0},{2,3},{3,2},{4,5},{5,4},{6,7},{7,6},{8,9},{9,8},{10,11... | collective-permute-start | bytes 2764808 | tf_op jit(solution)/shard_map/ppermute | solution.py:434
  2.7 25.3 %collective-permute-start.5 = (bf16[960,480]{1,0:T(8,128)(2,1)S(1)}, bf16[960,480]{1,0:T(8,128)(2,1)}, u32[]{:S(2)}, u32[]{:S(2)}) collective-permute-start(bf16[960,480]{1,0:T(8,128)(2,1)S(1)} %pad_maximum_fusion.2.refs_6_.refs_5_), channel_id=1, source_target_pairs={{0,2},{2,0},{1,3},{3,1},{4,6},{6,4},{5,7},{7,5},{8,10},{10,8},{9,1... | collective-permute-start | bytes 2764808 | tf_op jit(solution)/shard_map/ppermute | solution.py:434
  6.7 22.1 %collective-permute-start.1 = (bf16[480,512]{1,0:T(8,128)(2,1)}, bf16[480,512]{1,0:T(8,128)(2,1)S(1)}, u32[]{:S(2)}, u32[]{:S(2)}) collective-permute-start(bf16[480,512]{1,0:T(8,128)(2,1)} %get-tuple-element.195), channel_id=1, source_target_pairs={{0,1},{1,0},{2,3},{3,2},{4,5},{5,4},{6,7},{7,6},{8,9},{9,8},{10,11... | collective-permute-start | bytes 1474568 | tf_op jit(solution)/shard_map/ppermute | solution.py:434
  8.5 33.1 %collective-permute-start.8 = (bf16[576,480]{1,0:T(8,128)(2,1)}, bf16[576,480]{1,0:T(8,128)(2,1)}, u32[]{:S(2)}, u32[]{:S(2)}) collective-permute-start(bf16[576,480]{1,0:T(8,128)(2,1)} %bitcast.19.refs_2_.refs_6_), channel_id=1, source_target_pairs={{0,2},{2,0},{1,3},{3,1},{4,6},{6,4},{5,7},{7,5},{8,10},{10,8},{9,1... | collective-permute-start | bytes 1658888 | tf_op jit(solution)/shard_map/ppermute | solution.py:434
  28.8 37.3 %collective-permute-start.12 = (bf16[960,512]{1,0:T(8,128)(2,1)S(1)}, bf16[960,512]{1,0:T(8,128)(2,1)S(1)}, u32[]{:S(2)}, u32[]{:S(2)}) collective-permute-start(bf16[960,512]{1,0:T(8,128)(2,1)S(1)} %pad_maximum_fusion.3.refs_1_.refs_0_), channel_id=1, source_target_pairs={{0,2},{2,0},{1,3},{3,1},{4,6},{6,4},{5,7},{7,5},{8,10},{10,8},{9,1... | collective-permute-start | bytes 2949128 | tf_op jit(solution)/shard_map/ppermute | solution.py:434
  41.7 24.4 %collective-permute-start.10 = (bf16[576,480]{1,0:T(8,128)(2,1)}, bf16[576,480]{1,0:T(8,128)(2,1)S(1)}, u32[]{:S(2)}, u32[]{:S(2)}) collective-permute-start(bf16[576,480]{1,0:T(8,128)(2,1)} %collective-permute-done.8.refs_7_.refs_4_.refs_8_), channel_id=1, source_target_pairs={{0,1},{1,0},{2,3},{3,2},{4,5},{5,4},{6,7},{7,6},{8,9},{9,8},{10,11... | collective-permute-start | bytes 1658888 | tf_op jit(solution)/shard_map/ppermute | solution.py:434
  42.4 31.2 %collective-permute-start.15 = (bf16[480,1280]{1,0:T(8,128)(2,1)}, bf16[480,1280]{1,0:T(8,128)(2,1)}, u32[]{:S(2)}, u32[]{:S(2)}) collective-permute-start(bf16[480,1280]{1,0:T(8,128)(2,1)} %bitcast.228), channel_id=1, source_target_pairs={{0,1},{1,0},{2,3},{3,2},{4,5},{5,4},{6,7},{7,6},{8,9},{9,8},{10,11... | collective-permute-start | bytes 3686408 | tf_op jit(solution)/shard_map/ppermute | solution.py:434
  42.9 30.7 %collective-permute-start.13 = (bf16[480,1280]{1,0:T(8,128)(2,1)}, bf16[480,1280]{1,0:T(8,128)(2,1)}, u32[]{:S(2)}, u32[]{:S(2)}) collective-permute-start(bf16[480,1280]{1,0:T(8,128)(2,1)} %refs_2_.3), channel_id=1, source_target_pairs={{0,1},{1,0},{2,3},{3,2},{4,5},{5,4},{6,7},{7,6},{8,9},{9,8},{10,11... | collective-permute-start | bytes 3686408 | tf_op jit(solution)/shard_map/ppermute | solution.py:434
  43.2 30.3 %collective-permute-start.14 = (bf16[480,1280]{1,0:T(8,128)(2,1)}, bf16[480,1280]{1,0:T(8,128)(2,1)}, u32[]{:S(2)}, u32[]{:S(2)}) collective-permute-start(bf16[480,1280]{1,0:T(8,128)(2,1)} %refs_4_.3), channel_id=1, source_target_pairs={{0,1},{1,0},{2,3},{3,2},{4,5},{5,4},{6,7},{7,6},{8,9},{9,8},{10,11... | collective-permute-start | bytes 3686408 | tf_op jit(solution)/shard_map/ppermute | solution.py:434
  72.9 23.4 %collective-permute-start.16 = (bf16[960,512]{1,0:T(8,128)(2,1)}, bf16[960,512]{1,0:T(8,128)(2,1)S(1)}, u32[]{:S(2)}, u32[]{:S(2)}) collective-permute-start(bf16[960,512]{1,0:T(8,128)(2,1)} %get-tuple-element.100.refs_0_), channel_id=1, source_target_pairs={{0,2},{2,0},{1,3},{3,1},{4,6},{6,4},{5,7},{7,5},{8,10},{10,8},{9,1... | collective-permute-start | bytes 2949128 | tf_op jit(solution)/shard_map/ppermute | solution.py:434
  118.2 25.0 %collective-permute-start.21 = (bf16[960,640]{1,0:T(8,128)(2,1)}, bf16[960,640]{1,0:T(8,128)(2,1)}, u32[]{:S(2)}, u32[]{:S(2)}) collective-permute-start(bf16[960,640]{1,0:T(8,128)(2,1)} %get-tuple-element.115), channel_id=1, source_target_pairs={{0,1},{1,0},{2,3},{3,2},{4,5},{5,4},{6,7},{7,6},{8,9},{9,8},{10,11... | collective-permute-start | bytes 3686408 | tf_op jit(solution)/shard_map/ppermute | solution.py:434
  118.2 24.4 %collective-permute-start.17 = (bf16[960,512]{1,0:T(8,128)(2,1)}, bf16[960,512]{1,0:T(8,128)(2,1)S(1)}, u32[]{:S(2)}, u32[]{:S(2)}) collective-permute-start(bf16[960,512]{1,0:T(8,128)(2,1)} %get-tuple-element.104), channel_id=1, source_target_pairs={{0,2},{2,0},{1,3},{3,1},{4,6},{6,4},{5,7},{7,5},{8,10},{10,8},{9,1... | collective-permute-start | bytes 2949128 | tf_op jit(solution)/shard_map/ppermute | solution.py:434
  125.1 27.0 %collective-permute-start.20 = (bf16[960,640]{1,0:T(8,128)(2,1)}, bf16[960,640]{1,0:T(8,128)(2,1)S(1)}, u32[]{:S(2)}, u32[]{:S(2)}) collective-permute-start(bf16[960,640]{1,0:T(8,128)(2,1)} %get-tuple-element.112), channel_id=1, source_target_pairs={{0,1},{1,0},{2,3},{3,2},{4,5},{5,4},{6,7},{7,6},{8,9},{9,8},{10,11... | collective-permute-start | bytes 3686408 | tf_op jit(solution)/shard_map/ppermute | solution.py:434
  142.6 33.6 %collective-permute-start.18 = (bf16[960,512]{1,0:T(8,128)(2,1)}, bf16[960,512]{1,0:T(8,128)(2,1)}, u32[]{:S(2)}, u32[]{:S(2)}) collective-permute-start(bf16[960,512]{1,0:T(8,128)(2,1)} %get-tuple-element.105), channel_id=1, source_target_pairs={{0,2},{2,0},{1,3},{3,1},{4,6},{6,4},{5,7},{7,5},{8,10},{10,8},{9,1... | collective-permute-start | bytes 2949128 | tf_op jit(solution)/shard_map/ppermute | solution.py:434
  155.9 23.9 %collective-permute-start.23 = (bf16[960,640]{1,0:T(8,128)(2,1)}, bf16[960,640]{1,0:T(8,128)(2,1)}, u32[]{:S(2)}, u32[]{:S(2)}) collective-permute-start(bf16[960,640]{1,0:T(8,128)(2,1)} %get-tuple-element.125), channel_id=1, source_target_pairs={{0,1},{1,0},{2,3},{3,2},{4,5},{5,4},{6,7},{7,6},{8,9},{9,8},{10,11... | collective-permute-start | bytes 3686408 | tf_op jit(solution)/shard_map/ppermute | solution.py:434
  167.9 32.4 %collective-permute-start.30 = (bf16[576,480]{1,0:T(8,128)(2,1)}, bf16[576,480]{1,0:T(8,128)(2,1)}, u32[]{:S(2)}, u32[]{:S(2)}) collective-permute-start(bf16[576,480]{1,0:T(8,128)(2,1)} %convolution_convert_fusion), channel_id=1, source_target_pairs={{0,1},{1,0},{2,3},{3,2},{4,5},{5,4},{6,7},{7,6},{8,9},{9,8},{10,11... | collective-permute-start | bytes 1658888 | tf_op jit(solution)/shard_map/ppermute | solution.py:434
  169.4 31.4 %collective-permute-start.29 = (bf16[576,480]{1,0:T(8,128)(2,1)}, bf16[576,480]{1,0:T(8,128)(2,1)}, u32[]{:S(2)}, u32[]{:S(2)}) collective-permute-start(bf16[576,480]{1,0:T(8,128)(2,1)} %convolution_convert_fusion.1), channel_id=1, source_target_pairs={{0,1},{1,0},{2,3},{3,2},{4,5},{5,4},{6,7},{7,6},{8,9},{9,8},{10,11... | collective-permute-start | bytes 1658888 | tf_op jit(solution)/shard_map/ppermute | solution.py:434
  173.4 30.8 %collective-permute-start.25 = (bf16[4,120,640]{2,1,0:T(8,128)(2,1)}, bf16[4,120,640]{2,1,0:T(8,128)(2,1)}, u32[]{:S(2)}, u32[]{:S(2)}) collective-permute-start(bf16[4,120,640]{2,1,0:T(8,128)(2,1)} %dynamic-slice_bitcast_fusion.1), channel_id=1, source_target_pairs={{0,4},{4,0},{8,12},{12,8},{16,20},{20,16},{24,28},{28,24},{1,5},{5... | collective-permute-start | bytes 1843208 | tf_op jit(solution)/shard_map/ppermute | solution.py:468
  179.8 19.1 %collective-permute-start.27 = (bf16[120,640]{1,0:T(8,128)(2,1)S(1)}, bf16[120,640]{1,0:T(8,128)(2,1)S(1)}, u32[]{:S(2)}, u32[]{:S(2)}) collective-permute-start(bf16[120,640]{1,0:T(8,128)(2,1)S(1)} %get-tuple-element.214), channel_id=1, source_target_pairs={{0,16},{4,20},{8,24},{12,28},{16,0},{20,4},{24,8},{28,12},{1,17},{... | collective-permute-start | bytes 460808 | tf_op jit(solution)/shard_map/ppermute | solution.py:468
  200.3 36.0 %collective-permute-start.37 = (bf16[120,640]{1,0:T(8,128)(2,1)S(1)}, bf16[120,640]{1,0:T(8,128)(2,1)S(1)}, u32[]{:S(2)}, u32[]{:S(2)}) collective-permute-start(bf16[120,640]{1,0:T(8,128)(2,1)S(1)} %get-tuple-element.182.refs_9_), channel_id=1, source_target_pairs={{0,16},{4,20},{8,24},{12,28},{16,0},{20,4},{24,8},{28,12},{1,17},{... | collective-permute-start | bytes 460808 | tf_op jit(solution)/shard_map/ppermute | solution.py:478
  200.8 37.0 %collective-permute-start.38 = (bf16[120,640]{1,0:T(8,128)(2,1)S(1)}, bf16[120,640]{1,0:T(8,128)(2,1)S(1)}, u32[]{:S(2)}, u32[]{:S(2)}) collective-permute-start(bf16[120,640]{1,0:T(8,128)(2,1)S(1)} %get-tuple-element.182.refs_9_), channel_id=1, source_target_pairs={{0,24},{4,28},{8,0},{12,4},{16,8},{20,12},{24,16},{28,20},{1,25},{... | collective-permute-start | bytes 460808 | tf_op jit(solution)/shard_map/ppermute | solution.py:478
  210.4 27.9 %collective-permute-start.33 = (bf16[120,640]{1,0:T(8,128)(2,1)S(1)}, bf16[120,640]{1,0:T(8,128)(2,1)S(1)}, u32[]{:S(2)}, u32[]{:S(2)}) collective-permute-start(bf16[120,640]{1,0:T(8,128)(2,1)S(1)} %get-tuple-element.212), channel_id=1, source_target_pairs={{0,8},{4,12},{8,16},{12,20},{16,24},{20,28},{24,0},{28,4},{1,9},{5... | collective-permute-start | bytes 460808 | tf_op jit(solution)/shard_map/ppermute | solution.py:468
  212.2 26.2 %collective-permute-start.34 = (bf16[120,640]{1,0:T(8,128)(2,1)S(1)}, bf16[120,640]{1,0:T(8,128)(2,1)S(1)}, u32[]{:S(2)}, u32[]{:S(2)}) collective-permute-start(bf16[120,640]{1,0:T(8,128)(2,1)S(1)} %get-tuple-element.211), channel_id=1, source_target_pairs={{0,16},{4,20},{8,24},{12,28},{16,0},{20,4},{24,8},{28,12},{1,17},{... | collective-permute-start | bytes 460808 | tf_op jit(solution)/shard_map/ppermute | solution.py:468
  213.6 24.7 %collective-permute-start.35 = (bf16[120,640]{1,0:T(8,128)(2,1)S(1)}, bf16[120,640]{1,0:T(8,128)(2,1)S(1)}, u32[]{:S(2)}, u32[]{:S(2)}) collective-permute-start(bf16[120,640]{1,0:T(8,128)(2,1)S(1)} %get-tuple-element.210), channel_id=1, source_target_pairs={{0,24},{4,28},{8,0},{12,4},{16,8},{20,12},{24,16},{28,20},{1,25},{... | collective-permute-start | bytes 460808 | tf_op jit(solution)/shard_map/ppermute | solution.py:468
  238.4 21.7 %collective-permute-start.31 = (bf16[2,3,64,512]{3,2,1,0:T(8,128)(2,1)}, bf16[2,3,64,512]{3,2,1,0:T(8,128)(2,1)S(1)}, u32[]{:S(2)}, u32[]{:S(2)}) collective-permute-start(bf16[2,3,64,512]{3,2,1,0:T(8,128)(2,1)} %get-tuple-element.140), channel_id=1, source_target_pairs={{0,1},{1,0},{2,3},{3,2},{4,5},{5,4},{6,7},{7,6},{8,9},{9,8},{10,11... | collective-permute-start | bytes 1179656 | tf_op jit(solution)/shard_map/ppermute | solution.py:434
  239.0 39.5 %collective-permute-start.73 = (bf16[4,120,640]{2,1,0:T(8,128)(2,1)S(1)}, bf16[4,120,640]{2,1,0:T(8,128)(2,1)}, u32[]{:S(2)}, u32[]{:S(2)}) collective-permute-start(bf16[4,120,640]{2,1,0:T(8,128)(2,1)S(1)} %bitcast_dynamic-update-slice_fusion.18.refs_16_), channel_id=1, source_target_pairs={{0,4},{4,0},{8,12},{12,8},{16,20},{20,16},{24,28},{28,24},{1,5},{5... | collective-permute-start | bytes 1843208 | tf_op jit(solution)/shard_map/ppermute | solution.py:478
  278.5 49.7 %collective-permute-start.69 = (bf16[120,640]{1,0:T(8,128)(2,1)}, bf16[120,640]{1,0:T(8,128)(2,1)S(1)}, u32[]{:S(2)}, u32[]{:S(2)}) collective-permute-start(bf16[120,640]{1,0:T(8,128)(2,1)} %get-tuple-element.174), channel_id=1, source_target_pairs={{0,8},{4,12},{8,16},{12,20},{16,24},{20,28},{24,0},{28,4},{1,9},{5... | collective-permute-start | bytes 460808 | tf_op jit(solution)/shard_map/ppermute | solution.py:478
  279.5 50.6 %collective-permute-start.70 = (bf16[120,640]{1,0:T(8,128)(2,1)}, bf16[120,640]{1,0:T(8,128)(2,1)S(1)}, u32[]{:S(2)}, u32[]{:S(2)}) collective-permute-start(bf16[120,640]{1,0:T(8,128)(2,1)} %get-tuple-element.174), channel_id=1, source_target_pairs={{0,16},{4,20},{8,24},{12,28},{16,0},{20,4},{24,8},{28,12},{1,17},{... | collective-permute-start | bytes 460808 | tf_op jit(solution)/shard_map/ppermute | solution.py:478
  281.1 37.1 %collective-permute-start.43 = (bf16[960,480]{1,0:T(8,128)(2,1)S(1)}, bf16[960,480]{1,0:T(8,128)(2,1)S(1)}, u32[]{:S(2)}, u32[]{:S(2)}) collective-permute-start(bf16[960,480]{1,0:T(8,128)(2,1)S(1)} %copy-done.20), channel_id=1, source_target_pairs={{0,2},{2,0},{1,3},{3,1},{4,6},{6,4},{5,7},{7,5},{8,10},{10,8},{9,1... | collective-permute-start | bytes 2764808 | tf_op jit(solution)/shard_map/ppermute | solution.py:434
  332.1 44.4 %collective-permute-start.72 = (bf16[4,120,640]{2,1,0:T(8,128)(2,1)}, bf16[4,120,640]{2,1,0:T(8,128)(2,1)S(1)}, u32[]{:S(2)}, u32[]{:S(2)}) collective-permute-start(bf16[4,120,640]{2,1,0:T(8,128)(2,1)} %bitcast_dynamic-update-slice_fusion.10), channel_id=1, source_target_pairs={{0,4},{4,0},{8,12},{12,8},{16,20},{20,16},{24,28},{28,24},{1,5},{5... | collective-permute-start | bytes 1843208 | tf_op jit(solution)/shard_map/ppermute | solution.py:478
  334.5 23.2 %collective-permute-start.46 = (bf16[4,128,480]{2,1,0:T(8,128)(2,1)S(1)}, bf16[4,128,480]{2,1,0:T(8,128)(2,1)S(1)}, u32[]{:S(2)}, u32[]{:S(2)}) collective-permute-start(bf16[4,128,480]{2,1,0:T(8,128)(2,1)S(1)} %dynamic-slice_bitcast_fusion.3), channel_id=1, source_target_pairs={{0,4},{4,0},{8,12},{12,8},{16,20},{20,16},{24,28},{28,24},{1,5},{5... | collective-permute-start | bytes 1474568 | tf_op jit(solution)/shard_map/ppermute | solution.py:468
  335.6 27.0 %collective-permute-start.61 = (bf16[4,72,480]{2,1,0:T(8,128)(2,1)S(1)}, bf16[4,72,480]{2,1,0:T(8,128)(2,1)S(1)}, u32[]{:S(2)}, u32[]{:S(2)}) collective-permute-start(bf16[4,72,480]{2,1,0:T(8,128)(2,1)S(1)} %bitcast_dynamic-update-slice_fusion.26), channel_id=1, source_target_pairs={{0,4},{4,0},{8,12},{12,8},{16,20},{20,16},{24,28},{28,24},{1,5},{5... | collective-permute-start | bytes 829448 | tf_op jit(solution)/shard_map/ppermute | solution.py:478
  (93 other events, 699.1 us)

commit v4 on v3

--- a/solution.py
+++ b/solution.py
@@ -20,6 +20,7 @@
 BLOCK = MAXLEN // 4
 LOCAL = 2 * BLOCK
 LIVE = (3, 2)
+ROWS = 1024
 
 NORM_EPS = 1e-05
 ROPE_BASE = 100000.0
@@ -217,12 +218,27 @@
         gnm_ref[...] = gnm_sum[...].astype(gnm_ref.dtype)
 
 
-def grads_kernel(rows_ref, rows_far_ref, cols_ref, cols_far_ref, keep_ref, send_ref):
-    for half, out_ref in enumerate((keep_ref, send_ref)):
-        rows = slice(half * HALF, (half + 1) * HALF)
-        product = dot(rows_ref[rows, :], cols_ref[...], 1, 1)
-        product += dot(rows_far_ref[rows, :], cols_far_ref[...], 1, 1)
-        out_ref[...] = product.astype(BF16)
+def grads_kernel(
+    nm_ref, nm_far_ref, og_ref, og_far_ref, act_ref, act_far_ref, gg_ref, gg_far_ref, gu_ref,
+    gu_far_ref, *out_refs,
+):
+    sources = (
+        (og_ref, og_far_ref, act_ref, act_far_ref), (nm_ref, nm_far_ref, gg_ref, gg_far_ref),
+        (nm_ref, nm_far_ref, gu_ref, gu_far_ref),
+    )
+    for which, (rows_ref, rows_far_ref, cols_ref, cols_far_ref) in enumerate(sources):
+        for half in range(2):
+            rows = slice(half * HALF, (half + 1) * HALF)
+            product = dot(rows_ref[rows, :], cols_ref[...], 1, 1)
+            product += dot(rows_far_ref[rows, :], cols_far_ref[...], 1, 1)
+            out_refs[2 * which + half][...] = product.astype(BF16)
+
+
+def gain_rows(product):
+    return lax.dot_general(
+        jnp.ones((16, product.shape[1]), F32), product, (((1,), (1,)), ((), ())),
+        precision=lax.Precision.HIGHEST, preferred_element_type=F32,
+    )
 
 
 def mid_back_kernel(
@@ -239,7 +255,7 @@
     for rows, mid, scaled in (
         (slice(0, HALF), own, scaled_own), (slice(HALF, D), got, scaled_got)
     ):
-        ggain_ref[rows, :] = jnp.sum(gnm[rows] * mid * level, axis=1, keepdims=True)
+        ggain_ref[rows.start // HALF] = gain_rows(gnm[rows] * mid * level)
         gmid = og_ref[rows, :].astype(F32) + scaled * level - mid * pull
         gmid_ref[rows, :] = gmid
         gb_ref[rows, :] = gmid.astype(BF16)
@@ -320,20 +336,20 @@
 ):
     turn_back(cos_ref, sin_ref, dq_ref, own_ref, got_ref, gj_ref)
     gj = gj_ref[...]
-    send_ref[...] = dot(gj, nm_ref[HALF:, :], 1, 1).astype(BF16)
-    keep_ref[...] = dot(gj, nm_ref[:HALF, :], 1, 1).astype(BF16)
+    for half, out_ref in enumerate((keep_ref, send_ref)):
+        rows = slice(half * HALF, (half + 1) * HALF)
+        out_ref[:D, :] = dot(gj, nm_ref[rows, :], 1, 1).astype(BF16)
+        out_ref[D:, :] = jnp.zeros((ROWS - D, HALF), BF16)
     gnm_ref[:HALF, :] = dot(wo_ref[...], gj, 0, 0)
     gnm_ref[HALF:, :] = dot(wg_ref[...], gj, 0, 0)
 
 
 def joined_near_kernel(
     dq_ref, own_ref, got_ref, cos_ref, sin_ref, wo_ref, wg_ref, nm_ref, part_ref, xo_ref, xg_ref,
-    go_ref, gg_ref, gmid_ref, keep_ref, send_ref, grad_ref, ggain_ref, gj_ref,
+    go_ref, gg_ref, gmid_ref, ggain_ref, keep_ref, send_ref, grad_ref, gj_ref,
 ):
     turn_back(cos_ref, sin_ref, dq_ref, own_ref, got_ref, gj_ref)
     gj = gj_ref[...]
-    send_ref[...] = dot(gj, nm_ref[HALF:, :], 1, 1).astype(BF16)
-    keep_ref[...] = dot(gj, nm_ref[:HALF, :], 1, 1).astype(BF16)
     gnm_own = part_ref[:HALF, :] + dot(wo_ref[...], gj, 0, 0)
     gnm_got = part_ref[HALF:, :] + dot(wg_ref[...], gj, 0, 0)
     own, got = xo_ref[...].astype(F32), xg_ref[...].astype(F32)
@@ -345,7 +361,12 @@
     for rows, x, gnm, scaled in (
         (slice(0, HALF), own, gnm_own, scaled_own), (slice(HALF, D), got, gnm_got, scaled_got)
     ):
-        ggain_ref[rows, :] = jnp.sum(gnm * x * level, axis=1, keepdims=True)
+        half = rows.start // HALF
+        out_ref = (keep_ref, send_ref)[half]
+        out_ref[:D, :] = dot(gj, nm_ref[rows, :], 1, 1).astype(BF16)
+        out_ref[D : D + 16, :] = gain_rows(gnm * x * level).astype(BF16)
+        out_ref[D + 16 : D + 32, :] = ggain_ref[half].astype(BF16)
+        out_ref[D + 32 :, :] = jnp.zeros((ROWS - D - 32, HALF), BF16)
         grad_ref[rows, :] = (gmid_ref[rows, :] + scaled * level - x * pull).astype(BF16)
 
 
@@ -413,20 +434,19 @@
     )
 
 
-def weight_grads(rows, rows_far, cols, cols_far, after=()):
-    hidden = cols.shape[0]
-    part = hidden // 2
-    taken = pl.BlockSpec((part, LOCAL), lambda i: (i, 0))
-    given = pl.BlockSpec((HALF, part), lambda i: (i, 0))
+def weight_grads(nm, nm_far, og, og_far, act, act_far, gg, gg_far, gu, gu_far):
+    hidden = act.shape[0]
+    chunk = 256
+    taken = pl.BlockSpec((chunk, LOCAL), lambda i: (i, 0))
+    given = pl.BlockSpec((HALF, chunk), lambda i: (0, i))
     return run(
         grads_kernel,
-        (rows, rows_far, cols, cols_far),
-        (shape((2 * HALF, part)),) * 2,
-        4 * LOCAL * D * hidden,
-        grid=(2,),
-        in_specs=[whole((D, LOCAL))] * 2 + [taken] * 2,
-        out_specs=(given, given),
-        after=after,
+        (nm, nm_far, og, og_far, act, act_far, gg, gg_far, gu, gu_far),
+        (shape((HALF, hidden)),) * 6,
+        12 * LOCAL * D * hidden,
+        grid=(hidden // chunk,),
+        in_specs=[whole((D, LOCAL))] * 4 + [taken] * 6,
+        out_specs=(given,) * 6,
     )
 
 
@@ -514,8 +534,8 @@
     return lax.optimization_barrier((array,) + others)[0]
 
 
-def add(keep, got):
-    return (keep.astype(F32) + got.astype(F32)).astype(BF16)
+def add(*parts):
+    return sum(part.astype(F32) for part in parts).astype(BF16)
 
 
 def segment_begin(segment):
@@ -590,7 +610,7 @@
     wo_far = swap(wo_near, "row")
     wo_near_got = swap(wo_near, "col")
     att_near, lse_near = attend(where_near, begin, q_near, kv_near, kv_near_got)
-    w_far_got = swap(w_far, "col")
+    w_far_got = swap(hold(w_far, lse_near), "col")
     q_far, kv_far = run(
         project_far_kernel,
         (nm_in, cosine, sine, w_far, w_far_got),
@@ -623,11 +643,13 @@
         nm_far, og_far, mlp_weights, BF16, after=(act,)
     )
     gnm_back = swap(gnm_send, "row")
-    down_keep, down_send = weight_grads(og, og_far, act, act_far)
-    gate_keep, gate_send = weight_grads(nm, nm_far, gg, gg_far, after=(down_keep,))
-    down_sum = add(down_keep, hold(swap(down_send, "col"), gate_keep))
-    up_keep, up_send = weight_grads(nm, nm_far, gu, gu_far, after=(down_sum,))
-    gate_sum = add(gate_keep, hold(swap(gate_send, "col"), up_keep))
+    down_keep, down_send, gate_keep, gate_send, up_keep, up_send = weight_grads(
+        nm, nm_far, og, og_far, act, act_far, gg, gg_far, gu, gu_far
+    )
+    down_sum = add(down_keep, swap(down_send, "col"))
+    gate_sum = add(gate_keep, swap(gate_send, "col"))
+    up_sum = add(up_keep, swap(up_send, "col"))
+    down_grad = lax.psum(down_sum, "dp")
 
     gmid, gb, gatt_near, gatt_far, ggain_mid = run(
         mid_back_kernel,
@@ -637,19 +659,17 @@
         ),
         (
             shape((D, LOCAL), F32), shape((D, LOCAL)), shape((QUERY, LOCAL)),
-            shape((QUERY, LOCAL)), shape((D, 1), F32),
+            shape((QUERY, LOCAL)), shape((2, 16, HALF), F32),
         ),
         2 * LOCAL * D * D,
-        after=(gate_sum,),
-    )
-    up_sum = add(up_keep, hold(swap(up_send, "col"), ggain_mid))
-    down_x = reduce_first(down_sum, count, (ggain_mid,))
+        after=(up_keep,),
+    )
 
     dq_far, own_far, other_far = attend_back(
-        where_far, begin, q_far, kv_far, kv_far_got, gatt_far, lse_far, after=(down_x, up_sum)
-    )
-    gate_x = reduce_first(gate_sum, count, (dq_far,))
-    down_z = reduce_rest(down_x, count, (dq_far,))
+        where_far, begin, q_far, kv_far, kv_far_got, gatt_far, lse_far, after=(down_sum, gate_sum, up_sum)
+    )
+    out_back = hold(swap(hold(out_send, gnm_back), "row"), dq_far)
+    block = (mid + out_part + out_back.astype(F32)).astype(BF16)
 
     def out_grads(att):
         send = dot(att, gb[HALF:], 1, 1).astype(BF16)
@@ -658,13 +678,13 @@
     wo_far_sum = out_grads(att_far)
     wo_near_sum = out_grads(att_near)
     got_far = swap(other_far, "col")
-    joined = shape((D, HALF))
+    joined = shape((ROWS, HALF))
     gnm_in_part, far_keep, far_send = run(
         joined_far_kernel,
         (dq_far, own_far, got_far, cosine, sine, w_far, w_far_got, nm_in),
         (shape((D, LOCAL), F32), joined, joined),
         4 * LOCAL * D * D,
-        after=(gate_x, down_z, wo_far_sum, wo_near_sum),
+        after=(wo_far_sum, wo_near_sum, block),
         scratch=[pltpu.VMEM((D, LOCAL), BF16)],
     )
     dq_near, own_near, other_near = attend_back(
@@ -672,61 +692,46 @@
     )
     far_sum = add(far_keep, hold(swap(far_send, "col"), dq_near))
     wo_sum = add(wo_near_sum, hold(swap(wo_far_sum, "row"), dq_near))
-    up_x = reduce_first(up_sum, count, (dq_near,))
-    gate_z = reduce_rest(gate_x, count, (dq_near,))
-    down_y = gather_rest(down_z, count, (dq_near,))
+    down_grad = hold(down_grad, dq_near)
     got_near = swap(other_near, "col")
-    near_keep, near_send, grad, ggain_in = run(
+    near_keep, near_send, grad = run(
         joined_near_kernel,
         (
             dq_near, own_near, got_near, cosine, sine, w_near, w_near_got, nm_in, gnm_in_part,
-            x_own, x_got, gin_own, gin_got, gmid,
+            x_own, x_got, gin_own, gin_got, gmid, ggain_mid,
         ),
-        (joined, joined, shape((D, LOCAL)), shape((D, 1), F32)),
+        (joined, joined, shape((D, LOCAL))),
         4 * LOCAL * D * D,
-        after=(up_x, gate_z, down_y, wo_sum, far_sum),
+        after=(wo_sum, far_sum, down_grad),
         scratch=[pltpu.VMEM((D, LOCAL), BF16)],
     )
-    ggain = jnp.concatenate([ggain_in, ggain_mid], axis=1).T.astype(BF16)
-    ggain_sum = add(ggain[:, :HALF], swap(ggain[:, HALF:], "col"))
-    near_sum = add(near_keep, swap(near_send, "col"))
-    near_sum = add(near_sum, swap(far_sum, "row"))
-    ggain_sum = add(ggain_sum, swap(ggain_sum, "row"))
-    last_sum = jnp.concatenate([near_sum, jnp.pad(ggain_sum, ((0, 62), (0, 0)))], axis=0)
+    last_sum = add(near_keep, swap(near_send, "col"), swap(far_sum, "row"))
 
     def feature_cols(array):
         return in_window(array[:HALF], swap(array[HALF:], "col")).T
 
-    out_back = swap(hold(out_send, gnm_back), "row")
-    block_out = feature_cols((mid + out_part + out_back.astype(F32)).astype(BF16))
+    block_out = feature_cols(block)
     input_grad = feature_cols(grad)
 
-    def widened(part):
-        total = gather_first(part, count, (D, down_sum.shape[1]), (ggain_in,))
-        return jnp.concatenate([total[:HALF], total[HALF:]], axis=1)
-
-    down_grad = widened(down_y).T
-    up_z = reduce_rest(up_x, count, (ggain_in,))
-    gate_grad = widened(gather_rest(gate_z, count, (ggain_in,)))
-    up_grad = widened(gather_rest(up_z, count, (last_sum,)))
-    out_z = reduce_rest(
-        reduce_first(wo_sum, count, (ggain_in,)), count, (last_sum,)
-    )
-    out_weight_grad = gather_first(gather_rest(out_z, count), count, wo_sum.shape)
-    last_z = reduce_rest(reduce_first(last_sum, count), count)
+    gate_grad = lax.psum(hold(gate_sum, down_grad), "dp")
+    last_sum = jnp.concatenate([last_sum, wo_sum], axis=0)
+    last_z = reduce_rest(reduce_first(last_sum, count), count, (gate_grad,))
+    up_grad = lax.psum(hold(up_sum, gate_grad), "dp")
     last = gather_first(gather_rest(last_z, count), count, last_sum.shape)
+    gain_grads = jnp.stack([last[D], last[D + 16]])
+    gain_grads = gain_grads + swap(gain_grads, "row")
     return (
         block_out,
         input_grad,
         last[:QUERY].T[:, None, :],
         last[QUERY : QUERY + KEY].T[:, None, :],
         last[QUERY + KEY : D].T[:, None, :],
-        out_weight_grad[None],
-        gate_grad,
-        up_grad,
-        down_grad,
-        last[D],
-        last[D + 1],
+        last[ROWS:][None],
+        gate_grad.astype(F32),
+        up_grad.astype(F32),
+        down_grad.astype(F32).T,
+        gain_grads[0],
+        gain_grads[1],
     )
 
 

time: 399 us -> 507 us (1.27)
  waiting for transfers between devices: 115 us -> 261 us
  starting transfers between devices: 76.7 us -> 31 us
  between operations: 1.98 us -> 14.5 us
    psum x0 -> x3, waiting for transfers between devices: none -> 181 us  [the longest x1 67.5 us: per_device(): up_grad = lax.psum(hold(up_sum, gate_grad), 'dp')]
    ppermute x20 -> x4, starting transfers between devices: 31.3 us -> 5.9 us  [reduce_stage(): lax.ppermute(sent, 'dp', shift_pairs(count, stride, size, step))]
    ppermute x20 -> x4, starting transfers between devices: 29.7 us -> 6.04 us  [gather_stage(): lax.ppermute(part, 'dp', shift_pairs(count, stride, size, step))]
    ppermute x20 -> x4, waiting for transfers between devices: 34.7 us -> 18.4 us  [reduce_stage(): lax.ppermute(sent, 'dp', shift_pairs(count, stride, size, step))]
    ppermute x34 -> x33, waiting for transfers between devices: 59.8 us -> 43.9 us  [swap(): return lax.ppermute(array, axis, [(0, 1), (1, 0)])]
    dynamic_update_slice x20 -> x4, local copies, waits for them, and re-layouts: 6.39 us -> 1.04 us  [gather_stage(): lax.dynamic_update_index_in_dim(spread, got, (digit - step) % size, 0)]
    ppermute x20 -> x4, waiting for transfers between devices: 20.8 us -> 17.3 us  [gather_stage(): lax.ppermute(part, 'dp', shift_pairs(count, stride, size, step))]
    ppermute x34 -> x33, starting transfers between devices: 15.7 us -> 19 us  [swap(): return lax.ppermute(array, axis, [(0, 1), (1, 0)])]
  transfers between devices with their start and end apart: 74 -> 44, of which waited for: 20 -> 14; matrix products, arithmetic and copies ran while one was open for 15% -> 11% of each run, Pallas kernels for 27% -> 22%
where the time goes in v4:
time: 507 us; the launch traced here: 503 us
  waiting for transfers between devices  261 us (51%)
  Pallas kernels  125 us (25%)
  other arithmetic  32.5 us (6%)
  starting transfers between devices  31 us (6%)
  local copies, waits for them, and re-layouts  30 us (6%)
  between operations  14.5 us (3%)
  matrix products  9.18 us (2%)
    pallas_call x13, Pallas kernels, run(): pl.pallas_call(body, grid=grid if grid is not None else (1,), in_specs=li...  125 us
    psum x1, waiting for transfers between devices, per_device(): up_grad = lax.psum(hold(up_sum, gate_grad), 'dp')  67.5 us
    psum x1, waiting for transfers between devices, per_device(): gate_grad = lax.psum(hold(gate_sum, down_grad), 'dp')  59.5 us
    psum x1, waiting for transfers between devices, per_device(): down_grad = lax.psum(down_sum, 'dp')  53.6 us
    ppermute x33, waiting for transfers between devices, swap(): return lax.ppermute(array, axis, [(0, 1), (1, 0)])  43.9 us
    ppermute x33, starting transfers between devices, swap(): return lax.ppermute(array, axis, [(0, 1), (1, 0)])  19 us
    ppermute x4, waiting for transfers between devices, reduce_stage(): lax.ppermute(sent, 'dp', shift_pairs(count, stride, size, step))  18.4 us
    ppermute x4, waiting for transfers between devices, gather_stage(): lax.ppermute(part, 'dp', shift_pairs(count, stride, size, step))  17.3 us
  transfers between devices with their start and end apart: 44, of which 14 were waited for; matrix products, arithmetic and copies ran while one was open for 11% of the time, Pallas kernels for 22%

profile of v4, /device:TPU:0, one launch (start us, length us, event | category | flops | bytes accessed | tf_op | source)
XLA Modules:
  0.0 503.1 jit_solution(9229238154076802799)
XLA Ops:
  18.7 4.6 shard_map.203
  26.7 11.6 %shard_map.204 = (bf16[576,512]{1,0:T(8,128)(2,1)}, f32[3,8,512]{2,1,0:T(8,128)}) custom-call(s32[2]{0:T(128)} %pad_add_fusion.refs_0_, s32[1,512]{1,0:T(1,128)} %broadcast_select_fusion.8.refs_1_, bf16[576,512]{1,0:T(8,128)(2,1)} %get-tuple-element.68.refs_2_, bf16[384,512]{1,0:T(8,128)(2,1)} %get-tuple-element.69.refs_3_.refs_4_, ...), custom_call_target="tpu_custom_call" | custom-call | flops 180000000 | bytes 84111 | tf_op jit(solution)/shard_map/pallas_call | solution.py:68
  42.7 4.1 shard_map.205
  47.3 7.3 %collective-permute-done.8.refs_7_.refs_4_.refs_8_ = bf16[576,480]{1,0:T(8,128)(2,1)S(1)} collective-permute-done((bf16[576,480]{1,0:T(8,128)(2,1)S(1)}, bf16[576,480]{1,0:T(8,128)(2,1)S(1)}, u32[]{:S(2)}, u32[]{:S(2)}) %collective-permute-start.8) | collective-permute-done | bytes 552992 | tf_op jit(solution)/shard_map/ppermute | solution.py:454
  58.3 8.3 %shard_map.206 = (bf16[576,512]{1,0:T(8,128)(2,1)}, f32[3,8,512]{2,1,0:T(8,128)}) custom-call(s32[2]{0:T(128)} %pad_add_fusion.1.refs_0_, s32[1,512]{1,0:T(1,128)} %broadcast_select_fusion.8.refs_1_, bf16[576,512]{1,0:T(8,128)(2,1)} %get-tuple-element.74.refs_2_, bf16[384,512]{1,0:T(8,128)(2,1)} %get-tuple-element.75.refs_3_.refs_4_, ...), custom_call_target="tpu_custom_call" | custom-call | flops 180000000 | bytes 84111 | tf_op jit(solution)/shard_map/pallas_call | solution.py:68
  66.6 8.6 %collective-permute-done.12.refs_10_.refs_1_.refs_3_ = bf16[960,512]{1,0:T(8,128)(2,1)S(1)} collective-permute-done((bf16[960,512]{1,0:T(8,128)(2,1)S(1)}, bf16[960,512]{1,0:T(8,128)(2,1)S(1)}, u32[]{:S(2)}, u32[]{:S(2)}) %collective-permute-start.12) | collective-permute-done | bytes 983072 | tf_op jit(solution)/shard_map/ppermute | solution.py:454
  76.2 5.7 %shard_map.207 = (f32[960,512]{1,0:T(8,128)}, bf16[960,512]{1,0:T(8,128)(2,1)}) custom-call(bf16[576,512]{1,0:T(8,128)(2,1)} %get-tuple-element.70.refs_0_, bf16[576,512]{1,0:T(8,128)(2,1)} %get-tuple-element.76.refs_1_, bf16[576,480]{1,0:T(8,128)(2,1)} %bitcast.96, bf16[576,480]{1,0:T(8,128)(2,1)} %copy-done.17, bf16[576,480]{1,0:T(8,128)(2,1)} %copy-done.8, ...), custom_call_target="tpu_custom_call" | custom-call | flops 28311552 | bytes 219824 | tf_op jit(solution)/shard_map/pallas_call | solution.py:68
  82.2 15.3 %shard_map.208 = (f32[960,512]{1,0:T(8,128)}, f32[960,512]{1,0:T(8,128)}, bf16[1280,512]{1,0:T(8,128)(2,1)}, bf16[1280,512]{1,0:T(8,128)(2,1)}, bf16[1280,512]{1,0:T(8,128)(2,1)}) custom-call(bf16[960,512]{1,0:T(8,128)(2,1)} %get-tuple-element.78.refs_0_, bf16[960,512]{1,0:T(8,128)(2,1)} %copy-done, bf16[480,1280]{1,0:T(8,128)(2,1)} %refs_2_.3, ...), custom_call_target="tpu_custom_call" | custom-call | flops 226492416 | bytes 516096 | tf_op jit(solution)/shard_map/pallas_call | solution.py:68
  97.5 7.9 %collective-permute-done.16.refs_0_.refs_1_ = bf16[960,512]{1,0:T(8,128)(2,1)S(1)} collective-permute-done((bf16[960,512]{1,0:T(8,128)(2,1)}, bf16[960,512]{1,0:T(8,128)(2,1)S(1)}, u32[]{:S(2)}, u32[]{:S(2)}) %collective-permute-start.16) | collective-permute-done | bytes 983072 | tf_op jit(solution)/shard_map/ppermute | solution.py:454
  106.4 14.6 %shard_map.209 = (bf16[960,512]{1,0:T(8,128)(2,1)}, bf16[960,512]{1,0:T(8,128)(2,1)}, bf16[1280,512]{1,0:T(8,128)(2,1)}, bf16[1280,512]{1,0:T(8,128)(2,1)}, bf16[1280,512]{1,0:T(8,128)(2,1)}) custom-call(bf16[960,512]{1,0:T(8,128)(2,1)} %copy-done.15, bf16[960,512]{1,0:T(8,128)(2,1)} %copy-done.4, bf16[480,1280]{1,0:T(8,128)(2,1)} %refs_2_.3, ...), custom_call_target="tpu_custom_call" | custom-call | flops 226492416 | bytes 457113 | tf_op jit(solution)/shard_map/pallas_call | solution.py:68
  121.6 12.4 %shard_map.210 = (bf16[480,1280]{1,0:T(8,128)(2,1)}, bf16[480,1280]{1,0:T(8,128)(2,1)}, bf16[480,1280]{1,0:T(8,128)(2,1)}, bf16[480,1280]{1,0:T(8,128)(2,1)}, bf...) custom-call(bf16[960,512]{1,0:T(8,128)(2,1)} %get-tuple-element.78.refs_0_, bf16[960,512]{1,0:T(8,128)(2,1)} %copy-done.15, ...), custom_call_target="tpu_custom_call" | custom-call | flops 226492416 | bytes 575078 | tf_op jit(solution)/shard_map/pallas_call | solution.py:68
  134.6 9.1 %collective-permute-done.17.refs_3_ = bf16[960,512]{1,0:T(8,128)(2,1)S(1)} collective-permute-done((bf16[960,512]{1,0:T(8,128)(2,1)}, bf16[960,512]{1,0:T(8,128)(2,1)S(1)}, u32[]{:S(2)}, u32[]{:S(2)}) %collective-permute-start.17) | collective-permute-done | bytes 983072 | tf_op jit(solution)/shard_map/ppermute | solution.py:454
  144.7 8.2 %shard_map.211 = (f32[960,512]{1,0:T(8,128)}, bf16[960,512]{1,0:T(8,128)(2,1)}, bf16[576,512]{1,0:T(8,128)(2,1)}, bf16[576,512]{1,0:T(8,128)(2,1)}, f32[2,16,480]{2,1,0:T(8,128)}) custom-call(bf16[960,512]{1,0:T(8,128)(2,1)} %copy-done, f32[960,512]{1,0:T(8,128)} %get-tuple-element.77.refs_1_, f32[960,512]{1,0:T(8,128)} %get-tuple-element.84.refs_2_, ...), custom_call_target="tpu_custom_call" | custom-call | flops 28311552 | bytes 369123 | tf_op jit(solution)/shard_map/pallas_call | solution.py:68
  160.3 2.7 add_convert_fusion.2.refs_9_
  163.0 2.6 add_convert_fusion.1.refs_10_
  165.6 10.1 %shard_map.212 = (f32[576,512]{1,0:T(8,128)}, f32[2,3,64,512]{3,2,1,0:T(8,128)}, bf16[2,3,64,512]{3,2,1,0:T(8,128)(2,1)}) custom-call(s32[2]{0:T(128)} %pad_add_fusion.1.refs_0_, s32[1,512]{1,0:T(1,128)} %broadcast_select_fusion.8.refs_1_, bf16[576,512]{1,0:T(8,128)(2,1)} %get-tuple-element.74.refs_2_, bf16[384,512]{1,0:T(8,128)(2,1)} %get-tuple-element.75.refs_3_.refs_4_, ...), custom_call_target="tpu_custom_call" | custom-call | flops 420000000 | bytes 154890 | tf_op jit(solution)/shard_map/pallas_call | solution.py:68
  176.6 2.7 fusion.1.refs_8_
  179.3 2.7 fusion.2.refs_9_
  184.4 6.7 %shard_map.213 = (f32[960,512]{1,0:T(8,128)}, bf16[1024,480]{1,0:T(8,128)(2,1)}, bf16[1024,480]{1,0:T(8,128)(2,1)}) custom-call(f32[576,512]{1,0:T(8,128)} %get-tuple-element.98.refs_0_, f32[2,3,64,512]{3,2,1,0:T(8,128)} %get-tuple-element.101.refs_1_, bf16[2,3,64,512]{3,2,1,0:T(8,128)(2,1)} %copy-done.37, ...), custom_call_target="tpu_custom_call" | custom-call | flops 56623104 | bytes 277463 | tf_op jit(solution)/shard_map/pallas_call | solution.py:68
  193.4 4.9 collective-permute-start.27
  198.3 13.5 %shard_map.214 = (f32[576,512]{1,0:T(8,128)}, f32[2,3,64,512]{3,2,1,0:T(8,128)}, bf16[2,3,64,512]{3,2,1,0:T(8,128)(2,1)}) custom-call(s32[2]{0:T(128)} %pad_add_fusion.refs_0_, s32[1,512]{1,0:T(1,128)} %broadcast_select_fusion.8.refs_1_, bf16[576,512]{1,0:T(8,128)(2,1)} %get-tuple-element.68.refs_2_, bf16[384,512]{1,0:T(8,128)(2,1)} %get-tuple-element.69.refs_3_.refs_4_, ...), custom_call_target="tpu_custom_call" | custom-call | flops 420000000 | bytes 154890 | tf_op jit(solution)/shard_map/pallas_call | solution.py:68
  212.9 53.6 %all-reduce.4.cloned.1.call-done.refs_17_ = bf16[480,1280]{1,0:T(8,128)(2,1)} async-done(((bf16[480,1280]{1,0:T(8,128)(2,1)}), bf16[480,1280]{1,0:T(8,128)(2,1)}) %all-reduce.4.cloned.1.call-update) | async-done | bytes 1228816 | tf_op jit(solution)/shard_map/psum | solution.py:652
  272.0 10.0 %shard_map.215 = (bf16[1024,480]{1,0:T(8,128)(2,1)}, bf16[1024,480]{1,0:T(8,128)(2,1)}, bf16[960,512]{1,0:T(8,128)(2,1)}) custom-call(f32[576,512]{1,0:T(8,128)} %get-tuple-element.107.refs_0_, f32[2,3,64,512]{3,2,1,0:T(8,128)} %get-tuple-element.108.refs_1_, bf16[2,3,64,512]{3,2,1,0:T(8,128)(2,1)} %copy-done.36, ...), custom_call_target="tpu_custom_call" | custom-call | flops 56623104 | bytes 397386 | tf_op jit(solution)/shard_map/pallas_call | solution.py:68
  284.2 9.3 %collective-permute-done.31 = bf16[1024,480]{0,1:T(8,128)(2,1)S(1)} collective-permute-done((bf16[1024,480]{0,1:T(8,128)(2,1)}, bf16[1024,480]{0,1:T(8,128)(2,1)S(1)}, u32[]{:S(2)}, u32[]{:S(2)}) %collective-permute-start.31) | collective-permute-done | bytes 983072 | tf_op jit(solution)/shard_map/ppermute | solution.py:454
  299.4 2.9 convert_bitcast_fusion
  302.2 18.4 %collective-permute-done.32 = bf16[4,200,480]{2,1,0:T(8,128)(2,1)} collective-permute-done((bf16[4,200,480]{2,1,0:T(8,128)(2,1)S(1)}, bf16[4,200,480]{2,1,0:T(8,128)(2,1)}, u32[]{:S(2)}, u32[]{:S(2)}) %collective-permute-start.32) | collective-permute-done | bytes 768032 | tf_op jit(solution)/shard_map/ppermute | solution.py:488
  324.3 2.9 collective-permute-start.35
  328.3 59.5 %all-reduce.6.cloned.1.call-done = bf16[480,1280]{1,0:T(8,128)(2,1)} async-done(((bf16[480,1280]{1,0:T(8,128)(2,1)}), bf16[480,1280]{1,0:T(8,128)(2,1)}) %all-reduce.6.cloned.1.call-update) | async-done | bytes 1228816 | tf_op jit(solution)/shard_map/psum | solution.py:716
  396.1 3.7 collective-permute-done.36
  400.8 13.6 %collective-permute-done.37 = bf16[200,480]{1,0:T(8,128)(2,1)S(1)} collective-permute-done((bf16[200,480]{1,0:T(8,128)(2,1)}, bf16[200,480]{1,0:T(8,128)(2,1)S(1)}, u32[]{:S(2)}, u32[]{:S(2)}) %collective-permute-start.37) | collective-permute-done | bytes 192032 | tf_op jit(solution)/shard_map/ppermute | solution.py:498
  419.2 67.5 %all-reduce.8.cloned.1.call-done = bf16[480,1280]{1,0:T(8,128)(2,1)} async-done(((bf16[480,1280]{1,0:T(8,128)(2,1)}), bf16[480,1280]{1,0:T(8,128)(2,1)}) %all-reduce.8.cloned.1.call-update) | async-done | bytes 1228816 | tf_op jit(solution)/shard_map/psum | solution.py:719
  486.7 2.9 convert_element_type.176
  (240 shorter events, 80.8 us)
Async XLA Ops:
  9.2 29.1 %collective-permute-start.5 = (bf16[960,480]{1,0:T(8,128)(2,1)S(1)}, bf16[960,480]{1,0:T(8,128)(2,1)}, u32[]{:S(2)}, u32[]{:S(2)}) collective-permute-start(bf16[960,480]{1,0:T(8,128)(2,1)S(1)} %pad_maximum_fusion.1.refs_6_.refs_5_), channel_id=1, source_target_pairs={{0,2},{2,0},{1,3},{3,1},{4,6},{6,4},{5,7},{7,5},{8,10},{10,8},{9,1... | collective-permute-start | bytes 2764808 | tf_op jit(solution)/shard_map/ppermute | solution.py:454
  24.6 13.9 %collective-permute-start.11 = (bf16[480,512]{1,0:T(8,128)(2,1)S(1)}, bf16[480,512]{1,0:T(8,128)(2,1)}, u32[]{:S(2)}, u32[]{:S(2)}) collective-permute-start(bf16[480,512]{1,0:T(8,128)(2,1)S(1)} %get-tuple-element.140), channel_id=1, source_target_pairs={{0,1},{1,0},{2,3},{3,2},{4,5},{5,4},{6,7},{7,6},{8,9},{9,8},{10,11... | collective-permute-start | bytes 1474568 | tf_op jit(solution)/shard_map/ppermute | solution.py:454
  38.4 16.2 %collective-permute-start.8 = (bf16[576,480]{1,0:T(8,128)(2,1)S(1)}, bf16[576,480]{1,0:T(8,128)(2,1)S(1)}, u32[]{:S(2)}, u32[]{:S(2)}) collective-permute-start(bf16[576,480]{1,0:T(8,128)(2,1)S(1)} %bitcast.98), channel_id=1, source_target_pairs={{0,2},{2,0},{1,3},{3,1},{4,6},{6,4},{5,7},{7,5},{8,10},{10,8},{9,1... | collective-permute-start | bytes 1658888 | tf_op jit(solution)/shard_map/ppermute | solution.py:454
  39.6 35.6 %collective-permute-start.12 = (bf16[960,512]{1,0:T(8,128)(2,1)S(1)}, bf16[960,512]{1,0:T(8,128)(2,1)S(1)}, u32[]{:S(2)}, u32[]{:S(2)}) collective-permute-start(bf16[960,512]{1,0:T(8,128)(2,1)S(1)} %pad_maximum_fusion.2.refs_1_.refs_2_.refs_0_), channel_id=1, source_target_pairs={{0,2},{2,0},{1,3},{3,1},{4,6},{6,4},{5,7},{7,5},{8,10},{10,8},{9,1... | collective-permute-start | bytes 2949128 | tf_op jit(solution)/shard_map/ppermute | solution.py:454
  41.7 13.4 %collective-permute-start.9 = (bf16[576,480]{1,0:T(8,128)(2,1)S(1)}, bf16[576,480]{1,0:T(8,128)(2,1)S(1)}, u32[]{:S(2)}, u32[]{:S(2)}) collective-permute-start(bf16[576,480]{1,0:T(8,128)(2,1)S(1)} %bitcast.99), channel_id=1, source_target_pairs={{0,1},{1,0},{2,3},{3,2},{4,5},{5,4},{6,7},{7,6},{8,9},{9,8},{10,11... | collective-permute-start | bytes 1658888 | tf_op jit(solution)/shard_map/ppermute | solution.py:454
  54.6 27.6 %collective-permute-start.13 = (bf16[480,1280]{1,0:T(8,128)(2,1)}, bf16[480,1280]{1,0:T(8,128)(2,1)}, u32[]{:S(2)}, u32[]{:S(2)}) collective-permute-start(bf16[480,1280]{1,0:T(8,128)(2,1)} %refs_2_.3), channel_id=1, source_target_pairs={{0,1},{1,0},{2,3},{3,2},{4,5},{5,4},{6,7},{7,6},{8,9},{9,8},{10,11... | collective-permute-start | bytes 3686408 | tf_op jit(solution)/shard_map/ppermute | solution.py:454
  55.2 27.0 %collective-permute-start.14 = (bf16[480,1280]{1,0:T(8,128)(2,1)}, bf16[480,1280]{1,0:T(8,128)(2,1)}, u32[]{:S(2)}, u32[]{:S(2)}) collective-permute-start(bf16[480,1280]{1,0:T(8,128)(2,1)} %refs_4_.3), channel_id=1, source_target_pairs={{0,1},{1,0},{2,3},{3,2},{4,5},{5,4},{6,7},{7,6},{8,9},{9,8},{10,11... | collective-permute-start | bytes 3686408 | tf_op jit(solution)/shard_map/ppermute | solution.py:454
  56.0 26.2 %collective-permute-start.15 = (bf16[480,1280]{1,0:T(8,128)(2,1)}, bf16[480,1280]{1,0:T(8,128)(2,1)}, u32[]{:S(2)}, u32[]{:S(2)}) collective-permute-start(bf16[480,1280]{1,0:T(8,128)(2,1)} %bitcast.23.refs_6_), channel_id=1, source_target_pairs={{0,1},{1,0},{2,3},{3,2},{4,5},{5,4},{6,7},{7,6},{8,9},{9,8},{10,11... | collective-permute-start | bytes 3686408 | tf_op jit(solution)/shard_map/ppermute | solution.py:454
  81.9 23.5 %collective-permute-start.16 = (bf16[960,512]{1,0:T(8,128)(2,1)}, bf16[960,512]{1,0:T(8,128)(2,1)S(1)}, u32[]{:S(2)}, u32[]{:S(2)}) collective-permute-start(bf16[960,512]{1,0:T(8,128)(2,1)} %get-tuple-element.78.refs_0_), channel_id=1, source_target_pairs={{0,2},{2,0},{1,3},{3,1},{4,6},{6,4},{5,7},{7,5},{8,10},{10,8},{9,1... | collective-permute-start | bytes 2949128 | tf_op jit(solution)/shard_map/ppermute | solution.py:454
  121.0 22.7 %collective-permute-start.17 = (bf16[960,512]{1,0:T(8,128)(2,1)}, bf16[960,512]{1,0:T(8,128)(2,1)S(1)}, u32[]{:S(2)}, u32[]{:S(2)}) collective-permute-start(bf16[960,512]{1,0:T(8,128)(2,1)} %get-tuple-element.82), channel_id=1, source_target_pairs={{0,2},{2,0},{1,3},{3,1},{4,6},{6,4},{5,7},{7,5},{8,10},{10,8},{9,1... | collective-permute-start | bytes 2949128 | tf_op jit(solution)/shard_map/ppermute | solution.py:454
  134.0 23.4 %collective-permute-start.21 = (bf16[480,1280]{1,0:T(8,128)(2,1)}, bf16[480,1280]{1,0:T(8,128)(2,1)S(1)}, u32[]{:S(2)}, u32[]{:S(2)}) collective-permute-start(bf16[480,1280]{1,0:T(8,128)(2,1)} %get-tuple-element.97), channel_id=1, source_target_pairs={{0,1},{1,0},{2,3},{3,2},{4,5},{5,4},{6,7},{7,6},{8,9},{9,8},{10,11... | collective-permute-start | bytes 3686408 | tf_op jit(solution)/shard_map/ppermute | solution.py:454
  134.1 25.2 %collective-permute-start.19 = (bf16[480,1280]{1,0:T(8,128)(2,1)}, bf16[480,1280]{1,0:T(8,128)(2,1)S(1)}, u32[]{:S(2)}, u32[]{:S(2)}) collective-permute-start(bf16[480,1280]{1,0:T(8,128)(2,1)} %get-tuple-element.94), channel_id=1, source_target_pairs={{0,1},{1,0},{2,3},{3,2},{4,5},{5,4},{6,7},{7,6},{8,9},{9,8},{10,11... | collective-permute-start | bytes 3686408 | tf_op jit(solution)/shard_map/ppermute | solution.py:454
  134.6 28.5 %collective-permute-start.20 = (bf16[480,1280]{1,0:T(8,128)(2,1)}, bf16[480,1280]{1,0:T(8,128)(2,1)}, u32[]{:S(2)}, u32[]{:S(2)}) collective-permute-start(bf16[480,1280]{1,0:T(8,128)(2,1)} %get-tuple-element.96), channel_id=1, source_target_pairs={{0,1},{1,0},{2,3},{3,2},{4,5},{5,4},{6,7},{7,6},{8,9},{9,8},{10,11... | collective-permute-start | bytes 3686408 | tf_op jit(solution)/shard_map/ppermute | solution.py:454
  156.7 25.3 %collective-permute-start.18 = (bf16[960,512]{1,0:T(8,128)(2,1)}, bf16[960,512]{1,0:T(8,128)(2,1)S(1)}, u32[]{:S(2)}, u32[]{:S(2)}) collective-permute-start(bf16[960,512]{1,0:T(8,128)(2,1)} %get-tuple-element.83), channel_id=1, source_target_pairs={{0,2},{2,0},{1,3},{3,1},{4,6},{6,4},{5,7},{7,5},{8,10},{10,8},{9,1... | collective-permute-start | bytes 2949128 | tf_op jit(solution)/shard_map/ppermute | solution.py:454
  157.4 19.2 %collective-permute-start.24 = (bf16[576,480]{1,0:T(8,128)(2,1)}, bf16[576,480]{1,0:T(8,128)(2,1)}, u32[]{:S(2)}, u32[]{:S(2)}) collective-permute-start(bf16[576,480]{1,0:T(8,128)(2,1)} %convolution_convert_fusion.1), channel_id=1, source_target_pairs={{0,1},{1,0},{2,3},{3,2},{4,5},{5,4},{6,7},{7,6},{8,9},{9,8},{10,11... | collective-permute-start | bytes 1658888 | tf_op jit(solution)/shard_map/ppermute | solution.py:454
  157.4 19.2 %collective-permute-start.25 = (bf16[576,480]{1,0:T(8,128)(2,1)}, bf16[576,480]{1,0:T(8,128)(2,1)}, u32[]{:S(2)}, u32[]{:S(2)}) collective-permute-start(bf16[576,480]{1,0:T(8,128)(2,1)} %convolution_convert_fusion), channel_id=1, source_target_pairs={{0,1},{1,0},{2,3},{3,2},{4,5},{5,4},{6,7},{7,6},{8,9},{9,8},{10,11... | collective-permute-start | bytes 1658888 | tf_op jit(solution)/shard_map/ppermute | solution.py:454
  175.7 90.7 %all-reduce.4.cloned.1.call-start = ((), (), s32[]{:S(2)}) async-start(), calls=%async_computation | async-start | bytes 2457600 | tf_op jit(solution)/shard_map/psum | solution.py:652
  176.5 211.4 %all-reduce.6.cloned.1.call-start = ((), (), s32[]{:S(2)}) async-start(), calls=%async_computation.1 | async-start | bytes 2457600 | tf_op jit(solution)/shard_map/psum | solution.py:716
  192.9 73.5 %collective-permute-start.28 = (bf16[1024,480]{0,1:T(8,128)(2,1)S(1)}, bf16[1024,480]{0,1:T(8,128)(2,1)}, u32[]{:S(2)}, u32[]{:S(2)}) collective-permute-start(bf16[1024,480]{0,1:T(8,128)(2,1)S(1)} %copy.37), channel_id=1, source_target_pairs={{0,1},{1,0},{2,3},{3,2},{4,5},{5,4},{6,7},{7,6},{8,9},{9,8},{10,11... | collective-permute-start | bytes 2949128 | tf_op jit(solution)/shard_map/ppermute | solution.py:454
  193.4 18.5 %collective-permute-start.27 = (bf16[576,480]{1,0:T(8,128)(2,1)S(1)}, bf16[576,480]{1,0:T(8,128)(2,1)S(1)}, u32[]{:S(2)}, u32[]{:S(2)}) collective-permute-start(bf16[576,480]{1,0:T(8,128)(2,1)S(1)} %copy-done.35), channel_id=1, source_target_pairs={{0,2},{2,0},{1,3},{3,1},{4,6},{6,4},{5,7},{7,5},{8,10},{10,8},{9,1... | collective-permute-start | bytes 1658888 | tf_op jit(solution)/shard_map/ppermute | solution.py:454
  211.8 59.5 %collective-permute-start.26 = (bf16[2,3,64,512]{3,2,1,0:T(8,128)(2,1)}, bf16[2,3,64,512]{3,2,1,0:T(8,128)(2,1)S(1)}, u32[]{:S(2)}, u32[]{:S(2)}) collective-permute-start(bf16[2,3,64,512]{3,2,1,0:T(8,128)(2,1)} %get-tuple-element.109), channel_id=1, source_target_pairs={{0,1},{1,0},{2,3},{3,2},{4,5},{5,4},{6,7},{7,6},{8,9},{9,8},{10,11... | collective-permute-start | bytes 1179656 | tf_op jit(solution)/shard_map/ppermute | solution.py:454
  269.7 23.8 %collective-permute-start.31 = (bf16[1024,480]{0,1:T(8,128)(2,1)}, bf16[1024,480]{0,1:T(8,128)(2,1)S(1)}, u32[]{:S(2)}, u32[]{:S(2)}) collective-permute-start(bf16[1024,480]{0,1:T(8,128)(2,1)} %copy.43), channel_id=1, source_target_pairs={{0,2},{2,0},{1,3},{3,1},{4,6},{6,4},{5,7},{7,5},{8,10},{10,8},{9,1... | collective-permute-start | bytes 2949128 | tf_op jit(solution)/shard_map/ppermute | solution.py:454
  296.9 23.7 %collective-permute-start.32 = (bf16[4,200,480]{2,1,0:T(8,128)(2,1)S(1)}, bf16[4,200,480]{2,1,0:T(8,128)(2,1)}, u32[]{:S(2)}, u32[]{:S(2)}) collective-permute-start(bf16[4,200,480]{2,1,0:T(8,128)(2,1)S(1)} %dynamic-slice_bitcast_fusion), channel_id=1, source_target_pairs={{0,4},{4,0},{8,12},{12,8},{16,20},{20,16},{24,28},{28,24},{1,5},{5... | collective-permute-start | bytes 2304008 | tf_op jit(solution)/shard_map/ppermute | solution.py:488
  299.3 27.9 %collective-permute-start.22 = (bf16[480,512]{1,0:T(8,128)(2,1)}, bf16[480,512]{1,0:T(8,128)(2,1)}, u32[]{:S(2)}, u32[]{:S(2)}) collective-permute-start(bf16[480,512]{1,0:T(8,128)(2,1)} %slice.182), channel_id=1, source_target_pairs={{0,1},{1,0},{2,3},{3,2},{4,5},{5,4},{6,7},{7,6},{8,9},{9,8},{10,11... | collective-permute-start | bytes 1474568 | tf_op jit(solution)/shard_map/ppermute | solution.py:454
  299.3 187.4 %all-reduce.8.cloned.1.call-start = ((), (), s32[]{:S(2)}) async-start(), calls=%async_computation.2 | async-start | bytes 2457600 | tf_op jit(solution)/shard_map/psum | solution.py:719
  322.8 65.0 %collective-permute-start.33 = (bf16[200,480]{1,0:T(8,128)(2,1)}, bf16[200,480]{1,0:T(8,128)(2,1)S(1)}, u32[]{:S(2)}, u32[]{:S(2)}) collective-permute-start(bf16[200,480]{1,0:T(8,128)(2,1)} %get-tuple-element.149), channel_id=1, source_target_pairs={{0,8},{4,12},{8,16},{12,20},{16,24},{20,28},{24,0},{28,4},{1,9},{5... | collective-permute-start | bytes 576008 | tf_op jit(solution)/shard_map/ppermute | solution.py:488
  323.5 64.3 %collective-permute-start.34 = (bf16[200,480]{1,0:T(8,128)(2,1)}, bf16[200,480]{1,0:T(8,128)(2,1)S(1)}, u32[]{:S(2)}, u32[]{:S(2)}) collective-permute-start(bf16[200,480]{1,0:T(8,128)(2,1)} %get-tuple-element.148), channel_id=1, source_target_pairs={{0,16},{4,20},{8,24},{12,28},{16,0},{20,4},{24,8},{28,12},{1,17},{... | collective-permute-start | bytes 576008 | tf_op jit(solution)/shard_map/ppermute | solution.py:488
  324.3 63.6 %collective-permute-start.35 = (bf16[200,480]{1,0:T(8,128)(2,1)S(1)}, bf16[200,480]{1,0:T(8,128)(2,1)}, u32[]{:S(2)}, u32[]{:S(2)}) collective-permute-start(bf16[200,480]{1,0:T(8,128)(2,1)S(1)} %get-tuple-element.147), channel_id=1, source_target_pairs={{0,24},{4,28},{8,0},{12,4},{16,8},{20,12},{24,16},{28,20},{1,25},{... | collective-permute-start | bytes 576008 | tf_op jit(solution)/shard_map/ppermute | solution.py:488
  392.8 23.1 %collective-permute-start.29 = (bf16[480,512]{1,0:T(8,128)(2,1)}, bf16[480,512]{1,0:T(8,128)(2,1)S(1)}, u32[]{:S(2)}, u32[]{:S(2)}) collective-permute-start(bf16[480,512]{1,0:T(8,128)(2,1)} %slice.159), channel_id=1, source_target_pairs={{0,1},{1,0},{2,3},{3,2},{4,5},{5,4},{6,7},{7,6},{8,9},{9,8},{10,11... | collective-permute-start | bytes 1474568 | tf_op jit(solution)/shard_map/ppermute | solution.py:454
  392.8 21.5 %collective-permute-start.37 = (bf16[200,480]{1,0:T(8,128)(2,1)}, bf16[200,480]{1,0:T(8,128)(2,1)S(1)}, u32[]{:S(2)}, u32[]{:S(2)}) collective-permute-start(bf16[200,480]{1,0:T(8,128)(2,1)} %get-tuple-element.126), channel_id=1, source_target_pairs={{0,16},{4,20},{8,24},{12,28},{16,0},{20,4},{24,8},{28,12},{1,17},{... | collective-permute-start | bytes 576008 | tf_op jit(solution)/shard_map/ppermute | solution.py:498
  393.8 20.5 %collective-permute-start.38 = (bf16[200,480]{1,0:T(8,128)(2,1)}, bf16[200,480]{1,0:T(8,128)(2,1)S(1)}, u32[]{:S(2)}, u32[]{:S(2)}) collective-permute-start(bf16[200,480]{1,0:T(8,128)(2,1)} %get-tuple-element.126), channel_id=1, source_target_pairs={{0,24},{4,28},{8,0},{12,4},{16,8},{20,12},{24,16},{28,20},{1,25},{... | collective-permute-start | bytes 576008 | tf_op jit(solution)/shard_map/ppermute | solution.py:498
  414.4 75.5 %collective-permute-start.39 = (bf16[4,200,480]{2,1,0:T(8,128)(2,1)S(1)}, bf16[4,200,480]{2,1,0:T(8,128)(2,1)S(1)}, u32[]{:S(2)}, u32[]{:S(2)}) collective-permute-start(bf16[4,200,480]{2,1,0:T(8,128)(2,1)S(1)} %bitcast_dynamic-update-slice_fusion.2), channel_id=1, source_target_pairs={{0,4},{4,0},{8,12},{12,8},{16,20},{20,16},{24,28},{28,24},{1,5},{5... | collective-permute-start | bytes 2304008 | tf_op jit(solution)/shard_map/ppermute | solution.py:498
  (54 other events, 308.8 us)
Sparse Core Ops, SparseCore 0:
  180.7 85.6 all-reduce.3
  299.4 88.3 all-reduce.5
  392.9 93.7 all-reduce.7

commit v5 on v4

--- a/solution.py
+++ b/solution.py
@@ -19,6 +19,7 @@
 MAXLEN = 1024
 BLOCK = MAXLEN // 4
 LOCAL = 2 * BLOCK
+LANE = 128
 LIVE = (3, 2)
 ROWS = 1024
 
@@ -168,7 +169,7 @@
 
 def mid_kernel(
     near_ref, far_ref, no_ref, ng_ref, fo_ref, fg_ref, xo_ref, xg_ref, go_ref, gg_ref,
-    mid_ref, nm_ref,
+    mid_ref, nma_ref, nmb_ref,
 ):
     near, far = near_ref[...], far_ref[...]
     own = xo_ref[...].astype(F32) + dot(no_ref[...], near, 0, 0) + dot(fo_ref[...], far, 0, 0)
@@ -176,29 +177,30 @@
     mid_ref[:HALF, :] = own
     mid_ref[HALF:, :] = got
     level = level_of(own, got)
-    nm_ref[:HALF, :] = (own * level * go_ref[...]).astype(BF16)
-    nm_ref[HALF:, :] = (got * level * gg_ref[...]).astype(BF16)
-
-
-def mlp_kernel(
-    nm_ref, og_ref, wgo_ref, wgg_ref, wuo_ref, wug_ref, wdo_ref, wdg_ref,
-    out_ref, gnm_ref, act_ref, gg_ref, gu_ref, out_sum, gnm_sum,
-):
+    for rows, part, gain_ref in ((slice(0, HALF), own, go_ref), (slice(HALF, D), got, gg_ref)):
+        normed = (part * level * gain_ref[...]).astype(BF16)
+        nma_ref[rows, :] = normed[:, :BLOCK]
+        nmb_ref[rows, :] = normed[:, BLOCK:]
+
+
+def mlp_kernel(pieces, *refs):
+    nm_refs = refs[:pieces]
+    og_ref, wgo_ref, wgg_ref, wuo_ref, wug_ref, wdo_ref, wdg_ref = refs[pieces : pieces + 7]
+    out_ref, gnm_ref, act_ref, gg_ref, gu_ref, out_sum, gnm_sum = refs[pieces + 7 :]
     step = pl.program_id(0)
-
-    def inward(own_ref, got_ref, rows_ref):
-        return dot(own_ref[...], rows_ref[:HALF, :], 0, 0) + dot(
-            got_ref[...], rows_ref[HALF:, :], 0, 0
-        )
+    nm, og = jnp.concatenate([ref[...] for ref in nm_refs], axis=1), og_ref[...]
+
+    def inward(own_ref, got_ref, rows):
+        return dot(own_ref[...], rows[:HALF], 0, 0) + dot(got_ref[...], rows[HALF:], 0, 0)
 
     @pl.when(step == 0)
     def _():
         out_sum[...] = jnp.zeros_like(out_sum)
         gnm_sum[...] = jnp.zeros_like(gnm_sum)
 
-    gate = inward(wgo_ref, wgg_ref, nm_ref)
-    up = inward(wuo_ref, wug_ref, nm_ref)
-    grad_act = inward(wdo_ref, wdg_ref, og_ref)
+    gate = inward(wgo_ref, wgg_ref, nm)
+    up = inward(wuo_ref, wug_ref, nm)
+    grad_act = inward(wdo_ref, wdg_ref, og)
     sig = jax.nn.sigmoid(gate)
     silu = gate * sig
     act = (silu * up).astype(BF16)
@@ -218,20 +220,23 @@
         gnm_ref[...] = gnm_sum[...].astype(gnm_ref.dtype)
 
 
-def grads_kernel(
-    nm_ref, nm_far_ref, og_ref, og_far_ref, act_ref, act_far_ref, gg_ref, gg_far_ref, gu_ref,
-    gu_far_ref, *out_refs,
-):
-    sources = (
-        (og_ref, og_far_ref, act_ref, act_far_ref), (nm_ref, nm_far_ref, gg_ref, gg_far_ref),
-        (nm_ref, nm_far_ref, gu_ref, gu_far_ref),
-    )
-    for which, (rows_ref, rows_far_ref, cols_ref, cols_far_ref) in enumerate(sources):
+def grads_kernel(row_counts, col_counts, rows_of, *refs):
+    at = 0
+
+    def whole_tokens(count):
+        nonlocal at
+        at += count
+        return jnp.concatenate([ref[...] for ref in refs[at - count : at]], axis=1)
+
+    rows = [whole_tokens(count) for count in row_counts]
+    for kind, count in enumerate(col_counts):
+        cols = whole_tokens(count)
         for half in range(2):
-            rows = slice(half * HALF, (half + 1) * HALF)
-            product = dot(rows_ref[rows, :], cols_ref[...], 1, 1)
-            product += dot(rows_far_ref[rows, :], cols_far_ref[...], 1, 1)
-            out_refs[2 * which + half][...] = product.astype(BF16)
+            left = rows[rows_of[kind]][half * HALF : (half + 1) * HALF]
+            product = dot(left, cols, 1, 1).astype(BF16)
+            out_ref = refs[len(refs) - 2 * len(col_counts) + 2 * kind + half]
+            out_ref[:HALF, :] = product[:, :LANE]
+            out_ref[HALF:, :] = product[:, LANE:]
 
 
 def gain_rows(product):
@@ -242,12 +247,13 @@
 
 
 def mid_back_kernel(
-    og_ref, mid_ref, part_ref, back_ref, go_ref, gg_ref, no_ref, ng_ref, fo_ref, fg_ref,
+    og_ref, mid_ref, part_ref, bka_ref, bkb_ref, go_ref, gg_ref, no_ref, ng_ref, fo_ref, fg_ref,
     gmid_ref, gb_ref, near_ref, far_ref, ggain_ref,
 ):
     own, got = mid_ref[:HALF, :], mid_ref[HALF:, :]
     level = level_of(own, got)
-    gnm = part_ref[...] + back_ref[...].astype(F32)
+    back = jnp.concatenate([bka_ref[...], bkb_ref[...]], axis=1)
+    gnm = part_ref[...] + back.astype(F32)
     scaled_own, scaled_got = gnm[:HALF] * go_ref[...], gnm[HALF:] * gg_ref[...]
     inner = jnp.sum(scaled_own * own, axis=0, keepdims=True)
     inner += jnp.sum(scaled_got * got, axis=0, keepdims=True)
@@ -415,38 +421,44 @@
     )
 
 
-def feed_forward(nm, og, weights, dtype, after=()):
+def feed_forward(nms, og, at, weights, dtype, after=()):
     hidden = weights[0].shape[1]
+    tokens = sum(nm.shape[1] for nm in nms)
     chunk = 256
     cols = pl.BlockSpec((HALF, chunk), lambda i: (0, i))
-    rows = pl.BlockSpec((chunk, LOCAL), lambda i: (i, 0))
-    act = shape((hidden, LOCAL))
+    rows = pl.BlockSpec((chunk, tokens), lambda i: (i, 0))
+    act = shape((hidden, tokens))
     return run(
-        mlp_kernel,
-        (nm, og) + weights,
-        (shape((D, LOCAL), dtype), shape((D, LOCAL), dtype), act, act, act),
-        12 * LOCAL * D * hidden,
+        functools.partial(mlp_kernel, len(nms)),
+        tuple(nms) + (og,) + weights,
+        (shape((D, tokens), dtype), shape((D, tokens), dtype), act, act, act),
+        12 * tokens * D * hidden,
         grid=(hidden // chunk,),
-        in_specs=[whole((D, LOCAL))] * 2 + [cols] * 6,
-        out_specs=(whole((D, LOCAL)), whole((D, LOCAL)), rows, rows, rows),
-        scratch=[pltpu.VMEM((D, LOCAL), F32)] * 2,
+        in_specs=[whole(nm.shape) for nm in nms]
+        + [pl.BlockSpec((D, tokens), lambda i: (0, at))]
+        + [cols] * 6,
+        out_specs=(whole((D, tokens)), whole((D, tokens)), rows, rows, rows),
+        scratch=[pltpu.VMEM((D, tokens), F32)] * 2,
         after=after,
     )
 
 
-def weight_grads(nm, nm_far, og, og_far, act, act_far, gg, gg_far, gu, gu_far):
-    hidden = act.shape[0]
-    chunk = 256
-    taken = pl.BlockSpec((chunk, LOCAL), lambda i: (i, 0))
-    given = pl.BlockSpec((HALF, chunk), lambda i: (0, i))
+def weight_grads(rows, cols, rows_of, after=()):
+    hidden = cols[0][0].shape[0]
+    chunk = 2 * LANE
+    all_rows, all_cols = sum(rows, ()), sum(cols, ())
     return run(
-        grads_kernel,
-        (nm, nm_far, og, og_far, act, act_far, gg, gg_far, gu, gu_far),
-        (shape((HALF, hidden)),) * 6,
-        12 * LOCAL * D * hidden,
+        functools.partial(
+            grads_kernel, [len(pieces) for pieces in rows], [len(pieces) for pieces in cols], rows_of
+        ),
+        all_rows + all_cols,
+        (shape((hidden // LANE * HALF, LANE)),) * (2 * len(cols)),
+        4 * LOCAL * D * hidden * len(cols),
         grid=(hidden // chunk,),
-        in_specs=[whole((D, LOCAL))] * 4 + [taken] * 6,
-        out_specs=(given,) * 6,
+        in_specs=[whole(part.shape) for part in all_rows]
+        + [pl.BlockSpec((chunk, part.shape[1]), lambda i: (i, 0)) for part in all_cols],
+        out_specs=(pl.BlockSpec((2 * HALF, LANE), lambda i: (i, 0)),) * (2 * len(cols)),
+        after=after,
     )
 
 
@@ -475,35 +487,24 @@
 
 def split_rows(array, count):
     rows, cols = array.shape
-    return array.reshape(*[size for _, size in stages(count)], rows // count, cols)
+    sizes = [size for _, size in stages(count)]
+    return array.reshape(*sizes[::-1], rows // count, cols)
 
 
 def reduce_stage(total, count, stage, held=()):
     stride, size = stages(count)[stage]
     digit = lax.axis_index("dp") // stride % size
-    kept = lax.dynamic_index_in_dim(total, digit, 0, keepdims=False).astype(F32)
+    axis = total.ndim - 3
+    kept = lax.dynamic_index_in_dim(total, digit, axis, keepdims=False).astype(F32)
     found = []
     for step in range(1, size):
-        sent = lax.dynamic_index_in_dim(total, (digit + step) % size, 0, keepdims=False)
+        sent = lax.dynamic_index_in_dim(total, (digit + step) % size, axis, keepdims=False)
         found.append(lax.ppermute(sent, "dp", shift_pairs(count, stride, size, step)))
     for got in hold_all(found, held):
         kept = kept + got.astype(F32)
     return kept.astype(BF16)
 
 
-def gather_stage(part, count, stage, held=()):
-    stride, size = stages(count)[stage]
-    digit = lax.axis_index("dp") // stride % size
-    found = [
-        lax.ppermute(part, "dp", shift_pairs(count, stride, size, step)) for step in range(1, size)
-    ]
-    spread = jnp.zeros((size,) + part.shape, BF16)
-    spread = lax.dynamic_update_index_in_dim(spread, part, digit, 0)
-    for step, got in enumerate(hold_all(found, held), 1):
-        spread = lax.dynamic_update_index_in_dim(spread, got, (digit - step) % size, 0)
-    return spread
-
-
 def reduce_first(array, count, held=()):
     return reduce_stage(split_rows(array, count), count, 0, held)
 
@@ -514,14 +515,8 @@
     return total
 
 
-def gather_rest(total, count, held=()):
-    for stage in reversed(range(1, len(stages(count)))):
-        total = gather_stage(total, count, stage, held)
-    return total
-
-
-def gather_first(total, count, dims, held=()):
-    return gather_stage(total, count, 0, held).reshape(dims).astype(F32)
+def spread(part):
+    return lax.all_gather(part, "dp", axis=0, tiled=True)
 
 
 def hold_all(arrays, others):
@@ -623,38 +618,42 @@
     og_own, og_other = own_tokens(out_grad.T)
     og = jnp.concatenate([og_own, swap(og_other, "col")], axis=0)
     og_far = swap(og, "row")
-    mid, nm = run(
+    mid, nm_a, nm_b = run(
         mid_kernel,
         (
             att_near, att_far, wo_near, wo_near_got, wo_far, wo_far_got, x_own, x_got,
             gmid_own, gmid_got,
         ),
-        (shape((D, LOCAL), F32), shape((D, LOCAL))),
+        (shape((D, LOCAL), F32), shape((D, BLOCK)), shape((D, BLOCK))),
         2 * LOCAL * D * D,
-        after=(og_far,),
     )
 
     mlp_weights = ()
     for weight in (gate_weight, up_weight, down_weight.T):
         mlp_weights += (weight, swap(weight, "col"))
-    nm_far = swap(nm, "row")
-    out_part, gnm_part, act, gg, gu = feed_forward(nm, og, mlp_weights, F32)
-    out_send, gnm_send, act_far, gg_far, gu_far = feed_forward(
-        nm_far, og_far, mlp_weights, BF16, after=(act,)
-    )
-    gnm_back = swap(gnm_send, "row")
+    far_a, far_b = swap(nm_a, "row"), swap(nm_b, "row")
+    out_part, gnm_part, act, gg, gu = feed_forward(
+        (nm_a, nm_b), og, 0, mlp_weights, F32, after=(og_far,)
+    )
+    out_a, gnm_a, act_a, gg_a, gu_a = feed_forward(
+        (far_a,), og_far, 0, mlp_weights, BF16, after=(act,)
+    )
+    out_b, gnm_b, act_b, gg_b, gu_b = feed_forward(
+        (far_b,), og_far, 1, mlp_weights, BF16, after=(act_a,)
+    )
+    back_a, back_b = hold(swap(gnm_a, "row"), act_b), swap(gnm_b, "row")
     down_keep, down_send, gate_keep, gate_send, up_keep, up_send = weight_grads(
-        nm, nm_far, og, og_far, act, act_far, gg, gg_far, gu, gu_far
-    )
-    down_sum = add(down_keep, swap(down_send, "col"))
-    gate_sum = add(gate_keep, swap(gate_send, "col"))
-    up_sum = add(up_keep, swap(up_send, "col"))
-    down_grad = lax.psum(down_sum, "dp")
+        ((og, og_far), (nm_a, nm_b, far_a, far_b)),
+        ((act, act_a, act_b), (gg, gg_a, gg_b), (gu, gu_a, gu_b)),
+        (0, 1, 1),
+        after=(back_a,),
+    )
+    down_send, gate_send, up_send = hold_all((down_send, gate_send, up_send), (back_b,))
 
     gmid, gb, gatt_near, gatt_far, ggain_mid = run(
         mid_back_kernel,
         (
-            og, mid, gnm_part, gnm_back, gmid_own, gmid_got, wo_near, wo_near_got, wo_far,
+            og, mid, gnm_part, back_a, back_b, gmid_own, gmid_got, wo_near, wo_near_got, wo_far,
             wo_far_got,
         ),
         (
@@ -664,12 +663,16 @@
         2 * LOCAL * D * D,
         after=(up_keep,),
     )
+    down_sum = add(down_keep, hold(swap(down_send, "col"), ggain_mid))
+    gate_sum = add(gate_keep, hold(swap(gate_send, "col"), ggain_mid))
+    up_sum = add(up_keep, hold(swap(up_send, "col"), ggain_mid))
 
     dq_far, own_far, other_far = attend_back(
         where_far, begin, q_far, kv_far, kv_far_got, gatt_far, lse_far, after=(down_sum, gate_sum, up_sum)
     )
-    out_back = hold(swap(hold(out_send, gnm_back), "row"), dq_far)
-    block = (mid + out_part + out_back.astype(F32)).astype(BF16)
+    outs = [hold(swap(hold(out, back_b), "row"), dq_far) for out in (out_a, out_b)]
+    block = (mid + out_part + jnp.concatenate(outs, axis=1).astype(F32)).astype(BF16)
+    down_x = reduce_first(down_sum, count, (dq_far,))
 
     def out_grads(att):
         send = dot(att, gb[HALF:], 1, 1).astype(BF16)
@@ -684,7 +687,7 @@
         (dq_far, own_far, got_far, cosine, sine, w_far, w_far_got, nm_in),
         (shape((D, LOCAL), F32), joined, joined),
         4 * LOCAL * D * D,
-        after=(wo_far_sum, wo_near_sum, block),
+        after=(wo_far_sum, wo_near_sum, block, down_x),
         scratch=[pltpu.VMEM((D, LOCAL), BF16)],
     )
     dq_near, own_near, other_near = attend_back(
@@ -692,7 +695,8 @@
     )
     far_sum = add(far_keep, hold(swap(far_send, "col"), dq_near))
     wo_sum = add(wo_near_sum, hold(swap(wo_far_sum, "row"), dq_near))
-    down_grad = hold(down_grad, dq_near)
+    gate_x = reduce_first(gate_sum, count, (dq_near,))
+    down_z = reduce_rest(down_x, count, (dq_near,))
     got_near = swap(other_near, "col")
     near_keep, near_send, grad = run(
         joined_near_kernel,
@@ -702,7 +706,7 @@
         ),
         (joined, joined, shape((D, LOCAL))),
         4 * LOCAL * D * D,
-        after=(wo_sum, far_sum, down_grad),
+        after=(wo_sum, far_sum, down_z, gate_x),
         scratch=[pltpu.VMEM((D, LOCAL), BF16)],
     )
     last_sum = add(near_keep, swap(near_send, "col"), swap(far_sum, "row"))
@@ -713,11 +717,20 @@
     block_out = feature_cols(block)
     input_grad = feature_cols(grad)
 
-    gate_grad = lax.psum(hold(gate_sum, down_grad), "dp")
     last_sum = jnp.concatenate([last_sum, wo_sum], axis=0)
-    last_z = reduce_rest(reduce_first(last_sum, count), count, (gate_grad,))
-    up_grad = lax.psum(hold(up_sum, gate_grad), "dp")
-    last = gather_first(gather_rest(last_z, count), count, last_sum.shape)
+
+    def widened(part):
+        parts = spread(part).reshape(-1, HALF, LANE)
+        return parts.transpose(1, 0, 2).reshape(HALF, -1).astype(F32)
+
+    up_x = reduce_first(up_sum, count, (grad,))
+    gate_z = reduce_rest(gate_x, count, (grad,))
+    up_z = reduce_rest(up_x, count, (grad,))
+    last_z = reduce_rest(reduce_first(last_sum, count), count)
+    down_grad = widened(down_z)
+    gate_grad = widened(gate_z)
+    up_grad = widened(up_z)
+    last = spread(last_z).astype(F32)
     gain_grads = jnp.stack([last[D], last[D + 16]])
     gain_grads = gain_grads + swap(gain_grads, "row")
     return (
@@ -727,9 +740,9 @@
         last[QUERY : QUERY + KEY].T[:, None, :],
         last[QUERY + KEY : D].T[:, None, :],
         last[ROWS:][None],
-        gate_grad.astype(F32),
-        up_grad.astype(F32),
-        down_grad.astype(F32).T,
+        gate_grad,
+        up_grad,
+        down_grad.T,
         gain_grads[0],
         gain_grads[1],
     )

time: 507 us -> 421 us (0.83)
  waiting for transfers between devices: 261 us -> 124 us
  starting transfers between devices: 31 us -> 61.2 us
  local copies, waits for them, and re-layouts: 30 us -> 39.4 us
  Pallas kernels: 125 us -> 133 us
    psum x3 -> x0, waiting for transfers between devices: 181 us -> none  [the longest x1 67.5 us: per_device(): up_grad = lax.psum(hold(up_sum, gate_grad), 'dp')]
    ppermute x4 -> x16, waiting for transfers between devices: 18.4 us -> 59.3 us  [reduce_stage(): lax.ppermute(sent, 'dp', shift_pairs(count, stride, size, step))]
    all_gather x0 -> x4, waiting for transfers between devices: none -> 39.7 us  [spread(): return lax.all_gather(part, 'dp', axis=0, tiled=True)]
    ppermute x4 -> x16, starting transfers between devices: 5.9 us -> 41.4 us  [reduce_stage(): lax.ppermute(sent, 'dp', shift_pairs(count, stride, size, step))]
    ppermute x33 -> x36, waiting for transfers between devices: 43.9 us -> 25.3 us  [swap(): return lax.ppermute(array, axis, [(0, 1), (1, 0)])]
    ppermute x4 -> x0, waiting for transfers between devices: 17.3 us -> none  [gather_stage(): lax.ppermute(part, 'dp', shift_pairs(count, stride, size, step))]
    pallas_call x13 -> x14, Pallas kernels: 125 us -> 133 us  [run(): pl.pallas_call(body, grid=grid if grid is not None else (1,), in_specs=li...]
    convert_element_type x1 -> x8, other arithmetic: 1.37 us -> 7.97 us  [reduce_stage(): return kept.astype(BF16)]
  transfers between devices with their start and end apart: 44 -> 56, of which waited for: 14 -> 19; matrix products, arithmetic and copies ran while one was open for 11% -> 16% of each run, Pallas kernels for 22% -> 32%
where the time goes in v5:
time: 421 us; the launch traced here: 417 us
  Pallas kernels  133 us (32%)
  waiting for transfers between devices  124 us (29%)
  starting transfers between devices  61.2 us (15%)
  local copies, waits for them, and re-layouts  39.4 us (9%)
  other arithmetic  33.9 us (8%)
  between operations  14.7 us (3%)
  matrix products  9.73 us (2%)
    pallas_call x14, Pallas kernels, run(): pl.pallas_call(body, grid=grid if grid is not None else (1,), in_specs=li...  133 us
    ppermute x16, waiting for transfers between devices, reduce_stage(): lax.ppermute(sent, 'dp', shift_pairs(count, stride, size, step))  59.3 us
    ppermute x16, starting transfers between devices, reduce_stage(): lax.ppermute(sent, 'dp', shift_pairs(count, stride, size, step))  41.4 us
    all_gather x4, waiting for transfers between devices, spread(): return lax.all_gather(part, 'dp', axis=0, tiled=True)  39.7 us
    ppermute x36, waiting for transfers between devices, swap(): return lax.ppermute(array, axis, [(0, 1), (1, 0)])  25.3 us
    ppermute x36, starting transfers between devices, swap(): return lax.ppermute(array, axis, [(0, 1), (1, 0)])  19.7 us
    unnamed x87, local copies, waits for them, and re-layouts  14.7 us
    dot_general x4, matrix products, dot(): lax.dot_general(left, right, (((left_dim,), (right_dim,)), ((), ())), pre...  9.73 us
  transfers between devices with their start and end apart: 56, of which 19 were waited for; matrix products, arithmetic and copies ran while one was open for 16% of the time, Pallas kernels for 32%

profile of v5, /device:TPU:0, one launch (start us, length us, event | category | flops | bytes accessed | tf_op | source)
XLA Modules:
  0.0 416.6 jit_solution(6150560410935400221)
XLA Ops:
  9.3 2.6 collective-permute-start.5
  18.8 4.5 %shard_map.203 = (bf16[960,512]{1,0:T(8,128)(2,1)}, bf16[576,512]{1,0:T(8,128)(2,1)}, bf16[384,512]{1,0:T(8,128)(2,1)}) custom-call(bf16[480,512]{1,0:T(8,128)(2,1)} %get-tuple-element.215.refs_0_.refs_6_.refs_9_, bf16[480,512]{1,0:T(8,128)(2,1)} %copy-done.15, f32[480,1]{1,0:T(8,128)} %copy.61.refs_2_.refs_11_, f32[480,1]{1,0:T(8,128)} %copy.62.refs_3_.refs_12_, ...), custom_call_target="tpu_custom_call" | custom-call | flops 28311552 | bytes 147816 | tf_op jit(solution)/shard_map/pallas_call | solution.py:69
  26.0 11.3 %shard_map.204 = (bf16[576,512]{1,0:T(8,128)(2,1)}, f32[3,8,512]{2,1,0:T(8,128)}) custom-call(s32[2]{0:T(128)} %pad_add_fusion.refs_0_, s32[1,512]{1,0:T(1,128)} %broadcast_select_fusion.8.refs_1_, bf16[576,512]{1,0:T(8,128)(2,1)} %get-tuple-element.89.refs_2_, bf16[384,512]{1,0:T(8,128)(2,1)} %get-tuple-element.90.refs_3_.refs_4_, ...), custom_call_target="tpu_custom_call" | custom-call | flops 180000000 | bytes 84111 | tf_op jit(solution)/shard_map/pallas_call | solution.py:69
  41.8 4.0 shard_map.205
  46.3 7.0 %collective-permute-done.8.refs_7_.refs_4_.refs_9_ = bf16[576,480]{1,0:T(8,128)(2,1)} collective-permute-done((bf16[576,480]{1,0:T(8,128)(2,1)S(1)}, bf16[576,480]{1,0:T(8,128)(2,1)}, u32[]{:S(2)}, u32[]{:S(2)}) %collective-permute-start.8) | collective-permute-done | bytes 552992 | tf_op jit(solution)/shard_map/ppermute | solution.py:466
  56.8 8.5 %shard_map.206 = (bf16[576,512]{1,0:T(8,128)(2,1)}, f32[3,8,512]{2,1,0:T(8,128)}) custom-call(s32[2]{0:T(128)} %pad_add_fusion.1.refs_0_, s32[1,512]{1,0:T(1,128)} %broadcast_select_fusion.8.refs_1_, bf16[576,512]{1,0:T(8,128)(2,1)} %get-tuple-element.95.refs_2_, bf16[384,512]{1,0:T(8,128)(2,1)} %get-tuple-element.96.refs_3_.refs_4_, ...), custom_call_target="tpu_custom_call" | custom-call | flops 180000000 | bytes 84111 | tf_op jit(solution)/shard_map/pallas_call | solution.py:69
  65.3 5.7 %shard_map.207 = (f32[960,512]{1,0:T(8,128)}, bf16[960,256]{1,0:T(8,128)(2,1)}, bf16[960,256]{1,0:T(8,128)(2,1)}) custom-call(bf16[576,512]{1,0:T(8,128)(2,1)} %get-tuple-element.91.refs_0_, bf16[576,512]{1,0:T(8,128)(2,1)} %get-tuple-element.97.refs_1_, bf16[576,480]{1,0:T(8,128)(2,1)} %bitcast.157, bf16[576,480]{1,0:T(8,128)(2,1)} %copy-done.20, ...), custom_call_target="tpu_custom_call" | custom-call | flops 28311552 | bytes 219824 | tf_op jit(solution)/shard_map/pallas_call | solution.py:69
  71.1 4.8 %collective-permute-start.16 = (bf16[960,256]{1,0:T(8,128)(2,1)}, bf16[960,256]{1,0:T(8,128)(2,1)S(1)}, u32[]{:S(2)}, u32[]{:S(2)}) collective-permute-start(bf16[960,256]{1,0:T(8,128)(2,1)} %get-tuple-element.99.refs_0_.refs_2_), channel_id=1, source_target_pairs={{0,2},{2,0},{1,3},{3,1},{4,6},{6,4},{5,7},{7,5},{8,10},{10,8},{9,1... | collective-permute-start | bytes 1474568 | tf_op jit(solution)/shard_map/ppermute | solution.py:466
  75.9 2.8 collective-permute-done.15.refs_9_.refs_1_
  79.7 15.8 %shard_map.208 = (f32[960,512]{1,0:T(8,128)}, f32[960,512]{1,0:T(8,128)}, bf16[1280,512]{1,0:T(8,128)(2,1)}, bf16[1280,512]{1,0:T(8,128)(2,1)}, bf16[1280,512]{1,0:T(8,128)(2,1)}) custom-call(bf16[960,256]{1,0:T(8,128)(2,1)} %get-tuple-element.99.refs_0_.refs_2_, bf16[960,256]{1,0:T(8,128)(2,1)} %get-tuple-element.100.refs_1_.refs_3_, ...), custom_call_target="tpu_custom_call" | custom-call | flops 226492416 | bytes 516096 | tf_op jit(solution)/shard_map/pallas_call | solution.py:69
  96.4 11.0 %shard_map.209 = (bf16[960,256]{1,0:T(8,128)(2,1)}, bf16[960,256]{1,0:T(8,128)(2,1)}, bf16[1280,256]{1,0:T(8,128)(2,1)}, bf16[1280,256]{1,0:T(8,128)(2,1)}, bf16[1280,256]{1,0:T(8,128)(2,1)}) custom-call(bf16[960,256]{1,0:T(8,128)(2,1)} %copy-done.24, bf16[960,512]{1,0:T(8,128)(2,1)} %copy-done.1, bf16[480,1280]{1,0:T(8,128)(2,1)} %refs_2_.3, ...), custom_call_target="tpu_custom_call" | custom-call | flops 113246208 | bytes 353894 | tf_op jit(solution)/shard_map/pallas_call | solution.py:69
  108.2 11.0 %shard_map.210 = (bf16[960,256]{1,0:T(8,128)(2,1)}, bf16[960,256]{1,0:T(8,128)(2,1)}, bf16[1280,256]{1,0:T(8,128)(2,1)}, bf16[1280,256]{1,0:T(8,128)(2,1)}, bf16[1280,256]{1,0:T(8,128)(2,1)}) custom-call(bf16[960,256]{1,0:T(8,128)(2,1)} %copy-done.25, bf16[960,512]{1,0:T(8,128)(2,1)} %copy-done.1, bf16[480,1280]{1,0:T(8,128)(2,1)} %refs_2_.3, ...), custom_call_target="tpu_custom_call" | custom-call | flops 113246208 | bytes 353894 | tf_op jit(solution)/shard_map/pallas_call | solution.py:69
  122.0 12.6 %shard_map.211 = (bf16[4800,128]{1,0:T(8,128)(2,1)}, bf16[4800,128]{1,0:T(8,128)(2,1)}, bf16[4800,128]{1,0:T(8,128)(2,1)}, bf16[4800,128]{1,0:T(8,128)(2,1)}, bf...) custom-call(bf16[960,512]{1,0:T(8,128)(2,1)} %copy-done, bf16[960,512]{1,0:T(8,128)(2,1)} %copy-done.1, ...), custom_call_target="tpu_custom_call" | custom-call | flops 226492416 | bytes 575078 | tf_op jit(solution)/shard_map/pallas_call | solution.py:69
  137.3 8.2 %shard_map.212 = (f32[960,512]{1,0:T(8,128)}, bf16[960,512]{1,0:T(8,128)(2,1)}, bf16[576,512]{1,0:T(8,128)(2,1)}, bf16[576,512]{1,0:T(8,128)(2,1)}, f32[2,16,480]{2,1,0:T(8,128)}) custom-call(bf16[960,512]{1,0:T(8,128)(2,1)} %copy-done, f32[960,512]{1,0:T(8,128)} %get-tuple-element.98.refs_1_, f32[960,512]{1,0:T(8,128)} %get-tuple-element.107.refs_2_, ...), custom_call_target="tpu_custom_call" | custom-call | flops 28311552 | bytes 369123 | tf_op jit(solution)/shard_map/pallas_call | solution.py:69
  153.1 2.6 add_convert_fusion.2.refs_9_
  155.7 10.2 %shard_map.213 = (f32[576,512]{1,0:T(8,128)}, f32[2,3,64,512]{3,2,1,0:T(8,128)}, bf16[2,3,64,512]{3,2,1,0:T(8,128)(2,1)}) custom-call(s32[2]{0:T(128)} %pad_add_fusion.1.refs_0_, s32[1,512]{1,0:T(1,128)} %broadcast_select_fusion.8.refs_1_, bf16[576,512]{1,0:T(8,128)(2,1)} %get-tuple-element.95.refs_2_, bf16[384,512]{1,0:T(8,128)(2,1)} %get-tuple-element.96.refs_3_.refs_4_, ...), custom_call_target="tpu_custom_call" | custom-call | flops 420000000 | bytes 154890 | tf_op jit(solution)/shard_map/pallas_call | solution.py:69
  170.2 2.7 add_convert_fusion.5.refs_10_
  172.9 9.6 %collective-permute-done.29 = bf16[4,600,128]{2,1,0:T(8,128)(2,1)S(1)} collective-permute-done((bf16[4,600,128]{2,1,0:T(8,128)(2,1)S(1)}, bf16[4,600,128]{2,1,0:T(8,128)(2,1)S(1)}, u32[]{:S(2)}, u32[]{:S(2)}) %collective-permute-start.29) | collective-permute-done | bytes 614432 | tf_op jit(solution)/shard_map/ppermute | solution.py:502
  191.4 6.7 %shard_map.214 = (f32[960,512]{1,0:T(8,128)}, bf16[1024,480]{1,0:T(8,128)(2,1)}, bf16[1024,480]{1,0:T(8,128)(2,1)}) custom-call(f32[576,512]{1,0:T(8,128)} %get-tuple-element.132.refs_0_, f32[2,3,64,512]{3,2,1,0:T(8,128)} %get-tuple-element.138.refs_1_, bf16[2,3,64,512]{3,2,1,0:T(8,128)(2,1)} %copy-done.37, ...), custom_call_target="tpu_custom_call" | custom-call | flops 56623104 | bytes 277463 | tf_op jit(solution)/shard_map/pallas_call | solution.py:69
  198.1 13.7 %shard_map.215 = (f32[576,512]{1,0:T(8,128)}, f32[2,3,64,512]{3,2,1,0:T(8,128)}, bf16[2,3,64,512]{3,2,1,0:T(8,128)(2,1)}) custom-call(s32[2]{0:T(128)} %pad_add_fusion.refs_0_, s32[1,512]{1,0:T(1,128)} %broadcast_select_fusion.8.refs_1_, bf16[576,512]{1,0:T(8,128)(2,1)} %get-tuple-element.89.refs_2_, bf16[384,512]{1,0:T(8,128)(2,1)} %get-tuple-element.90.refs_3_.refs_4_, ...), custom_call_target="tpu_custom_call" | custom-call | flops 420000000 | bytes 154890 | tf_op jit(solution)/shard_map/pallas_call | solution.py:69
  217.2 12.2 %collective-permute-done.31 = bf16[576,480]{1,0:T(8,128)(2,1)} collective-permute-done((bf16[576,480]{1,0:T(8,128)(2,1)}, bf16[576,480]{1,0:T(8,128)(2,1)}, u32[]{:S(2)}, u32[]{:S(2)}) %collective-permute-start.31) | collective-permute-done | bytes 552992 | tf_op jit(solution)/shard_map/ppermute | solution.py:466
  235.5 2.8 collective-permute-start.46
  242.0 10.0 %shard_map.216 = (bf16[1024,480]{1,0:T(8,128)(2,1)}, bf16[1024,480]{1,0:T(8,128)(2,1)}, bf16[960,512]{1,0:T(8,128)(2,1)}) custom-call(f32[576,512]{1,0:T(8,128)} %get-tuple-element.145.refs_0_, f32[2,3,64,512]{3,2,1,0:T(8,128)} %get-tuple-element.146.refs_1_, bf16[2,3,64,512]{3,2,1,0:T(8,128)(2,1)} %copy-done.36, ...), custom_call_target="tpu_custom_call" | custom-call | flops 56623104 | bytes 397386 | tf_op jit(solution)/shard_map/pallas_call | solution.py:69
  261.0 8.0 %collective-permute-done.47 = bf16[4,600,128]{2,1,0:T(8,128)(2,1)} collective-permute-done((bf16[4,600,128]{2,1,0:T(8,128)(2,1)}, bf16[4,600,128]{2,1,0:T(8,128)(2,1)}, u32[]{:S(2)}, u32[]{:S(2)}) %collective-permute-start.47) | collective-permute-done | bytes 614432 | tf_op jit(solution)/shard_map/ppermute | solution.py:502
  270.3 11.2 %collective-permute-start.48 = (bf16[600,128]{1,0:T(8,128)(2,1)S(1)}, bf16[600,128]{1,0:T(8,128)(2,1)S(1)}, u32[]{:S(2)}, u32[]{:S(2)}) collective-permute-start(bf16[600,128]{1,0:T(8,128)(2,1)S(1)} %get-tuple-element.225), channel_id=1, source_target_pairs={{0,8},{4,12},{8,16},{12,20},{16,24},{20,28},{24,0},{28,4},{1,9},{5... | collective-permute-start | bytes 460808 | tf_op jit(solution)/shard_map/ppermute | solution.py:502
  286.1 8.8 %collective-permute-done.49 = bf16[600,128]{1,0:T(8,128)(2,1)S(1)} collective-permute-done((bf16[600,128]{1,0:T(8,128)(2,1)S(1)}, bf16[600,128]{1,0:T(8,128)(2,1)S(1)}, u32[]{:S(2)}, u32[]{:S(2)}) %collective-permute-start.49) | collective-permute-done | bytes 153632 | tf_op jit(solution)/shard_map/ppermute | solution.py:502
  303.5 11.3 %collective-permute-done.40 = bf16[4,200,480]{2,1,0:T(8,128)(2,1)S(1)} collective-permute-done((bf16[4,200,480]{2,1,0:T(8,128)(2,1)S(1)}, bf16[4,200,480]{2,1,0:T(8,128)(2,1)S(1)}, u32[]{:S(2)}, u32[]{:S(2)}) %collective-permute-start.40) | collective-permute-done | bytes 768032 | tf_op jit(solution)/shard_map/ppermute | solution.py:502
  315.2 10.0 %collective-permute-start.43 = (bf16[200,480]{1,0:T(8,128)(2,1)S(1)}, bf16[200,480]{1,0:T(8,128)(2,1)S(1)}, u32[]{:S(2)}, u32[]{:S(2)}) collective-permute-start(bf16[200,480]{1,0:T(8,128)(2,1)S(1)} %get-tuple-element.221), channel_id=1, source_target_pairs={{0,24},{4,28},{8,0},{12,4},{16,8},{20,12},{24,16},{28,20},{1,25},{... | collective-permute-start | bytes 576008 | tf_op jit(solution)/shard_map/ppermute | solution.py:502
  327.3 6.5 %collective-permute-done.43 = bf16[200,480]{1,0:T(8,128)(2,1)S(1)} collective-permute-done((bf16[200,480]{1,0:T(8,128)(2,1)S(1)}, bf16[200,480]{1,0:T(8,128)(2,1)S(1)}, u32[]{:S(2)}, u32[]{:S(2)}) %collective-permute-start.43) | collective-permute-done | bytes 192032 | tf_op jit(solution)/shard_map/ppermute | solution.py:502
  333.8 8.3 %collective-permute-done.42 = bf16[200,480]{1,0:T(8,128)(2,1)S(1)} collective-permute-done((bf16[200,480]{1,0:T(8,128)(2,1)S(1)}, bf16[200,480]{1,0:T(8,128)(2,1)S(1)}, u32[]{:S(2)}, u32[]{:S(2)}) %collective-permute-start.42) | collective-permute-done | bytes 192032 | tf_op jit(solution)/shard_map/ppermute | solution.py:502
  355.3 2.9 convert_bitcast_fusion
  362.4 38.9 %all-gather.5.cloned.1.call-done = bf16[1600,480]{1,0:T(8,128)(2,1)} async-done(((bf16[200,480]{1,0:T(8,128)(2,1)}), bf16[1600,480]{1,0:T(8,128)(2,1)}) %all-gather.5.cloned.1.call-update) | async-done | bytes 1536016 | tf_op jit(solution)/shard_map/all_gather | solution.py:519
  (274 shorter events, 115.6 us)
Async XLA Ops:
  7.2 340.1 %all-gather.11.cloned.1.call-start = ((), (), s32[]{:S(2)}) async-start(), calls=%async_computation.3 | async-start | bytes 1382400 | tf_op jit(solution)/shard_map/all_gather | solution.py:519
  9.3 28.0 %collective-permute-start.5 = (bf16[960,480]{1,0:T(8,128)(2,1)S(1)}, bf16[960,480]{1,0:T(8,128)(2,1)}, u32[]{:S(2)}, u32[]{:S(2)}) collective-permute-start(bf16[960,480]{1,0:T(8,128)(2,1)S(1)} %pad_maximum_fusion.1.refs_6_.refs_5_), channel_id=1, source_target_pairs={{0,2},{2,0},{1,3},{3,1},{4,6},{6,4},{5,7},{7,5},{8,10},{10,8},{9,1... | collective-permute-start | bytes 2764808 | tf_op jit(solution)/shard_map/ppermute | solution.py:466
  37.4 15.8 %collective-permute-start.8 = (bf16[576,480]{1,0:T(8,128)(2,1)S(1)}, bf16[576,480]{1,0:T(8,128)(2,1)}, u32[]{:S(2)}, u32[]{:S(2)}) collective-permute-start(bf16[576,480]{1,0:T(8,128)(2,1)S(1)} %bitcast.159), channel_id=1, source_target_pairs={{0,2},{2,0},{1,3},{3,1},{4,6},{6,4},{5,7},{7,5},{8,10},{10,8},{9,1... | collective-permute-start | bytes 1658888 | tf_op jit(solution)/shard_map/ppermute | solution.py:466
  40.3 35.6 %collective-permute-start.12 = (bf16[480,1280]{1,0:T(8,128)(2,1)S(1)}, bf16[480,1280]{1,0:T(8,128)(2,1)}, u32[]{:S(2)}, u32[]{:S(2)}) collective-permute-start(bf16[480,1280]{1,0:T(8,128)(2,1)S(1)} %copy-done.5), channel_id=1, source_target_pairs={{0,1},{1,0},{2,3},{3,2},{4,5},{5,4},{6,7},{7,6},{8,9},{9,8},{10,11... | collective-permute-start | bytes 3686408 | tf_op jit(solution)/shard_map/ppermute | solution.py:466
  46.0 30.0 %collective-permute-start.13 = (bf16[480,1280]{1,0:T(8,128)(2,1)}, bf16[480,1280]{1,0:T(8,128)(2,1)}, u32[]{:S(2)}, u32[]{:S(2)}) collective-permute-start(bf16[480,1280]{1,0:T(8,128)(2,1)} %refs_4_.3), channel_id=1, source_target_pairs={{0,1},{1,0},{2,3},{3,2},{4,5},{5,4},{6,7},{7,6},{8,9},{9,8},{10,11... | collective-permute-start | bytes 3686408 | tf_op jit(solution)/shard_map/ppermute | solution.py:466
  53.2 22.7 %collective-permute-start.14 = (bf16[480,1280]{1,0:T(8,128)(2,1)}, bf16[480,1280]{1,0:T(8,128)(2,1)}, u32[]{:S(2)}, u32[]{:S(2)}) collective-permute-start(bf16[480,1280]{1,0:T(8,128)(2,1)} %bitcast.23.refs_7_.refs_6_), channel_id=1, source_target_pairs={{0,1},{1,0},{2,3},{3,2},{4,5},{5,4},{6,7},{7,6},{8,9},{9,8},{10,11... | collective-permute-start | bytes 3686408 | tf_op jit(solution)/shard_map/ppermute | solution.py:466
  54.2 24.6 %collective-permute-start.15 = (bf16[960,512]{1,0:T(8,128)(2,1)S(1)}, bf16[960,512]{1,0:T(8,128)(2,1)S(1)}, u32[]{:S(2)}, u32[]{:S(2)}) collective-permute-start(bf16[960,512]{1,0:T(8,128)(2,1)S(1)} %pad_maximum_fusion.2.refs_2_.refs_0_), channel_id=1, source_target_pairs={{0,2},{2,0},{1,3},{3,1},{4,6},{6,4},{5,7},{7,5},{8,10},{10,8},{9,1... | collective-permute-start | bytes 2949128 | tf_op jit(solution)/shard_map/ppermute | solution.py:466
  71.1 24.5 %collective-permute-start.16 = (bf16[960,256]{1,0:T(8,128)(2,1)}, bf16[960,256]{1,0:T(8,128)(2,1)S(1)}, u32[]{:S(2)}, u32[]{:S(2)}) collective-permute-start(bf16[960,256]{1,0:T(8,128)(2,1)} %get-tuple-element.99.refs_0_.refs_2_), channel_id=1, source_target_pairs={{0,2},{2,0},{1,3},{3,1},{4,6},{6,4},{5,7},{7,5},{8,10},{10,8},{9,1... | collective-permute-start | bytes 1474568 | tf_op jit(solution)/shard_map/ppermute | solution.py:466
  75.8 31.6 %collective-permute-start.17 = (bf16[960,256]{1,0:T(8,128)(2,1)}, bf16[960,256]{1,0:T(8,128)(2,1)S(1)}, u32[]{:S(2)}, u32[]{:S(2)}) collective-permute-start(bf16[960,256]{1,0:T(8,128)(2,1)} %get-tuple-element.100.refs_1_.refs_3_), channel_id=1, source_target_pairs={{0,2},{2,0},{1,3},{3,1},{4,6},{6,4},{5,7},{7,5},{8,10},{10,8},{9,1... | collective-permute-start | bytes 1474568 | tf_op jit(solution)/shard_map/ppermute | solution.py:466
  134.6 15.8 %collective-permute-start.21 = (bf16[4800,128]{1,0:T(8,128)(2,1)}, bf16[4800,128]{1,0:T(8,128)(2,1)}, u32[]{:S(2)}, u32[]{:S(2)}) collective-permute-start(bf16[4800,128]{1,0:T(8,128)(2,1)} %get-tuple-element.124), channel_id=1, source_target_pairs={{0,1},{1,0},{2,3},{3,2},{4,5},{5,4},{6,7},{7,6},{8,9},{9,8},{10,11... | collective-permute-start | bytes 3686408 | tf_op jit(solution)/shard_map/ppermute | solution.py:466
  135.2 15.8 %collective-permute-start.22 = (bf16[4800,128]{1,0:T(8,128)(2,1)}, bf16[4800,128]{1,0:T(8,128)(2,1)S(1)}, u32[]{:S(2)}, u32[]{:S(2)}) collective-permute-start(bf16[4800,128]{1,0:T(8,128)(2,1)} %get-tuple-element.128), channel_id=1, source_target_pairs={{0,1},{1,0},{2,3},{3,2},{4,5},{5,4},{6,7},{7,6},{8,9},{9,8},{10,11... | collective-permute-start | bytes 3686408 | tf_op jit(solution)/shard_map/ppermute | solution.py:466
  135.3 30.7 %collective-permute-start.24 = (bf16[960,256]{1,0:T(8,128)(2,1)}, bf16[960,256]{1,0:T(8,128)(2,1)S(1)}, u32[]{:S(2)}, u32[]{:S(2)}) collective-permute-start(bf16[960,256]{1,0:T(8,128)(2,1)} %get-tuple-element.135), channel_id=1, source_target_pairs={{0,2},{2,0},{1,3},{3,1},{4,6},{6,4},{5,7},{7,5},{8,10},{10,8},{9,1... | collective-permute-start | bytes 1474568 | tf_op jit(solution)/shard_map/ppermute | solution.py:466
  135.4 30.6 %collective-permute-start.19 = (bf16[960,256]{1,0:T(8,128)(2,1)}, bf16[960,256]{1,0:T(8,128)(2,1)}, u32[]{:S(2)}, u32[]{:S(2)}) collective-permute-start(bf16[960,256]{1,0:T(8,128)(2,1)} %get-tuple-element.106), channel_id=1, source_target_pairs={{0,2},{2,0},{1,3},{3,1},{4,6},{6,4},{5,7},{7,5},{8,10},{10,8},{9,1... | collective-permute-start | bytes 1474568 | tf_op jit(solution)/shard_map/ppermute | solution.py:466
  166.0 24.7 %collective-permute-start.26 = (bf16[2,3,64,512]{3,2,1,0:T(8,128)(2,1)}, bf16[2,3,64,512]{3,2,1,0:T(8,128)(2,1)S(1)}, u32[]{:S(2)}, u32[]{:S(2)}) collective-permute-start(bf16[2,3,64,512]{3,2,1,0:T(8,128)(2,1)} %get-tuple-element.139), channel_id=1, source_target_pairs={{0,1},{1,0},{2,3},{3,2},{4,5},{5,4},{6,7},{7,6},{8,9},{9,8},{10,11... | collective-permute-start | bytes 1179656 | tf_op jit(solution)/shard_map/ppermute | solution.py:466
  166.2 16.3 %collective-permute-start.29 = (bf16[4,600,128]{2,1,0:T(8,128)(2,1)S(1)}, bf16[4,600,128]{2,1,0:T(8,128)(2,1)S(1)}, u32[]{:S(2)}, u32[]{:S(2)}) collective-permute-start(bf16[4,600,128]{2,1,0:T(8,128)(2,1)S(1)} %dynamic-slice_bitcast_fusion.3), channel_id=1, source_target_pairs={{0,4},{4,0},{8,12},{12,8},{16,20},{20,16},{24,28},{28,24},{1,5},{5... | collective-permute-start | bytes 1843208 | tf_op jit(solution)/shard_map/ppermute | solution.py:502
  182.7 29.1 %collective-permute-start.33 = (bf16[600,128]{1,0:T(8,128)(2,1)S(1)}, bf16[600,128]{1,0:T(8,128)(2,1)S(1)}, u32[]{:S(2)}, u32[]{:S(2)}) collective-permute-start(bf16[600,128]{1,0:T(8,128)(2,1)S(1)} %get-tuple-element.231), channel_id=1, source_target_pairs={{0,8},{4,12},{8,16},{12,20},{16,24},{20,28},{24,0},{28,4},{1,9},{5... | collective-permute-start | bytes 460808 | tf_op jit(solution)/shard_map/ppermute | solution.py:502
  184.3 27.5 %collective-permute-start.34 = (bf16[600,128]{1,0:T(8,128)(2,1)S(1)}, bf16[600,128]{1,0:T(8,128)(2,1)S(1)}, u32[]{:S(2)}, u32[]{:S(2)}) collective-permute-start(bf16[600,128]{1,0:T(8,128)(2,1)S(1)} %get-tuple-element.230), channel_id=1, source_target_pairs={{0,16},{4,20},{8,24},{12,28},{16,0},{20,4},{24,8},{28,12},{1,17},{... | collective-permute-start | bytes 460808 | tf_op jit(solution)/shard_map/ppermute | solution.py:502
  186.9 24.9 %collective-permute-start.35 = (bf16[600,128]{1,0:T(8,128)(2,1)S(1)}, bf16[600,128]{1,0:T(8,128)(2,1)S(1)}, u32[]{:S(2)}, u32[]{:S(2)}) collective-permute-start(bf16[600,128]{1,0:T(8,128)(2,1)S(1)} %get-tuple-element.229), channel_id=1, source_target_pairs={{0,24},{4,28},{8,0},{12,4},{16,8},{20,12},{24,16},{28,20},{1,25},{... | collective-permute-start | bytes 460808 | tf_op jit(solution)/shard_map/ppermute | solution.py:502
  213.6 137.3 %all-gather.7.cloned.1.call-start = ((), (), s32[]{:S(2)}) async-start(), calls=%async_computation.1 | async-start | bytes 1382400 | tf_op jit(solution)/shard_map/all_gather | solution.py:519
  213.7 16.4 %collective-permute-start.36 = (bf16[4,600,128]{2,1,0:T(8,128)(2,1)S(1)}, bf16[4,600,128]{2,1,0:T(8,128)(2,1)}, u32[]{:S(2)}, u32[]{:S(2)}) collective-permute-start(bf16[4,600,128]{2,1,0:T(8,128)(2,1)S(1)} %dynamic-slice_bitcast_fusion.2), channel_id=1, source_target_pairs={{0,4},{4,0},{8,12},{12,8},{16,20},{20,16},{24,28},{28,24},{1,5},{5... | collective-permute-start | bytes 1843208 | tf_op jit(solution)/shard_map/ppermute | solution.py:502
  216.6 21.6 %collective-permute-start.32 = (bf16[1024,480]{0,1:T(8,128)(2,1)}, bf16[1024,480]{0,1:T(8,128)(2,1)}, u32[]{:S(2)}, u32[]{:S(2)}) collective-permute-start(bf16[1024,480]{0,1:T(8,128)(2,1)} %copy.68), channel_id=1, source_target_pairs={{0,1},{1,0},{2,3},{3,2},{4,5},{5,4},{6,7},{7,6},{8,9},{9,8},{10,11... | collective-permute-start | bytes 2949128 | tf_op jit(solution)/shard_map/ppermute | solution.py:466
  216.7 24.6 %collective-permute-start.30 = (bf16[2,3,64,512]{3,2,1,0:T(8,128)(2,1)}, bf16[2,3,64,512]{3,2,1,0:T(8,128)(2,1)S(1)}, u32[]{:S(2)}, u32[]{:S(2)}) collective-permute-start(bf16[2,3,64,512]{3,2,1,0:T(8,128)(2,1)} %get-tuple-element.147), channel_id=1, source_target_pairs={{0,1},{1,0},{2,3},{3,2},{4,5},{5,4},{6,7},{7,6},{8,9},{9,8},{10,11... | collective-permute-start | bytes 1179656 | tf_op jit(solution)/shard_map/ppermute | solution.py:466
  234.4 17.6 %collective-permute-start.44 = (bf16[600,128]{1,0:T(8,128)(2,1)}, bf16[600,128]{1,0:T(8,128)(2,1)S(1)}, u32[]{:S(2)}, u32[]{:S(2)}) collective-permute-start(bf16[600,128]{1,0:T(8,128)(2,1)} %get-tuple-element.228), channel_id=1, source_target_pairs={{0,8},{4,12},{8,16},{12,20},{16,24},{20,28},{24,0},{28,4},{1,9},{5... | collective-permute-start | bytes 460808 | tf_op jit(solution)/shard_map/ppermute | solution.py:502
  235.1 19.0 %collective-permute-start.45 = (bf16[600,128]{1,0:T(8,128)(2,1)}, bf16[600,128]{1,0:T(8,128)(2,1)}, u32[]{:S(2)}, u32[]{:S(2)}) collective-permute-start(bf16[600,128]{1,0:T(8,128)(2,1)} %get-tuple-element.227), channel_id=1, source_target_pairs={{0,16},{4,20},{8,24},{12,28},{16,0},{20,4},{24,8},{28,12},{1,17},{... | collective-permute-start | bytes 460808 | tf_op jit(solution)/shard_map/ppermute | solution.py:502
  235.5 18.6 %collective-permute-start.46 = (bf16[600,128]{1,0:T(8,128)(2,1)}, bf16[600,128]{1,0:T(8,128)(2,1)}, u32[]{:S(2)}, u32[]{:S(2)}) collective-permute-start(bf16[600,128]{1,0:T(8,128)(2,1)} %get-tuple-element.226), channel_id=1, source_target_pairs={{0,24},{4,28},{8,0},{12,4},{16,8},{20,12},{24,16},{28,20},{1,25},{... | collective-permute-start | bytes 460808 | tf_op jit(solution)/shard_map/ppermute | solution.py:502
  255.9 99.4 %all-gather.9.cloned.1.call-start = ((), (), s32[]{:S(2)}) async-start(), calls=%async_computation.2 | async-start | bytes 1382400 | tf_op jit(solution)/shard_map/all_gather | solution.py:519
  259.7 37.8 %collective-permute-start.39 = (bf16[1024,480]{0,1:T(8,128)(2,1)}, bf16[1024,480]{0,1:T(8,128)(2,1)}, u32[]{:S(2)}, u32[]{:S(2)}) collective-permute-start(bf16[1024,480]{0,1:T(8,128)(2,1)} %copy.75), channel_id=1, source_target_pairs={{0,2},{2,0},{1,3},{3,1},{4,6},{6,4},{5,7},{7,5},{8,10},{10,8},{9,1... | collective-permute-start | bytes 2949128 | tf_op jit(solution)/shard_map/ppermute | solution.py:466
  261.0 38.1 %collective-permute-start.38 = (bf16[1024,480]{0,1:T(8,128)(2,1)}, bf16[1024,480]{0,1:T(8,128)(2,1)}, u32[]{:S(2)}, u32[]{:S(2)}) collective-permute-start(bf16[1024,480]{0,1:T(8,128)(2,1)} %copy.73), channel_id=1, source_target_pairs={{0,1},{1,0},{2,3},{3,2},{4,5},{5,4},{6,7},{7,6},{8,9},{9,8},{10,11... | collective-permute-start | bytes 2949128 | tf_op jit(solution)/shard_map/ppermute | solution.py:466
  270.3 15.8 %collective-permute-start.48 = (bf16[600,128]{1,0:T(8,128)(2,1)S(1)}, bf16[600,128]{1,0:T(8,128)(2,1)S(1)}, u32[]{:S(2)}, u32[]{:S(2)}) collective-permute-start(bf16[600,128]{1,0:T(8,128)(2,1)S(1)} %get-tuple-element.225), channel_id=1, source_target_pairs={{0,8},{4,12},{8,16},{12,20},{16,24},{20,28},{24,0},{28,4},{1,9},{5... | collective-permute-start | bytes 460808 | tf_op jit(solution)/shard_map/ppermute | solution.py:502
  297.5 103.8 %all-gather.5.cloned.1.call-start = ((), (), s32[]{:S(2)}) async-start(), calls=%async_computation | async-start | bytes 1843200 | tf_op jit(solution)/shard_map/all_gather | solution.py:519
  315.2 18.6 %collective-permute-start.43 = (bf16[200,480]{1,0:T(8,128)(2,1)S(1)}, bf16[200,480]{1,0:T(8,128)(2,1)S(1)}, u32[]{:S(2)}, u32[]{:S(2)}) collective-permute-start(bf16[200,480]{1,0:T(8,128)(2,1)S(1)} %get-tuple-element.221), channel_id=1, source_target_pairs={{0,24},{4,28},{8,0},{12,4},{16,8},{20,12},{24,16},{28,20},{1,25},{... | collective-permute-start | bytes 576008 | tf_op jit(solution)/shard_map/ppermute | solution.py:502
  325.2 16.9 %collective-permute-start.42 = (bf16[200,480]{1,0:T(8,128)(2,1)S(1)}, bf16[200,480]{1,0:T(8,128)(2,1)S(1)}, u32[]{:S(2)}, u32[]{:S(2)}) collective-permute-start(bf16[200,480]{1,0:T(8,128)(2,1)S(1)} %get-tuple-element.222), channel_id=1, source_target_pairs={{0,16},{4,20},{8,24},{12,28},{16,0},{20,4},{24,8},{28,12},{1,17},{... | collective-permute-start | bytes 576008 | tf_op jit(solution)/shard_map/ppermute | solution.py:502
  (66 other events, 509.7 us)
Sparse Core Ops, SparseCore 0:
  213.7 45.2 all-gather.10
  261.2 42.4 all-gather.6
  306.5 48.7 all-gather.8
  357.9 43.3 all-gather.4

commit v6 on v5

--- a/solution.py
+++ b/solution.py
@@ -169,7 +169,7 @@
 
 def mid_kernel(
     near_ref, far_ref, no_ref, ng_ref, fo_ref, fg_ref, xo_ref, xg_ref, go_ref, gg_ref,
-    mid_ref, nma_ref, nmb_ref,
+    mid_ref, nm_ref,
 ):
     near, far = near_ref[...], far_ref[...]
     own = xo_ref[...].astype(F32) + dot(no_ref[...], near, 0, 0) + dot(fo_ref[...], far, 0, 0)
@@ -177,18 +177,16 @@
     mid_ref[:HALF, :] = own
     mid_ref[HALF:, :] = got
     level = level_of(own, got)
-    for rows, part, gain_ref in ((slice(0, HALF), own, go_ref), (slice(HALF, D), got, gg_ref)):
-        normed = (part * level * gain_ref[...]).astype(BF16)
-        nma_ref[rows, :] = normed[:, :BLOCK]
-        nmb_ref[rows, :] = normed[:, BLOCK:]
-
-
-def mlp_kernel(pieces, *refs):
-    nm_refs = refs[:pieces]
-    og_ref, wgo_ref, wgg_ref, wuo_ref, wug_ref, wdo_ref, wdg_ref = refs[pieces : pieces + 7]
-    out_ref, gnm_ref, act_ref, gg_ref, gu_ref, out_sum, gnm_sum = refs[pieces + 7 :]
+    nm_ref[:HALF, :] = (own * level * go_ref[...]).astype(BF16)
+    nm_ref[HALF:, :] = (got * level * gg_ref[...]).astype(BF16)
+
+
+def mlp_kernel(
+    nm_ref, og_ref, wgo_ref, wgg_ref, wuo_ref, wug_ref, wdo_ref, wdg_ref,
+    out_ref, gnm_ref, act_ref, gg_ref, gu_ref, out_sum, gnm_sum,
+):
     step = pl.program_id(0)
-    nm, og = jnp.concatenate([ref[...] for ref in nm_refs], axis=1), og_ref[...]
+    nm, og = nm_ref[...], og_ref[...]
 
     def inward(own_ref, got_ref, rows):
         return dot(own_ref[...], rows[:HALF], 0, 0) + dot(got_ref[...], rows[HALF:], 0, 0)
@@ -247,13 +245,12 @@
 
 
 def mid_back_kernel(
-    og_ref, mid_ref, part_ref, bka_ref, bkb_ref, go_ref, gg_ref, no_ref, ng_ref, fo_ref, fg_ref,
+    og_ref, mid_ref, part_ref, back_ref, go_ref, gg_ref, no_ref, ng_ref, fo_ref, fg_ref,
     gmid_ref, gb_ref, near_ref, far_ref, ggain_ref,
 ):
     own, got = mid_ref[:HALF, :], mid_ref[HALF:, :]
     level = level_of(own, got)
-    back = jnp.concatenate([bka_ref[...], bkb_ref[...]], axis=1)
-    gnm = part_ref[...] + back.astype(F32)
+    gnm = part_ref[...] + back_ref[...].astype(F32)
     scaled_own, scaled_got = gnm[:HALF] * go_ref[...], gnm[HALF:] * gg_ref[...]
     inner = jnp.sum(scaled_own * own, axis=0, keepdims=True)
     inner += jnp.sum(scaled_got * got, axis=0, keepdims=True)
@@ -421,24 +418,21 @@
     )
 
 
-def feed_forward(nms, og, at, weights, dtype, after=()):
+def feed_forward(nm, og, weights, dtype, after=()):
     hidden = weights[0].shape[1]
-    tokens = sum(nm.shape[1] for nm in nms)
     chunk = 256
     cols = pl.BlockSpec((HALF, chunk), lambda i: (0, i))
-    rows = pl.BlockSpec((chunk, tokens), lambda i: (i, 0))
-    act = shape((hidden, tokens))
+    rows = pl.BlockSpec((chunk, LOCAL), lambda i: (i, 0))
+    act = shape((hidden, LOCAL))
     return run(
-        functools.partial(mlp_kernel, len(nms)),
-        tuple(nms) + (og,) + weights,
-        (shape((D, tokens), dtype), shape((D, tokens), dtype), act, act, act),
-        12 * tokens * D * hidden,
+        mlp_kernel,
+        (nm, og) + weights,
+        (shape((D, LOCAL), dtype), shape((D, LOCAL), dtype), act, act, act),
+        12 * LOCAL * D * hidden,
         grid=(hidden // chunk,),
-        in_specs=[whole(nm.shape) for nm in nms]
-        + [pl.BlockSpec((D, tokens), lambda i: (0, at))]
-        + [cols] * 6,
-        out_specs=(whole((D, tokens)), whole((D, tokens)), rows, rows, rows),
-        scratch=[pltpu.VMEM((D, tokens), F32)] * 2,
+        in_specs=[whole((D, LOCAL))] * 2 + [cols] * 6,
+        out_specs=(whole((D, LOCAL)), whole((D, LOCAL)), rows, rows, rows),
+        scratch=[pltpu.VMEM((D, LOCAL), F32)] * 2,
         after=after,
     )
 
@@ -513,6 +507,37 @@
     for stage in range(1, len(stages(count))):
         total = reduce_stage(total, count, stage, held)
     return total
+
+
+def gather_stage(part, count, stage, held=()):
+    stride, size = stages(count)[stage]
+    digit = lax.axis_index("dp") // stride % size
+    axis = part.ndim - 2
+    found = [
+        lax.ppermute(part, "dp", shift_pairs(count, stride, size, step)) for step in range(1, size)
+    ]
+    if size == 2:
+        got = hold_all(found, held)[0]
+        return jnp.stack(
+            [jnp.where(digit == 0, part, got), jnp.where(digit == 0, got, part)], axis=axis
+        )
+    dims = part.shape[:axis] + (size,) + part.shape[axis:]
+    whole_parts = lax.dynamic_update_index_in_dim(jnp.zeros(dims, BF16), part, digit, axis)
+    for step, got in enumerate(hold_all(found, held), 1):
+        whole_parts = lax.dynamic_update_index_in_dim(
+            whole_parts, got, (digit - step) % size, axis
+        )
+    return whole_parts
+
+
+def gather_rest(part, count, held=()):
+    for stage in reversed(range(1, len(stages(count)))):
+        part = gather_stage(part, count, stage, held)
+    return part
+
+
+def gather_first(part, count, held=()):
+    return gather_stage(part, count, 0, held)
 
 
 def spread(part):
@@ -618,42 +643,34 @@
     og_own, og_other = own_tokens(out_grad.T)
     og = jnp.concatenate([og_own, swap(og_other, "col")], axis=0)
     og_far = swap(og, "row")
-    mid, nm_a, nm_b = run(
+    mid, nm = run(
         mid_kernel,
         (
             att_near, att_far, wo_near, wo_near_got, wo_far, wo_far_got, x_own, x_got,
             gmid_own, gmid_got,
         ),
-        (shape((D, LOCAL), F32), shape((D, BLOCK)), shape((D, BLOCK))),
+        (shape((D, LOCAL), F32), shape((D, LOCAL))),
         2 * LOCAL * D * D,
     )
 
     mlp_weights = ()
     for weight in (gate_weight, up_weight, down_weight.T):
         mlp_weights += (weight, swap(weight, "col"))
-    far_a, far_b = swap(nm_a, "row"), swap(nm_b, "row")
-    out_part, gnm_part, act, gg, gu = feed_forward(
-        (nm_a, nm_b), og, 0, mlp_weights, F32, after=(og_far,)
-    )
-    out_a, gnm_a, act_a, gg_a, gu_a = feed_forward(
-        (far_a,), og_far, 0, mlp_weights, BF16, after=(act,)
-    )
-    out_b, gnm_b, act_b, gg_b, gu_b = feed_forward(
-        (far_b,), og_far, 1, mlp_weights, BF16, after=(act_a,)
-    )
-    back_a, back_b = hold(swap(gnm_a, "row"), act_b), swap(gnm_b, "row")
+    nm_far = swap(nm, "row")
+    out_part, gnm_part, act, gg, gu = feed_forward(nm, og, mlp_weights, F32, after=(og_far,))
+    out_send, gnm_send, act_far, gg_far, gu_far = feed_forward(
+        nm_far, og_far, mlp_weights, BF16, after=(act,)
+    )
+    gnm_back = swap(gnm_send, "row")
     down_keep, down_send, gate_keep, gate_send, up_keep, up_send = weight_grads(
-        ((og, og_far), (nm_a, nm_b, far_a, far_b)),
-        ((act, act_a, act_b), (gg, gg_a, gg_b), (gu, gu_a, gu_b)),
-        (0, 1, 1),
-        after=(back_a,),
-    )
-    down_send, gate_send, up_send = hold_all((down_send, gate_send, up_send), (back_b,))
+        ((og, og_far), (nm, nm_far)), ((act, act_far), (gg, gg_far), (gu, gu_far)), (0, 1, 1)
+    )
+    down_send, gate_send, up_send = hold_all((down_send, gate_send, up_send), (gnm_back,))
 
     gmid, gb, gatt_near, gatt_far, ggain_mid = run(
         mid_back_kernel,
         (
-            og, mid, gnm_part, back_a, back_b, gmid_own, gmid_got, wo_near, wo_near_got, wo_far,
+            og, mid, gnm_part, gnm_back, gmid_own, gmid_got, wo_near, wo_near_got, wo_far,
             wo_far_got,
         ),
         (
@@ -670,8 +687,8 @@
     dq_far, own_far, other_far = attend_back(
         where_far, begin, q_far, kv_far, kv_far_got, gatt_far, lse_far, after=(down_sum, gate_sum, up_sum)
     )
-    outs = [hold(swap(hold(out, back_b), "row"), dq_far) for out in (out_a, out_b)]
-    block = (mid + out_part + jnp.concatenate(outs, axis=1).astype(F32)).astype(BF16)
+    out_back = hold(swap(hold(out_send, gnm_back), "row"), dq_far)
+    block = (mid + out_part + out_back.astype(F32)).astype(BF16)
     down_x = reduce_first(down_sum, count, (dq_far,))
 
     def out_grads(att):
@@ -680,7 +697,7 @@
 
     wo_far_sum = out_grads(att_far)
     wo_near_sum = out_grads(att_near)
-    got_far = swap(other_far, "col")
+    got_far = swap(hold(other_far, down_x), "col")
     joined = shape((ROWS, HALF))
     gnm_in_part, far_keep, far_send = run(
         joined_far_kernel,
@@ -690,14 +707,15 @@
         after=(wo_far_sum, wo_near_sum, block, down_x),
         scratch=[pltpu.VMEM((D, LOCAL), BF16)],
     )
+    gate_x = reduce_first(gate_sum, count, (far_keep,))
     dq_near, own_near, other_near = attend_back(
-        where_near, begin, q_near, kv_near, kv_near_got, gatt_near, lse_near, after=(far_keep,)
+        where_near, begin, q_near, kv_near, kv_near_got, gatt_near, lse_near, after=(gate_x,)
     )
     far_sum = add(far_keep, hold(swap(far_send, "col"), dq_near))
     wo_sum = add(wo_near_sum, hold(swap(wo_far_sum, "row"), dq_near))
-    gate_x = reduce_first(gate_sum, count, (dq_near,))
     down_z = reduce_rest(down_x, count, (dq_near,))
-    got_near = swap(other_near, "col")
+    up_x = reduce_first(hold(up_sum, gate_x), count, (dq_near,))
+    got_near = swap(hold(other_near, up_x, down_z, far_sum, wo_sum), "col")
     near_keep, near_send, grad = run(
         joined_near_kernel,
         (
@@ -706,9 +724,11 @@
         ),
         (joined, joined, shape((D, LOCAL))),
         4 * LOCAL * D * D,
-        after=(wo_sum, far_sum, down_z, gate_x),
+        after=(wo_sum, far_sum, down_z, up_x),
         scratch=[pltpu.VMEM((D, LOCAL), BF16)],
     )
+    gate_z = reduce_rest(gate_x, count, (grad,))
+    near_send = hold(near_send, gate_z)
     last_sum = add(near_keep, swap(near_send, "col"), swap(far_sum, "row"))
 
     def feature_cols(array):
@@ -717,20 +737,23 @@
     block_out = feature_cols(block)
     input_grad = feature_cols(grad)
 
-    last_sum = jnp.concatenate([last_sum, wo_sum], axis=0)
-
-    def widened(part):
-        parts = spread(part).reshape(-1, HALF, LANE)
+
+    def widened(whole_sum):
+        parts = whole_sum.reshape(-1, HALF, LANE)
         return parts.transpose(1, 0, 2).reshape(HALF, -1).astype(F32)
 
-    up_x = reduce_first(up_sum, count, (grad,))
-    gate_z = reduce_rest(gate_x, count, (grad,))
     up_z = reduce_rest(up_x, count, (grad,))
-    last_z = reduce_rest(reduce_first(last_sum, count), count)
-    down_grad = widened(down_z)
-    gate_grad = widened(gate_z)
-    up_grad = widened(up_z)
-    last = spread(last_z).astype(F32)
+    down_grad = widened(spread(down_z))
+    gate_grad = widened(spread(gate_z))
+    up_rest = gather_rest(up_z, count, (last_sum,))
+    out_x = reduce_first(wo_sum, count, (grad,))
+    last_x = reduce_first(last_sum, count)
+    up_grad = widened(gather_first(up_rest, count).reshape(up_sum.shape))
+    last_z = reduce_rest(jnp.concatenate([last_x, out_x], axis=-2), count)
+    last = gather_first(gather_rest(last_z, count), count)
+    last, out_weight_grad = last[..., : ROWS // count, :], last[..., ROWS // count :, :]
+    last = last.reshape(last_sum.shape).astype(F32)
+    out_weight_grad = out_weight_grad.reshape(wo_sum.shape).astype(F32)
     gain_grads = jnp.stack([last[D], last[D + 16]])
     gain_grads = gain_grads + swap(gain_grads, "row")
     return (
@@ -739,7 +762,7 @@
         last[:QUERY].T[:, None, :],
         last[QUERY : QUERY + KEY].T[:, None, :],
         last[QUERY + KEY : D].T[:, None, :],
-        last[ROWS:][None],
+        out_weight_grad[None],
         gate_grad,
         up_grad,
         down_grad.T,

time: 421 us -> 411 us (0.976)
  waiting for transfers between devices: 124 us -> 113 us
  Pallas kernels: 133 us -> 126 us
  other arithmetic: 33.9 us -> 39.6 us
    all_gather x4 -> x2, waiting for transfers between devices: 39.7 us -> 0.01 us  [spread(): return lax.all_gather(part, 'dp', axis=0, tiled=True)]
    ppermute x16 -> x17, starting transfers between devices: 41.4 us -> 24 us  [reduce_stage(): lax.ppermute(sent, 'dp', shift_pairs(count, stride, size, step))]
    ppermute x0 -> x8, starting transfers between devices: none -> 15.3 us  [gather_stage(): lax.ppermute(part, 'dp', shift_pairs(count, stride, size, step))]
    ppermute x0 -> x8, waiting for transfers between devices: none -> 13.6 us  [gather_stage(): lax.ppermute(part, 'dp', shift_pairs(count, stride, size, step))]
    ppermute x36 -> x33, waiting for transfers between devices: 25.3 us -> 34.5 us  [swap(): return lax.ppermute(array, axis, [(0, 1), (1, 0)])]
    pallas_call x14 -> x13, Pallas kernels: 133 us -> 126 us  [run(): pl.pallas_call(body, grid=grid if grid is not None else (1,), in_specs=li...]
    ppermute x16 -> x17, waiting for transfers between devices: 59.3 us -> 64.7 us  [reduce_stage(): lax.ppermute(sent, 'dp', shift_pairs(count, stride, size, step))]
    unnamed x87 -> x91, local copies, waits for them, and re-layouts: 14.7 us -> 12.3 us
  transfers between devices with their start and end apart: 56 -> 60, of which waited for: 19 -> 17; matrix products, arithmetic and copies ran while one was open for 16% -> 20% of each run, Pallas kernels for 32% -> 27%
where the time goes in v6:
time: 411 us; the launch traced here: 405 us
  Pallas kernels  126 us (31%)
  waiting for transfers between devices  113 us (27%)
  starting transfers between devices  59.7 us (15%)
  local copies, waits for them, and re-layouts  42 us (10%)
  other arithmetic  39.6 us (10%)
  between operations  15.2 us (4%)
  matrix products  9.86 us (2%)
    pallas_call x13, Pallas kernels, run(): pl.pallas_call(body, grid=grid if grid is not None else (1,), in_specs=li...  126 us
    ppermute x17, waiting for transfers between devices, reduce_stage(): lax.ppermute(sent, 'dp', shift_pairs(count, stride, size, step))  64.7 us
    ppermute x33, waiting for transfers between devices, swap(): return lax.ppermute(array, axis, [(0, 1), (1, 0)])  34.5 us
    ppermute x17, starting transfers between devices, reduce_stage(): lax.ppermute(sent, 'dp', shift_pairs(count, stride, size, step))  24 us
    ppermute x33, starting transfers between devices, swap(): return lax.ppermute(array, axis, [(0, 1), (1, 0)])  20.4 us
    ppermute x8, starting transfers between devices, gather_stage(): lax.ppermute(part, 'dp', shift_pairs(count, stride, size, step))  15.3 us
    ppermute x8, waiting for transfers between devices, gather_stage(): lax.ppermute(part, 'dp', shift_pairs(count, stride, size, step))  13.6 us
    unnamed x91, local copies, waits for them, and re-layouts  12.3 us
  transfers between devices with their start and end apart: 60, of which 17 were waited for; matrix products, arithmetic and copies ran while one was open for 20% of the time, Pallas kernels for 27%

profile of v6, /device:TPU:0, one launch (start us, length us, event | category | flops | bytes accessed | tf_op | source)
XLA Modules:
  0.0 405.2 jit_solution(13459465166891134243)
XLA Ops:
  20.8 4.5 %shard_map.203 = (bf16[960,512]{1,0:T(8,128)(2,1)}, bf16[576,512]{1,0:T(8,128)(2,1)}, bf16[384,512]{1,0:T(8,128)(2,1)}) custom-call(bf16[480,512]{1,0:T(8,128)(2,1)} %get-tuple-element.206.refs_0_.refs_6_.refs_9_, bf16[480,512]{1,0:T(8,128)(2,1)} %copy-done.17, f32[480,1]{1,0:T(8,128)} %copy.47.refs_2_.refs_11_, f32[480,1]{1,0:T(8,128)} %copy.48.refs_3_.refs_12_, ...), custom_call_target="tpu_custom_call" | custom-call | flops 28311552 | bytes 147816 | tf_op jit(solution)/shard_map/pallas_call | solution.py:69
  28.0 11.3 %shard_map.204 = (bf16[576,512]{1,0:T(8,128)(2,1)}, f32[3,8,512]{2,1,0:T(8,128)}) custom-call(s32[2]{0:T(128)} %pad_add_fusion.refs_0_, s32[1,512]{1,0:T(1,128)} %broadcast_select_fusion.8.refs_1_, bf16[576,512]{1,0:T(8,128)(2,1)} %get-tuple-element.88.refs_2_, bf16[384,512]{1,0:T(8,128)(2,1)} %get-tuple-element.89.refs_3_.refs_4_, ...), custom_call_target="tpu_custom_call" | custom-call | flops 180000000 | bytes 84111 | tf_op jit(solution)/shard_map/pallas_call | solution.py:69
  41.2 13.9 %collective-permute-done.8.refs_7_.refs_4_.refs_8_ = bf16[576,480]{1,0:T(8,128)(2,1)S(1)} collective-permute-done((bf16[576,480]{1,0:T(8,128)(2,1)S(1)}, bf16[576,480]{1,0:T(8,128)(2,1)S(1)}, u32[]{:S(2)}, u32[]{:S(2)}) %collective-permute-start.8) | collective-permute-done | bytes 552992 | tf_op jit(solution)/shard_map/ppermute | solution.py:460
  56.2 4.1 %shard_map.205 = (bf16[576,512]{1,0:T(8,128)(2,1)}, bf16[384,512]{1,0:T(8,128)(2,1)}) custom-call(bf16[960,512]{1,0:T(8,128)(2,1)} %get-tuple-element.91.refs_0_.refs_7_, f32[32,512]{1,0:T(8,128)} %get-tuple-element.240.refs_4_.refs_1_.refs_3_, f32[32,512]{1,0:T(8,128)} %get-tuple-element.239.refs_5_.refs_2_.refs_4_, bf16[960,480]{1,0:T(8,128)(2,1)} %copy-done.19, ...), custom_call_target="tpu_custom_call" | custom-call | flops 28311552 | bytes 118210 | tf_op jit(solution)/shard_map/pallas_call | solution.py:69
  65.1 8.6 %shard_map.206 = (bf16[576,512]{1,0:T(8,128)(2,1)}, f32[3,8,512]{2,1,0:T(8,128)}) custom-call(s32[2]{0:T(128)} %pad_add_fusion.1.refs_0_, s32[1,512]{1,0:T(1,128)} %broadcast_select_fusion.8.refs_1_, bf16[576,512]{1,0:T(8,128)(2,1)} %get-tuple-element.94.refs_2_, bf16[384,512]{1,0:T(8,128)(2,1)} %get-tuple-element.95.refs_3_.refs_4_, ...), custom_call_target="tpu_custom_call" | custom-call | flops 180000000 | bytes 84111 | tf_op jit(solution)/shard_map/pallas_call | solution.py:69
  73.7 5.7 %shard_map.207 = (f32[960,512]{1,0:T(8,128)}, bf16[960,512]{1,0:T(8,128)(2,1)}) custom-call(bf16[576,512]{1,0:T(8,128)(2,1)} %get-tuple-element.90.refs_0_, bf16[576,512]{1,0:T(8,128)(2,1)} %get-tuple-element.96.refs_1_, bf16[576,480]{1,0:T(8,128)(2,1)} %bitcast.199, bf16[576,480]{1,0:T(8,128)(2,1)} %collective-permute-done.9.refs_3_.refs_7_, ...), custom_call_target="tpu_custom_call" | custom-call | flops 28311552 | bytes 219824 | tf_op jit(solution)/shard_map/pallas_call | solution.py:69
  79.5 4.8 %collective-permute-start.16 = (bf16[960,512]{1,0:T(8,128)(2,1)}, bf16[960,512]{1,0:T(8,128)(2,1)S(1)}, u32[]{:S(2)}, u32[]{:S(2)}) collective-permute-start(bf16[960,512]{1,0:T(8,128)(2,1)} %get-tuple-element.98.refs_0_.refs_2_), channel_id=1, source_target_pairs={{0,2},{2,0},{1,3},{3,1},{4,6},{6,4},{5,7},{7,5},{8,10},{10,8},{9,1... | collective-permute-start | bytes 2949128 | tf_op jit(solution)/shard_map/ppermute | solution.py:460
  84.3 2.8 collective-permute-done.15.refs_8_.refs_1_
  88.0 15.8 %shard_map.208 = (f32[960,512]{1,0:T(8,128)}, f32[960,512]{1,0:T(8,128)}, bf16[1280,512]{1,0:T(8,128)(2,1)}, bf16[1280,512]{1,0:T(8,128)(2,1)}, bf16[1280,512]{1,0:T(8,128)(2,1)}) custom-call(bf16[960,512]{1,0:T(8,128)(2,1)} %get-tuple-element.98.refs_0_.refs_2_, bf16[960,512]{1,0:T(8,128)(2,1)} %copy-done, bf16[480,1280]{1,0:T(8,128)(2,1)} %refs_2_.3, ...), custom_call_target="tpu_custom_call" | custom-call | flops 226492416 | bytes 516096 | tf_op jit(solution)/shard_map/pallas_call | solution.py:69
  103.9 3.8 collective-permute-done.16.refs_0_.refs_3_
  108.6 15.1 %shard_map.209 = (bf16[960,512]{1,0:T(8,128)(2,1)}, bf16[960,512]{1,0:T(8,128)(2,1)}, bf16[1280,512]{1,0:T(8,128)(2,1)}, bf16[1280,512]{1,0:T(8,128)(2,1)}, bf16[1280,512]{1,0:T(8,128)(2,1)}) custom-call(bf16[960,512]{1,0:T(8,128)(2,1)} %copy-done.21, bf16[960,512]{1,0:T(8,128)(2,1)} %copy-done.7, bf16[480,1280]{1,0:T(8,128)(2,1)} %refs_2_.3, ...), custom_call_target="tpu_custom_call" | custom-call | flops 226492416 | bytes 457113 | tf_op jit(solution)/shard_map/pallas_call | solution.py:69
  124.1 12.4 %shard_map.210 = (bf16[4800,128]{1,0:T(8,128)(2,1)}, bf16[4800,128]{1,0:T(8,128)(2,1)}, bf16[4800,128]{1,0:T(8,128)(2,1)}, bf16[4800,128]{1,0:T(8,128)(2,1)}, bf...) custom-call(bf16[960,512]{1,0:T(8,128)(2,1)} %copy-done, bf16[960,512]{1,0:T(8,128)(2,1)} %copy-done.7, ...), custom_call_target="tpu_custom_call" | custom-call | flops 226492416 | bytes 575078 | tf_op jit(solution)/shard_map/pallas_call | solution.py:69
  136.5 10.8 %collective-permute-done.17.refs_3_ = bf16[960,512]{1,0:T(8,128)(2,1)S(1)} collective-permute-done((bf16[960,512]{1,0:T(8,128)(2,1)}, bf16[960,512]{1,0:T(8,128)(2,1)S(1)}, u32[]{:S(2)}, u32[]{:S(2)}) %collective-permute-start.17) | collective-permute-done | bytes 983072 | tf_op jit(solution)/shard_map/ppermute | solution.py:460
  148.3 8.2 %shard_map.211 = (f32[960,512]{1,0:T(8,128)}, bf16[960,512]{1,0:T(8,128)(2,1)}, bf16[576,512]{1,0:T(8,128)(2,1)}, bf16[576,512]{1,0:T(8,128)(2,1)}, f32[2,16,480]{2,1,0:T(8,128)}) custom-call(bf16[960,512]{1,0:T(8,128)(2,1)} %copy-done, f32[960,512]{1,0:T(8,128)} %get-tuple-element.97.refs_1_, f32[960,512]{1,0:T(8,128)} %get-tuple-element.104.refs_2_, ...), custom_call_target="tpu_custom_call" | custom-call | flops 28311552 | bytes 369123 | tf_op jit(solution)/shard_map/pallas_call | solution.py:69
  164.0 2.6 add_convert_fusion.2.refs_9_
  166.6 10.2 %shard_map.212 = (f32[576,512]{1,0:T(8,128)}, f32[2,3,64,512]{3,2,1,0:T(8,128)}, bf16[2,3,64,512]{3,2,1,0:T(8,128)(2,1)}) custom-call(s32[2]{0:T(128)} %pad_add_fusion.1.refs_0_, s32[1,512]{1,0:T(1,128)} %broadcast_select_fusion.8.refs_1_, bf16[576,512]{1,0:T(8,128)(2,1)} %get-tuple-element.94.refs_2_, bf16[384,512]{1,0:T(8,128)(2,1)} %get-tuple-element.95.refs_3_.refs_4_, ...), custom_call_target="tpu_custom_call" | custom-call | flops 420000000 | bytes 154890 | tf_op jit(solution)/shard_map/pallas_call | solution.py:69
  182.2 5.2 %collective-permute-start.33 = (bf16[576,480]{1,0:T(8,128)(2,1)}, bf16[576,480]{1,0:T(8,128)(2,1)}, u32[]{:S(2)}, u32[]{:S(2)}) collective-permute-start(bf16[576,480]{1,0:T(8,128)(2,1)} %fusion.refs_8_), channel_id=1, source_target_pairs={{0,2},{2,0},{1,3},{3,1},{4,6},{6,4},{5,7},{7,5},{8,10},{10,8},{9,1... | collective-permute-start | bytes 1658888 | tf_op jit(solution)/shard_map/ppermute | solution.py:460
  188.9 17.2 %collective-permute-done.24 = bf16[4,600,128]{2,1,0:T(8,128)(2,1)S(1)} collective-permute-done((bf16[4,600,128]{2,1,0:T(8,128)(2,1)S(1)}, bf16[4,600,128]{2,1,0:T(8,128)(2,1)S(1)}, u32[]{:S(2)}, u32[]{:S(2)}) %collective-permute-start.24) | collective-permute-done | bytes 614432 | tf_op jit(solution)/shard_map/ppermute | solution.py:496
  215.2 6.7 %shard_map.213 = (f32[960,512]{1,0:T(8,128)}, bf16[1024,480]{1,0:T(8,128)(2,1)}, bf16[1024,480]{1,0:T(8,128)(2,1)}) custom-call(f32[576,512]{1,0:T(8,128)} %get-tuple-element.125.refs_0_, f32[2,3,64,512]{3,2,1,0:T(8,128)} %get-tuple-element.128.refs_1_, bf16[2,3,64,512]{3,2,1,0:T(8,128)(2,1)} %copy-done.38, ...), custom_call_target="tpu_custom_call" | custom-call | flops 56623104 | bytes 277463 | tf_op jit(solution)/shard_map/pallas_call | solution.py:69
  227.3 13.4 %shard_map.214 = (f32[576,512]{1,0:T(8,128)}, f32[2,3,64,512]{3,2,1,0:T(8,128)}, bf16[2,3,64,512]{3,2,1,0:T(8,128)(2,1)}) custom-call(s32[2]{0:T(128)} %pad_add_fusion.refs_0_, s32[1,512]{1,0:T(1,128)} %broadcast_select_fusion.8.refs_1_, bf16[576,512]{1,0:T(8,128)(2,1)} %get-tuple-element.88.refs_2_, bf16[384,512]{1,0:T(8,128)(2,1)} %get-tuple-element.89.refs_3_.refs_4_, ...), custom_call_target="tpu_custom_call" | custom-call | flops 420000000 | bytes 154890 | tf_op jit(solution)/shard_map/pallas_call | solution.py:69
  253.8 2.7 collective-permute-start.38
  262.4 9.9 %shard_map.215 = (bf16[1024,480]{1,0:T(8,128)(2,1)}, bf16[1024,480]{1,0:T(8,128)(2,1)}, bf16[960,512]{1,0:T(8,128)(2,1)}) custom-call(f32[576,512]{1,0:T(8,128)} %get-tuple-element.137.refs_0_, f32[2,3,64,512]{3,2,1,0:T(8,128)} %get-tuple-element.138.refs_1_, bf16[2,3,64,512]{3,2,1,0:T(8,128)(2,1)} %copy-done.37, ...), custom_call_target="tpu_custom_call" | custom-call | flops 56623104 | bytes 397386 | tf_op jit(solution)/shard_map/pallas_call | solution.py:69
  278.8 2.7 collective-permute-start.52
  281.6 6.8 %collective-permute-done.50 = bf16[600,128]{1,0:T(8,128)(2,1)S(1)} collective-permute-done((bf16[600,128]{1,0:T(8,128)(2,1)S(1)}, bf16[600,128]{1,0:T(8,128)(2,1)S(1)}, u32[]{:S(2)}, u32[]{:S(2)}) %collective-permute-start.50) | collective-permute-done | bytes 153632 | tf_op jit(solution)/shard_map/ppermute | solution.py:496
  291.5 5.5 %collective-permute-done.51 = bf16[600,128]{1,0:T(8,128)(2,1)S(1)} collective-permute-done((bf16[600,128]{1,0:T(8,128)(2,1)S(1)}, bf16[600,128]{1,0:T(8,128)(2,1)S(1)}, u32[]{:S(2)}, u32[]{:S(2)}) %collective-permute-start.51) | collective-permute-done | bytes 153632 | tf_op jit(solution)/shard_map/ppermute | solution.py:496
  298.7 3.8 collective-permute-start.53
  310.5 3.5 collective-permute-done.54
  315.6 9.4 %collective-permute-done.41 = bf16[4,128,480]{2,1,0:T(8,128)(2,1)S(1)} collective-permute-done((bf16[4,128,480]{2,1,0:T(8,128)(2,1)S(1)}, bf16[4,128,480]{2,1,0:T(8,128)(2,1)S(1)}, u32[]{:S(2)}, u32[]{:S(2)}) %collective-permute-start.41) | collective-permute-done | bytes 491552 | tf_op jit(solution)/shard_map/ppermute | solution.py:496
  328.7 6.9 %collective-permute-done.45 = bf16[200,480]{1,0:T(8,128)(2,1)S(1)} collective-permute-done((bf16[200,480]{1,0:T(8,128)(2,1)S(1)}, bf16[200,480]{1,0:T(8,128)(2,1)S(1)}, u32[]{:S(2)}, u32[]{:S(2)}) %collective-permute-start.45) | collective-permute-done | bytes 192032 | tf_op jit(solution)/shard_map/ppermute | solution.py:496
  335.6 19.0 %collective-permute-done.44 = bf16[200,480]{1,0:T(8,128)(2,1)S(1)} collective-permute-done((bf16[200,480]{1,0:T(8,128)(2,1)S(1)}, bf16[200,480]{1,0:T(8,128)(2,1)S(1)}, u32[]{:S(2)}, u32[]{:S(2)}) %collective-permute-start.44) | collective-permute-done | bytes 192032 | tf_op jit(solution)/shard_map/ppermute | solution.py:496
  359.7 2.9 collective-permute-start.48
  363.2 8.1 %collective-permute-done.47 = bf16[200,480]{1,0:T(8,128)(2,1)S(1)} collective-permute-done((bf16[200,480]{1,0:T(8,128)(2,1)S(1)}, bf16[200,480]{1,0:T(8,128)(2,1)S(1)}, u32[]{:S(2)}, u32[]{:S(2)}) %collective-permute-start.47) | collective-permute-done | bytes 192032 | tf_op jit(solution)/shard_map/ppermute | solution.py:517
  (298 shorter events, 131.8 us)
Async XLA Ops:
  7.2 366.8 %all-gather.5.cloned.1.call-start = ((), (), s32[]{:S(2)}) async-start(), calls=%async_computation.1 | async-start | bytes 1382400 | tf_op jit(solution)/shard_map/all_gather | solution.py:544
  9.2 30.2 %collective-permute-start.5 = (bf16[960,480]{1,0:T(8,128)(2,1)S(1)}, bf16[960,480]{1,0:T(8,128)(2,1)S(1)}, u32[]{:S(2)}, u32[]{:S(2)}) collective-permute-start(bf16[960,480]{1,0:T(8,128)(2,1)S(1)} %pad_maximum_fusion.1.refs_6_.refs_5_), channel_id=1, source_target_pairs={{0,2},{2,0},{1,3},{3,1},{4,6},{6,4},{5,7},{7,5},{8,10},{10,8},{9,1... | collective-permute-start | bytes 2764808 | tf_op jit(solution)/shard_map/ppermute | solution.py:460
  39.5 21.7 %collective-permute-start.9 = (bf16[576,480]{1,0:T(8,128)(2,1)S(1)}, bf16[576,480]{1,0:T(8,128)(2,1)}, u32[]{:S(2)}, u32[]{:S(2)}) collective-permute-start(bf16[576,480]{1,0:T(8,128)(2,1)S(1)} %bitcast.202), channel_id=1, source_target_pairs={{0,1},{1,0},{2,3},{3,2},{4,5},{5,4},{6,7},{7,6},{8,9},{9,8},{10,11... | collective-permute-start | bytes 1658888 | tf_op jit(solution)/shard_map/ppermute | solution.py:460
  41.1 19.7 %collective-permute-start.11 = (bf16[480,512]{1,0:T(8,128)(2,1)}, bf16[480,512]{1,0:T(8,128)(2,1)}, u32[]{:S(2)}, u32[]{:S(2)}) collective-permute-start(bf16[480,512]{1,0:T(8,128)(2,1)} %get-tuple-element.204), channel_id=1, source_target_pairs={{0,1},{1,0},{2,3},{3,2},{4,5},{5,4},{6,7},{7,6},{8,9},{9,8},{10,11... | collective-permute-start | bytes 1474568 | tf_op jit(solution)/shard_map/ppermute | solution.py:460
  55.2 18.6 %collective-permute-start.10 = (bf16[576,480]{1,0:T(8,128)(2,1)S(1)}, bf16[576,480]{1,0:T(8,128)(2,1)}, u32[]{:S(2)}, u32[]{:S(2)}) collective-permute-start(bf16[576,480]{1,0:T(8,128)(2,1)S(1)} %collective-permute-done.8.refs_7_.refs_4_.refs_8_), channel_id=1, source_target_pairs={{0,1},{1,0},{2,3},{3,2},{4,5},{5,4},{6,7},{7,6},{8,9},{9,8},{10,11... | collective-permute-start | bytes 1658888 | tf_op jit(solution)/shard_map/ppermute | solution.py:460
  60.7 23.5 %collective-permute-start.12 = (bf16[480,1280]{1,0:T(8,128)(2,1)}, bf16[480,1280]{1,0:T(8,128)(2,1)}, u32[]{:S(2)}, u32[]{:S(2)}) collective-permute-start(bf16[480,1280]{1,0:T(8,128)(2,1)} %refs_2_.3), channel_id=1, source_target_pairs={{0,1},{1,0},{2,3},{3,2},{4,5},{5,4},{6,7},{7,6},{8,9},{9,8},{10,11... | collective-permute-start | bytes 3686408 | tf_op jit(solution)/shard_map/ppermute | solution.py:460
  60.8 23.5 %collective-permute-start.13 = (bf16[480,1280]{1,0:T(8,128)(2,1)}, bf16[480,1280]{1,0:T(8,128)(2,1)}, u32[]{:S(2)}, u32[]{:S(2)}) collective-permute-start(bf16[480,1280]{1,0:T(8,128)(2,1)} %refs_4_.3), channel_id=1, source_target_pairs={{0,1},{1,0},{2,3},{3,2},{4,5},{5,4},{6,7},{7,6},{8,9},{9,8},{10,11... | collective-permute-start | bytes 3686408 | tf_op jit(solution)/shard_map/ppermute | solution.py:460
  61.2 23.0 %collective-permute-start.14 = (bf16[480,1280]{1,0:T(8,128)(2,1)}, bf16[480,1280]{1,0:T(8,128)(2,1)}, u32[]{:S(2)}, u32[]{:S(2)}) collective-permute-start(bf16[480,1280]{1,0:T(8,128)(2,1)} %bitcast.23.refs_6_), channel_id=1, source_target_pairs={{0,1},{1,0},{2,3},{3,2},{4,5},{5,4},{6,7},{7,6},{8,9},{9,8},{10,11... | collective-permute-start | bytes 3686408 | tf_op jit(solution)/shard_map/ppermute | solution.py:460
  62.4 24.6 %collective-permute-start.15 = (bf16[960,512]{1,0:T(8,128)(2,1)S(1)}, bf16[960,512]{1,0:T(8,128)(2,1)S(1)}, u32[]{:S(2)}, u32[]{:S(2)}) collective-permute-start(bf16[960,512]{1,0:T(8,128)(2,1)S(1)} %pad_maximum_fusion.2.refs_1_.refs_0_), channel_id=1, source_target_pairs={{0,2},{2,0},{1,3},{3,1},{4,6},{6,4},{5,7},{7,5},{8,10},{10,8},{9,1... | collective-permute-start | bytes 2949128 | tf_op jit(solution)/shard_map/ppermute | solution.py:460
  79.5 28.2 %collective-permute-start.16 = (bf16[960,512]{1,0:T(8,128)(2,1)}, bf16[960,512]{1,0:T(8,128)(2,1)S(1)}, u32[]{:S(2)}, u32[]{:S(2)}) collective-permute-start(bf16[960,512]{1,0:T(8,128)(2,1)} %get-tuple-element.98.refs_0_.refs_2_), channel_id=1, source_target_pairs={{0,2},{2,0},{1,3},{3,1},{4,6},{6,4},{5,7},{7,5},{8,10},{10,8},{9,1... | collective-permute-start | bytes 2949128 | tf_op jit(solution)/shard_map/ppermute | solution.py:460
  123.8 23.6 %collective-permute-start.17 = (bf16[960,512]{1,0:T(8,128)(2,1)}, bf16[960,512]{1,0:T(8,128)(2,1)S(1)}, u32[]{:S(2)}, u32[]{:S(2)}) collective-permute-start(bf16[960,512]{1,0:T(8,128)(2,1)} %get-tuple-element.102), channel_id=1, source_target_pairs={{0,2},{2,0},{1,3},{3,1},{4,6},{6,4},{5,7},{7,5},{8,10},{10,8},{9,1... | collective-permute-start | bytes 2949128 | tf_op jit(solution)/shard_map/ppermute | solution.py:460
  147.9 29.0 %collective-permute-start.18 = (bf16[960,512]{1,0:T(8,128)(2,1)}, bf16[960,512]{1,0:T(8,128)(2,1)S(1)}, u32[]{:S(2)}, u32[]{:S(2)}) collective-permute-start(bf16[960,512]{1,0:T(8,128)(2,1)} %get-tuple-element.103), channel_id=1, source_target_pairs={{0,2},{2,0},{1,3},{3,1},{4,6},{6,4},{5,7},{7,5},{8,10},{10,8},{9,1... | collective-permute-start | bytes 2949128 | tf_op jit(solution)/shard_map/ppermute | solution.py:460
  159.0 20.7 %collective-permute-start.26 = (bf16[576,480]{1,0:T(8,128)(2,1)}, bf16[576,480]{1,0:T(8,128)(2,1)}, u32[]{:S(2)}, u32[]{:S(2)}) collective-permute-start(bf16[576,480]{1,0:T(8,128)(2,1)} %convolution_convert_fusion.1), channel_id=1, source_target_pairs={{0,1},{1,0},{2,3},{3,2},{4,5},{5,4},{6,7},{7,6},{8,9},{9,8},{10,11... | collective-permute-start | bytes 1658888 | tf_op jit(solution)/shard_map/ppermute | solution.py:460
  176.9 45.0 %collective-permute-start.23 = (bf16[4,600,128]{2,1,0:T(8,128)(2,1)S(1)}, bf16[4,600,128]{2,1,0:T(8,128)(2,1)S(1)}, u32[]{:S(2)}, u32[]{:S(2)}) collective-permute-start(bf16[4,600,128]{2,1,0:T(8,128)(2,1)S(1)} %dynamic-slice_bitcast_fusion.2), channel_id=1, source_target_pairs={{0,4},{4,0},{8,12},{12,8},{16,20},{20,16},{24,28},{28,24},{1,5},{5... | collective-permute-start | bytes 1843208 | tf_op jit(solution)/shard_map/ppermute | solution.py:496
  178.5 27.6 %collective-permute-start.24 = (bf16[4,600,128]{2,1,0:T(8,128)(2,1)S(1)}, bf16[4,600,128]{2,1,0:T(8,128)(2,1)S(1)}, u32[]{:S(2)}, u32[]{:S(2)}) collective-permute-start(bf16[4,600,128]{2,1,0:T(8,128)(2,1)S(1)} %dynamic-slice_bitcast_fusion.1), channel_id=1, source_target_pairs={{0,4},{4,0},{8,12},{12,8},{16,20},{20,16},{24,28},{28,24},{1,5},{5... | collective-permute-start | bytes 1843208 | tf_op jit(solution)/shard_map/ppermute | solution.py:496
  182.2 58.9 %collective-permute-start.33 = (bf16[576,480]{1,0:T(8,128)(2,1)}, bf16[576,480]{1,0:T(8,128)(2,1)}, u32[]{:S(2)}, u32[]{:S(2)}) collective-permute-start(bf16[576,480]{1,0:T(8,128)(2,1)} %fusion.refs_8_), channel_id=1, source_target_pairs={{0,2},{2,0},{1,3},{3,1},{4,6},{6,4},{5,7},{7,5},{8,10},{10,8},{9,1... | collective-permute-start | bytes 1658888 | tf_op jit(solution)/shard_map/ppermute | solution.py:460
  211.3 29.4 %collective-permute-start.30 = (bf16[600,128]{1,0:T(8,128)(2,1)}, bf16[600,128]{1,0:T(8,128)(2,1)}, u32[]{:S(2)}, u32[]{:S(2)}) collective-permute-start(bf16[600,128]{1,0:T(8,128)(2,1)} %get-tuple-element.223), channel_id=1, source_target_pairs={{0,16},{4,20},{8,24},{12,28},{16,0},{20,4},{24,8},{28,12},{1,17},{... | collective-permute-start | bytes 460808 | tf_op jit(solution)/shard_map/ppermute | solution.py:496
  213.9 27.1 %collective-permute-start.31 = (bf16[600,128]{1,0:T(8,128)(2,1)}, bf16[600,128]{1,0:T(8,128)(2,1)}, u32[]{:S(2)}, u32[]{:S(2)}) collective-permute-start(bf16[600,128]{1,0:T(8,128)(2,1)} %get-tuple-element.222), channel_id=1, source_target_pairs={{0,24},{4,28},{8,0},{12,4},{16,8},{20,12},{24,16},{28,20},{1,25},{... | collective-permute-start | bytes 460808 | tf_op jit(solution)/shard_map/ppermute | solution.py:496
  224.8 22.3 %collective-permute-start.32 = (bf16[1024,480]{0,1:T(8,128)(2,1)}, bf16[1024,480]{0,1:T(8,128)(2,1)}, u32[]{:S(2)}, u32[]{:S(2)}) collective-permute-start(bf16[1024,480]{0,1:T(8,128)(2,1)} %copy.56), channel_id=1, source_target_pairs={{0,1},{1,0},{2,3},{3,2},{4,5},{5,4},{6,7},{7,6},{8,9},{9,8},{10,11... | collective-permute-start | bytes 2949128 | tf_op jit(solution)/shard_map/ppermute | solution.py:460
  224.9 20.1 %collective-permute-start.28 = (bf16[4,600,128]{2,1,0:T(8,128)(2,1)S(1)}, bf16[4,600,128]{2,1,0:T(8,128)(2,1)}, u32[]{:S(2)}, u32[]{:S(2)}) collective-permute-start(bf16[4,600,128]{2,1,0:T(8,128)(2,1)S(1)} %dynamic-slice_bitcast_fusion), channel_id=1, source_target_pairs={{0,4},{4,0},{8,12},{12,8},{16,20},{20,16},{24,28},{28,24},{1,5},{5... | collective-permute-start | bytes 1843208 | tf_op jit(solution)/shard_map/ppermute | solution.py:496
  242.9 142.0 %all-gather.3.cloned.1.call-start = ((), (), s32[]{:S(2)}) async-start(), calls=%async_computation | async-start | bytes 1382400 | tf_op jit(solution)/shard_map/all_gather | solution.py:544
  252.5 19.9 %collective-permute-start.36 = (bf16[600,128]{1,0:T(8,128)(2,1)}, bf16[600,128]{1,0:T(8,128)(2,1)}, u32[]{:S(2)}, u32[]{:S(2)}) collective-permute-start(bf16[600,128]{1,0:T(8,128)(2,1)} %get-tuple-element.221), channel_id=1, source_target_pairs={{0,8},{4,12},{8,16},{12,20},{16,24},{20,28},{24,0},{28,4},{1,9},{5... | collective-permute-start | bytes 460808 | tf_op jit(solution)/shard_map/ppermute | solution.py:496
  253.2 19.2 %collective-permute-start.37 = (bf16[600,128]{1,0:T(8,128)(2,1)}, bf16[600,128]{1,0:T(8,128)(2,1)}, u32[]{:S(2)}, u32[]{:S(2)}) collective-permute-start(bf16[600,128]{1,0:T(8,128)(2,1)} %get-tuple-element.220), channel_id=1, source_target_pairs={{0,16},{4,20},{8,24},{12,28},{16,0},{20,4},{24,8},{28,12},{1,17},{... | collective-permute-start | bytes 460808 | tf_op jit(solution)/shard_map/ppermute | solution.py:496
  253.8 18.6 %collective-permute-start.38 = (bf16[600,128]{1,0:T(8,128)(2,1)}, bf16[600,128]{1,0:T(8,128)(2,1)}, u32[]{:S(2)}, u32[]{:S(2)}) collective-permute-start(bf16[600,128]{1,0:T(8,128)(2,1)} %get-tuple-element.219), channel_id=1, source_target_pairs={{0,24},{4,28},{8,0},{12,4},{16,8},{20,12},{24,16},{28,20},{1,25},{... | collective-permute-start | bytes 460808 | tf_op jit(solution)/shard_map/ppermute | solution.py:496
  259.9 43.8 %collective-permute-start.40 = (bf16[1024,480]{0,1:T(8,128)(2,1)}, bf16[1024,480]{0,1:T(8,128)(2,1)S(1)}, u32[]{:S(2)}, u32[]{:S(2)}) collective-permute-start(bf16[1024,480]{0,1:T(8,128)(2,1)} %copy.62), channel_id=1, source_target_pairs={{0,2},{2,0},{1,3},{3,1},{4,6},{6,4},{5,7},{7,5},{8,10},{10,8},{9,1... | collective-permute-start | bytes 2949128 | tf_op jit(solution)/shard_map/ppermute | solution.py:460
  276.5 29.5 %collective-permute-start.39 = (bf16[1024,480]{0,1:T(8,128)(2,1)}, bf16[1024,480]{0,1:T(8,128)(2,1)}, u32[]{:S(2)}, u32[]{:S(2)}) collective-permute-start(bf16[1024,480]{0,1:T(8,128)(2,1)} %copy.60), channel_id=1, source_target_pairs={{0,1},{1,0},{2,3},{3,2},{4,5},{5,4},{6,7},{7,6},{8,9},{9,8},{10,11... | collective-permute-start | bytes 2949128 | tf_op jit(solution)/shard_map/ppermute | solution.py:460
  277.7 19.3 %collective-permute-start.51 = (bf16[600,128]{1,0:T(8,128)(2,1)S(1)}, bf16[600,128]{1,0:T(8,128)(2,1)S(1)}, u32[]{:S(2)}, u32[]{:S(2)}) collective-permute-start(bf16[600,128]{1,0:T(8,128)(2,1)S(1)} %get-tuple-element.217), channel_id=1, source_target_pairs={{0,16},{4,20},{8,24},{12,28},{16,0},{20,4},{24,8},{28,12},{1,17},{... | collective-permute-start | bytes 460808 | tf_op jit(solution)/shard_map/ppermute | solution.py:496
  278.8 18.2 %collective-permute-start.52 = (bf16[600,128]{1,0:T(8,128)(2,1)S(1)}, bf16[600,128]{1,0:T(8,128)(2,1)S(1)}, u32[]{:S(2)}, u32[]{:S(2)}) collective-permute-start(bf16[600,128]{1,0:T(8,128)(2,1)S(1)} %get-tuple-element.216), channel_id=1, source_target_pairs={{0,24},{4,28},{8,0},{12,4},{16,8},{20,12},{24,16},{28,20},{1,25},{... | collective-permute-start | bytes 460808 | tf_op jit(solution)/shard_map/ppermute | solution.py:496
  327.2 27.4 %collective-permute-start.44 = (bf16[200,480]{1,0:T(8,128)(2,1)S(1)}, bf16[200,480]{1,0:T(8,128)(2,1)S(1)}, u32[]{:S(2)}, u32[]{:S(2)}) collective-permute-start(bf16[200,480]{1,0:T(8,128)(2,1)S(1)} %get-tuple-element.214), channel_id=1, source_target_pairs={{0,16},{4,20},{8,24},{12,28},{16,0},{20,4},{24,8},{28,12},{1,17},{... | collective-permute-start | bytes 576008 | tf_op jit(solution)/shard_map/ppermute | solution.py:496
  327.2 27.4 %collective-permute-start.43 = (bf16[200,480]{1,0:T(8,128)(2,1)S(1)}, bf16[200,480]{1,0:T(8,128)(2,1)S(1)}, u32[]{:S(2)}, u32[]{:S(2)}) collective-permute-start(bf16[200,480]{1,0:T(8,128)(2,1)S(1)} %get-tuple-element.213), channel_id=1, source_target_pairs={{0,8},{4,12},{8,16},{12,20},{16,24},{20,28},{24,0},{28,4},{1,9},{5... | collective-permute-start | bytes 576008 | tf_op jit(solution)/shard_map/ppermute | solution.py:496
  356.0 21.6 %collective-permute-start.56 = (bf16[4,600,128]{2,1,0:T(8,128)(2,1)}, bf16[4,600,128]{2,1,0:T(8,128)(2,1)}, u32[]{:S(2)}, u32[]{:S(2)}) collective-permute-start(bf16[4,600,128]{2,1,0:T(8,128)(2,1)} %bitcast_dynamic-update-slice_fusion.4), channel_id=1, source_target_pairs={{0,4},{4,0},{8,12},{12,8},{16,20},{20,16},{24,28},{28,24},{1,5},{5... | collective-permute-start | bytes 1843208 | tf_op jit(solution)/shard_map/ppermute | solution.py:517
  371.4 18.5 %collective-permute-start.49 = (bf16[4,200,480]{2,1,0:T(8,128)(2,1)S(1)}, bf16[4,200,480]{2,1,0:T(8,128)(2,1)}, u32[]{:S(2)}, u32[]{:S(2)}) collective-permute-start(bf16[4,200,480]{2,1,0:T(8,128)(2,1)S(1)} %bitcast_dynamic-update-slice_fusion), channel_id=1, source_target_pairs={{0,4},{4,0},{8,12},{12,8},{16,20},{20,16},{24,28},{28,24},{1,5},{5... | collective-permute-start | bytes 2304008 | tf_op jit(solution)/shard_map/ppermute | solution.py:517
  (72 other events, 528.8 us)
Sparse Core Ops, SparseCore 0:
  243.1 54.1 all-gather.4
  303.8 50.9 all-gather.2

commit v7 on v6

--- a/solution.py
+++ b/solution.py
@@ -420,7 +420,7 @@
 
 def feed_forward(nm, og, weights, dtype, after=()):
     hidden = weights[0].shape[1]
-    chunk = 256
+    chunk = 2 * LANE
     cols = pl.BlockSpec((HALF, chunk), lambda i: (0, i))
     rows = pl.BlockSpec((chunk, LOCAL), lambda i: (i, 0))
     act = shape((hidden, LOCAL))
@@ -601,6 +601,8 @@
         [query_weight[:, 0].T, key_weight[:, 0].T, value_weight[:, 0].T], axis=0
     )
     w_far = swap(w_near, "row")
+    wo_near = output_weight[0]
+    wo_far = swap(wo_near, "row")
     x_own, x_other = own_tokens(hidden_in.T)
     x_got = swap(x_other, "col")
     gains = jnp.stack([attn_gain, ffn_gain])
@@ -626,8 +628,6 @@
         2 * LOCAL * D * D,
     )
     kv_near_got = swap(kv_near, "col")
-    wo_near = output_weight[0]
-    wo_far = swap(wo_near, "row")
     wo_near_got = swap(wo_near, "col")
     att_near, lse_near = attend(where_near, begin, q_near, kv_near, kv_near_got)
     w_far_got = swap(hold(w_far, lse_near), "col")
@@ -638,8 +638,8 @@
         2 * LOCAL * D * D,
     )
     kv_far_got = swap(kv_far, "col")
-    att_far, lse_far = attend(where_far, begin, q_far, kv_far, kv_far_got, after=(wo_far,))
-    wo_far_got = swap(wo_far, "col")
+    att_far, lse_far = attend(where_far, begin, q_far, kv_far, kv_far_got)
+    wo_far_got = swap(hold(wo_far, kv_far), "col")
     og_own, og_other = own_tokens(out_grad.T)
     og = jnp.concatenate([og_own, swap(og_other, "col")], axis=0)
     og_far = swap(og, "row")
@@ -662,10 +662,13 @@
         nm_far, og_far, mlp_weights, BF16, after=(act,)
     )
     gnm_back = swap(gnm_send, "row")
-    down_keep, down_send, gate_keep, gate_send, up_keep, up_send = weight_grads(
-        ((og, og_far), (nm, nm_far)), ((act, act_far), (gg, gg_far), (gu, gu_far)), (0, 1, 1)
-    )
-    down_send, gate_send, up_send = hold_all((down_send, gate_send, up_send), (gnm_back,))
+    down_keep, down_send = weight_grads(((og, og_far),), ((act, act_far),), (0,))
+    down_got = swap(down_send, "col")
+    gate_keep, gate_send, up_keep, up_send = weight_grads(
+        ((nm, nm_far),), ((gg, gg_far), (gu, gu_far)), (0, 0), after=(down_keep,)
+    )
+    down_sum = add(down_keep, hold(down_got, gate_keep))
+    gate_send, up_send = hold_all((gate_send, up_send), (gnm_back,))
 
     gmid, gb, gatt_near, gatt_far, ggain_mid = run(
         mid_back_kernel,
@@ -678,44 +681,41 @@
             shape((QUERY, LOCAL)), shape((2, 16, HALF), F32),
         ),
         2 * LOCAL * D * D,
-        after=(up_keep,),
-    )
-    down_sum = add(down_keep, hold(swap(down_send, "col"), ggain_mid))
+        after=(down_sum,),
+    )
+    down_x = reduce_first(down_sum, count, (ggain_mid,))
     gate_sum = add(gate_keep, hold(swap(gate_send, "col"), ggain_mid))
     up_sum = add(up_keep, hold(swap(up_send, "col"), ggain_mid))
 
     dq_far, own_far, other_far = attend_back(
-        where_far, begin, q_far, kv_far, kv_far_got, gatt_far, lse_far, after=(down_sum, gate_sum, up_sum)
-    )
-    out_back = hold(swap(hold(out_send, gnm_back), "row"), dq_far)
-    block = (mid + out_part + out_back.astype(F32)).astype(BF16)
-    down_x = reduce_first(down_sum, count, (dq_far,))
+        where_far, begin, q_far, kv_far, kv_far_got, gatt_far, lse_far, after=(down_x, gate_sum, up_sum)
+    )
+    gate_x = reduce_first(gate_sum, count, (dq_far,))
 
     def out_grads(att):
         send = dot(att, gb[HALF:], 1, 1).astype(BF16)
-        return add(dot(att, gb[:HALF], 1, 1), hold(swap(send, "col"), dq_far))
+        return add(dot(att, gb[:HALF], 1, 1), swap(send, "col"))
 
     wo_far_sum = out_grads(att_far)
     wo_near_sum = out_grads(att_near)
-    got_far = swap(hold(other_far, down_x), "col")
+    got_far = swap(hold(other_far, gate_x), "col")
     joined = shape((ROWS, HALF))
     gnm_in_part, far_keep, far_send = run(
         joined_far_kernel,
         (dq_far, own_far, got_far, cosine, sine, w_far, w_far_got, nm_in),
         (shape((D, LOCAL), F32), joined, joined),
         4 * LOCAL * D * D,
-        after=(wo_far_sum, wo_near_sum, block, down_x),
+        after=(gate_x,),
         scratch=[pltpu.VMEM((D, LOCAL), BF16)],
     )
-    gate_x = reduce_first(gate_sum, count, (far_keep,))
+    down_z = reduce_rest(down_x, count, (far_keep,))
+    up_x = reduce_first(hold(up_sum, gate_x), count, (far_keep,))
     dq_near, own_near, other_near = attend_back(
-        where_near, begin, q_near, kv_near, kv_near_got, gatt_near, lse_near, after=(gate_x,)
-    )
-    far_sum = add(far_keep, hold(swap(far_send, "col"), dq_near))
-    wo_sum = add(wo_near_sum, hold(swap(wo_far_sum, "row"), dq_near))
-    down_z = reduce_rest(down_x, count, (dq_near,))
-    up_x = reduce_first(hold(up_sum, gate_x), count, (dq_near,))
-    got_near = swap(hold(other_near, up_x, down_z, far_sum, wo_sum), "col")
+        where_near, begin, q_near, kv_near, kv_near_got, gatt_near, lse_near, after=(down_z, up_x, wo_far_sum, wo_near_sum)
+    )
+    wo_sum = add(wo_near_sum, swap(wo_far_sum, "row"))
+    far_sum = add(far_keep, hold(swap(hold(far_send, down_z, up_x), "col"), dq_near))
+    got_near = swap(hold(other_near, far_sum, wo_sum), "col")
     near_keep, near_send, grad = run(
         joined_near_kernel,
         (
@@ -724,32 +724,31 @@
         ),
         (joined, joined, shape((D, LOCAL))),
         4 * LOCAL * D * D,
-        after=(wo_sum, far_sum, down_z, up_x),
         scratch=[pltpu.VMEM((D, LOCAL), BF16)],
     )
     gate_z = reduce_rest(gate_x, count, (grad,))
-    near_send = hold(near_send, gate_z)
-    last_sum = add(near_keep, swap(near_send, "col"), swap(far_sum, "row"))
+    far_back = swap(far_sum, "row")
+    last_sum = add(near_keep, swap(hold(near_send, far_back, gate_z), "col"), far_back)
 
     def feature_cols(array):
         return in_window(array[:HALF], swap(array[HALF:], "col")).T
-
-    block_out = feature_cols(block)
-    input_grad = feature_cols(grad)
 
 
     def widened(whole_sum):
         parts = whole_sum.reshape(-1, HALF, LANE)
         return parts.transpose(1, 0, 2).reshape(HALF, -1).astype(F32)
 
-    up_z = reduce_rest(up_x, count, (grad,))
-    down_grad = widened(spread(down_z))
-    gate_grad = widened(spread(gate_z))
-    up_rest = gather_rest(up_z, count, (last_sum,))
-    out_x = reduce_first(wo_sum, count, (grad,))
     last_x = reduce_first(last_sum, count)
+    out_x = reduce_first(wo_sum, count)
+    up_z = reduce_rest(up_x, count, (last_x,))
+    last_z = reduce_rest(jnp.concatenate([last_x, out_x], axis=-2), count)
+    out_back = hold(swap(hold(out_send, gnm_back), "row"), last_z)
+    block_out = feature_cols((mid + out_part + out_back.astype(F32)).astype(BF16))
+    input_grad = feature_cols(hold(grad, last_x))
+    down_grad = widened(hold(spread(down_z), last_x))
+    gate_grad = widened(hold(spread(gate_z), last_x))
+    up_rest = gather_rest(up_z, count, (last_z,))
     up_grad = widened(gather_first(up_rest, count).reshape(up_sum.shape))
-    last_z = reduce_rest(jnp.concatenate([last_x, out_x], axis=-2), count)
     last = gather_first(gather_rest(last_z, count), count)
     last, out_weight_grad = last[..., : ROWS // count, :], last[..., ROWS // count :, :]
     last = last.reshape(last_sum.shape).astype(F32)

time: 411 us -> 391 us (0.951)
  waiting for transfers between devices: 113 us -> 76.4 us
  starting transfers between devices: 59.7 us -> 77.7 us
    ppermute x17, waiting for transfers between devices: 64.7 us -> 16.5 us  [reduce_stage(): lax.ppermute(sent, 'dp', shift_pairs(count, stride, size, step))]
    ppermute x17, starting transfers between devices: 24 us -> 35.8 us  [reduce_stage(): lax.ppermute(sent, 'dp', shift_pairs(count, stride, size, step))]
    ppermute x8, starting transfers between devices: 15.3 us -> 23.8 us  [gather_stage(): lax.ppermute(part, 'dp', shift_pairs(count, stride, size, step))]
    ppermute x8, waiting for transfers between devices: 13.6 us -> 22.1 us  [gather_stage(): lax.ppermute(part, 'dp', shift_pairs(count, stride, size, step))]
    pallas_call x13 -> x14, Pallas kernels: 126 us -> 130 us  [run(): pl.pallas_call(body, grid=grid if grid is not None else (1,), in_specs=li...]
    unnamed x91 -> x97, local copies, waits for them, and re-layouts: 12.3 us -> 14.5 us
  transfers between devices with their start and end apart: 60 -> 60, of which waited for: 17 -> 22; matrix products, arithmetic and copies ran while one was open for 20% -> 18% of each run, Pallas kernels for 27% -> 28%
where the time goes in v7:
time: 391 us; the launch traced here: 387 us
  Pallas kernels  130 us (33%)
  starting transfers between devices  77.7 us (20%)
  waiting for transfers between devices  76.4 us (20%)
  local copies, waits for them, and re-layouts  42.8 us (11%)
  other arithmetic  35.8 us (9%)
  between operations  15.3 us (4%)
  matrix products  8.7 us (2%)
    pallas_call x14, Pallas kernels, run(): pl.pallas_call(body, grid=grid if grid is not None else (1,), in_specs=li...  130 us
    ppermute x17, starting transfers between devices, reduce_stage(): lax.ppermute(sent, 'dp', shift_pairs(count, stride, size, step))  35.8 us
    ppermute x33, waiting for transfers between devices, swap(): return lax.ppermute(array, axis, [(0, 1), (1, 0)])  33.9 us
    ppermute x8, starting transfers between devices, gather_stage(): lax.ppermute(part, 'dp', shift_pairs(count, stride, size, step))  23.8 us
    ppermute x8, waiting for transfers between devices, gather_stage(): lax.ppermute(part, 'dp', shift_pairs(count, stride, size, step))  22.1 us
    ppermute x33, starting transfers between devices, swap(): return lax.ppermute(array, axis, [(0, 1), (1, 0)])  18.1 us
    ppermute x17, waiting for transfers between devices, reduce_stage(): lax.ppermute(sent, 'dp', shift_pairs(count, stride, size, step))  16.5 us
    unnamed x97, local copies, waits for them, and re-layouts  14.5 us
  transfers between devices with their start and end apart: 60, of which 22 were waited for; matrix products, arithmetic and copies ran while one was open for 18% of the time, Pallas kernels for 28%

profile of v7, /device:TPU:0, one launch (start us, length us, event | category | flops | bytes accessed | tf_op | source)
XLA Modules:
  0.0 386.9 jit_solution(2758601266497092578)
XLA Ops:
  20.1 4.5 %shard_map.203 = (bf16[960,512]{1,0:T(8,128)(2,1)}, bf16[576,512]{1,0:T(8,128)(2,1)}, bf16[384,512]{1,0:T(8,128)(2,1)}) custom-call(bf16[480,512]{1,0:T(8,128)(2,1)} %get-tuple-element.206.refs_0_.refs_6_.refs_9_, bf16[480,512]{1,0:T(8,128)(2,1)} %copy-done.15, f32[480,1]{1,0:T(8,128)} %copy.47.refs_2_.refs_11_, f32[480,1]{1,0:T(8,128)} %copy.48.refs_3_.refs_12_, ...), custom_call_target="tpu_custom_call" | custom-call | flops 28311552 | bytes 147816 | tf_op jit(solution)/shard_map/pallas_call | solution.py:69
  27.2 11.3 %shard_map.204 = (bf16[576,512]{1,0:T(8,128)(2,1)}, f32[3,8,512]{2,1,0:T(8,128)}) custom-call(s32[2]{0:T(128)} %pad_add_fusion.refs_0_, s32[1,512]{1,0:T(1,128)} %broadcast_select_fusion.8.refs_1_, bf16[576,512]{1,0:T(8,128)(2,1)} %get-tuple-element.88.refs_2_, bf16[384,512]{1,0:T(8,128)(2,1)} %get-tuple-element.89.refs_3_.refs_4_, ...), custom_call_target="tpu_custom_call" | custom-call | flops 180000000 | bytes 84111 | tf_op jit(solution)/shard_map/pallas_call | solution.py:69
  42.2 4.0 %shard_map.205 = (bf16[576,512]{1,0:T(8,128)(2,1)}, bf16[384,512]{1,0:T(8,128)(2,1)}) custom-call(bf16[960,512]{1,0:T(8,128)(2,1)} %get-tuple-element.91.refs_0_.refs_7_, f32[32,512]{1,0:T(8,128)} %get-tuple-element.240.refs_4_.refs_1_.refs_3_, f32[32,512]{1,0:T(8,128)} %get-tuple-element.239.refs_5_.refs_2_.refs_4_, bf16[960,480]{1,0:T(8,128)(2,1)} %copy-done.16, ...), custom_call_target="tpu_custom_call" | custom-call | flops 28311552 | bytes 118210 | tf_op jit(solution)/shard_map/pallas_call | solution.py:69
  46.2 8.2 %collective-permute-done.9.refs_4_.refs_8_ = bf16[576,480]{1,0:T(8,128)(2,1)S(1)} collective-permute-done((bf16[576,480]{1,0:T(8,128)(2,1)S(1)}, bf16[576,480]{1,0:T(8,128)(2,1)S(1)}, u32[]{:S(2)}, u32[]{:S(2)}) %collective-permute-start.9) | collective-permute-done | bytes 552992 | tf_op jit(solution)/shard_map/ppermute | solution.py:460
  60.0 8.6 %shard_map.206 = (bf16[576,512]{1,0:T(8,128)(2,1)}, f32[3,8,512]{2,1,0:T(8,128)}) custom-call(s32[2]{0:T(128)} %pad_add_fusion.1.refs_0_, s32[1,512]{1,0:T(1,128)} %broadcast_select_fusion.8.refs_1_, bf16[576,512]{1,0:T(8,128)(2,1)} %get-tuple-element.94.refs_2_, bf16[384,512]{1,0:T(8,128)(2,1)} %get-tuple-element.95.refs_3_.refs_4_, ...), custom_call_target="tpu_custom_call" | custom-call | flops 180000000 | bytes 84111 | tf_op jit(solution)/shard_map/pallas_call | solution.py:69
  68.7 5.7 %shard_map.207 = (f32[960,512]{1,0:T(8,128)}, bf16[960,512]{1,0:T(8,128)(2,1)}) custom-call(bf16[576,512]{1,0:T(8,128)(2,1)} %get-tuple-element.90.refs_0_, bf16[576,512]{1,0:T(8,128)(2,1)} %get-tuple-element.96.refs_1_, bf16[576,480]{1,0:T(8,128)(2,1)} %bitcast.199, bf16[576,480]{1,0:T(8,128)(2,1)} %collective-permute-done.8.refs_3_.refs_7_, ...), custom_call_target="tpu_custom_call" | custom-call | flops 28311552 | bytes 219824 | tf_op jit(solution)/shard_map/pallas_call | solution.py:69
  74.4 4.8 %collective-permute-start.16 = (bf16[960,512]{1,0:T(8,128)(2,1)}, bf16[960,512]{1,0:T(8,128)(2,1)S(1)}, u32[]{:S(2)}, u32[]{:S(2)}) collective-permute-start(bf16[960,512]{1,0:T(8,128)(2,1)} %get-tuple-element.99.refs_0_), channel_id=1, source_target_pairs={{0,2},{2,0},{1,3},{3,1},{4,6},{6,4},{5,7},{7,5},{8,10},{10,8},{9,1... | collective-permute-start | bytes 2949128 | tf_op jit(solution)/shard_map/ppermute | solution.py:460
  79.2 2.8 collective-permute-done.15.refs_8_.refs_1_
  83.0 15.8 %shard_map.208 = (f32[960,512]{1,0:T(8,128)}, f32[960,512]{1,0:T(8,128)}, bf16[1280,512]{1,0:T(8,128)(2,1)}, bf16[1280,512]{1,0:T(8,128)(2,1)}, bf16[1280,512]{1,0:T(8,128)(2,1)}) custom-call(bf16[960,512]{1,0:T(8,128)(2,1)} %get-tuple-element.99.refs_0_, bf16[960,512]{1,0:T(8,128)(2,1)} %copy-done, bf16[480,1280]{1,0:T(8,128)(2,1)} %refs_2_.3, ...), custom_call_target="tpu_custom_call" | custom-call | flops 226492416 | bytes 516096 | tf_op jit(solution)/shard_map/pallas_call | solution.py:69
  98.8 3.7 collective-permute-done.16.refs_0_.refs_1_
  103.4 15.2 %shard_map.209 = (bf16[960,512]{1,0:T(8,128)(2,1)}, bf16[960,512]{1,0:T(8,128)(2,1)}, bf16[1280,512]{1,0:T(8,128)(2,1)}, bf16[1280,512]{1,0:T(8,128)(2,1)}, bf16[1280,512]{1,0:T(8,128)(2,1)}) custom-call(bf16[960,512]{1,0:T(8,128)(2,1)} %copy-done.18, bf16[960,512]{1,0:T(8,128)(2,1)} %copy-done.7, bf16[480,1280]{1,0:T(8,128)(2,1)} %refs_2_.3, ...), custom_call_target="tpu_custom_call" | custom-call | flops 226492416 | bytes 457113 | tf_op jit(solution)/shard_map/pallas_call | solution.py:69
  118.6 7.1 %shard_map.210 = (bf16[4800,128]{1,0:T(8,128)(2,1)}, bf16[4800,128]{1,0:T(8,128)(2,1)}) custom-call(bf16[960,512]{1,0:T(8,128)(2,1)} %copy-done, bf16[960,512]{1,0:T(8,128)(2,1)} %copy-done.7, bf16[1280,512]{1,0:T(8,128)(2,1)} %get-tuple-element.101.refs_8_.refs_2_, bf16[1280,512]{1,0:T(8,128)(2,1)} %get-tuple-element.106.refs_3_), custom_call_target="tpu_custom_call" | custom-call | flops 75497472 | bytes 211353 | tf_op jit(solution)/shard_map/pallas_call | solution.py:69
  126.1 9.2 %shard_map.211 = (bf16[4800,128]{1,0:T(8,128)(2,1)}, bf16[4800,128]{1,0:T(8,128)(2,1)}, bf16[4800,128]{1,0:T(8,128)(2,1)}, bf16[4800,128]{1,0:T(8,128)(2,1)}) custom-call(bf16[960,512]{1,0:T(8,128)(2,1)} %get-tuple-element.99.refs_0_, bf16[960,512]{1,0:T(8,128)(2,1)} %copy-done.18, bf16[1280,512]{1,0:T(8,128)(2,1)} %get-tuple-element.109.refs_2_, ...), custom_call_target="tpu_custom_call" | custom-call | flops 150994944 | bytes 363724 | tf_op jit(solution)/shard_map/pallas_call | solution.py:69
  135.4 14.6 %collective-permute-done.17.refs_3_ = bf16[960,512]{1,0:T(8,128)(2,1)S(1)} collective-permute-done((bf16[960,512]{1,0:T(8,128)(2,1)S(1)}, bf16[960,512]{1,0:T(8,128)(2,1)S(1)}, u32[]{:S(2)}, u32[]{:S(2)}) %collective-permute-start.17) | collective-permute-done | bytes 983072 | tf_op jit(solution)/shard_map/ppermute | solution.py:460
  153.3 8.3 %shard_map.212 = (f32[960,512]{1,0:T(8,128)}, bf16[960,512]{1,0:T(8,128)(2,1)}, bf16[576,512]{1,0:T(8,128)(2,1)}, bf16[576,512]{1,0:T(8,128)(2,1)}, f32[2,16,480]{2,1,0:T(8,128)}) custom-call(bf16[960,512]{1,0:T(8,128)(2,1)} %copy-done, f32[960,512]{1,0:T(8,128)} %get-tuple-element.98.refs_1_, f32[960,512]{1,0:T(8,128)} %get-tuple-element.105.refs_2_, ...), custom_call_target="tpu_custom_call" | custom-call | flops 28311552 | bytes 369123 | tf_op jit(solution)/shard_map/pallas_call | solution.py:69
  161.6 3.0 add_convert_fusion
  168.7 10.2 %shard_map.213 = (f32[576,512]{1,0:T(8,128)}, f32[2,3,64,512]{3,2,1,0:T(8,128)}, bf16[2,3,64,512]{3,2,1,0:T(8,128)(2,1)}) custom-call(s32[2]{0:T(128)} %pad_add_fusion.1.refs_0_, s32[1,512]{1,0:T(1,128)} %broadcast_select_fusion.8.refs_1_, bf16[576,512]{1,0:T(8,128)(2,1)} %get-tuple-element.94.refs_2_, bf16[384,512]{1,0:T(8,128)(2,1)} %get-tuple-element.95.refs_3_.refs_4_, ...), custom_call_target="tpu_custom_call" | custom-call | flops 420000000 | bytes 154890 | tf_op jit(solution)/shard_map/pallas_call | solution.py:69
  192.5 6.7 %shard_map.214 = (f32[960,512]{1,0:T(8,128)}, bf16[1024,480]{1,0:T(8,128)(2,1)}, bf16[1024,480]{1,0:T(8,128)(2,1)}) custom-call(f32[576,512]{1,0:T(8,128)} %get-tuple-element.127.refs_0_, f32[2,3,64,512]{3,2,1,0:T(8,128)} %get-tuple-element.128.refs_1_, bf16[2,3,64,512]{3,2,1,0:T(8,128)(2,1)} %copy-done.37, ...), custom_call_target="tpu_custom_call" | custom-call | flops 56623104 | bytes 277463 | tf_op jit(solution)/shard_map/pallas_call | solution.py:69
  212.4 13.6 %shard_map.215 = (f32[576,512]{1,0:T(8,128)}, f32[2,3,64,512]{3,2,1,0:T(8,128)}, bf16[2,3,64,512]{3,2,1,0:T(8,128)(2,1)}) custom-call(s32[2]{0:T(128)} %pad_add_fusion.refs_0_, s32[1,512]{1,0:T(1,128)} %broadcast_select_fusion.8.refs_1_, bf16[576,512]{1,0:T(8,128)(2,1)} %get-tuple-element.88.refs_2_, bf16[384,512]{1,0:T(8,128)(2,1)} %get-tuple-element.89.refs_3_.refs_4_, ...), custom_call_target="tpu_custom_call" | custom-call | flops 420000000 | bytes 154890 | tf_op jit(solution)/shard_map/pallas_call | solution.py:69
  230.1 3.8 collective-permute-start.35
  237.4 9.9 %shard_map.216 = (bf16[1024,480]{1,0:T(8,128)(2,1)}, bf16[1024,480]{1,0:T(8,128)(2,1)}, bf16[960,512]{1,0:T(8,128)(2,1)}) custom-call(f32[576,512]{1,0:T(8,128)} %get-tuple-element.139.refs_0_, f32[2,3,64,512]{3,2,1,0:T(8,128)} %get-tuple-element.140.refs_1_, bf16[2,3,64,512]{3,2,1,0:T(8,128)(2,1)} %copy-done.38, ...), custom_call_target="tpu_custom_call" | custom-call | flops 56623104 | bytes 397386 | tf_op jit(solution)/shard_map/pallas_call | solution.py:69
  247.3 7.0 %collective-permute-done.36 = bf16[600,128]{1,0:T(8,128)(2,1)S(1)} collective-permute-done((bf16[600,128]{1,0:T(8,128)(2,1)S(1)}, bf16[600,128]{1,0:T(8,128)(2,1)S(1)}, u32[]{:S(2)}, u32[]{:S(2)}) %collective-permute-start.36) | collective-permute-done | bytes 153632 | tf_op jit(solution)/shard_map/ppermute | solution.py:496
  268.4 5.2 %collective-permute-start.50 = (bf16[600,128]{1,0:T(8,128)(2,1)S(1)}, bf16[600,128]{1,0:T(8,128)(2,1)S(1)}, u32[]{:S(2)}, u32[]{:S(2)}) collective-permute-start(bf16[600,128]{1,0:T(8,128)(2,1)S(1)} %get-tuple-element.218), channel_id=1, source_target_pairs={{0,8},{4,12},{8,16},{12,20},{16,24},{20,28},{24,0},{28,4},{1,9},{5... | collective-permute-start | bytes 460808 | tf_op jit(solution)/shard_map/ppermute | solution.py:496
  276.0 4.5 %collective-permute-done.39 = bf16[4,128,480]{2,1,0:T(8,128)(2,1)S(1)} collective-permute-done((bf16[4,128,480]{2,1,0:T(8,128)(2,1)S(1)}, bf16[4,128,480]{2,1,0:T(8,128)(2,1)S(1)}, u32[]{:S(2)}, u32[]{:S(2)}) %collective-permute-start.39) | collective-permute-done | bytes 491552 | tf_op jit(solution)/shard_map/ppermute | solution.py:496
  281.5 5.2 %collective-permute-start.41 = (bf16[200,480]{1,0:T(8,128)(2,1)}, bf16[200,480]{1,0:T(8,128)(2,1)}, u32[]{:S(2)}, u32[]{:S(2)}) collective-permute-start(bf16[200,480]{1,0:T(8,128)(2,1)} %get-tuple-element.213), channel_id=1, source_target_pairs={{0,8},{4,12},{8,16},{12,20},{16,24},{20,28},{24,0},{28,4},{1,9},{5... | collective-permute-start | bytes 576008 | tf_op jit(solution)/shard_map/ppermute | solution.py:496
  288.5 5.4 %collective-permute-start.43 = (bf16[200,480]{1,0:T(8,128)(2,1)}, bf16[200,480]{1,0:T(8,128)(2,1)}, u32[]{:S(2)}, u32[]{:S(2)}) collective-permute-start(bf16[200,480]{1,0:T(8,128)(2,1)} %get-tuple-element.215), channel_id=1, source_target_pairs={{0,24},{4,28},{8,0},{12,4},{16,8},{20,12},{24,16},{28,20},{1,25},{... | collective-permute-start | bytes 576008 | tf_op jit(solution)/shard_map/ppermute | solution.py:496
  299.2 12.6 %collective-permute-start.53 = (bf16[600,128]{1,0:T(8,128)(2,1)}, bf16[600,128]{1,0:T(8,128)(2,1)}, u32[]{:S(2)}, u32[]{:S(2)}) collective-permute-start(bf16[600,128]{1,0:T(8,128)(2,1)} %get-tuple-element.188), channel_id=1, source_target_pairs={{0,8},{4,12},{8,16},{12,20},{16,24},{20,28},{24,0},{28,4},{1,9},{5... | collective-permute-start | bytes 460808 | tf_op jit(solution)/shard_map/ppermute | solution.py:517
  313.7 3.8 all-gather.3.cloned.1.call-done
  328.4 3.7 collective-permute-done.54
  332.2 5.3 %collective-permute-start.48 = (bf16[200,480]{1,0:T(8,128)(2,1)S(1)}, bf16[200,480]{1,0:T(8,128)(2,1)S(1)}, u32[]{:S(2)}, u32[]{:S(2)}) collective-permute-start(bf16[200,480]{1,0:T(8,128)(2,1)S(1)} %get-tuple-element.190), channel_id=1, source_target_pairs={{0,24},{4,28},{8,0},{12,4},{16,8},{20,12},{24,16},{28,20},{1,25},{... | collective-permute-start | bytes 576008 | tf_op jit(solution)/shard_map/ppermute | solution.py:517
  342.3 6.4 %collective-permute-done.47 = bf16[200,480]{1,0:T(8,128)(2,1)S(1)} collective-permute-done((bf16[200,480]{1,0:T(8,128)(2,1)S(1)}, bf16[200,480]{1,0:T(8,128)(2,1)S(1)}, u32[]{:S(2)}, u32[]{:S(2)}) %collective-permute-start.47) | collective-permute-done | bytes 192032 | tf_op jit(solution)/shard_map/ppermute | solution.py:517
  361.3 10.2 %collective-permute-done.49 = bf16[4,200,480]{2,1,0:T(8,128)(2,1)S(1)} collective-permute-done((bf16[4,200,480]{2,1,0:T(8,128)(2,1)}, bf16[4,200,480]{2,1,0:T(8,128)(2,1)S(1)}, u32[]{:S(2)}, u32[]{:S(2)}) %collective-permute-start.49) | collective-permute-done | bytes 768032 | tf_op jit(solution)/shard_map/ppermute | solution.py:517
  (305 shorter events, 131.3 us)
Async XLA Ops:
  7.2 287.6 %all-gather.5.cloned.1.call-start = ((), (), s32[]{:S(2)}) async-start(), calls=%async_computation.1 | async-start | bytes 1382400 | tf_op jit(solution)/shard_map/all_gather | solution.py:544
  9.2 29.4 %collective-permute-start.5 = (bf16[960,480]{1,0:T(8,128)(2,1)S(1)}, bf16[960,480]{1,0:T(8,128)(2,1)S(1)}, u32[]{:S(2)}, u32[]{:S(2)}) collective-permute-start(bf16[960,480]{1,0:T(8,128)(2,1)S(1)} %pad_maximum_fusion.1.refs_6_.refs_5_), channel_id=1, source_target_pairs={{0,2},{2,0},{1,3},{3,1},{4,6},{6,4},{5,7},{7,5},{8,10},{10,8},{9,1... | collective-permute-start | bytes 2764808 | tf_op jit(solution)/shard_map/ppermute | solution.py:460
  38.7 15.7 %collective-permute-start.9 = (bf16[576,480]{1,0:T(8,128)(2,1)S(1)}, bf16[576,480]{1,0:T(8,128)(2,1)S(1)}, u32[]{:S(2)}, u32[]{:S(2)}) collective-permute-start(bf16[576,480]{1,0:T(8,128)(2,1)S(1)} %bitcast.201), channel_id=1, source_target_pairs={{0,2},{2,0},{1,3},{3,1},{4,6},{6,4},{5,7},{7,5},{8,10},{10,8},{9,1... | collective-permute-start | bytes 1658888 | tf_op jit(solution)/shard_map/ppermute | solution.py:460
  38.8 16.7 %collective-permute-start.8 = (bf16[576,480]{1,0:T(8,128)(2,1)S(1)}, bf16[576,480]{1,0:T(8,128)(2,1)}, u32[]{:S(2)}, u32[]{:S(2)}) collective-permute-start(bf16[576,480]{1,0:T(8,128)(2,1)S(1)} %bitcast.202), channel_id=1, source_target_pairs={{0,1},{1,0},{2,3},{3,2},{4,5},{5,4},{6,7},{7,6},{8,9},{9,8},{10,11... | collective-permute-start | bytes 1658888 | tf_op jit(solution)/shard_map/ppermute | solution.py:460
  54.9 24.2 %collective-permute-start.14 = (bf16[480,1280]{1,0:T(8,128)(2,1)}, bf16[480,1280]{1,0:T(8,128)(2,1)}, u32[]{:S(2)}, u32[]{:S(2)}) collective-permute-start(bf16[480,1280]{1,0:T(8,128)(2,1)} %bitcast.23.refs_6_), channel_id=1, source_target_pairs={{0,1},{1,0},{2,3},{3,2},{4,5},{5,4},{6,7},{7,6},{8,9},{9,8},{10,11... | collective-permute-start | bytes 3686408 | tf_op jit(solution)/shard_map/ppermute | solution.py:460
  54.9 24.2 %collective-permute-start.12 = (bf16[480,1280]{1,0:T(8,128)(2,1)}, bf16[480,1280]{1,0:T(8,128)(2,1)}, u32[]{:S(2)}, u32[]{:S(2)}) collective-permute-start(bf16[480,1280]{1,0:T(8,128)(2,1)} %refs_2_.3), channel_id=1, source_target_pairs={{0,1},{1,0},{2,3},{3,2},{4,5},{5,4},{6,7},{7,6},{8,9},{9,8},{10,11... | collective-permute-start | bytes 3686408 | tf_op jit(solution)/shard_map/ppermute | solution.py:460
  55.5 23.7 %collective-permute-start.13 = (bf16[480,1280]{1,0:T(8,128)(2,1)}, bf16[480,1280]{1,0:T(8,128)(2,1)}, u32[]{:S(2)}, u32[]{:S(2)}) collective-permute-start(bf16[480,1280]{1,0:T(8,128)(2,1)} %refs_4_.3), channel_id=1, source_target_pairs={{0,1},{1,0},{2,3},{3,2},{4,5},{5,4},{6,7},{7,6},{8,9},{9,8},{10,11... | collective-permute-start | bytes 3686408 | tf_op jit(solution)/shard_map/ppermute | solution.py:460
  57.4 24.6 %collective-permute-start.15 = (bf16[960,512]{1,0:T(8,128)(2,1)S(1)}, bf16[960,512]{1,0:T(8,128)(2,1)S(1)}, u32[]{:S(2)}, u32[]{:S(2)}) collective-permute-start(bf16[960,512]{1,0:T(8,128)(2,1)S(1)} %pad_maximum_fusion.2.refs_1_.refs_0_), channel_id=1, source_target_pairs={{0,2},{2,0},{1,3},{3,1},{4,6},{6,4},{5,7},{7,5},{8,10},{10,8},{9,1... | collective-permute-start | bytes 2949128 | tf_op jit(solution)/shard_map/ppermute | solution.py:460
  74.4 28.1 %collective-permute-start.16 = (bf16[960,512]{1,0:T(8,128)(2,1)}, bf16[960,512]{1,0:T(8,128)(2,1)S(1)}, u32[]{:S(2)}, u32[]{:S(2)}) collective-permute-start(bf16[960,512]{1,0:T(8,128)(2,1)} %get-tuple-element.99.refs_0_), channel_id=1, source_target_pairs={{0,2},{2,0},{1,3},{3,1},{4,6},{6,4},{5,7},{7,5},{8,10},{10,8},{9,1... | collective-permute-start | bytes 2949128 | tf_op jit(solution)/shard_map/ppermute | solution.py:460
  125.8 24.7 %collective-permute-start.19 = (bf16[4800,128]{1,0:T(8,128)(2,1)}, bf16[4800,128]{1,0:T(8,128)(2,1)S(1)}, u32[]{:S(2)}, u32[]{:S(2)}) collective-permute-start(bf16[4800,128]{1,0:T(8,128)(2,1)} %get-tuple-element.108), channel_id=1, source_target_pairs={{0,1},{1,0},{2,3},{3,2},{4,5},{5,4},{6,7},{7,6},{8,9},{9,8},{10,11... | collective-permute-start | bytes 3686408 | tf_op jit(solution)/shard_map/ppermute | solution.py:460
  125.8 24.2 %collective-permute-start.17 = (bf16[960,512]{1,0:T(8,128)(2,1)S(1)}, bf16[960,512]{1,0:T(8,128)(2,1)S(1)}, u32[]{:S(2)}, u32[]{:S(2)}) collective-permute-start(bf16[960,512]{1,0:T(8,128)(2,1)S(1)} %copy-done.44), channel_id=1, source_target_pairs={{0,2},{2,0},{1,3},{3,1},{4,6},{6,4},{5,7},{7,5},{8,10},{10,8},{9,1... | collective-permute-start | bytes 2949128 | tf_op jit(solution)/shard_map/ppermute | solution.py:460
  151.8 15.9 %collective-permute-start.20 = (bf16[4,600,128]{2,1,0:T(8,128)(2,1)}, bf16[4,600,128]{2,1,0:T(8,128)(2,1)S(1)}, u32[]{:S(2)}, u32[]{:S(2)}) collective-permute-start(bf16[4,600,128]{2,1,0:T(8,128)(2,1)} %dynamic-slice_bitcast_fusion.2), channel_id=1, source_target_pairs={{0,4},{4,0},{8,12},{12,8},{16,20},{20,16},{24,28},{28,24},{1,5},{5... | collective-permute-start | bytes 1843208 | tf_op jit(solution)/shard_map/ppermute | solution.py:496
  183.4 16.9 %collective-permute-start.28 = (bf16[4,600,128]{2,1,0:T(8,128)(2,1)S(1)}, bf16[4,600,128]{2,1,0:T(8,128)(2,1)S(1)}, u32[]{:S(2)}, u32[]{:S(2)}) collective-permute-start(bf16[4,600,128]{2,1,0:T(8,128)(2,1)S(1)} %dynamic-slice_bitcast_fusion), channel_id=1, source_target_pairs={{0,4},{4,0},{8,12},{12,8},{16,20},{20,16},{24,28},{28,24},{1,5},{5... | collective-permute-start | bytes 1843208 | tf_op jit(solution)/shard_map/ppermute | solution.py:496
  201.8 24.2 %collective-permute-start.31 = (bf16[1024,480]{0,1:T(8,128)(2,1)S(1)}, bf16[1024,480]{0,1:T(8,128)(2,1)S(1)}, u32[]{:S(2)}, u32[]{:S(2)}) collective-permute-start(bf16[1024,480]{0,1:T(8,128)(2,1)S(1)} %copy.56), channel_id=1, source_target_pairs={{0,1},{1,0},{2,3},{3,2},{4,5},{5,4},{6,7},{7,6},{8,9},{9,8},{10,11... | collective-permute-start | bytes 2949128 | tf_op jit(solution)/shard_map/ppermute | solution.py:460
  204.8 112.7 %all-gather.3.cloned.1.call-start = ((), (), s32[]{:S(2)}) async-start(), calls=%async_computation | async-start | bytes 1382400 | tf_op jit(solution)/shard_map/all_gather | solution.py:544
  207.5 20.7 %collective-permute-start.32 = (bf16[576,480]{1,0:T(8,128)(2,1)}, bf16[576,480]{1,0:T(8,128)(2,1)}, u32[]{:S(2)}, u32[]{:S(2)}) collective-permute-start(bf16[576,480]{1,0:T(8,128)(2,1)} %fusion.refs_11_), channel_id=1, source_target_pairs={{0,2},{2,0},{1,3},{3,1},{4,6},{6,4},{5,7},{7,5},{8,10},{10,8},{9,1... | collective-permute-start | bytes 1658888 | tf_op jit(solution)/shard_map/ppermute | solution.py:460
  228.1 27.0 %collective-permute-start.34 = (bf16[1024,480]{0,1:T(8,128)(2,1)S(1)}, bf16[1024,480]{0,1:T(8,128)(2,1)S(1)}, u32[]{:S(2)}, u32[]{:S(2)}) collective-permute-start(bf16[1024,480]{0,1:T(8,128)(2,1)S(1)} %copy.60), channel_id=1, source_target_pairs={{0,2},{2,0},{1,3},{3,1},{4,6},{6,4},{5,7},{7,5},{8,10},{10,8},{9,1... | collective-permute-start | bytes 2949128 | tf_op jit(solution)/shard_map/ppermute | solution.py:460
  230.1 17.2 %collective-permute-start.35 = (bf16[600,128]{1,0:T(8,128)(2,1)S(1)}, bf16[600,128]{1,0:T(8,128)(2,1)S(1)}, u32[]{:S(2)}, u32[]{:S(2)}) collective-permute-start(bf16[600,128]{1,0:T(8,128)(2,1)S(1)} %get-tuple-element.221), channel_id=1, source_target_pairs={{0,8},{4,12},{8,16},{12,20},{16,24},{20,28},{24,0},{28,4},{1,9},{5... | collective-permute-start | bytes 460808 | tf_op jit(solution)/shard_map/ppermute | solution.py:496
  234.0 20.3 %collective-permute-start.36 = (bf16[600,128]{1,0:T(8,128)(2,1)S(1)}, bf16[600,128]{1,0:T(8,128)(2,1)S(1)}, u32[]{:S(2)}, u32[]{:S(2)}) collective-permute-start(bf16[600,128]{1,0:T(8,128)(2,1)S(1)} %get-tuple-element.220), channel_id=1, source_target_pairs={{0,16},{4,20},{8,24},{12,28},{16,0},{20,4},{24,8},{28,12},{1,17},{... | collective-permute-start | bytes 460808 | tf_op jit(solution)/shard_map/ppermute | solution.py:496
  235.6 18.7 %collective-permute-start.37 = (bf16[600,128]{1,0:T(8,128)(2,1)S(1)}, bf16[600,128]{1,0:T(8,128)(2,1)S(1)}, u32[]{:S(2)}, u32[]{:S(2)}) collective-permute-start(bf16[600,128]{1,0:T(8,128)(2,1)S(1)} %get-tuple-element.219), channel_id=1, source_target_pairs={{0,24},{4,28},{8,0},{12,4},{16,8},{20,12},{24,16},{28,20},{1,25},{... | collective-permute-start | bytes 460808 | tf_op jit(solution)/shard_map/ppermute | solution.py:496
  265.7 72.8 %collective-permute-start.18 = (bf16[960,512]{1,0:T(8,128)(2,1)}, bf16[960,512]{1,0:T(8,128)(2,1)}, u32[]{:S(2)}, u32[]{:S(2)}) collective-permute-start(bf16[960,512]{1,0:T(8,128)(2,1)} %get-tuple-element.104), channel_id=1, source_target_pairs={{0,2},{2,0},{1,3},{3,1},{4,6},{6,4},{5,7},{7,5},{8,10},{10,8},{9,1... | collective-permute-start | bytes 2949128 | tf_op jit(solution)/shard_map/ppermute | solution.py:460
  268.4 18.3 %collective-permute-start.50 = (bf16[600,128]{1,0:T(8,128)(2,1)S(1)}, bf16[600,128]{1,0:T(8,128)(2,1)S(1)}, u32[]{:S(2)}, u32[]{:S(2)}) collective-permute-start(bf16[600,128]{1,0:T(8,128)(2,1)S(1)} %get-tuple-element.218), channel_id=1, source_target_pairs={{0,8},{4,12},{8,16},{12,20},{16,24},{20,28},{24,0},{28,4},{1,9},{5... | collective-permute-start | bytes 460808 | tf_op jit(solution)/shard_map/ppermute | solution.py:496
  275.0 18.9 %collective-permute-start.52 = (bf16[600,128]{1,0:T(8,128)(2,1)S(1)}, bf16[600,128]{1,0:T(8,128)(2,1)S(1)}, u32[]{:S(2)}, u32[]{:S(2)}) collective-permute-start(bf16[600,128]{1,0:T(8,128)(2,1)S(1)} %get-tuple-element.216), channel_id=1, source_target_pairs={{0,24},{4,28},{8,0},{12,4},{16,8},{20,12},{24,16},{28,20},{1,25},{... | collective-permute-start | bytes 460808 | tf_op jit(solution)/shard_map/ppermute | solution.py:496
  281.5 39.6 %collective-permute-start.41 = (bf16[200,480]{1,0:T(8,128)(2,1)}, bf16[200,480]{1,0:T(8,128)(2,1)}, u32[]{:S(2)}, u32[]{:S(2)}) collective-permute-start(bf16[200,480]{1,0:T(8,128)(2,1)} %get-tuple-element.213), channel_id=1, source_target_pairs={{0,8},{4,12},{8,16},{12,20},{16,24},{20,28},{24,0},{28,4},{1,9},{5... | collective-permute-start | bytes 576008 | tf_op jit(solution)/shard_map/ppermute | solution.py:496
  286.7 36.4 %collective-permute-start.42 = (bf16[200,480]{1,0:T(8,128)(2,1)}, bf16[200,480]{1,0:T(8,128)(2,1)}, u32[]{:S(2)}, u32[]{:S(2)}) collective-permute-start(bf16[200,480]{1,0:T(8,128)(2,1)} %get-tuple-element.214), channel_id=1, source_target_pairs={{0,16},{4,20},{8,24},{12,28},{16,0},{20,4},{24,8},{28,12},{1,17},{... | collective-permute-start | bytes 576008 | tf_op jit(solution)/shard_map/ppermute | solution.py:496
  288.5 36.7 %collective-permute-start.43 = (bf16[200,480]{1,0:T(8,128)(2,1)}, bf16[200,480]{1,0:T(8,128)(2,1)}, u32[]{:S(2)}, u32[]{:S(2)}) collective-permute-start(bf16[200,480]{1,0:T(8,128)(2,1)} %get-tuple-element.215), channel_id=1, source_target_pairs={{0,24},{4,28},{8,0},{12,4},{16,8},{20,12},{24,16},{28,20},{1,25},{... | collective-permute-start | bytes 576008 | tf_op jit(solution)/shard_map/ppermute | solution.py:496
  299.2 28.9 %collective-permute-start.53 = (bf16[600,128]{1,0:T(8,128)(2,1)}, bf16[600,128]{1,0:T(8,128)(2,1)}, u32[]{:S(2)}, u32[]{:S(2)}) collective-permute-start(bf16[600,128]{1,0:T(8,128)(2,1)} %get-tuple-element.188), channel_id=1, source_target_pairs={{0,8},{4,12},{8,16},{12,20},{16,24},{20,28},{24,0},{28,4},{1,9},{5... | collective-permute-start | bytes 460808 | tf_op jit(solution)/shard_map/ppermute | solution.py:517
  325.1 26.5 %collective-permute-start.45 = (bf16[480,512]{1,0:T(8,128)(2,1)}, bf16[480,512]{1,0:T(8,128)(2,1)S(1)}, u32[]{:S(2)}, u32[]{:S(2)}) collective-permute-start(bf16[480,512]{1,0:T(8,128)(2,1)} %slice.162), channel_id=1, source_target_pairs={{0,1},{1,0},{2,3},{3,2},{4,5},{5,4},{6,7},{7,6},{8,9},{9,8},{10,11... | collective-permute-start | bytes 1474568 | tf_op jit(solution)/shard_map/ppermute | solution.py:460
  332.2 16.5 %collective-permute-start.47 = (bf16[200,480]{1,0:T(8,128)(2,1)S(1)}, bf16[200,480]{1,0:T(8,128)(2,1)S(1)}, u32[]{:S(2)}, u32[]{:S(2)}) collective-permute-start(bf16[200,480]{1,0:T(8,128)(2,1)S(1)} %get-tuple-element.190), channel_id=1, source_target_pairs={{0,16},{4,20},{8,24},{12,28},{16,0},{20,4},{24,8},{28,12},{1,17},{... | collective-permute-start | bytes 576008 | tf_op jit(solution)/shard_map/ppermute | solution.py:517
  332.2 17.6 %collective-permute-start.48 = (bf16[200,480]{1,0:T(8,128)(2,1)S(1)}, bf16[200,480]{1,0:T(8,128)(2,1)S(1)}, u32[]{:S(2)}, u32[]{:S(2)}) collective-permute-start(bf16[200,480]{1,0:T(8,128)(2,1)S(1)} %get-tuple-element.190), channel_id=1, source_target_pairs={{0,24},{4,28},{8,0},{12,4},{16,8},{20,12},{24,16},{28,20},{1,25},{... | collective-permute-start | bytes 576008 | tf_op jit(solution)/shard_map/ppermute | solution.py:517
  338.5 16.8 %collective-permute-start.56 = (bf16[4,600,128]{2,1,0:T(8,128)(2,1)S(1)}, bf16[4,600,128]{2,1,0:T(8,128)(2,1)S(1)}, u32[]{:S(2)}, u32[]{:S(2)}) collective-permute-start(bf16[4,600,128]{2,1,0:T(8,128)(2,1)S(1)} %bitcast_dynamic-update-slice_fusion.4), channel_id=1, source_target_pairs={{0,4},{4,0},{8,12},{12,8},{16,20},{20,16},{24,28},{28,24},{1,5},{5... | collective-permute-start | bytes 1843208 | tf_op jit(solution)/shard_map/ppermute | solution.py:517
  350.5 21.0 %collective-permute-start.49 = (bf16[4,200,480]{2,1,0:T(8,128)(2,1)}, bf16[4,200,480]{2,1,0:T(8,128)(2,1)S(1)}, u32[]{:S(2)}, u32[]{:S(2)}) collective-permute-start(bf16[4,200,480]{2,1,0:T(8,128)(2,1)} %bitcast_dynamic-update-slice_fusion), channel_id=1, source_target_pairs={{0,4},{4,0},{8,12},{12,8},{16,20},{20,16},{24,28},{28,24},{1,5},{5... | collective-permute-start | bytes 2304008 | tf_op jit(solution)/shard_map/ppermute | solution.py:517
  (75 other events, 526.6 us)
Sparse Core Ops, SparseCore 0:
  204.9 52.6 all-gather.4
  260.3 57.0 all-gather.2

commit v8 on v7

--- a/solution.py
+++ b/solution.py
@@ -22,6 +22,7 @@
 LANE = 128
 LIVE = (3, 2)
 ROWS = 1024
+WIDE = 512
 
 NORM_EPS = 1e-05
 ROPE_BASE = 100000.0
@@ -341,8 +342,9 @@
     gj = gj_ref[...]
     for half, out_ref in enumerate((keep_ref, send_ref)):
         rows = slice(half * HALF, (half + 1) * HALF)
-        out_ref[:D, :] = dot(gj, nm_ref[rows, :], 1, 1).astype(BF16)
-        out_ref[D:, :] = jnp.zeros((ROWS - D, HALF), BF16)
+        out_ref[:D, :HALF] = dot(gj, nm_ref[rows, :], 1, 1).astype(BF16)
+        out_ref[D:, :] = jnp.zeros((ROWS - D, WIDE), BF16)
+        out_ref[:D, HALF:] = jnp.zeros((D, WIDE - HALF), BF16)
     gnm_ref[:HALF, :] = dot(wo_ref[...], gj, 0, 0)
     gnm_ref[HALF:, :] = dot(wg_ref[...], gj, 0, 0)
 
@@ -366,10 +368,11 @@
     ):
         half = rows.start // HALF
         out_ref = (keep_ref, send_ref)[half]
-        out_ref[:D, :] = dot(gj, nm_ref[rows, :], 1, 1).astype(BF16)
-        out_ref[D : D + 16, :] = gain_rows(gnm * x * level).astype(BF16)
-        out_ref[D + 16 : D + 32, :] = ggain_ref[half].astype(BF16)
-        out_ref[D + 32 :, :] = jnp.zeros((ROWS - D - 32, HALF), BF16)
+        out_ref[:D, :HALF] = dot(gj, nm_ref[rows, :], 1, 1).astype(BF16)
+        out_ref[D : D + 16, :HALF] = gain_rows(gnm * x * level).astype(BF16)
+        out_ref[D + 16 : D + 32, :HALF] = ggain_ref[half].astype(BF16)
+        out_ref[D + 32 :, :HALF] = jnp.zeros((ROWS - D - 32, HALF), BF16)
+        out_ref[:, HALF:] = jnp.zeros((ROWS, WIDE - HALF), BF16)
         grad_ref[rows, :] = (gmid_ref[rows, :] + scaled * level - x * pull).astype(BF16)
 
 
@@ -687,19 +690,21 @@
     gate_sum = add(gate_keep, hold(swap(gate_send, "col"), ggain_mid))
     up_sum = add(up_keep, hold(swap(up_send, "col"), ggain_mid))
 
-    dq_far, own_far, other_far = attend_back(
-        where_far, begin, q_far, kv_far, kv_far_got, gatt_far, lse_far, after=(down_x, gate_sum, up_sum)
-    )
-    gate_x = reduce_first(gate_sum, count, (dq_far,))
-
     def out_grads(att):
         send = dot(att, gb[HALF:], 1, 1).astype(BF16)
         return add(dot(att, gb[:HALF], 1, 1), swap(send, "col"))
 
     wo_far_sum = out_grads(att_far)
     wo_near_sum = out_grads(att_near)
-    got_far = swap(hold(other_far, gate_x), "col")
-    joined = shape((ROWS, HALF))
+
+    dq_far, own_far, other_far = attend_back(
+        where_far, begin, q_far, kv_far, kv_far_got, gatt_far, lse_far, after=(down_x, gate_sum, up_sum)
+    )
+    gate_x = reduce_first(gate_sum, count, (dq_far,))
+    down_z = reduce_rest(down_x, count, (dq_far,))
+
+    got_far = swap(hold(other_far, gate_x, down_z), "col")
+    joined = shape((ROWS, WIDE))
     gnm_in_part, far_keep, far_send = run(
         joined_far_kernel,
         (dq_far, own_far, got_far, cosine, sine, w_far, w_far_got, nm_in),
@@ -708,13 +713,14 @@
         after=(gate_x,),
         scratch=[pltpu.VMEM((D, LOCAL), BF16)],
     )
-    down_z = reduce_rest(down_x, count, (far_keep,))
+    gate_z = reduce_rest(gate_x, count, (far_keep,))
     up_x = reduce_first(hold(up_sum, gate_x), count, (far_keep,))
+    wo_sum = add(wo_near_sum, swap(wo_far_sum, "row"))
+    wo_sum = jnp.pad(wo_sum, ((0, 0), (0, WIDE - HALF)))
     dq_near, own_near, other_near = attend_back(
-        where_near, begin, q_near, kv_near, kv_near_got, gatt_near, lse_near, after=(down_z, up_x, wo_far_sum, wo_near_sum)
-    )
-    wo_sum = add(wo_near_sum, swap(wo_far_sum, "row"))
-    far_sum = add(far_keep, hold(swap(hold(far_send, down_z, up_x), "col"), dq_near))
+        where_near, begin, q_near, kv_near, kv_near_got, gatt_near, lse_near, after=(gate_z, up_x, wo_far_sum, wo_near_sum)
+    )
+    far_sum = add(far_keep, hold(swap(hold(far_send, gate_z, up_x), "col"), dq_near))
     got_near = swap(hold(other_near, far_sum, wo_sum), "col")
     near_keep, near_send, grad = run(
         joined_near_kernel,
@@ -726,9 +732,9 @@
         4 * LOCAL * D * D,
         scratch=[pltpu.VMEM((D, LOCAL), BF16)],
     )
-    gate_z = reduce_rest(gate_x, count, (grad,))
+    up_z = reduce_rest(up_x, count, (grad,))
     far_back = swap(far_sum, "row")
-    last_sum = add(near_keep, swap(hold(near_send, far_back, gate_z), "col"), far_back)
+    last_sum = add(near_keep, swap(hold(near_send, far_back, up_z), "col"), far_back)
 
     def feature_cols(array):
         return in_window(array[:HALF], swap(array[HALF:], "col")).T
@@ -740,19 +746,18 @@
 
     last_x = reduce_first(last_sum, count)
     out_x = reduce_first(wo_sum, count)
-    up_z = reduce_rest(up_x, count, (last_x,))
     last_z = reduce_rest(jnp.concatenate([last_x, out_x], axis=-2), count)
     out_back = hold(swap(hold(out_send, gnm_back), "row"), last_z)
     block_out = feature_cols((mid + out_part + out_back.astype(F32)).astype(BF16))
     input_grad = feature_cols(hold(grad, last_x))
     down_grad = widened(hold(spread(down_z), last_x))
     gate_grad = widened(hold(spread(gate_z), last_x))
-    up_rest = gather_rest(up_z, count, (last_z,))
-    up_grad = widened(gather_first(up_rest, count).reshape(up_sum.shape))
+    up_rest = gather_rest(up_z, count, (last_x,))
+    up_grad = widened(gather_first(up_rest, count, (last_z,)).reshape(up_sum.shape))
     last = gather_first(gather_rest(last_z, count), count)
     last, out_weight_grad = last[..., : ROWS // count, :], last[..., ROWS // count :, :]
-    last = last.reshape(last_sum.shape).astype(F32)
-    out_weight_grad = out_weight_grad.reshape(wo_sum.shape).astype(F32)
+    last = last.reshape(last_sum.shape)[:, :HALF].astype(F32)
+    out_weight_grad = out_weight_grad.reshape(wo_sum.shape)[:, :HALF].astype(F32)
     gain_grads = jnp.stack([last[D], last[D + 16]])
     gain_grads = gain_grads + swap(gain_grads, "row")
     return (

time: 391 us -> 390 us (level)
  waiting for transfers between devices: 76.4 us -> 94.5 us
  starting transfers between devices: 77.7 us -> 61.9 us
    all_gather x2, waiting for transfers between devices: 3.82 us -> 20.1 us  [spread(): return lax.all_gather(part, 'dp', axis=0, tiled=True)]
    ppermute x8, starting transfers between devices: 23.8 us -> 13.6 us  [gather_stage(): lax.ppermute(part, 'dp', shift_pairs(count, stride, size, step))]
    ppermute x17, starting transfers between devices: 35.8 us -> 30.2 us  [reduce_stage(): lax.ppermute(sent, 'dp', shift_pairs(count, stride, size, step))]
    ppermute x8, waiting for transfers between devices: 22.1 us -> 17.3 us  [gather_stage(): lax.ppermute(part, 'dp', shift_pairs(count, stride, size, step))]
    unnamed x97 -> x93, local copies, waits for them, and re-layouts: 14.5 us -> 14.2 us
  transfers between devices with their start and end apart: 60 -> 60, of which waited for: 22 -> 21; matrix products, arithmetic and copies ran while one was open for 18% -> 17% of each run, Pallas kernels for 28% -> 28%
where the time goes in v8:
time: 390 us; the launch traced here: 385 us
  Pallas kernels  130 us (33%)
  waiting for transfers between devices  94.5 us (24%)
  starting transfers between devices  61.9 us (16%)
  local copies, waits for them, and re-layouts  39.4 us (10%)
  other arithmetic  38.9 us (10%)
  between operations  15 us (4%)
  matrix products  5.56 us (1%)
    pallas_call x14, Pallas kernels, run(): pl.pallas_call(body, grid=grid if grid is not None else (1,), in_specs=li...  130 us
    ppermute x33, waiting for transfers between devices, swap(): return lax.ppermute(array, axis, [(0, 1), (1, 0)])  37.1 us
    ppermute x17, starting transfers between devices, reduce_stage(): lax.ppermute(sent, 'dp', shift_pairs(count, stride, size, step))  30.2 us
    all_gather x2, waiting for transfers between devices, spread(): return lax.all_gather(part, 'dp', axis=0, tiled=True)  20.1 us
    ppermute x17, waiting for transfers between devices, reduce_stage(): lax.ppermute(sent, 'dp', shift_pairs(count, stride, size, step))  20 us
    ppermute x33, starting transfers between devices, swap(): return lax.ppermute(array, axis, [(0, 1), (1, 0)])  18 us
    ppermute x8, waiting for transfers between devices, gather_stage(): lax.ppermute(part, 'dp', shift_pairs(count, stride, size, step))  17.3 us
    unnamed x93, local copies, waits for them, and re-layouts  14.2 us
  transfers between devices with their start and end apart: 60, of which 21 were waited for; matrix products, arithmetic and copies ran while one was open for 17% of the time, Pallas kernels for 28%

profile of v8, /device:TPU:0, one launch (start us, length us, event | category | flops | bytes accessed | tf_op | source)
XLA Modules:
  0.0 385.0 jit_solution(4088574489331084689)
XLA Ops:
  20.1 4.5 %shard_map.203 = (bf16[960,512]{1,0:T(8,128)(2,1)}, bf16[576,512]{1,0:T(8,128)(2,1)}, bf16[384,512]{1,0:T(8,128)(2,1)}) custom-call(bf16[480,512]{1,0:T(8,128)(2,1)} %get-tuple-element.197.refs_0_.refs_6_.refs_9_, bf16[480,512]{1,0:T(8,128)(2,1)} %copy-done.15, f32[480,1]{1,0:T(8,128)} %copy.27.refs_2_.refs_11_, f32[480,1]{1,0:T(8,128)} %copy.28.refs_3_.refs_12_, ...), custom_call_target="tpu_custom_call" | custom-call | flops 28311552 | bytes 147816 | tf_op jit(solution)/shard_map/pallas_call | solution.py:70
  27.3 11.3 %shard_map.204 = (bf16[576,512]{1,0:T(8,128)(2,1)}, f32[3,8,512]{2,1,0:T(8,128)}) custom-call(s32[2]{0:T(128)} %pad_add_fusion.refs_0_, s32[1,512]{1,0:T(1,128)} %broadcast_select_fusion.8.refs_1_, bf16[576,512]{1,0:T(8,128)(2,1)} %get-tuple-element.89.refs_2_, bf16[384,512]{1,0:T(8,128)(2,1)} %get-tuple-element.90.refs_3_.refs_4_, ...), custom_call_target="tpu_custom_call" | custom-call | flops 180000000 | bytes 84111 | tf_op jit(solution)/shard_map/pallas_call | solution.py:70
  42.2 4.0 %shard_map.205 = (bf16[576,512]{1,0:T(8,128)(2,1)}, bf16[384,512]{1,0:T(8,128)(2,1)}) custom-call(bf16[960,512]{1,0:T(8,128)(2,1)} %get-tuple-element.92.refs_0_.refs_7_, f32[32,512]{1,0:T(8,128)} %get-tuple-element.231.refs_4_.refs_1_.refs_3_, f32[32,512]{1,0:T(8,128)} %get-tuple-element.230.refs_5_.refs_2_.refs_4_, bf16[960,480]{1,0:T(8,128)(2,1)} %copy-done.16, ...), custom_call_target="tpu_custom_call" | custom-call | flops 28311552 | bytes 118210 | tf_op jit(solution)/shard_map/pallas_call | solution.py:70
  46.2 8.2 %collective-permute-done.9.refs_4_.refs_8_ = bf16[576,480]{1,0:T(8,128)(2,1)S(1)} collective-permute-done((bf16[576,480]{1,0:T(8,128)(2,1)S(1)}, bf16[576,480]{1,0:T(8,128)(2,1)S(1)}, u32[]{:S(2)}, u32[]{:S(2)}) %collective-permute-start.9) | collective-permute-done | bytes 552992 | tf_op jit(solution)/shard_map/ppermute | solution.py:463
  60.0 8.6 %shard_map.206 = (bf16[576,512]{1,0:T(8,128)(2,1)}, f32[3,8,512]{2,1,0:T(8,128)}) custom-call(s32[2]{0:T(128)} %pad_add_fusion.1.refs_0_, s32[1,512]{1,0:T(1,128)} %broadcast_select_fusion.8.refs_1_, bf16[576,512]{1,0:T(8,128)(2,1)} %get-tuple-element.95.refs_2_, bf16[384,512]{1,0:T(8,128)(2,1)} %get-tuple-element.96.refs_3_.refs_4_, ...), custom_call_target="tpu_custom_call" | custom-call | flops 180000000 | bytes 84111 | tf_op jit(solution)/shard_map/pallas_call | solution.py:70
  68.6 5.7 %shard_map.207 = (f32[960,512]{1,0:T(8,128)}, bf16[960,512]{1,0:T(8,128)(2,1)}) custom-call(bf16[576,512]{1,0:T(8,128)(2,1)} %get-tuple-element.91.refs_0_, bf16[576,512]{1,0:T(8,128)(2,1)} %get-tuple-element.97.refs_1_, bf16[576,480]{1,0:T(8,128)(2,1)} %bitcast.202, bf16[576,480]{1,0:T(8,128)(2,1)} %collective-permute-done.8.refs_3_.refs_7_, ...), custom_call_target="tpu_custom_call" | custom-call | flops 28311552 | bytes 219824 | tf_op jit(solution)/shard_map/pallas_call | solution.py:70
  74.3 4.8 %collective-permute-start.16 = (bf16[960,512]{1,0:T(8,128)(2,1)}, bf16[960,512]{1,0:T(8,128)(2,1)S(1)}, u32[]{:S(2)}, u32[]{:S(2)}) collective-permute-start(bf16[960,512]{1,0:T(8,128)(2,1)} %get-tuple-element.100.refs_0_), channel_id=1, source_target_pairs={{0,2},{2,0},{1,3},{3,1},{4,6},{6,4},{5,7},{7,5},{8,10},{10,8},{9,1... | collective-permute-start | bytes 2949128 | tf_op jit(solution)/shard_map/ppermute | solution.py:463
  79.1 2.9 collective-permute-done.15.refs_8_.refs_1_
  83.0 15.8 %shard_map.208 = (f32[960,512]{1,0:T(8,128)}, f32[960,512]{1,0:T(8,128)}, bf16[1280,512]{1,0:T(8,128)(2,1)}, bf16[1280,512]{1,0:T(8,128)(2,1)}, bf16[1280,512]{1,0:T(8,128)(2,1)}) custom-call(bf16[960,512]{1,0:T(8,128)(2,1)} %get-tuple-element.100.refs_0_, bf16[960,512]{1,0:T(8,128)(2,1)} %copy-done, bf16[480,1280]{1,0:T(8,128)(2,1)} %refs_2_.3, ...), custom_call_target="tpu_custom_call" | custom-call | flops 226492416 | bytes 516096 | tf_op jit(solution)/shard_map/pallas_call | solution.py:70
  98.8 3.7 collective-permute-done.16.refs_0_.refs_1_
  103.4 15.1 %shard_map.209 = (bf16[960,512]{1,0:T(8,128)(2,1)}, bf16[960,512]{1,0:T(8,128)(2,1)}, bf16[1280,512]{1,0:T(8,128)(2,1)}, bf16[1280,512]{1,0:T(8,128)(2,1)}, bf16[1280,512]{1,0:T(8,128)(2,1)}) custom-call(bf16[960,512]{1,0:T(8,128)(2,1)} %copy-done.19, bf16[960,512]{1,0:T(8,128)(2,1)} %copy-done.7, bf16[480,1280]{1,0:T(8,128)(2,1)} %refs_2_.3, ...), custom_call_target="tpu_custom_call" | custom-call | flops 226492416 | bytes 457113 | tf_op jit(solution)/shard_map/pallas_call | solution.py:70
  118.6 7.1 %shard_map.210 = (bf16[4800,128]{1,0:T(8,128)(2,1)}, bf16[4800,128]{1,0:T(8,128)(2,1)}) custom-call(bf16[960,512]{1,0:T(8,128)(2,1)} %copy-done, bf16[960,512]{1,0:T(8,128)(2,1)} %copy-done.7, bf16[1280,512]{1,0:T(8,128)(2,1)} %get-tuple-element.102.refs_8_.refs_2_, bf16[1280,512]{1,0:T(8,128)(2,1)} %get-tuple-element.107.refs_3_), custom_call_target="tpu_custom_call" | custom-call | flops 75497472 | bytes 211353 | tf_op jit(solution)/shard_map/pallas_call | solution.py:70
  126.1 9.2 %shard_map.211 = (bf16[4800,128]{1,0:T(8,128)(2,1)}, bf16[4800,128]{1,0:T(8,128)(2,1)}, bf16[4800,128]{1,0:T(8,128)(2,1)}, bf16[4800,128]{1,0:T(8,128)(2,1)}) custom-call(bf16[960,512]{1,0:T(8,128)(2,1)} %get-tuple-element.100.refs_0_, bf16[960,512]{1,0:T(8,128)(2,1)} %copy-done.19, bf16[1280,512]{1,0:T(8,128)(2,1)} %get-tuple-element.110.refs_2_, ...), custom_call_target="tpu_custom_call" | custom-call | flops 150994944 | bytes 363724 | tf_op jit(solution)/shard_map/pallas_call | solution.py:70
  135.3 14.6 %collective-permute-done.17.refs_3_ = bf16[960,512]{1,0:T(8,128)(2,1)S(1)} collective-permute-done((bf16[960,512]{1,0:T(8,128)(2,1)S(1)}, bf16[960,512]{1,0:T(8,128)(2,1)S(1)}, u32[]{:S(2)}, u32[]{:S(2)}) %collective-permute-start.17) | collective-permute-done | bytes 983072 | tf_op jit(solution)/shard_map/ppermute | solution.py:463
  154.5 8.3 %shard_map.212 = (f32[960,512]{1,0:T(8,128)}, bf16[960,512]{1,0:T(8,128)(2,1)}, bf16[576,512]{1,0:T(8,128)(2,1)}, bf16[576,512]{1,0:T(8,128)(2,1)}, f32[2,16,480]{2,1,0:T(8,128)}) custom-call(bf16[960,512]{1,0:T(8,128)(2,1)} %copy-done, f32[960,512]{1,0:T(8,128)} %get-tuple-element.99.refs_1_, f32[960,512]{1,0:T(8,128)} %get-tuple-element.106.refs_2_, ...), custom_call_target="tpu_custom_call" | custom-call | flops 28311552 | bytes 369123 | tf_op jit(solution)/shard_map/pallas_call | solution.py:70
  162.7 6.2 %collective-permute-done.22 = bf16[4,600,128]{2,1,0:T(8,128)(2,1)S(1)} collective-permute-done((bf16[4,600,128]{2,1,0:T(8,128)(2,1)}, bf16[4,600,128]{2,1,0:T(8,128)(2,1)S(1)}, u32[]{:S(2)}, u32[]{:S(2)}) %collective-permute-start.22) | collective-permute-done | bytes 614432 | tf_op jit(solution)/shard_map/ppermute | solution.py:499
  169.0 3.2 add_convert_fusion
  181.4 10.2 %shard_map.213 = (f32[576,512]{1,0:T(8,128)}, f32[2,3,64,512]{3,2,1,0:T(8,128)}, bf16[2,3,64,512]{3,2,1,0:T(8,128)(2,1)}) custom-call(s32[2]{0:T(128)} %pad_add_fusion.1.refs_0_, s32[1,512]{1,0:T(1,128)} %broadcast_select_fusion.8.refs_1_, bf16[576,512]{1,0:T(8,128)(2,1)} %get-tuple-element.95.refs_2_, bf16[384,512]{1,0:T(8,128)(2,1)} %get-tuple-element.96.refs_3_.refs_4_, ...), custom_call_target="tpu_custom_call" | custom-call | flops 420000000 | bytes 154890 | tf_op jit(solution)/shard_map/pallas_call | solution.py:70
  202.3 6.1 %shard_map.214 = (f32[960,512]{1,0:T(8,128)}, bf16[1024,512]{1,0:T(8,128)(2,1)}, bf16[1024,512]{1,0:T(8,128)(2,1)}) custom-call(f32[576,512]{1,0:T(8,128)} %get-tuple-element.128.refs_0_, f32[2,3,64,512]{3,2,1,0:T(8,128)} %get-tuple-element.130.refs_1_, bf16[2,3,64,512]{3,2,1,0:T(8,128)(2,1)} %copy-done.35, ...), custom_call_target="tpu_custom_call" | custom-call | flops 56623104 | bytes 281395 | tf_op jit(solution)/shard_map/pallas_call | solution.py:70
  216.9 3.8 collective-permute-start.35
  222.2 13.7 %shard_map.215 = (f32[576,512]{1,0:T(8,128)}, f32[2,3,64,512]{3,2,1,0:T(8,128)}, bf16[2,3,64,512]{3,2,1,0:T(8,128)(2,1)}) custom-call(s32[2]{0:T(128)} %pad_add_fusion.refs_0_, s32[1,512]{1,0:T(1,128)} %broadcast_select_fusion.8.refs_1_, bf16[576,512]{1,0:T(8,128)(2,1)} %get-tuple-element.89.refs_2_, bf16[384,512]{1,0:T(8,128)(2,1)} %get-tuple-element.90.refs_3_.refs_4_, ...), custom_call_target="tpu_custom_call" | custom-call | flops 420000000 | bytes 154890 | tf_op jit(solution)/shard_map/pallas_call | solution.py:70
  237.5 3.3 collective-permute-start.38
  244.3 10.1 %shard_map.216 = (bf16[1024,512]{1,0:T(8,128)(2,1)}, bf16[1024,512]{1,0:T(8,128)(2,1)}, bf16[960,512]{1,0:T(8,128)(2,1)}) custom-call(f32[576,512]{1,0:T(8,128)} %get-tuple-element.143.refs_0_, f32[2,3,64,512]{3,2,1,0:T(8,128)} %get-tuple-element.144.refs_1_, bf16[2,3,64,512]{3,2,1,0:T(8,128)(2,1)} %copy-done.36, ...), custom_call_target="tpu_custom_call" | custom-call | flops 56623104 | bytes 401318 | tf_op jit(solution)/shard_map/pallas_call | solution.py:70
  258.3 3.2 collective-permute-done.37
  268.6 2.8 collective-permute-done.43
  271.6 3.5 collective-permute-start.53
  277.5 6.5 %collective-permute-done.42 = bf16[4,128,512]{2,1,0:T(8,128)(2,1)S(1)} collective-permute-done((bf16[4,128,512]{2,1,0:T(8,128)(2,1)S(1)}, bf16[4,128,512]{2,1,0:T(8,128)(2,1)S(1)}, u32[]{:S(2)}, u32[]{:S(2)}) %collective-permute-start.42) | collective-permute-done | bytes 524320 | tf_op jit(solution)/shard_map/ppermute | solution.py:499
  284.9 3.3 collective-permute-start.44
  293.9 3.4 collective-permute-start.46
  303.2 20.1 %all-gather.3.cloned.1.call-done = bf16[4800,128]{1,0:T(8,128)(2,1)} async-done(((bf16[600,128]{1,0:T(8,128)(2,1)}), bf16[4800,128]{1,0:T(8,128)(2,1)}) %all-gather.3.cloned.1.call-update) | async-done | bytes 1228816 | tf_op jit(solution)/shard_map/all_gather | solution.py:547
  341.4 7.6 %collective-permute-done.50 = bf16[200,512]{1,0:T(8,128)(2,1)S(1)} collective-permute-done((bf16[200,512]{1,0:T(8,128)(2,1)S(1)}, bf16[200,512]{1,0:T(8,128)(2,1)S(1)}, u32[]{:S(2)}, u32[]{:S(2)}) %collective-permute-start.50) | collective-permute-done | bytes 204832 | tf_op jit(solution)/shard_map/ppermute | solution.py:520
  362.3 8.5 %collective-permute-done.52 = bf16[4,200,512]{2,1,0:T(8,128)(2,1)S(1)} collective-permute-done((bf16[4,200,512]{2,1,0:T(8,128)(2,1)}, bf16[4,200,512]{2,1,0:T(8,128)(2,1)S(1)}, u32[]{:S(2)}, u32[]{:S(2)}) %collective-permute-start.52) | collective-permute-done | bytes 819232 | tf_op jit(solution)/shard_map/ppermute | solution.py:520
  (296 shorter events, 130.6 us)
Async XLA Ops:
  7.2 281.0 %all-gather.5.cloned.1.call-start = ((), (), s32[]{:S(2)}) async-start(), calls=%async_computation.1 | async-start | bytes 1382400 | tf_op jit(solution)/shard_map/all_gather | solution.py:547
  9.2 29.4 %collective-permute-start.5 = (bf16[960,480]{1,0:T(8,128)(2,1)S(1)}, bf16[960,480]{1,0:T(8,128)(2,1)S(1)}, u32[]{:S(2)}, u32[]{:S(2)}) collective-permute-start(bf16[960,480]{1,0:T(8,128)(2,1)S(1)} %pad_maximum_fusion.1.refs_6_.refs_5_), channel_id=1, source_target_pairs={{0,2},{2,0},{1,3},{3,1},{4,6},{6,4},{5,7},{7,5},{8,10},{10,8},{9,1... | collective-permute-start | bytes 2764808 | tf_op jit(solution)/shard_map/ppermute | solution.py:463
  38.8 16.7 %collective-permute-start.8 = (bf16[576,480]{1,0:T(8,128)(2,1)S(1)}, bf16[576,480]{1,0:T(8,128)(2,1)}, u32[]{:S(2)}, u32[]{:S(2)}) collective-permute-start(bf16[576,480]{1,0:T(8,128)(2,1)S(1)} %bitcast.205), channel_id=1, source_target_pairs={{0,1},{1,0},{2,3},{3,2},{4,5},{5,4},{6,7},{7,6},{8,9},{9,8},{10,11... | collective-permute-start | bytes 1658888 | tf_op jit(solution)/shard_map/ppermute | solution.py:463
  54.9 24.1 %collective-permute-start.14 = (bf16[480,1280]{1,0:T(8,128)(2,1)}, bf16[480,1280]{1,0:T(8,128)(2,1)}, u32[]{:S(2)}, u32[]{:S(2)}) collective-permute-start(bf16[480,1280]{1,0:T(8,128)(2,1)} %bitcast.23.refs_6_), channel_id=1, source_target_pairs={{0,1},{1,0},{2,3},{3,2},{4,5},{5,4},{6,7},{7,6},{8,9},{9,8},{10,11... | collective-permute-start | bytes 3686408 | tf_op jit(solution)/shard_map/ppermute | solution.py:463
  55.0 24.1 %collective-permute-start.12 = (bf16[480,1280]{1,0:T(8,128)(2,1)}, bf16[480,1280]{1,0:T(8,128)(2,1)}, u32[]{:S(2)}, u32[]{:S(2)}) collective-permute-start(bf16[480,1280]{1,0:T(8,128)(2,1)} %refs_2_.3), channel_id=1, source_target_pairs={{0,1},{1,0},{2,3},{3,2},{4,5},{5,4},{6,7},{7,6},{8,9},{9,8},{10,11... | collective-permute-start | bytes 3686408 | tf_op jit(solution)/shard_map/ppermute | solution.py:463
  55.5 23.6 %collective-permute-start.13 = (bf16[480,1280]{1,0:T(8,128)(2,1)}, bf16[480,1280]{1,0:T(8,128)(2,1)}, u32[]{:S(2)}, u32[]{:S(2)}) collective-permute-start(bf16[480,1280]{1,0:T(8,128)(2,1)} %refs_4_.3), channel_id=1, source_target_pairs={{0,1},{1,0},{2,3},{3,2},{4,5},{5,4},{6,7},{7,6},{8,9},{9,8},{10,11... | collective-permute-start | bytes 3686408 | tf_op jit(solution)/shard_map/ppermute | solution.py:463
  57.4 24.6 %collective-permute-start.15 = (bf16[960,512]{1,0:T(8,128)(2,1)S(1)}, bf16[960,512]{1,0:T(8,128)(2,1)S(1)}, u32[]{:S(2)}, u32[]{:S(2)}) collective-permute-start(bf16[960,512]{1,0:T(8,128)(2,1)S(1)} %pad_maximum_fusion.2.refs_1_.refs_0_), channel_id=1, source_target_pairs={{0,2},{2,0},{1,3},{3,1},{4,6},{6,4},{5,7},{7,5},{8,10},{10,8},{9,1... | collective-permute-start | bytes 2949128 | tf_op jit(solution)/shard_map/ppermute | solution.py:463
  74.3 28.2 %collective-permute-start.16 = (bf16[960,512]{1,0:T(8,128)(2,1)}, bf16[960,512]{1,0:T(8,128)(2,1)S(1)}, u32[]{:S(2)}, u32[]{:S(2)}) collective-permute-start(bf16[960,512]{1,0:T(8,128)(2,1)} %get-tuple-element.100.refs_0_), channel_id=1, source_target_pairs={{0,2},{2,0},{1,3},{3,1},{4,6},{6,4},{5,7},{7,5},{8,10},{10,8},{9,1... | collective-permute-start | bytes 2949128 | tf_op jit(solution)/shard_map/ppermute | solution.py:463
  125.7 24.7 %collective-permute-start.19 = (bf16[4800,128]{1,0:T(8,128)(2,1)}, bf16[4800,128]{1,0:T(8,128)(2,1)}, u32[]{:S(2)}, u32[]{:S(2)}) collective-permute-start(bf16[4800,128]{1,0:T(8,128)(2,1)} %get-tuple-element.109), channel_id=1, source_target_pairs={{0,1},{1,0},{2,3},{3,2},{4,5},{5,4},{6,7},{7,6},{8,9},{9,8},{10,11... | collective-permute-start | bytes 3686408 | tf_op jit(solution)/shard_map/ppermute | solution.py:463
  125.7 24.2 %collective-permute-start.17 = (bf16[960,512]{1,0:T(8,128)(2,1)S(1)}, bf16[960,512]{1,0:T(8,128)(2,1)S(1)}, u32[]{:S(2)}, u32[]{:S(2)}) collective-permute-start(bf16[960,512]{1,0:T(8,128)(2,1)S(1)} %copy-done.42), channel_id=1, source_target_pairs={{0,2},{2,0},{1,3},{3,1},{4,6},{6,4},{5,7},{7,5},{8,10},{10,8},{9,1... | collective-permute-start | bytes 2949128 | tf_op jit(solution)/shard_map/ppermute | solution.py:463
  149.9 19.1 %collective-permute-start.20 = (bf16[4800,128]{1,0:T(8,128)(2,1)}, bf16[4800,128]{1,0:T(8,128)(2,1)S(1)}, u32[]{:S(2)}, u32[]{:S(2)}) collective-permute-start(bf16[4800,128]{1,0:T(8,128)(2,1)} %get-tuple-element.119), channel_id=1, source_target_pairs={{0,1},{1,0},{2,3},{3,2},{4,5},{5,4},{6,7},{7,6},{8,9},{9,8},{10,11... | collective-permute-start | bytes 3686408 | tf_op jit(solution)/shard_map/ppermute | solution.py:463
  149.9 19.1 %collective-permute-start.23 = (bf16[4800,128]{1,0:T(8,128)(2,1)}, bf16[4800,128]{1,0:T(8,128)(2,1)}, u32[]{:S(2)}, u32[]{:S(2)}) collective-permute-start(bf16[4800,128]{1,0:T(8,128)(2,1)} %get-tuple-element.126), channel_id=1, source_target_pairs={{0,1},{1,0},{2,3},{3,2},{4,5},{5,4},{6,7},{7,6},{8,9},{9,8},{10,11... | collective-permute-start | bytes 3686408 | tf_op jit(solution)/shard_map/ppermute | solution.py:463
  173.0 20.4 %collective-permute-start.21 = (bf16[4,600,128]{2,1,0:T(8,128)(2,1)}, bf16[4,600,128]{2,1,0:T(8,128)(2,1)}, u32[]{:S(2)}, u32[]{:S(2)}) collective-permute-start(bf16[4,600,128]{2,1,0:T(8,128)(2,1)} %dynamic-slice_bitcast_fusion.2), channel_id=1, source_target_pairs={{0,4},{4,0},{8,12},{12,8},{16,20},{20,16},{24,28},{28,24},{1,5},{5... | collective-permute-start | bytes 1843208 | tf_op jit(solution)/shard_map/ppermute | solution.py:499
  194.8 17.6 %collective-permute-start.31 = (bf16[4,600,128]{2,1,0:T(8,128)(2,1)S(1)}, bf16[4,600,128]{2,1,0:T(8,128)(2,1)S(1)}, u32[]{:S(2)}, u32[]{:S(2)}) collective-permute-start(bf16[4,600,128]{2,1,0:T(8,128)(2,1)S(1)} %dynamic-slice_bitcast_fusion), channel_id=1, source_target_pairs={{0,4},{4,0},{8,12},{12,8},{16,20},{20,16},{24,28},{28,24},{1,5},{5... | collective-permute-start | bytes 1843208 | tf_op jit(solution)/shard_map/ppermute | solution.py:499
  213.4 22.5 %collective-permute-start.34 = (bf16[1024,512]{1,0:T(8,128)(2,1)}, bf16[1024,512]{1,0:T(8,128)(2,1)S(1)}, u32[]{:S(2)}, u32[]{:S(2)}) collective-permute-start(bf16[1024,512]{1,0:T(8,128)(2,1)} %get-tuple-element.147), channel_id=1, source_target_pairs={{0,1},{1,0},{2,3},{3,2},{4,5},{5,4},{6,7},{7,6},{8,9},{9,8},{10,11... | collective-permute-start | bytes 3145736 | tf_op jit(solution)/shard_map/ppermute | solution.py:463
  216.9 19.4 %collective-permute-start.35 = (bf16[576,480]{1,0:T(8,128)(2,1)}, bf16[576,480]{1,0:T(8,128)(2,1)S(1)}, u32[]{:S(2)}, u32[]{:S(2)}) collective-permute-start(bf16[576,480]{1,0:T(8,128)(2,1)} %fusion.refs_11_), channel_id=1, source_target_pairs={{0,2},{2,0},{1,3},{3,1},{4,6},{6,4},{5,7},{7,5},{8,10},{10,8},{9,1... | collective-permute-start | bytes 1658888 | tf_op jit(solution)/shard_map/ppermute | solution.py:463
  222.2 101.1 %all-gather.3.cloned.1.call-start = ((), (), s32[]{:S(2)}) async-start(), calls=%async_computation | async-start | bytes 1382400 | tf_op jit(solution)/shard_map/all_gather | solution.py:547
  236.3 25.3 %collective-permute-start.37 = (bf16[1024,512]{1,0:T(8,128)(2,1)S(1)}, bf16[1024,512]{1,0:T(8,128)(2,1)S(1)}, u32[]{:S(2)}, u32[]{:S(2)}) collective-permute-start(bf16[1024,512]{1,0:T(8,128)(2,1)S(1)} %add_convert_fusion.4), channel_id=1, source_target_pairs={{0,2},{2,0},{1,3},{3,1},{4,6},{6,4},{5,7},{7,5},{8,10},{10,8},{9,1... | collective-permute-start | bytes 3145736 | tf_op jit(solution)/shard_map/ppermute | solution.py:463
  237.5 16.9 %collective-permute-start.38 = (bf16[600,128]{1,0:T(8,128)(2,1)S(1)}, bf16[600,128]{1,0:T(8,128)(2,1)S(1)}, u32[]{:S(2)}, u32[]{:S(2)}) collective-permute-start(bf16[600,128]{1,0:T(8,128)(2,1)S(1)} %get-tuple-element.209), channel_id=1, source_target_pairs={{0,8},{4,12},{8,16},{12,20},{16,24},{20,28},{24,0},{28,4},{1,9},{5... | collective-permute-start | bytes 460808 | tf_op jit(solution)/shard_map/ppermute | solution.py:499
  267.4 16.6 %collective-permute-start.42 = (bf16[4,128,512]{2,1,0:T(8,128)(2,1)S(1)}, bf16[4,128,512]{2,1,0:T(8,128)(2,1)S(1)}, u32[]{:S(2)}, u32[]{:S(2)}) collective-permute-start(bf16[4,128,512]{2,1,0:T(8,128)(2,1)S(1)} %dynamic-slice_bitcast_fusion.3), channel_id=1, source_target_pairs={{0,4},{4,0},{8,12},{12,8},{16,20},{20,16},{24,28},{28,24},{1,5},{5... | collective-permute-start | bytes 1572872 | tf_op jit(solution)/shard_map/ppermute | solution.py:499
  268.4 65.4 %collective-permute-start.18 = (bf16[960,512]{1,0:T(8,128)(2,1)}, bf16[960,512]{1,0:T(8,128)(2,1)}, u32[]{:S(2)}, u32[]{:S(2)}) collective-permute-start(bf16[960,512]{1,0:T(8,128)(2,1)} %get-tuple-element.105), channel_id=1, source_target_pairs={{0,2},{2,0},{1,3},{3,1},{4,6},{6,4},{5,7},{7,5},{8,10},{10,8},{9,1... | collective-permute-start | bytes 2949128 | tf_op jit(solution)/shard_map/ppermute | solution.py:463
  271.6 20.3 %collective-permute-start.53 = (bf16[600,128]{1,0:T(8,128)(2,1)}, bf16[600,128]{1,0:T(8,128)(2,1)}, u32[]{:S(2)}, u32[]{:S(2)}) collective-permute-start(bf16[600,128]{1,0:T(8,128)(2,1)} %get-tuple-element.179), channel_id=1, source_target_pairs={{0,8},{4,12},{8,16},{12,20},{16,24},{20,28},{24,0},{28,4},{1,9},{5... | collective-permute-start | bytes 460808 | tf_op jit(solution)/shard_map/ppermute | solution.py:520
  275.1 18.9 %collective-permute-start.54 = (bf16[600,128]{1,0:T(8,128)(2,1)}, bf16[600,128]{1,0:T(8,128)(2,1)}, u32[]{:S(2)}, u32[]{:S(2)}) collective-permute-start(bf16[600,128]{1,0:T(8,128)(2,1)} %get-tuple-element.179), channel_id=1, source_target_pairs={{0,16},{4,20},{8,24},{12,28},{16,0},{20,4},{24,8},{28,12},{1,17},{... | collective-permute-start | bytes 460808 | tf_op jit(solution)/shard_map/ppermute | solution.py:520
  276.7 20.6 %collective-permute-start.55 = (bf16[600,128]{1,0:T(8,128)(2,1)}, bf16[600,128]{1,0:T(8,128)(2,1)}, u32[]{:S(2)}, u32[]{:S(2)}) collective-permute-start(bf16[600,128]{1,0:T(8,128)(2,1)} %get-tuple-element.179), channel_id=1, source_target_pairs={{0,24},{4,28},{8,0},{12,4},{16,8},{20,12},{24,16},{28,20},{1,25},{... | collective-permute-start | bytes 460808 | tf_op jit(solution)/shard_map/ppermute | solution.py:520
  284.9 43.0 %collective-permute-start.44 = (bf16[200,512]{1,0:T(8,128)(2,1)}, bf16[200,512]{1,0:T(8,128)(2,1)}, u32[]{:S(2)}, u32[]{:S(2)}) collective-permute-start(bf16[200,512]{1,0:T(8,128)(2,1)} %get-tuple-element.204), channel_id=1, source_target_pairs={{0,8},{4,12},{8,16},{12,20},{16,24},{20,28},{24,0},{28,4},{1,9},{5... | collective-permute-start | bytes 614408 | tf_op jit(solution)/shard_map/ppermute | solution.py:499
  291.8 36.2 %collective-permute-start.45 = (bf16[200,512]{1,0:T(8,128)(2,1)}, bf16[200,512]{1,0:T(8,128)(2,1)}, u32[]{:S(2)}, u32[]{:S(2)}) collective-permute-start(bf16[200,512]{1,0:T(8,128)(2,1)} %get-tuple-element.205), channel_id=1, source_target_pairs={{0,16},{4,20},{8,24},{12,28},{16,0},{20,4},{24,8},{28,12},{1,17},{... | collective-permute-start | bytes 614408 | tf_op jit(solution)/shard_map/ppermute | solution.py:499
  293.9 34.1 %collective-permute-start.46 = (bf16[200,512]{1,0:T(8,128)(2,1)}, bf16[200,512]{1,0:T(8,128)(2,1)}, u32[]{:S(2)}, u32[]{:S(2)}) collective-permute-start(bf16[200,512]{1,0:T(8,128)(2,1)} %get-tuple-element.206), channel_id=1, source_target_pairs={{0,24},{4,28},{8,0},{12,4},{16,8},{20,12},{24,16},{28,20},{1,25},{... | collective-permute-start | bytes 614408 | tf_op jit(solution)/shard_map/ppermute | solution.py:499
  302.1 50.6 %collective-permute-start.56 = (bf16[4,600,128]{2,1,0:T(8,128)(2,1)}, bf16[4,600,128]{2,1,0:T(8,128)(2,1)}, u32[]{:S(2)}, u32[]{:S(2)}) collective-permute-start(bf16[4,600,128]{2,1,0:T(8,128)(2,1)} %bitcast_dynamic-update-slice_fusion.4), channel_id=1, source_target_pairs={{0,4},{4,0},{8,12},{12,8},{16,20},{20,16},{24,28},{28,24},{1,5},{5... | collective-permute-start | bytes 1843208 | tf_op jit(solution)/shard_map/ppermute | solution.py:520
  328.0 23.5 %collective-permute-start.48 = (bf16[480,512]{1,0:T(8,128)(2,1)S(1)}, bf16[480,512]{1,0:T(8,128)(2,1)S(1)}, u32[]{:S(2)}, u32[]{:S(2)}) collective-permute-start(bf16[480,512]{1,0:T(8,128)(2,1)S(1)} %slice.168), channel_id=1, source_target_pairs={{0,1},{1,0},{2,3},{3,2},{4,5},{5,4},{6,7},{7,6},{8,9},{9,8},{10,11... | collective-permute-start | bytes 1474568 | tf_op jit(solution)/shard_map/ppermute | solution.py:463
  333.7 16.0 %collective-permute-start.51 = (bf16[200,512]{1,0:T(8,128)(2,1)S(1)}, bf16[200,512]{1,0:T(8,128)(2,1)S(1)}, u32[]{:S(2)}, u32[]{:S(2)}) collective-permute-start(bf16[200,512]{1,0:T(8,128)(2,1)S(1)} %get-tuple-element.181), channel_id=1, source_target_pairs={{0,24},{4,28},{8,0},{12,4},{16,8},{20,12},{24,16},{28,20},{1,25},{... | collective-permute-start | bytes 614408 | tf_op jit(solution)/shard_map/ppermute | solution.py:520
  340.7 19.2 %collective-permute-start.47 = (bf16[480,512]{1,0:T(8,128)(2,1)}, bf16[480,512]{1,0:T(8,128)(2,1)}, u32[]{:S(2)}, u32[]{:S(2)}) collective-permute-start(bf16[480,512]{1,0:T(8,128)(2,1)} %slice.194), channel_id=1, source_target_pairs={{0,1},{1,0},{2,3},{3,2},{4,5},{5,4},{6,7},{7,6},{8,9},{9,8},{10,11... | collective-permute-start | bytes 1474568 | tf_op jit(solution)/shard_map/ppermute | solution.py:463
  350.5 20.3 %collective-permute-start.52 = (bf16[4,200,512]{2,1,0:T(8,128)(2,1)}, bf16[4,200,512]{2,1,0:T(8,128)(2,1)S(1)}, u32[]{:S(2)}, u32[]{:S(2)}) collective-permute-start(bf16[4,200,512]{2,1,0:T(8,128)(2,1)} %bitcast_dynamic-update-slice_fusion), channel_id=1, source_target_pairs={{0,4},{4,0},{8,12},{12,8},{16,20},{20,16},{24,28},{28,24},{1,5},{5... | collective-permute-start | bytes 2457608 | tf_op jit(solution)/shard_map/ppermute | solution.py:520
  (73 other events, 525.7 us)
Sparse Core Ops, SparseCore 0:
  222.3 45.8 all-gather.4
  270.4 52.8 all-gather.2

commit v9 on v8

--- a/solution.py
+++ b/solution.py
@@ -747,14 +747,15 @@
     last_x = reduce_first(last_sum, count)
     out_x = reduce_first(wo_sum, count)
     last_z = reduce_rest(jnp.concatenate([last_x, out_x], axis=-2), count)
+    last_rest = gather_rest(last_z, count)
     out_back = hold(swap(hold(out_send, gnm_back), "row"), last_z)
     block_out = feature_cols((mid + out_part + out_back.astype(F32)).astype(BF16))
     input_grad = feature_cols(hold(grad, last_x))
-    down_grad = widened(hold(spread(down_z), last_x))
-    gate_grad = widened(hold(spread(gate_z), last_x))
+    down_grad = widened(hold(spread(down_z), last_rest))
+    gate_grad = widened(hold(spread(gate_z), last_rest))
     up_rest = gather_rest(up_z, count, (last_x,))
     up_grad = widened(gather_first(up_rest, count, (last_z,)).reshape(up_sum.shape))
-    last = gather_first(gather_rest(last_z, count), count)
+    last = gather_first(last_rest, count)
     last, out_weight_grad = last[..., : ROWS // count, :], last[..., ROWS // count :, :]
     last = last.reshape(last_sum.shape)[:, :HALF].astype(F32)
     out_weight_grad = out_weight_grad.reshape(wo_sum.shape)[:, :HALF].astype(F32)

time: 390 us -> 389 us (level)
  starting transfers between devices: 61.9 us -> 70.9 us
    ppermute x17, waiting for transfers between devices: 20 us -> 27.6 us  [reduce_stage(): lax.ppermute(sent, 'dp', shift_pairs(count, stride, size, step))]
    ppermute x8, waiting for transfers between devices: 17.3 us -> 11.7 us  [gather_stage(): lax.ppermute(part, 'dp', shift_pairs(count, stride, size, step))]
    all_gather x2, waiting for transfers between devices: 20.1 us -> 14.7 us  [spread(): return lax.all_gather(part, 'dp', axis=0, tiled=True)]
    ppermute x8, starting transfers between devices: 13.6 us -> 18.8 us  [gather_stage(): lax.ppermute(part, 'dp', shift_pairs(count, stride, size, step))]
    dynamic_update_slice x6, local copies, waits for them, and re-layouts: 6.85 us -> 2.07 us  [gather_stage(): lax.dynamic_update_index_in_dim(whole_parts, got, (digit - step) % size,...]
    unnamed x93 -> x97, local copies, waits for them, and re-layouts: 14.2 us -> 15.6 us
  transfers between devices with their start and end apart: 60 -> 60, of which waited for: 21 -> 18; matrix products, arithmetic and copies ran while one was open for 17% -> 15% of each run, Pallas kernels for 28% -> 28%
where the time goes in v9:
time: 389 us; the launch traced here: 385 us
  Pallas kernels  129 us (33%)
  waiting for transfers between devices  91.7 us (24%)
  starting transfers between devices  70.9 us (18%)
  local copies, waits for them, and re-layouts  36.6 us (9%)
  other arithmetic  35.1 us (9%)
  between operations  15.1 us (4%)
  matrix products  5.77 us (1%)
    pallas_call x14, Pallas kernels, run(): pl.pallas_call(body, grid=grid if grid is not None else (1,), in_specs=li...  129 us
    ppermute x33, waiting for transfers between devices, swap(): return lax.ppermute(array, axis, [(0, 1), (1, 0)])  37.7 us
    ppermute x17, starting transfers between devices, reduce_stage(): lax.ppermute(sent, 'dp', shift_pairs(count, stride, size, step))  32.4 us
    ppermute x17, waiting for transfers between devices, reduce_stage(): lax.ppermute(sent, 'dp', shift_pairs(count, stride, size, step))  27.6 us
    ppermute x33, starting transfers between devices, swap(): return lax.ppermute(array, axis, [(0, 1), (1, 0)])  19.3 us
    ppermute x8, starting transfers between devices, gather_stage(): lax.ppermute(part, 'dp', shift_pairs(count, stride, size, step))  18.8 us
    unnamed x97, local copies, waits for them, and re-layouts  15.6 us
    all_gather x2, waiting for transfers between devices, spread(): return lax.all_gather(part, 'dp', axis=0, tiled=True)  14.7 us
  transfers between devices with their start and end apart: 60, of which 18 were waited for; matrix products, arithmetic and copies ran while one was open for 15% of the time, Pallas kernels for 28%

profile of v9, /device:TPU:0, one launch (start us, length us, event | category | flops | bytes accessed | tf_op | source)
XLA Modules:
  0.0 384.7 jit_solution(11061704591466031462)
XLA Ops:
  20.8 4.5 %shard_map.203 = (bf16[960,512]{1,0:T(8,128)(2,1)}, bf16[576,512]{1,0:T(8,128)(2,1)}, bf16[384,512]{1,0:T(8,128)(2,1)}) custom-call(bf16[480,512]{1,0:T(8,128)(2,1)} %get-tuple-element.197.refs_0_.refs_6_.refs_9_, bf16[480,512]{1,0:T(8,128)(2,1)} %copy-done.15, f32[480,1]{1,0:T(8,128)} %copy.27.refs_2_.refs_11_, f32[480,1]{1,0:T(8,128)} %copy.28.refs_3_.refs_12_, ...), custom_call_target="tpu_custom_call" | custom-call | flops 28311552 | bytes 147816 | tf_op jit(solution)/shard_map/pallas_call | solution.py:70
  28.0 11.3 %shard_map.204 = (bf16[576,512]{1,0:T(8,128)(2,1)}, f32[3,8,512]{2,1,0:T(8,128)}) custom-call(s32[2]{0:T(128)} %pad_add_fusion.refs_0_, s32[1,512]{1,0:T(1,128)} %broadcast_select_fusion.8.refs_1_, bf16[576,512]{1,0:T(8,128)(2,1)} %get-tuple-element.89.refs_2_, bf16[384,512]{1,0:T(8,128)(2,1)} %get-tuple-element.90.refs_3_.refs_4_, ...), custom_call_target="tpu_custom_call" | custom-call | flops 180000000 | bytes 84111 | tf_op jit(solution)/shard_map/pallas_call | solution.py:70
  43.0 4.0 %shard_map.205 = (bf16[576,512]{1,0:T(8,128)(2,1)}, bf16[384,512]{1,0:T(8,128)(2,1)}) custom-call(bf16[960,512]{1,0:T(8,128)(2,1)} %get-tuple-element.92.refs_0_.refs_7_, f32[32,512]{1,0:T(8,128)} %get-tuple-element.231.refs_4_.refs_1_.refs_3_, f32[32,512]{1,0:T(8,128)} %get-tuple-element.230.refs_5_.refs_2_.refs_4_, bf16[960,480]{1,0:T(8,128)(2,1)} %copy-done.16, ...), custom_call_target="tpu_custom_call" | custom-call | flops 28311552 | bytes 118210 | tf_op jit(solution)/shard_map/pallas_call | solution.py:70
  47.0 8.2 %collective-permute-done.9.refs_4_.refs_8_ = bf16[576,480]{1,0:T(8,128)(2,1)S(1)} collective-permute-done((bf16[576,480]{1,0:T(8,128)(2,1)S(1)}, bf16[576,480]{1,0:T(8,128)(2,1)S(1)}, u32[]{:S(2)}, u32[]{:S(2)}) %collective-permute-start.9) | collective-permute-done | bytes 552992 | tf_op jit(solution)/shard_map/ppermute | solution.py:463
  60.7 8.5 %shard_map.206 = (bf16[576,512]{1,0:T(8,128)(2,1)}, f32[3,8,512]{2,1,0:T(8,128)}) custom-call(s32[2]{0:T(128)} %pad_add_fusion.1.refs_0_, s32[1,512]{1,0:T(1,128)} %broadcast_select_fusion.8.refs_1_, bf16[576,512]{1,0:T(8,128)(2,1)} %get-tuple-element.95.refs_2_, bf16[384,512]{1,0:T(8,128)(2,1)} %get-tuple-element.96.refs_3_.refs_4_, ...), custom_call_target="tpu_custom_call" | custom-call | flops 180000000 | bytes 84111 | tf_op jit(solution)/shard_map/pallas_call | solution.py:70
  69.2 5.7 %shard_map.207 = (f32[960,512]{1,0:T(8,128)}, bf16[960,512]{1,0:T(8,128)(2,1)}) custom-call(bf16[576,512]{1,0:T(8,128)(2,1)} %get-tuple-element.91.refs_0_, bf16[576,512]{1,0:T(8,128)(2,1)} %get-tuple-element.97.refs_1_, bf16[576,480]{1,0:T(8,128)(2,1)} %bitcast.202, bf16[576,480]{1,0:T(8,128)(2,1)} %copy-done.23, bf16[576,480]{1,0:T(8,128)(2,1)} %copy-done.22, ...), custom_call_target="tpu_custom_call" | custom-call | flops 28311552 | bytes 219824 | tf_op jit(solution)/shard_map/pallas_call | solution.py:70
  75.0 4.8 %collective-permute-start.16 = (bf16[960,512]{1,0:T(8,128)(2,1)}, bf16[960,512]{1,0:T(8,128)(2,1)S(1)}, u32[]{:S(2)}, u32[]{:S(2)}) collective-permute-start(bf16[960,512]{1,0:T(8,128)(2,1)} %get-tuple-element.100.refs_0_), channel_id=1, source_target_pairs={{0,2},{2,0},{1,3},{3,1},{4,6},{6,4},{5,7},{7,5},{8,10},{10,8},{9,1... | collective-permute-start | bytes 2949128 | tf_op jit(solution)/shard_map/ppermute | solution.py:463
  83.7 15.8 %shard_map.208 = (f32[960,512]{1,0:T(8,128)}, f32[960,512]{1,0:T(8,128)}, bf16[1280,512]{1,0:T(8,128)(2,1)}, bf16[1280,512]{1,0:T(8,128)(2,1)}, bf16[1280,512]{1,0:T(8,128)(2,1)}) custom-call(bf16[960,512]{1,0:T(8,128)(2,1)} %get-tuple-element.100.refs_0_, bf16[960,512]{1,0:T(8,128)(2,1)} %copy-done, bf16[480,1280]{1,0:T(8,128)(2,1)} %refs_2_.3, ...), custom_call_target="tpu_custom_call" | custom-call | flops 226492416 | bytes 516096 | tf_op jit(solution)/shard_map/pallas_call | solution.py:70
  99.5 3.7 collective-permute-done.16.refs_0_.refs_1_
  104.2 15.1 %shard_map.209 = (bf16[960,512]{1,0:T(8,128)(2,1)}, bf16[960,512]{1,0:T(8,128)(2,1)}, bf16[1280,512]{1,0:T(8,128)(2,1)}, bf16[1280,512]{1,0:T(8,128)(2,1)}, bf16[1280,512]{1,0:T(8,128)(2,1)}) custom-call(bf16[960,512]{1,0:T(8,128)(2,1)} %copy-done.20, bf16[960,512]{1,0:T(8,128)(2,1)} %copy-done.7, bf16[480,1280]{1,0:T(8,128)(2,1)} %refs_2_.3, ...), custom_call_target="tpu_custom_call" | custom-call | flops 226492416 | bytes 457113 | tf_op jit(solution)/shard_map/pallas_call | solution.py:70
  119.3 7.2 %shard_map.210 = (bf16[4800,128]{1,0:T(8,128)(2,1)}, bf16[4800,128]{1,0:T(8,128)(2,1)}) custom-call(bf16[960,512]{1,0:T(8,128)(2,1)} %copy-done, bf16[960,512]{1,0:T(8,128)(2,1)} %copy-done.7, bf16[1280,512]{1,0:T(8,128)(2,1)} %get-tuple-element.102.refs_8_.refs_2_, bf16[1280,512]{1,0:T(8,128)(2,1)} %get-tuple-element.107.refs_3_), custom_call_target="tpu_custom_call" | custom-call | flops 75497472 | bytes 211353 | tf_op jit(solution)/shard_map/pallas_call | solution.py:70
  126.9 9.2 %shard_map.211 = (bf16[4800,128]{1,0:T(8,128)(2,1)}, bf16[4800,128]{1,0:T(8,128)(2,1)}, bf16[4800,128]{1,0:T(8,128)(2,1)}, bf16[4800,128]{1,0:T(8,128)(2,1)}) custom-call(bf16[960,512]{1,0:T(8,128)(2,1)} %get-tuple-element.100.refs_0_, bf16[960,512]{1,0:T(8,128)(2,1)} %copy-done.20, bf16[1280,512]{1,0:T(8,128)(2,1)} %get-tuple-element.110.refs_2_, ...), custom_call_target="tpu_custom_call" | custom-call | flops 150994944 | bytes 363724 | tf_op jit(solution)/shard_map/pallas_call | solution.py:70
  136.1 14.6 %collective-permute-done.17.refs_3_ = bf16[960,512]{1,0:T(8,128)(2,1)S(1)} collective-permute-done((bf16[960,512]{1,0:T(8,128)(2,1)S(1)}, bf16[960,512]{1,0:T(8,128)(2,1)S(1)}, u32[]{:S(2)}, u32[]{:S(2)}) %collective-permute-start.17) | collective-permute-done | bytes 983072 | tf_op jit(solution)/shard_map/ppermute | solution.py:463
  156.3 8.3 %shard_map.212 = (f32[960,512]{1,0:T(8,128)}, bf16[960,512]{1,0:T(8,128)(2,1)}, bf16[576,512]{1,0:T(8,128)(2,1)}, bf16[576,512]{1,0:T(8,128)(2,1)}, f32[2,16,480]{2,1,0:T(8,128)}) custom-call(bf16[960,512]{1,0:T(8,128)(2,1)} %copy-done, f32[960,512]{1,0:T(8,128)} %get-tuple-element.99.refs_1_, f32[960,512]{1,0:T(8,128)} %get-tuple-element.106.refs_2_, ...), custom_call_target="tpu_custom_call" | custom-call | flops 28311552 | bytes 369123 | tf_op jit(solution)/shard_map/pallas_call | solution.py:70
  164.6 6.3 %collective-permute-done.22 = bf16[4,600,128]{2,1,0:T(8,128)(2,1)} collective-permute-done((bf16[4,600,128]{2,1,0:T(8,128)(2,1)}, bf16[4,600,128]{2,1,0:T(8,128)(2,1)}, u32[]{:S(2)}, u32[]{:S(2)}) %collective-permute-start.22) | collective-permute-done | bytes 614432 | tf_op jit(solution)/shard_map/ppermute | solution.py:499
  183.1 10.1 %shard_map.213 = (f32[576,512]{1,0:T(8,128)}, f32[2,3,64,512]{3,2,1,0:T(8,128)}, bf16[2,3,64,512]{3,2,1,0:T(8,128)(2,1)}) custom-call(s32[2]{0:T(128)} %pad_add_fusion.1.refs_0_, s32[1,512]{1,0:T(1,128)} %broadcast_select_fusion.8.refs_1_, bf16[576,512]{1,0:T(8,128)(2,1)} %get-tuple-element.95.refs_2_, bf16[384,512]{1,0:T(8,128)(2,1)} %get-tuple-element.96.refs_3_.refs_4_, ...), custom_call_target="tpu_custom_call" | custom-call | flops 420000000 | bytes 154890 | tf_op jit(solution)/shard_map/pallas_call | solution.py:70
  203.6 6.1 %shard_map.214 = (f32[960,512]{1,0:T(8,128)}, bf16[1024,512]{1,0:T(8,128)(2,1)}, bf16[1024,512]{1,0:T(8,128)(2,1)}) custom-call(f32[576,512]{1,0:T(8,128)} %get-tuple-element.128.refs_0_, f32[2,3,64,512]{3,2,1,0:T(8,128)} %get-tuple-element.130.refs_1_, bf16[2,3,64,512]{3,2,1,0:T(8,128)(2,1)} %copy-done.38, ...), custom_call_target="tpu_custom_call" | custom-call | flops 56623104 | bytes 281395 | tf_op jit(solution)/shard_map/pallas_call | solution.py:70
  218.9 3.9 %collective-permute-start.35 = (bf16[576,480]{1,0:T(8,128)(2,1)S(1)}, bf16[576,480]{1,0:T(8,128)(2,1)S(1)}, u32[]{:S(2)}, u32[]{:S(2)}) collective-permute-start(bf16[576,480]{1,0:T(8,128)(2,1)S(1)} %fusion.refs_11_), channel_id=1, source_target_pairs={{0,2},{2,0},{1,3},{3,1},{4,6},{6,4},{5,7},{7,5},{8,10},{10,8},{9,1... | collective-permute-start | bytes 1658888 | tf_op jit(solution)/shard_map/ppermute | solution.py:463
  224.1 13.7 %shard_map.215 = (f32[576,512]{1,0:T(8,128)}, f32[2,3,64,512]{3,2,1,0:T(8,128)}, bf16[2,3,64,512]{3,2,1,0:T(8,128)(2,1)}) custom-call(s32[2]{0:T(128)} %pad_add_fusion.refs_0_, s32[1,512]{1,0:T(1,128)} %broadcast_select_fusion.8.refs_1_, bf16[576,512]{1,0:T(8,128)(2,1)} %get-tuple-element.89.refs_2_, bf16[384,512]{1,0:T(8,128)(2,1)} %get-tuple-element.90.refs_3_.refs_4_, ...), custom_call_target="tpu_custom_call" | custom-call | flops 420000000 | bytes 154890 | tf_op jit(solution)/shard_map/pallas_call | solution.py:70
  246.0 9.9 %shard_map.216 = (bf16[1024,512]{1,0:T(8,128)(2,1)}, bf16[1024,512]{1,0:T(8,128)(2,1)}, bf16[960,512]{1,0:T(8,128)(2,1)}) custom-call(f32[576,512]{1,0:T(8,128)} %get-tuple-element.143.refs_0_, f32[2,3,64,512]{3,2,1,0:T(8,128)} %get-tuple-element.144.refs_1_, bf16[2,3,64,512]{3,2,1,0:T(8,128)(2,1)} %collective-permute-done.36.refs_2_, ...), custom_call_target="tpu_custom_call" | custom-call | flops 56623104 | bytes 401318 | tf_op jit(solution)/shard_map/pallas_call | solution.py:70
  258.6 4.5 %collective-permute-done.37 = bf16[1024,512]{1,0:T(8,128)(2,1)S(1)} collective-permute-done((bf16[1024,512]{1,0:T(8,128)(2,1)S(1)}, bf16[1024,512]{1,0:T(8,128)(2,1)S(1)}, u32[]{:S(2)}, u32[]{:S(2)}) %collective-permute-start.37) | collective-permute-done | bytes 1048608 | tf_op jit(solution)/shard_map/ppermute | solution.py:463
  268.4 4.7 %collective-permute-done.43 = bf16[4,72,512]{2,1,0:T(8,128)(2,1)} collective-permute-done((bf16[4,72,512]{2,1,0:T(8,128)(2,1)S(1)}, bf16[4,72,512]{2,1,0:T(8,128)(2,1)}, u32[]{:S(2)}, u32[]{:S(2)}) %collective-permute-start.43) | collective-permute-done | bytes 294944 | tf_op jit(solution)/shard_map/ppermute | solution.py:499
  274.1 5.1 %collective-permute-start.53 = (bf16[600,128]{1,0:T(8,128)(2,1)}, bf16[600,128]{1,0:T(8,128)(2,1)S(1)}, u32[]{:S(2)}, u32[]{:S(2)}) collective-permute-start(bf16[600,128]{1,0:T(8,128)(2,1)} %get-tuple-element.179), channel_id=1, source_target_pairs={{0,8},{4,12},{8,16},{12,20},{16,24},{20,28},{24,0},{28,4},{1,9},{5... | collective-permute-start | bytes 460808 | tf_op jit(solution)/shard_map/ppermute | solution.py:520
  281.7 8.7 %collective-permute-done.42 = bf16[4,128,512]{2,1,0:T(8,128)(2,1)S(1)} collective-permute-done((bf16[4,128,512]{2,1,0:T(8,128)(2,1)}, bf16[4,128,512]{2,1,0:T(8,128)(2,1)S(1)}, u32[]{:S(2)}, u32[]{:S(2)}) %collective-permute-start.42) | collective-permute-done | bytes 524320 | tf_op jit(solution)/shard_map/ppermute | solution.py:499
  290.6 3.3 collective-permute-start.44
  296.6 5.1 %collective-permute-start.46 = (bf16[200,512]{1,0:T(8,128)(2,1)S(1)}, bf16[200,512]{1,0:T(8,128)(2,1)S(1)}, u32[]{:S(2)}, u32[]{:S(2)}) collective-permute-start(bf16[200,512]{1,0:T(8,128)(2,1)S(1)} %get-tuple-element.206), channel_id=1, source_target_pairs={{0,24},{4,28},{8,0},{12,4},{16,8},{20,12},{24,16},{28,20},{1,25},{... | collective-permute-start | bytes 614408 | tf_op jit(solution)/shard_map/ppermute | solution.py:499
  305.5 5.5 %collective-permute-done.45 = bf16[200,512]{1,0:T(8,128)(2,1)S(1)} collective-permute-done((bf16[200,512]{1,0:T(8,128)(2,1)S(1)}, bf16[200,512]{1,0:T(8,128)(2,1)S(1)}, u32[]{:S(2)}, u32[]{:S(2)}) %collective-permute-start.45) | collective-permute-done | bytes 204832 | tf_op jit(solution)/shard_map/ppermute | solution.py:499
  311.2 5.6 %collective-permute-start.49 = (bf16[200,512]{1,0:T(8,128)(2,1)S(1)}, bf16[200,512]{1,0:T(8,128)(2,1)S(1)}, u32[]{:S(2)}, u32[]{:S(2)}) collective-permute-start(bf16[200,512]{1,0:T(8,128)(2,1)S(1)} %get-tuple-element.181), channel_id=1, source_target_pairs={{0,8},{4,12},{8,16},{12,20},{16,24},{20,28},{24,0},{28,4},{1,9},{5... | collective-permute-start | bytes 614408 | tf_op jit(solution)/shard_map/ppermute | solution.py:520
  316.8 3.4 collective-permute-start.50
  322.6 5.1 %collective-permute-done.49 = bf16[200,512]{1,0:T(8,128)(2,1)S(1)} collective-permute-done((bf16[200,512]{1,0:T(8,128)(2,1)S(1)}, bf16[200,512]{1,0:T(8,128)(2,1)S(1)}, u32[]{:S(2)}, u32[]{:S(2)}) %collective-permute-start.49) | collective-permute-done | bytes 204832 | tf_op jit(solution)/shard_map/ppermute | solution.py:520
  327.7 6.6 %collective-permute-done.50 = bf16[200,512]{1,0:T(8,128)(2,1)S(1)} collective-permute-done((bf16[200,512]{1,0:T(8,128)(2,1)S(1)}, bf16[200,512]{1,0:T(8,128)(2,1)S(1)}, u32[]{:S(2)}, u32[]{:S(2)}) %collective-permute-start.50) | collective-permute-done | bytes 204832 | tf_op jit(solution)/shard_map/ppermute | solution.py:520
  339.4 14.7 %all-gather.3.cloned.1.call-done = bf16[4800,128]{1,0:T(8,128)(2,1)} async-done(((bf16[600,128]{1,0:T(8,128)(2,1)}), bf16[4800,128]{1,0:T(8,128)(2,1)}) %all-gather.3.cloned.1.call-update) | async-done | bytes 1228816 | tf_op jit(solution)/shard_map/all_gather | solution.py:547
  (300 shorter events, 126.4 us)
Async XLA Ops:
  7.2 328.6 %all-gather.5.cloned.1.call-start = ((), (), s32[]{:S(2)}) async-start(), calls=%async_computation.1 | async-start | bytes 1382400 | tf_op jit(solution)/shard_map/all_gather | solution.py:547
  9.2 30.1 %collective-permute-start.5 = (bf16[960,480]{1,0:T(8,128)(2,1)S(1)}, bf16[960,480]{1,0:T(8,128)(2,1)S(1)}, u32[]{:S(2)}, u32[]{:S(2)}) collective-permute-start(bf16[960,480]{1,0:T(8,128)(2,1)S(1)} %pad_maximum_fusion.1.refs_6_.refs_5_), channel_id=1, source_target_pairs={{0,2},{2,0},{1,3},{3,1},{4,6},{6,4},{5,7},{7,5},{8,10},{10,8},{9,1... | collective-permute-start | bytes 2764808 | tf_op jit(solution)/shard_map/ppermute | solution.py:463
  39.5 16.7 %collective-permute-start.8 = (bf16[576,480]{1,0:T(8,128)(2,1)S(1)}, bf16[576,480]{1,0:T(8,128)(2,1)S(1)}, u32[]{:S(2)}, u32[]{:S(2)}) collective-permute-start(bf16[576,480]{1,0:T(8,128)(2,1)S(1)} %bitcast.205), channel_id=1, source_target_pairs={{0,1},{1,0},{2,3},{3,2},{4,5},{5,4},{6,7},{7,6},{8,9},{9,8},{10,11... | collective-permute-start | bytes 1658888 | tf_op jit(solution)/shard_map/ppermute | solution.py:463
  55.7 24.1 %collective-permute-start.14 = (bf16[480,1280]{1,0:T(8,128)(2,1)}, bf16[480,1280]{1,0:T(8,128)(2,1)}, u32[]{:S(2)}, u32[]{:S(2)}) collective-permute-start(bf16[480,1280]{1,0:T(8,128)(2,1)} %bitcast.23.refs_6_), channel_id=1, source_target_pairs={{0,1},{1,0},{2,3},{3,2},{4,5},{5,4},{6,7},{7,6},{8,9},{9,8},{10,11... | collective-permute-start | bytes 3686408 | tf_op jit(solution)/shard_map/ppermute | solution.py:463
  55.7 24.1 %collective-permute-start.12 = (bf16[480,1280]{1,0:T(8,128)(2,1)}, bf16[480,1280]{1,0:T(8,128)(2,1)}, u32[]{:S(2)}, u32[]{:S(2)}) collective-permute-start(bf16[480,1280]{1,0:T(8,128)(2,1)} %refs_2_.3), channel_id=1, source_target_pairs={{0,1},{1,0},{2,3},{3,2},{4,5},{5,4},{6,7},{7,6},{8,9},{9,8},{10,11... | collective-permute-start | bytes 3686408 | tf_op jit(solution)/shard_map/ppermute | solution.py:463
  56.2 23.6 %collective-permute-start.13 = (bf16[480,1280]{1,0:T(8,128)(2,1)}, bf16[480,1280]{1,0:T(8,128)(2,1)}, u32[]{:S(2)}, u32[]{:S(2)}) collective-permute-start(bf16[480,1280]{1,0:T(8,128)(2,1)} %refs_4_.3), channel_id=1, source_target_pairs={{0,1},{1,0},{2,3},{3,2},{4,5},{5,4},{6,7},{7,6},{8,9},{9,8},{10,11... | collective-permute-start | bytes 3686408 | tf_op jit(solution)/shard_map/ppermute | solution.py:463
  58.1 24.6 %collective-permute-start.15 = (bf16[960,512]{1,0:T(8,128)(2,1)S(1)}, bf16[960,512]{1,0:T(8,128)(2,1)S(1)}, u32[]{:S(2)}, u32[]{:S(2)}) collective-permute-start(bf16[960,512]{1,0:T(8,128)(2,1)S(1)} %pad_maximum_fusion.2.refs_1_.refs_0_), channel_id=1, source_target_pairs={{0,2},{2,0},{1,3},{3,1},{4,6},{6,4},{5,7},{7,5},{8,10},{10,8},{9,1... | collective-permute-start | bytes 2949128 | tf_op jit(solution)/shard_map/ppermute | solution.py:463
  75.0 28.2 %collective-permute-start.16 = (bf16[960,512]{1,0:T(8,128)(2,1)}, bf16[960,512]{1,0:T(8,128)(2,1)S(1)}, u32[]{:S(2)}, u32[]{:S(2)}) collective-permute-start(bf16[960,512]{1,0:T(8,128)(2,1)} %get-tuple-element.100.refs_0_), channel_id=1, source_target_pairs={{0,2},{2,0},{1,3},{3,1},{4,6},{6,4},{5,7},{7,5},{8,10},{10,8},{9,1... | collective-permute-start | bytes 2949128 | tf_op jit(solution)/shard_map/ppermute | solution.py:463
  126.5 24.7 %collective-permute-start.19 = (bf16[4800,128]{1,0:T(8,128)(2,1)}, bf16[4800,128]{1,0:T(8,128)(2,1)S(1)}, u32[]{:S(2)}, u32[]{:S(2)}) collective-permute-start(bf16[4800,128]{1,0:T(8,128)(2,1)} %get-tuple-element.109), channel_id=1, source_target_pairs={{0,1},{1,0},{2,3},{3,2},{4,5},{5,4},{6,7},{7,6},{8,9},{9,8},{10,11... | collective-permute-start | bytes 3686408 | tf_op jit(solution)/shard_map/ppermute | solution.py:463
  126.5 24.2 %collective-permute-start.17 = (bf16[960,512]{1,0:T(8,128)(2,1)S(1)}, bf16[960,512]{1,0:T(8,128)(2,1)S(1)}, u32[]{:S(2)}, u32[]{:S(2)}) collective-permute-start(bf16[960,512]{1,0:T(8,128)(2,1)S(1)} %copy-done.45), channel_id=1, source_target_pairs={{0,2},{2,0},{1,3},{3,1},{4,6},{6,4},{5,7},{7,5},{8,10},{10,8},{9,1... | collective-permute-start | bytes 2949128 | tf_op jit(solution)/shard_map/ppermute | solution.py:463
  150.7 20.3 %collective-permute-start.20 = (bf16[4800,128]{1,0:T(8,128)(2,1)}, bf16[4800,128]{1,0:T(8,128)(2,1)S(1)}, u32[]{:S(2)}, u32[]{:S(2)}) collective-permute-start(bf16[4800,128]{1,0:T(8,128)(2,1)} %get-tuple-element.119), channel_id=1, source_target_pairs={{0,1},{1,0},{2,3},{3,2},{4,5},{5,4},{6,7},{7,6},{8,9},{9,8},{10,11... | collective-permute-start | bytes 3686408 | tf_op jit(solution)/shard_map/ppermute | solution.py:463
  150.7 20.3 %collective-permute-start.23 = (bf16[4800,128]{1,0:T(8,128)(2,1)}, bf16[4800,128]{1,0:T(8,128)(2,1)}, u32[]{:S(2)}, u32[]{:S(2)}) collective-permute-start(bf16[4800,128]{1,0:T(8,128)(2,1)} %get-tuple-element.126), channel_id=1, source_target_pairs={{0,1},{1,0},{2,3},{3,2},{4,5},{5,4},{6,7},{7,6},{8,9},{9,8},{10,11... | collective-permute-start | bytes 3686408 | tf_op jit(solution)/shard_map/ppermute | solution.py:463
  154.8 16.1 %collective-permute-start.22 = (bf16[4,600,128]{2,1,0:T(8,128)(2,1)}, bf16[4,600,128]{2,1,0:T(8,128)(2,1)}, u32[]{:S(2)}, u32[]{:S(2)}) collective-permute-start(bf16[4,600,128]{2,1,0:T(8,128)(2,1)} %dynamic-slice_bitcast_fusion.1), channel_id=1, source_target_pairs={{0,4},{4,0},{8,12},{12,8},{16,20},{20,16},{24,28},{28,24},{1,5},{5... | collective-permute-start | bytes 1843208 | tf_op jit(solution)/shard_map/ppermute | solution.py:499
  174.8 20.3 %collective-permute-start.21 = (bf16[4,600,128]{2,1,0:T(8,128)(2,1)}, bf16[4,600,128]{2,1,0:T(8,128)(2,1)S(1)}, u32[]{:S(2)}, u32[]{:S(2)}) collective-permute-start(bf16[4,600,128]{2,1,0:T(8,128)(2,1)} %dynamic-slice_bitcast_fusion.2), channel_id=1, source_target_pairs={{0,4},{4,0},{8,12},{12,8},{16,20},{20,16},{24,28},{28,24},{1,5},{5... | collective-permute-start | bytes 1843208 | tf_op jit(solution)/shard_map/ppermute | solution.py:499
  196.1 17.6 %collective-permute-start.31 = (bf16[4,600,128]{2,1,0:T(8,128)(2,1)S(1)}, bf16[4,600,128]{2,1,0:T(8,128)(2,1)S(1)}, u32[]{:S(2)}, u32[]{:S(2)}) collective-permute-start(bf16[4,600,128]{2,1,0:T(8,128)(2,1)S(1)} %dynamic-slice_bitcast_fusion), channel_id=1, source_target_pairs={{0,4},{4,0},{8,12},{12,8},{16,20},{20,16},{24,28},{28,24},{1,5},{5... | collective-permute-start | bytes 1843208 | tf_op jit(solution)/shard_map/ppermute | solution.py:499
  215.2 22.6 %collective-permute-start.34 = (bf16[1024,512]{1,0:T(8,128)(2,1)S(1)}, bf16[1024,512]{1,0:T(8,128)(2,1)S(1)}, u32[]{:S(2)}, u32[]{:S(2)}) collective-permute-start(bf16[1024,512]{1,0:T(8,128)(2,1)S(1)} %copy-done.42), channel_id=1, source_target_pairs={{0,1},{1,0},{2,3},{3,2},{4,5},{5,4},{6,7},{7,6},{8,9},{9,8},{10,11... | collective-permute-start | bytes 3145736 | tf_op jit(solution)/shard_map/ppermute | solution.py:463
  218.9 19.3 %collective-permute-start.35 = (bf16[576,480]{1,0:T(8,128)(2,1)S(1)}, bf16[576,480]{1,0:T(8,128)(2,1)S(1)}, u32[]{:S(2)}, u32[]{:S(2)}) collective-permute-start(bf16[576,480]{1,0:T(8,128)(2,1)S(1)} %fusion.refs_11_), channel_id=1, source_target_pairs={{0,2},{2,0},{1,3},{3,1},{4,6},{6,4},{5,7},{7,5},{8,10},{10,8},{9,1... | collective-permute-start | bytes 1658888 | tf_op jit(solution)/shard_map/ppermute | solution.py:463
  238.1 24.9 %collective-permute-start.37 = (bf16[1024,512]{1,0:T(8,128)(2,1)S(1)}, bf16[1024,512]{1,0:T(8,128)(2,1)S(1)}, u32[]{:S(2)}, u32[]{:S(2)}) collective-permute-start(bf16[1024,512]{1,0:T(8,128)(2,1)S(1)} %add_convert_fusion.4), channel_id=1, source_target_pairs={{0,2},{2,0},{1,3},{3,1},{4,6},{6,4},{5,7},{7,5},{8,10},{10,8},{9,1... | collective-permute-start | bytes 3145736 | tf_op jit(solution)/shard_map/ppermute | solution.py:463
  240.0 15.9 %collective-permute-start.38 = (bf16[600,128]{1,0:T(8,128)(2,1)}, bf16[600,128]{1,0:T(8,128)(2,1)S(1)}, u32[]{:S(2)}, u32[]{:S(2)}) collective-permute-start(bf16[600,128]{1,0:T(8,128)(2,1)} %get-tuple-element.209), channel_id=1, source_target_pairs={{0,8},{4,12},{8,16},{12,20},{16,24},{20,28},{24,0},{28,4},{1,9},{5... | collective-permute-start | bytes 460808 | tf_op jit(solution)/shard_map/ppermute | solution.py:499
  245.6 108.4 %all-gather.3.cloned.1.call-start = ((), (), s32[]{:S(2)}) async-start(), calls=%async_computation | async-start | bytes 1382400 | tf_op jit(solution)/shard_map/all_gather | solution.py:547
  267.2 23.2 %collective-permute-start.42 = (bf16[4,128,512]{2,1,0:T(8,128)(2,1)}, bf16[4,128,512]{2,1,0:T(8,128)(2,1)S(1)}, u32[]{:S(2)}, u32[]{:S(2)}) collective-permute-start(bf16[4,128,512]{2,1,0:T(8,128)(2,1)} %dynamic-slice_bitcast_fusion.3), channel_id=1, source_target_pairs={{0,4},{4,0},{8,12},{12,8},{16,20},{20,16},{24,28},{28,24},{1,5},{5... | collective-permute-start | bytes 1572872 | tf_op jit(solution)/shard_map/ppermute | solution.py:499
  268.1 52.1 %collective-permute-start.18 = (bf16[960,512]{1,0:T(8,128)(2,1)}, bf16[960,512]{1,0:T(8,128)(2,1)S(1)}, u32[]{:S(2)}, u32[]{:S(2)}) collective-permute-start(bf16[960,512]{1,0:T(8,128)(2,1)} %get-tuple-element.105), channel_id=1, source_target_pairs={{0,2},{2,0},{1,3},{3,1},{4,6},{6,4},{5,7},{7,5},{8,10},{10,8},{9,1... | collective-permute-start | bytes 2949128 | tf_op jit(solution)/shard_map/ppermute | solution.py:463
  274.1 19.8 %collective-permute-start.53 = (bf16[600,128]{1,0:T(8,128)(2,1)}, bf16[600,128]{1,0:T(8,128)(2,1)S(1)}, u32[]{:S(2)}, u32[]{:S(2)}) collective-permute-start(bf16[600,128]{1,0:T(8,128)(2,1)} %get-tuple-element.179), channel_id=1, source_target_pairs={{0,8},{4,12},{8,16},{12,20},{16,24},{20,28},{24,0},{28,4},{1,9},{5... | collective-permute-start | bytes 460808 | tf_op jit(solution)/shard_map/ppermute | solution.py:520
  279.2 17.3 %collective-permute-start.54 = (bf16[600,128]{1,0:T(8,128)(2,1)}, bf16[600,128]{1,0:T(8,128)(2,1)S(1)}, u32[]{:S(2)}, u32[]{:S(2)}) collective-permute-start(bf16[600,128]{1,0:T(8,128)(2,1)} %get-tuple-element.179), channel_id=1, source_target_pairs={{0,16},{4,20},{8,24},{12,28},{16,0},{20,4},{24,8},{28,12},{1,17},{... | collective-permute-start | bytes 460808 | tf_op jit(solution)/shard_map/ppermute | solution.py:520
  279.2 22.4 %collective-permute-start.55 = (bf16[600,128]{1,0:T(8,128)(2,1)}, bf16[600,128]{1,0:T(8,128)(2,1)S(1)}, u32[]{:S(2)}, u32[]{:S(2)}) collective-permute-start(bf16[600,128]{1,0:T(8,128)(2,1)} %get-tuple-element.179), channel_id=1, source_target_pairs={{0,24},{4,28},{8,0},{12,4},{16,8},{20,12},{24,16},{28,20},{1,25},{... | collective-permute-start | bytes 460808 | tf_op jit(solution)/shard_map/ppermute | solution.py:520
  293.9 17.1 %collective-permute-start.45 = (bf16[200,512]{1,0:T(8,128)(2,1)S(1)}, bf16[200,512]{1,0:T(8,128)(2,1)S(1)}, u32[]{:S(2)}, u32[]{:S(2)}) collective-permute-start(bf16[200,512]{1,0:T(8,128)(2,1)S(1)} %get-tuple-element.205), channel_id=1, source_target_pairs={{0,16},{4,20},{8,24},{12,28},{16,0},{20,4},{24,8},{28,12},{1,17},{... | collective-permute-start | bytes 614408 | tf_op jit(solution)/shard_map/ppermute | solution.py:499
  303.7 56.3 %collective-permute-start.56 = (bf16[4,600,128]{2,1,0:T(8,128)(2,1)}, bf16[4,600,128]{2,1,0:T(8,128)(2,1)}, u32[]{:S(2)}, u32[]{:S(2)}) collective-permute-start(bf16[4,600,128]{2,1,0:T(8,128)(2,1)} %bitcast_dynamic-update-slice_fusion.4), channel_id=1, source_target_pairs={{0,4},{4,0},{8,12},{12,8},{16,20},{20,16},{24,28},{28,24},{1,5},{5... | collective-permute-start | bytes 1843208 | tf_op jit(solution)/shard_map/ppermute | solution.py:520
  305.4 52.2 %collective-permute-start.48 = (bf16[480,512]{1,0:T(8,128)(2,1)}, bf16[480,512]{1,0:T(8,128)(2,1)}, u32[]{:S(2)}, u32[]{:S(2)}) collective-permute-start(bf16[480,512]{1,0:T(8,128)(2,1)} %slice.168), channel_id=1, source_target_pairs={{0,1},{1,0},{2,3},{3,2},{4,5},{5,4},{6,7},{7,6},{8,9},{9,8},{10,11... | collective-permute-start | bytes 1474568 | tf_op jit(solution)/shard_map/ppermute | solution.py:463
  311.2 16.5 %collective-permute-start.49 = (bf16[200,512]{1,0:T(8,128)(2,1)S(1)}, bf16[200,512]{1,0:T(8,128)(2,1)S(1)}, u32[]{:S(2)}, u32[]{:S(2)}) collective-permute-start(bf16[200,512]{1,0:T(8,128)(2,1)S(1)} %get-tuple-element.181), channel_id=1, source_target_pairs={{0,8},{4,12},{8,16},{12,20},{16,24},{20,28},{24,0},{28,4},{1,9},{5... | collective-permute-start | bytes 614408 | tf_op jit(solution)/shard_map/ppermute | solution.py:520
  316.8 17.6 %collective-permute-start.50 = (bf16[200,512]{1,0:T(8,128)(2,1)S(1)}, bf16[200,512]{1,0:T(8,128)(2,1)S(1)}, u32[]{:S(2)}, u32[]{:S(2)}) collective-permute-start(bf16[200,512]{1,0:T(8,128)(2,1)S(1)} %get-tuple-element.181), channel_id=1, source_target_pairs={{0,16},{4,20},{8,24},{12,28},{16,0},{20,4},{24,8},{28,12},{1,17},{... | collective-permute-start | bytes 614408 | tf_op jit(solution)/shard_map/ppermute | solution.py:520
  327.7 39.5 %collective-permute-start.47 = (bf16[480,512]{1,0:T(8,128)(2,1)}, bf16[480,512]{1,0:T(8,128)(2,1)}, u32[]{:S(2)}, u32[]{:S(2)}) collective-permute-start(bf16[480,512]{1,0:T(8,128)(2,1)} %slice.194), channel_id=1, source_target_pairs={{0,1},{1,0},{2,3},{3,2},{4,5},{5,4},{6,7},{7,6},{8,9},{9,8},{10,11... | collective-permute-start | bytes 1474568 | tf_op jit(solution)/shard_map/ppermute | solution.py:463
  334.4 35.2 %collective-permute-start.52 = (bf16[4,200,512]{2,1,0:T(8,128)(2,1)S(1)}, bf16[4,200,512]{2,1,0:T(8,128)(2,1)}, u32[]{:S(2)}, u32[]{:S(2)}) collective-permute-start(bf16[4,200,512]{2,1,0:T(8,128)(2,1)S(1)} %bitcast_dynamic-update-slice_fusion), channel_id=1, source_target_pairs={{0,4},{4,0},{8,12},{12,8},{16,20},{20,16},{24,28},{28,24},{1,5},{5... | collective-permute-start | bytes 2457608 | tf_op jit(solution)/shard_map/ppermute | solution.py:520
  (75 other events, 553.4 us)
Sparse Core Ops, SparseCore 0:
  245.8 49.5 all-gather.4
  297.6 56.3 all-gather.2
